TPU v7x, 32 devices: a whole 2x2x4 slice. The times are simulated.
32 devices in a mesh: dp: 8 (over y, x, core), seq: 4 (over z).
Axes of the slice: x: 2, y: 2, z: 4, core: 2. Of those that a mesh axis runs over, the one named last changes fastest.
Arguments:
- audio: float32 [8, 163840], P(None, ('dp', 'seq')), may hold values from -0.4 to 0.4
- starts: int32 [8], replicated, may hold values from 0 to 81919, as said below
- lengths: int32 [8], replicated, may hold values from 40960 to 163840, as said below
- slots: int32 [8], replicated, may hold values from 0 to 7, each once
- conv1_weight: bfloat16 [9, 256], replicated, may hold values from -2 to 2
- conv2_weight: bfloat16 [2304, 256], replicated, may hold values from -0.125 to 0.125
- proj_weight: bfloat16 [5120, 1024], P('dp'), may hold values from -0.078125 to 0.078125
- qkv_weight: bfloat16 [1024, 3072], P('dp'), may hold values from -8 to 8
- out_weight: bfloat16 [1024, 1024], P(None, 'dp'), may hold values from -0.1875 to 0.1875
Outputs:
- regrouped: bfloat16 [8, 8, 4, 8, 1024], P('dp', None, 'seq')
- attended: bfloat16 [8, 8, 4, 8, 1024], P('dp', None, 'seq')
Inputs may be any that keep to these rules, and one draw needn't show every extreme that they name: starts plus lengths is at most 163840 for every stream; some stream's utterance covers the whole stream, and some other stream's utterance starts at 81919. `lengths`: some stream's utterance has exactly 40960 samples. `slots`: every row number appears once.
All inputs are finite; a program needn't handle non-finite values.
Results may differ from a plain program's by a relative error of at most 0.013.
Values may be sent and summed in bfloat16 or wider, within the bound.
No kernel may reach another device: no remote copies, remote signals or barrier semaphores. Data moves between devices by JAX's collectives and lax.ppermute only.
A program may use at most 128 MiB of HBM per device.

v0:
```python
import functools
import math

import jax
import jax.numpy as jnp
import numpy as np
from jax import lax
from jax.experimental import pallas as pl
from jax.experimental.pallas import tpu as pltpu
from jax.sharding import PartitionSpec as P

HEADS = 8
HEAD_DIM = 128
MELS = 80
BANDS = MELS // 4
N_FFT = 512
HOP = 160
W = 8
RIM = 384
SPAN = 4 * HOP
JS = W + 1
LANES = 128
SAMPLE_RATE = 16000.0
EPS_LOG = 1e-06
EPS_NORM = 1e-05
MASKED = -1e30
F32 = jnp.float32
BF16 = jnp.bfloat16
MIB = 1 << 20


def mel_table(size, bands):
    count = size // 2 + 1
    highest = 2595.0 * math.log10(1.0 + SAMPLE_RATE / 1400.0)
    points = np.linspace(0.0, highest, bands + 2)
    edges = 700.0 * (10.0 ** (points / 2595.0) - 1.0)
    edges[0] = 0.0
    edges[-1] = SAMPLE_RATE / 2.0
    frequency = np.arange(count) * (SAMPLE_RATE / size)
    lower = edges[:-2][None, :]
    middle = edges[1:-1][None, :]
    upper = edges[2:][None, :]
    rising = (frequency[:, None] - lower) / (middle - lower)
    falling = (upper - frequency[:, None]) / (upper - middle)
    return np.maximum(0.0, np.minimum(rising, falling)).astype(np.float32)


def spectrum_table(size):
    sample = np.arange(size)
    phase = sample[:, None] * np.arange(size // 2)[None, :] % size
    angle = phase * (2.0 * math.pi / size)
    window = 0.5 - 0.5 * np.cos(sample * (2.0 * math.pi / size))
    both = np.concatenate([np.cos(angle), np.sin(angle)], axis=1) * window[:, None]
    filters = np.zeros((size, LANES))
    filters[: size // 2, :MELS] = mel_table(size, MELS)[: size // 2]
    return np.concatenate([both, filters], axis=1).astype(np.float32)


def vmem():
    return pl.BlockSpec(memory_space=pltpu.VMEM)


def smem():
    return pl.BlockSpec(memory_space=pltpu.SMEM)


def anywhere():
    return pl.BlockSpec(memory_space=pl.ANY)


def params(mib):
    return pltpu.CompilerParams(vmem_limit_bytes=mib * MIB)


def cost(flops, moved):
    return pl.CostEstimate(flops=int(flops), bytes_accessed=int(moved), transcendentals=0)


def place(parts):
    mine = lax.axis_index("dp")
    copies = lax.axis_size("dp") // parts
    return mine // copies, mine % copies


def start_all(copies):
    for copy in copies:
        copy.start()


def wait_all(copies):
    for copy in copies:
        copy.wait()


def iota(rows, columns, axis):
    return lax.broadcasted_iota(jnp.int32, (rows, columns), axis)


def quotient(index, step, count):
    result = jnp.zeros_like(index)
    for i in range(1, count):
        result += (index >= i * step).astype(jnp.int32)
    return result


def one_hot(target, count):
    return (iota(target.shape[0], count, 1) == target).astype(F32).astype(BF16)


def frame_order(windows):
    count = windows * W
    row = iota(count, 1, 0)
    k = quotient(row, W, windows)
    return one_hot((row - k * W) * windows + k, count)


def first_samples(windows, group):
    row = iota(windows * W, 1, 0)
    return (row + quotient(row, W, windows) * (group - 1) * W) * SPAN


def key_samples(windows, group):
    lane = iota(1, windows * W, 1)
    t = quotient(lane, windows, W)
    return ((lane - t * windows) * group * W + t) * SPAN


def mix_columns(parts, qkv, mix_outs, sems):
    part, _ = place(parts)
    features = qkv.shape[1] // 3
    width = features // parts
    copies = []
    for step in range(parts):
        first = pl.multiple_of((part ^ step) * width, LANES)
        for kind in range(3):
            source = qkv.at[:, pl.ds(kind * features + first, width)]
            target = mix_outs[step].at[:, pl.ds(kind * width, width)]
            copies.append(pltpu.make_async_copy(source, target, sems.at[len(copies)]))
    return copies


def banded_weights(width, conv1_ref, banded_out):
    taps, channels = conv1_ref.shape
    row = lax.broadcasted_iota(jnp.int32, (LANES, taps), 0)
    tap = lax.broadcasted_iota(jnp.int32, (LANES, taps), 1)
    line = (tap >= 3).astype(jnp.int32) + (tap >= 6).astype(jnp.int32)
    target = line * (width - 3) + tap + 1
    weight = conv1_ref[...]
    for g in range(banded_out.shape[1] // channels):
        select = (row == target + 2 * g).astype(F32).astype(BF16)
        banded_out[:, g * channels : (g + 1) * channels] = jnp.dot(
            select, weight, preferred_element_type=F32
        ).astype(BF16)


def mel_kernel(parts, group, slots_ref, rim_ref, audio_ref, table_ref, qkv_ref, out_ref, *refs):
    mix_outs, (ext, table, qkv, mix_sems, sems) = refs[:parts], refs[parts:]
    load_audio = pltpu.make_async_copy(audio_ref, ext.at[:, pl.ds(RIM, audio_ref.shape[1])], sems.at[0])
    load_table = pltpu.make_async_copy(table_ref, table, sems.at[1])
    load_audio.start()
    load_table.start()
    load_qkv = pltpu.make_async_copy(qkv_ref, qkv, sems.at[2])
    load_qkv.start()
    streams = audio_ref.shape[0]
    rows = W * streams
    ext[:, :RIM] = rim_ref[...]
    column = iota(1, rows, 1)
    early = quotient(column, streams, W)
    target = jnp.zeros((1, rows), jnp.int32)
    for u in range(streams):
        target = jnp.where(column - early * streams == u, slots_ref[u] * W + early, target)
    routing = (target == iota(rows, rows, 0)).astype(F32).astype(BF16)
    load_audio.wait()
    phases = []
    for phase in range(4):
        start = HOP * phase + 32
        base, shift = start // LANES * LANES, start % LANES
        length = N_FFT + (LANES if shift else 0)
        block = jnp.concatenate(
            [ext[:, SPAN * j + base : SPAN * j + base + length] for j in range(W)], axis=0
        )
        if shift:
            block = pltpu.roll(block, length - shift, 1)[:, :N_FFT]
        phases.append(block)
    frames = jnp.concatenate(phases, axis=0)
    load_table.wait()
    spectrum = jnp.dot(
        frames, table[:, :N_FFT], precision=lax.Precision.HIGHEST, preferred_element_type=F32
    )
    load_qkv.wait()
    pieces = mix_columns(parts, qkv, mix_outs, mix_sems)
    start_all(pieces)
    half = N_FFT // 2
    real, imag = spectrum[:, :half], spectrum[:, half:]
    power = real * real + imag * imag
    mel_power = jnp.dot(
        power, table[:half, N_FFT:], precision=lax.Precision.HIGHEST, preferred_element_type=F32
    )
    log_mel = jnp.log(mel_power + EPS_LOG)
    share = BANDS // parts
    width = 4 * share + 4
    lane = iota(rows, LANES, 1)
    blocks = []
    for part in range(parts):
        first = 4 * share * part - 4
        block = jnp.zeros((rows, LANES), F32)
        for phase in range(4):
            band = lane - width * phase + first
            here = (lane >= width * phase) & (lane < width * (phase + 1)) & (band >= 0) & (band < MELS)
            shift = (width * phase - first) % LANES
            frame = log_mel[phase * rows : (phase + 1) * rows]
            block = jnp.where(here, pltpu.roll(frame, shift, 1) if shift else frame, block)
        blocks.append(block.astype(BF16))
    routed = jnp.dot(routing, jnp.concatenate(blocks, axis=1), preferred_element_type=F32)
    copies = streams // group
    for part in range(parts):
        for copy in range(copies):
            for plane in range(group):
                row = plane * copies + copy
                out_ref[(part * copies + copy) * group + plane] = routed[
                    row * W : (row + 1) * W, part * LANES : (part + 1) * LANES
                ].astype(BF16)
    wait_all(pieces)


def stacked(parts, pieces, stack_out, sems, base):
    part, _ = place(parts)
    return [
        pltpu.make_async_copy(pieces[step], stack_out.at[part ^ step], sems.at[base + step])
        for step in range(parts)
    ]


def five_frames(part, width, windows, group, payload):
    n = windows * group
    row = iota(JS * n, 1, 0)
    j = quotient(row, n, JS)
    s = quotient(row - j * n, windows, group)
    window = (row - j * n - s * windows) * group + s
    before = jnp.where(j > 0, window * W + j - 1, window * W - 1)
    same = jnp.where(j < W, window * W + j, -1)
    lane = iota(payload.shape[0], LANES, 1)
    first = jnp.where(lane < 3 * width, pltpu.roll(payload, LANES - width, 1), 0.0).astype(BF16)
    last = (lane >= 3 * width) & (lane < 5 * width)
    second = jnp.where(last, pltpu.roll(payload, 3 * width, 1), 0.0).astype(BF16)
    result = jnp.dot(one_hot(before, n * W), first, preferred_element_type=F32)
    result += jnp.dot(one_hot(same, n * W), second, preferred_element_type=F32)
    lane = iota(1, LANES, 1)
    band = lane - quotient(lane, width, 3) * width - 4 + (width - 4) * part
    silent = (row == 0) & ((lane < 3 * width) & (band >= 0))
    return jnp.where(silent, jnp.log(jnp.full(result.shape, EPS_LOG, F32)), result)


def conv_kernel(parts, width, windows, mel_ref, conv1_ref, conv2_ref, *refs):
    part, copy_index = place(parts)
    copies = lax.axis_size("dp") // parts
    proj_refs, refs = refs[:copies], refs[copies:]
    weight_refs, refs = refs[:parts], refs[parts:]
    outs_refs, refs = refs[:parts], refs[parts:]
    stack_out, banded_ref, even, odd, second, conv2, proj, partial, sems = refs
    load_conv2 = pltpu.make_async_copy(conv2_ref, conv2, sems.at[0])
    load_conv2.start()
    loads = []
    for step in range(copies):
        slot = copy_index ^ step
        loads.append(pltpu.make_async_copy(proj_refs[step], proj.at[slot], sems.at[1 + step]))
    loads += stacked(parts, weight_refs, stack_out, sems, 1 + copies)
    start_all(loads)
    banded_weights(width, conv1_ref, banded_ref)
    n = mel_ref.shape[0]
    payload = mel_ref[...].astype(F32).reshape(n * W, LANES)
    evens = five_frames(part, width, windows, n // windows, payload)
    odds = pltpu.roll(evens[: W * n], LANES - 2 * width, 1).astype(BF16)
    evens = evens.astype(BF16)
    channels = conv2.shape[1]
    outs = banded_ref.shape[1] // channels
    for g in range(outs):
        lanes = slice(g * channels, (g + 1) * channels)
        weight = banded_ref[:, lanes]
        even[:, lanes] = jax.nn.relu(jnp.dot(evens, weight, preferred_element_type=F32)).astype(BF16)
        odd[:, lanes] = jax.nn.relu(jnp.dot(odds, weight, preferred_element_type=F32)).astype(BF16)

    load_conv2.wait()
    for h in range((outs - 1) // 2):
        lanes = slice(2 * h * channels, (2 * h + 3) * channels)
        depth = 3 * channels
        total = jnp.dot(even[: W * n, lanes], conv2[:depth], preferred_element_type=F32)
        total += jnp.dot(odd[:, lanes], conv2[depth : 2 * depth], preferred_element_type=F32)
        total += jnp.dot(even[n:, lanes], conv2[2 * depth :], preferred_element_type=F32)
        second[:, h * channels : (h + 1) * channels] = jax.nn.relu(total).astype(BF16)
    wait_all(loads)
    weights = proj[...].reshape(second.shape[1], proj.shape[2])
    partial[...] = jnp.dot(second[...], weights, preferred_element_type=F32)
    for step in range(parts):
        plane = (part ^ step)
        outs_refs[step][...] = jnp.concatenate(
            [partial[pl.ds(pl.multiple_of(t * n + plane * windows, 8), windows), :] for t in range(W)], axis=0
        ).astype(BF16)


def bounds(row, slots_ref, starts_ref, lengths_ref):
    begin, span = jnp.int32(0), jnp.int32(0)
    for u in range(slots_ref.shape[0]):
        chosen = slots_ref[u] == row
        begin = begin + jnp.where(chosen, starts_ref[u], 0)
        span = span + jnp.where(chosen, lengths_ref[u], 0)
    return begin, begin + span


def norm_kernel(parts, windows, group, slots_ref, starts_ref, lengths_ref, *refs):
    part, copy_index = place(parts)
    copies = lax.axis_size("dp") // parts
    part_refs, refs = refs[:parts], refs[parts:]
    piece_refs, refs = refs[:parts], refs[parts:]
    rows_out, normed_out, stack_out, sems = refs
    moves = stacked(parts, piece_refs, stack_out, sems, 0)
    start_all(moves)
    row = lax.axis_index("seq") * copies + copy_index
    begin, end = bounds(row, slots_ref, starts_ref, lengths_ref)
    total = part_refs[0][...].astype(F32)
    for step in range(1, parts):
        total += part_refs[step][...].astype(F32)
    encoded = total.astype(BF16)
    values = encoded.astype(F32)
    mean = jnp.mean(values, axis=-1, keepdims=True)
    centered = values - mean
    variance = jnp.mean(centered * centered, axis=-1, keepdims=True)
    normed_out[...] = (centered * lax.rsqrt(variance + EPS_NORM)).astype(BF16)
    ordered = jnp.dot(frame_order(windows), encoded, preferred_element_type=F32)
    sample = first_samples(windows, group) + part * (W * SPAN)
    valid = (sample >= begin) & (sample < end)
    rows_out[...] = jnp.where(valid, ordered, 0.0).astype(BF16)
    wait_all(moves)


def attention_kernel(parts, windows, group, slots_ref, starts_ref, lengths_ref, rows_ref, *refs):
    part, copy_index = place(parts)
    copies = lax.axis_size("dp") // parts
    normed_refs, refs = refs[:parts], refs[parts:]
    stack_refs, refs = refs[:copies], refs[copies:]
    outs_refs, (pieces,) = refs[:parts], refs[parts:]
    row = lax.axis_index("seq") * copies + copy_index
    begin, end = bounds(row, slots_ref, starts_ref, lengths_ref)
    masks = []
    for step in range(parts):
        plane = part ^ step
        sample = key_samples(windows, group) + plane * (W * SPAN)
        masks.append(((sample >= begin) & (sample < end)).astype(F32))
    valid = jnp.concatenate(masks, axis=1) > 0.5
    local = normed_refs[0].shape[0]
    depth = pieces.shape[2]
    for step in range(parts):
        for piece in range(windows):
            pieces[piece, step * local : (step + 1) * local, :] = normed_refs[step][
                :, piece * depth : (piece + 1) * depth
            ]
    mixed = 0.0
    for step in range(copies):
        slot = copy_index ^ step
        normed = jnp.concatenate([pieces[piece * copies + slot] for piece in range(parts)], axis=1)
        weights = stack_refs[step][...].reshape(parts * depth, stack_refs[step].shape[2])
        mixed += jnp.dot(normed, weights, preferred_element_type=F32)
    mixed = mixed.astype(BF16)
    width = mixed.shape[1] // 3
    scale = HEAD_DIM ** (-0.5)
    for head in range(width // HEAD_DIM):
        at = head * HEAD_DIM
        query = mixed[:, at : at + HEAD_DIM]
        key = mixed[:, width + at : width + at + HEAD_DIM]
        value = mixed[:, 2 * width + at : 2 * width + at + HEAD_DIM]
        scores = lax.dot_general(query, key, (((1,), (1,)), ((), ())), preferred_element_type=F32) * scale
        masked = jnp.where(valid, scores, MASKED)
        peak = jnp.max(masked, axis=1, keepdims=True)
        weight = jnp.where(valid, jnp.exp(masked - peak), 0.0)
        total = jnp.sum(weight, axis=1, keepdims=True)
        summed = jnp.dot(weight.astype(BF16), value, preferred_element_type=F32)
        context = (summed / total).astype(BF16)
        for step in range(parts):
            outs_refs[step][:, at : at + HEAD_DIM] = context[step * local : (step + 1) * local]
    outs_refs[0][:, width:] = rows_ref[...]


def output_kernel(parts, windows, group, slots_ref, starts_ref, lengths_ref, *refs):
    context_refs, refs = refs[:parts], refs[parts:]
    stack_refs, refs = refs[: windows // parts], refs[windows // parts :]
    rows_out, out_ref, context, pieces = refs
    _, copy_index = place(parts)
    copies = windows // parts
    plane = lax.axis_index("seq")
    begin, end = bounds(lax.axis_index("dp"), slots_ref, starts_ref, lengths_ref)
    head_width = context_refs[-1].shape[1]
    rows_out[...] = context_refs[0][:, head_width:]
    for step in range(parts):
        at = pl.multiple_of((plane ^ step) * head_width, LANES)
        context[:, pl.ds(at, head_width)] = context_refs[step][:, :head_width]
    ordered = jnp.dot(frame_order(windows), context[...], preferred_element_type=F32).astype(BF16)
    sample = first_samples(windows, group) + plane * (W * SPAN)
    valid = (sample >= begin) & (sample < end)
    for step in range(copies):
        slot = copy_index ^ step
        for piece in range(parts):
            pieces[piece * copies + slot] = jnp.dot(
                ordered, stack_refs[step][piece], preferred_element_type=F32
            )
    result = jnp.concatenate([pieces[d] for d in range(windows)], axis=1)
    out_ref[...] = jnp.where(valid, result, 0.0).astype(BF16)


def on_device(
    audio, starts, lengths, slots, conv1_weight, conv2_weight, proj_weight, qkv_weight, out_weight
):
    streams = audio.shape[0]
    windows = lax.axis_size("dp")
    group = lax.axis_size("seq")
    parts = group
    copies = windows // parts
    assert BANDS % parts == 0 and streams == copies * group and streams == windows
    assert parts & (parts - 1) == 0 and copies & (copies - 1) == 0
    share = BANDS // parts
    width = 4 * share + 4
    channels = conv1_weight.shape[1]
    features = proj_weight.shape[1]
    head_width = features // parts
    local = windows * W
    sources = windows * group
    n = sources
    outs = 2 * share + 1

    route = [(i, i + 1) for i in range(sources - 1)]
    rim = lax.ppermute(audio[:, audio.shape[1] - RIM :], ("dp", "seq"), route)

    def to_part(block, step):
        pairs = [(p * copies + c, (p ^ step) * copies + c) for p in range(parts) for c in range(copies)]
        return lax.ppermute(block, "dp", pairs)

    def to_copy(block, step):
        pairs = [(p * copies + c, p * copies + (c ^ step)) for p in range(parts) for c in range(copies)]
        return lax.ppermute(block, "dp", pairs)

    def to_owner(block, step):
        pairs = []
        for p in range(parts):
            for c in range(copies):
                for z in range(group):
                    pairs.append(((p * copies + c) * group + z, (z * copies + c) * group + (p ^ step)))
        return lax.ppermute(block, ("dp", "seq"), pairs)

    scale = sources // 32
    proj_all = [proj_weight] + [to_copy(proj_weight, step) for step in range(1, copies)]

    out_all = [out_weight] + [to_part(out_weight, step) for step in range(1, parts)]
    mix_piece = jax.ShapeDtypeStruct((qkv_weight.shape[0], 3 * head_width), BF16)

    table = jnp.asarray(spectrum_table(N_FFT))
    mel, *mix_all = pl.pallas_call(
        functools.partial(mel_kernel, parts, group),
        out_shape=tuple([jax.ShapeDtypeStruct((sources, W, LANES), BF16)] + [mix_piece] * parts),
        in_specs=[smem(), vmem()] + [anywhere()] * 3,
        out_specs=tuple([vmem()] + [anywhere()] * parts),
        scratch_shapes=[
            pltpu.VMEM((streams, RIM + audio.shape[1]), F32),
            pltpu.VMEM(table.shape, F32),
            pltpu.VMEM(qkv_weight.shape, BF16),
            pltpu.SemaphoreType.DMA((3 * parts,)),
            pltpu.SemaphoreType.DMA((3,)),
        ],
        compiler_params=params(60),
        cost_estimate=cost(2e9, 2e6),
        name="log_mel",
    )(slots, rim, audio, table, qkv_weight)
    mix_all = [mix_all[0]] + [to_part(mix_all[step], step) for step in range(1, parts)]
    mel = lax.all_to_all(mel, ("dp", "seq"), split_axis=0, concat_axis=0, tiled=True)

    block = jax.ShapeDtypeStruct((local, features), BF16)
    *partials, stack = pl.pallas_call(
        functools.partial(conv_kernel, parts, width, windows),
        out_shape=tuple([block] * parts + [jax.ShapeDtypeStruct((parts,) + out_weight.shape, BF16)]),
        in_specs=[vmem()] * 2 + [anywhere()] * (1 + copies + parts),
        out_specs=tuple([vmem()] * (parts + 1)),
        scratch_shapes=[
            pltpu.VMEM((LANES, outs * channels), BF16),
            pltpu.VMEM((JS * n, outs * channels), BF16),
            pltpu.VMEM((W * n, outs * channels), BF16),
            pltpu.VMEM((W * n, share * channels), BF16),
            pltpu.VMEM(conv2_weight.shape, BF16),
            pltpu.VMEM((copies,) + proj_weight.shape, BF16),
            pltpu.VMEM((W * n, features), F32),
            pltpu.SemaphoreType.DMA((1 + copies + parts,)),
        ],
        compiler_params=params(min(40 + 4 * scale, 56)),
        cost_estimate=cost(2e9, 4e6),
        name="conv",
    )(mel, conv1_weight, conv2_weight, *proj_all, *out_all)
    out_stacks = [stack] + [to_copy(stack, step) for step in range(1, copies)]
    partials = [partials[0]] + [to_part(partials[step], step) for step in range(1, parts)]

    regrouped, normed, stack = pl.pallas_call(
        functools.partial(norm_kernel, parts, windows, group),
        out_shape=(block, block, jax.ShapeDtypeStruct((parts,) + mix_piece.shape, BF16)),
        in_specs=[smem()] * 3 + [vmem()] * parts + [anywhere()] * parts,
        out_specs=(vmem(), vmem(), vmem()),
        scratch_shapes=[pltpu.SemaphoreType.DMA((parts,))],
        compiler_params=params(min(12 * scale, 32)),
        cost_estimate=cost(1e8, 1e6),
        name="layer_norm",
    )(slots, starts, lengths, *partials, *mix_all)
    mix_stacks = [stack] + [to_copy(stack, step) for step in range(1, copies)]
    normed = [normed] + [to_part(normed, step) for step in range(1, parts)]

    first = jax.ShapeDtypeStruct((local, head_width + features), BF16)
    context = pl.pallas_call(
        functools.partial(attention_kernel, parts, windows, group),
        out_shape=tuple([first] + [jax.ShapeDtypeStruct((local, head_width), BF16)] * (parts - 1)),
        in_specs=[smem()] * 3 + [vmem()] * (1 + parts + copies),
        out_specs=tuple([vmem()] * parts),
        scratch_shapes=[pltpu.VMEM((windows, group * local, qkv_weight.shape[0]), BF16)],
        compiler_params=params(min(16 * scale, 48)),
        cost_estimate=cost(1e9, 2e6),
        name="attention",
    )(slots, starts, lengths, regrouped, *normed, *mix_stacks)
    context = [to_owner(context[step], step) for step in range(parts)]

    regrouped, attended = pl.pallas_call(
        functools.partial(output_kernel, parts, windows, group),
        out_shape=(block, block),
        in_specs=[smem()] * 3 + [vmem()] * (parts + copies),
        out_specs=(vmem(), vmem()),
        scratch_shapes=[
            pltpu.VMEM((local, features), BF16),
            pltpu.VMEM((windows, local, out_weight.shape[1]), F32),
        ],
        compiler_params=params(min(12 * scale, 32)),
        cost_estimate=cost(1e8, 3e6),
        name="output",
    )(slots, starts, lengths, *context, *out_stacks)
    shape = (1, windows, 1, W, features)
    return (regrouped.reshape(shape), attended.reshape(shape))


def solution(mesh):
    in_specs = (
        P(None, ("dp", "seq")),
        P(),
        P(),
        P(),
        P(),
        P(),
        P("dp", None),
        P("dp", None),
        P(None, "dp"),
    )
    out_specs = (P("dp", None, "seq", None, None), P("dp", None, "seq", None, None))
    return jax.shard_map(
        on_device, mesh=mesh, in_specs=in_specs, out_specs=out_specs, check_vma=False
    )
```

profile of v0, /device:TPU:2, one launch (start us, length us, event | category | flops | bytes accessed | tf_op | source)
XLA Modules:
  0.0 74.5 jit_solution(11368273368000133057)
XLA Ops:
  0.6 0.1 collective-permute-start.1
  0.7 0.7 slice.3
  1.4 3.6 %collective-permute-start = (f32[8,384]{1,0:T(8,128)S(1)}, f32[8,384]{1,0:T(8,128)S(1)}, u32[]{:S(2)}, u32[]{:S(2)}) collective-permute-start(f32[8,384]{1,0:T(8,128)S(1)} %slice.3), channel_id=1, source_target_pairs={{0,1},{1,2},{2,3},{3,4},{4,5},{5,6},{6,7},{7,8},{8,9},{9,10},{10,1... | collective-permute-start | bytes 36872 | tf_op jit(solution)/shard_map/ppermute | solution.py:430
  5.0 1.6 %collective-permute-start.3 = (bf16[1024,128]{1,0:T(8,128)(2,1)}, bf16[1024,128]{1,0:T(8,128)(2,1)S(1)}, u32[]{:S(2)}, u32[]{:S(2)}) collective-permute-start(bf16[1024,128]{1,0:T(8,128)(2,1)} %refs_2_.1), channel_id=1, source_target_pairs={{0,16},{4,20},{8,24},{12,28},{16,0},{20,4},{24,8},{28,12},{1,17},{... | collective-permute-start | bytes 786440 | tf_op jit(solution)/shard_map/ppermute | solution.py:434
  6.6 0.5 collective-permute-start.2
  7.2 1.4 %collective-permute-start.4 = (bf16[1024,128]{1,0:T(8,128)(2,1)}, bf16[1024,128]{1,0:T(8,128)(2,1)}, u32[]{:S(2)}, u32[]{:S(2)}) collective-permute-start(bf16[1024,128]{1,0:T(8,128)(2,1)} %refs_2_.1), channel_id=1, source_target_pairs={{0,24},{4,28},{8,16},{12,20},{16,8},{20,12},{24,0},{28,4},{1,25},{... | collective-permute-start | bytes 786440 | tf_op jit(solution)/shard_map/ppermute | solution.py:434
  8.6 0.7 collective-permute-done.rim_ref
  9.3 0.6 copy-done.10
  9.9 5.5 %log_mel.1 = (bf16[32,8,128]{2,1,0:T(8,128)(2,1)}, bf16[128,768]{1,0:T(8,128)(2,1)}, bf16[128,768]{1,0:T(8,128)(2,1)}, bf16[128,768]{1,0:T(8,128)(2,1)}, bf16[128,768]{1,0:T(8,128)(2,1)}) custom-call(s32[8]{0:T(128)} %slots_ref.7, f32[8,384]{1,0:T(8,128)} %copy-done.10, f32[8,5120]{1,0:T(8,128)} %audio_ref.1, f32[512,640]{1,0:T(8,128)} %constant.2.clone.table_ref, ...), custom_call_target="tpu_custom_call" | custom-call | flops 2000000000 | bytes 2000000 | tf_op jit(solution)/shard_map/log_mel/pallas_call | solution.py:455
  15.4 4.5 %all-to-all-start = ((bf16[32,8,128]{2,1,0:T(8,128)(2,1)}), bf16[32,8,128]{2,1,0:T(8,128)(2,1)S(1)}, u32[]{:S(2)}, u32[]{:S(2)}) async-start(bf16[32,8,128]{2,1,0:T(8,128)(2,1)} %get-tuple-element.21), calls=%async_computation | async-start | bytes 131072 | tf_op jit(solution)/shard_map/all_to_all | solution.py:472
  19.8 0.3 collective-permute-start.8
  20.2 0.0 collective-permute-done.3.refs_4_
  20.2 0.7 copy-done.7
  20.9 1.8 %collective-permute-start.9 = (bf16[128,768]{1,0:T(8,128)(2,1)}, bf16[128,768]{1,0:T(8,128)(2,1)S(1)}, u32[]{:S(2)}, u32[]{:S(2)}) collective-permute-start(bf16[128,768]{1,0:T(8,128)(2,1)} %get-tuple-element.28), channel_id=1, source_target_pairs={{0,16},{4,20},{8,24},{12,28},{16,0},{20,4},{24,8},{28,12},{1,17},{... | collective-permute-start | bytes 589832 | tf_op jit(solution)/shard_map/ppermute | solution.py:434
  22.6 0.0 copy-start.3
  22.6 1.5 %collective-permute-start.10 = (bf16[128,768]{1,0:T(8,128)(2,1)}, bf16[128,768]{1,0:T(8,128)(2,1)S(1)}, u32[]{:S(2)}, u32[]{:S(2)}) collective-permute-start(bf16[128,768]{1,0:T(8,128)(2,1)} %get-tuple-element.29), channel_id=1, source_target_pairs={{0,24},{4,28},{8,16},{12,20},{16,8},{20,12},{24,0},{28,4},{1,25},{... | collective-permute-start | bytes 589832 | tf_op jit(solution)/shard_map/ppermute | solution.py:434
  24.2 2.0 %all-to-all-done.mel_ref = bf16[32,8,128]{2,1,0:T(8,128)(2,1)S(1)} async-done(((bf16[32,8,128]{2,1,0:T(8,128)(2,1)}), bf16[32,8,128]{2,1,0:T(8,128)(2,1)S(1)}, u32[]{:S(2)}, u32[]{:S(2)}) %all-to-all-start) | async-done | bytes 65568 | tf_op jit(solution)/shard_map/all_to_all | solution.py:472
  26.2 0.0 copy-start.5
  26.3 1.3 %copy-done.5 = bf16[2304,256]{1,0:T(8,128)(2,1)S(1)} copy-done((bf16[2304,256]{1,0:T(8,128)(2,1)S(1)}, bf16[2304,256]{1,0:T(8,128)(2,1)}, u32[]{:S(2)}) %copy-start.5) | copy-done | bytes 1179672
  27.5 0.9 %copy-done.6 = bf16[1024,128]{1,0:T(8,128)(2,1)S(1)} copy-done((bf16[1024,128]{1,0:T(8,128)(2,1)S(1)}, bf16[1024,128]{1,0:T(8,128)(2,1)}, u32[]{:S(2)}) %copy-start.6) | copy-done | bytes 262168
  28.5 0.9 %copy-done.8 = bf16[1024,128]{1,0:T(8,128)(2,1)S(1)} copy-done((bf16[1024,128]{1,0:T(8,128)(2,1)S(1)}, bf16[1024,128]{1,0:T(8,128)(2,1)}, u32[]{:S(2)}) %copy-start.8) | copy-done | bytes 262168
  29.4 5.1 %conv.1 = (bf16[64,1024]{1,0:T(8,128)(2,1)S(1)}, bf16[64,1024]{1,0:T(8,128)(2,1)S(1)}, bf16[64,1024]{1,0:T(8,128)(2,1)S(1)}, bf16[64,1024]{1,0:T(8,128)(2,1)S(1)}, bf16[4,1024,128]{2,1,0:T(8,128)(2,1)S(1)}) custom-call(bf16[32,8,128]{2,1,0:T(8,128)(2,1)S(1)} %all-to-all-done.mel_ref, bf16[9,256]{1,0:T(8,128)(2,1)S(1)} %copy-done.9, ...), custom_call_target="tpu_custom_call" | custom-call | flops 2000000000 | bytes 4000000 | tf_op jit(solution)/shard_map/conv/pallas_call | solution.py:475
  34.5 1.4 %collective-permute-start.5 = (bf16[64,1024]{1,0:T(8,128)(2,1)S(1)}, bf16[64,1024]{1,0:T(8,128)(2,1)S(1)}, u32[]{:S(2)}, u32[]{:S(2)}) collective-permute-start(bf16[64,1024]{1,0:T(8,128)(2,1)S(1)} %get-tuple-element.23), channel_id=1, source_target_pairs={{0,8},{4,12},{8,0},{12,4},{16,24},{20,28},{24,16},{28,20},{1,9},{5... | collective-permute-start | bytes 393224 | tf_op jit(solution)/shard_map/ppermute | solution.py:434
  36.0 0.7 collective-permute-start.6
  36.6 0.0 collective-permute-done.8.refs_5_
  36.6 1.4 %collective-permute-start.7 = (bf16[64,1024]{1,0:T(8,128)(2,1)S(1)}, bf16[64,1024]{1,0:T(8,128)(2,1)S(1)}, u32[]{:S(2)}, u32[]{:S(2)}) collective-permute-start(bf16[64,1024]{1,0:T(8,128)(2,1)S(1)} %get-tuple-element.25), channel_id=1, source_target_pairs={{0,24},{4,28},{8,16},{12,20},{16,8},{20,12},{24,0},{28,4},{1,25},{... | collective-permute-start | bytes 393224 | tf_op jit(solution)/shard_map/ppermute | solution.py:434
  38.1 0.0 collective-permute-done.9.refs_6_
  38.1 0.0 collective-permute-start.19
  38.1 0.0 collective-permute-done.10.refs_7_
  38.1 2.5 %collective-permute-done.5.refs_1_ = bf16[64,1024]{1,0:T(8,128)(2,1)S(1)} collective-permute-done((bf16[64,1024]{1,0:T(8,128)(2,1)S(1)}, bf16[64,1024]{1,0:T(8,128)(2,1)S(1)}, u32[]{:S(2)}, u32[]{:S(2)}) %collective-permute-start.5) | collective-permute-done | bytes 131104 | tf_op jit(solution)/shard_map/ppermute | solution.py:434
  40.6 3.1 %collective-permute-done.6.refs_2_ = bf16[64,1024]{1,0:T(8,128)(2,1)S(1)} collective-permute-done((bf16[64,1024]{1,0:T(8,128)(2,1)S(1)}, bf16[64,1024]{1,0:T(8,128)(2,1)S(1)}, u32[]{:S(2)}, u32[]{:S(2)}) %collective-permute-start.6) | collective-permute-done | bytes 131104 | tf_op jit(solution)/shard_map/ppermute | solution.py:434
  43.7 0.0 collective-permute-done.7.refs_3_
  43.7 1.9 %layer_norm.1 = (bf16[64,1024]{1,0:T(8,128)(2,1)S(1)}, bf16[64,1024]{1,0:T(8,128)(2,1)S(1)}, bf16[4,128,768]{2,1,0:T(8,128)(2,1)S(1)}) custom-call(s32[8]{0:T(128)S(1)} %copy-done.1, s32[8]{0:T(128)S(1)} %copy-done.2, s32[8]{0:T(128)S(1)} %copy-done.3, bf16[64,1024]{1,0:T(8,128)(2,1)S(1)} %get-tuple-element.22.refs_0_, ...), custom_call_target="tpu_custom_call" | custom-call | flops 100000000 | bytes 1000000 | tf_op jit(solution)/shard_map/layer_norm/pallas_call | solution.py:497
  45.6 0.1 collective-permute-start.14
  45.7 1.0 %collective-permute-start.13 = (bf16[64,1024]{1,0:T(8,128)(2,1)S(1)}, bf16[64,1024]{1,0:T(8,128)(2,1)S(1)}, u32[]{:S(2)}, u32[]{:S(2)}) collective-permute-start(bf16[64,1024]{1,0:T(8,128)(2,1)S(1)} %get-tuple-element.31.refs_0_), channel_id=1, source_target_pairs={{0,24},{4,28},{8,16},{12,20},{16,8},{20,12},{24,0},{28,4},{1,25},{... | collective-permute-start | bytes 393224 | tf_op jit(solution)/shard_map/ppermute | solution.py:434
  46.7 1.2 %collective-permute-start.12 = (bf16[64,1024]{1,0:T(8,128)(2,1)S(1)}, bf16[64,1024]{1,0:T(8,128)(2,1)S(1)}, u32[]{:S(2)}, u32[]{:S(2)}) collective-permute-start(bf16[64,1024]{1,0:T(8,128)(2,1)S(1)} %get-tuple-element.31.refs_0_), channel_id=1, source_target_pairs={{0,16},{4,20},{8,24},{12,28},{16,0},{20,4},{24,8},{28,12},{1,17},{... | collective-permute-start | bytes 393224 | tf_op jit(solution)/shard_map/ppermute | solution.py:434
  47.9 1.3 %collective-permute-start.11 = (bf16[64,1024]{1,0:T(8,128)(2,1)S(1)}, bf16[64,1024]{1,0:T(8,128)(2,1)S(1)}, u32[]{:S(2)}, u32[]{:S(2)}) collective-permute-start(bf16[64,1024]{1,0:T(8,128)(2,1)S(1)} %get-tuple-element.31.refs_0_), channel_id=1, source_target_pairs={{0,8},{4,12},{8,0},{12,4},{16,24},{20,28},{24,16},{28,20},{1,9},{5... | collective-permute-start | bytes 393224 | tf_op jit(solution)/shard_map/ppermute | solution.py:434
  49.3 3.8 %collective-permute-done.13.refs_3_ = bf16[64,1024]{1,0:T(8,128)(2,1)S(1)} collective-permute-done((bf16[64,1024]{1,0:T(8,128)(2,1)S(1)}, bf16[64,1024]{1,0:T(8,128)(2,1)S(1)}, u32[]{:S(2)}, u32[]{:S(2)}) %collective-permute-start.13) | collective-permute-done | bytes 131104 | tf_op jit(solution)/shard_map/ppermute | solution.py:434
  53.0 2.1 %collective-permute-done.12.refs_2_ = bf16[64,1024]{1,0:T(8,128)(2,1)S(1)} collective-permute-done((bf16[64,1024]{1,0:T(8,128)(2,1)S(1)}, bf16[64,1024]{1,0:T(8,128)(2,1)S(1)}, u32[]{:S(2)}, u32[]{:S(2)}) %collective-permute-start.12) | collective-permute-done | bytes 131104 | tf_op jit(solution)/shard_map/ppermute | solution.py:434
  55.1 1.8 %attention.1 = (bf16[64,1280]{1,0:T(8,128)(2,1)S(1)}, bf16[64,256]{1,0:T(8,128)(2,1)S(1)}, bf16[64,256]{1,0:T(8,128)(2,1)S(1)}, bf16[64,256]{1,0:T(8,128)(2,1)S(1)}) custom-call(s32[8]{0:T(128)S(1)} %copy-done.1, s32[8]{0:T(128)S(1)} %copy-done.2, s32[8]{0:T(128)S(1)} %copy-done.3, bf16[64,1024]{1,0:T(8,128)(2,1)S(1)} %get-tuple-element.30.rows_ref, ...), custom_call_target="tpu_custom_call" | custom-call | flops 1000000000 | bytes 2000000 | tf_op jit(solution)/shard_map/attention/pallas_call | solution.py:511
  56.9 2.8 %collective-permute-start.15 = (bf16[64,1280]{1,0:T(8,128)(2,1)S(1)}, bf16[64,1280]{1,0:T(8,128)(2,1)S(1)}, u32[]{:S(2)}, u32[]{:S(2)}) collective-permute-start(bf16[64,1280]{1,0:T(8,128)(2,1)S(1)} %get-tuple-element.33), channel_id=1, source_target_pairs={{0,0},{1,8},{2,16},{3,24},{4,4},{5,12},{6,20},{7,28},{8,1},{9,9},{... | collective-permute-start | bytes 491528 | tf_op jit(solution)/shard_map/ppermute | solution.py:446
  59.7 0.1 collective-permute-start.16
  59.8 4.9 %collective-permute-start.17 = (bf16[64,256]{1,0:T(8,128)(2,1)S(1)}, bf16[64,256]{1,0:T(8,128)(2,1)S(1)}, u32[]{:S(2)}, u32[]{:S(2)}) collective-permute-start(bf16[64,256]{1,0:T(8,128)(2,1)S(1)} %get-tuple-element.35), channel_id=1, source_target_pairs={{0,2},{1,10},{2,18},{3,26},{4,6},{5,14},{6,22},{7,30},{8,3},{9,11}... | collective-permute-start | bytes 98312 | tf_op jit(solution)/shard_map/ppermute | solution.py:446
  64.7 1.7 %collective-permute-done.17.refs_2_ = bf16[64,256]{1,0:T(8,128)(2,1)S(1)} collective-permute-done((bf16[64,256]{1,0:T(8,128)(2,1)S(1)}, bf16[64,256]{1,0:T(8,128)(2,1)S(1)}, u32[]{:S(2)}, u32[]{:S(2)}) %collective-permute-start.17) | collective-permute-done | bytes 32800 | tf_op jit(solution)/shard_map/ppermute | solution.py:446
  66.4 3.4 %collective-permute-done.18.refs_3_ = bf16[64,256]{1,0:T(8,128)(2,1)S(1)} collective-permute-done((bf16[64,256]{1,0:T(8,128)(2,1)S(1)}, bf16[64,256]{1,0:T(8,128)(2,1)S(1)}, u32[]{:S(2)}, u32[]{:S(2)}) %collective-permute-start.18) | collective-permute-done | bytes 32800 | tf_op jit(solution)/shard_map/ppermute | solution.py:446
  69.8 0.0 collective-permute-done.19.refs_5_
  69.8 2.8 %collective-permute-done.15.refs_0_ = bf16[64,1280]{1,0:T(8,128)(2,1)S(1)} collective-permute-done((bf16[64,1280]{1,0:T(8,128)(2,1)S(1)}, bf16[64,1280]{1,0:T(8,128)(2,1)S(1)}, u32[]{:S(2)}, u32[]{:S(2)}) %collective-permute-start.15) | collective-permute-done | bytes 163872 | tf_op jit(solution)/shard_map/ppermute | solution.py:446
  72.7 1.8 %output.1 = (bf16[64,1024]{1,0:T(8,128)(2,1)}, bf16[64,1024]{1,0:T(8,128)(2,1)}) custom-call(s32[8]{0:T(128)S(1)} %copy-done.1, s32[8]{0:T(128)S(1)} %copy-done.2, s32[8]{0:T(128)S(1)} %copy-done.3, bf16[64,1280]{1,0:T(8,128)(2,1)S(1)} %collective-permute-done.15.refs_0_, bf16[64,256]{1,0:T(8,128)(2,1)S(1)} %collective-permute-done.16.refs_1_, ...), custom_call_target="tpu_custom_call" | custom-call | flops 100000000 | bytes 3000000 | tf_op jit(solution)/shard_map/output/pallas_call | solution.py:523
  (22 shorter events, 0.0 us)
Async XLA Ops:
  0.6 25.6 %collective-permute-start.1 = (bf16[640,1024]{1,0:T(8,128)(2,1)}, bf16[640,1024]{1,0:T(8,128)(2,1)S(1)}, u32[]{:S(2)}, u32[]{:S(2)}) collective-permute-start(bf16[640,1024]{1,0:T(8,128)(2,1)} %refs_0_.1), channel_id=1, source_target_pairs={{0,4},{4,0},{8,12},{12,8},{16,20},{20,16},{24,28},{28,24},{1,5},{5... | collective-permute-start | bytes 3932168 | tf_op jit(solution)/shard_map/ppermute | solution.py:438
  1.4 24.8 %copy-start.4 = (bf16[640,1024]{1,0:T(8,128)(2,1)S(1)}, bf16[640,1024]{1,0:T(8,128)(2,1)}, u32[]{:S(2)}) copy-start(bf16[640,1024]{1,0:T(8,128)(2,1)} %refs_0_.1) | copy-start | bytes 3932164
  1.4 24.8 %copy-start.9 = (bf16[9,256]{1,0:T(8,128)(2,1)S(1)}, bf16[9,256]{1,0:T(8,128)(2,1)}, u32[]{:S(2)}) copy-start(bf16[9,256]{1,0:T(8,128)(2,1)} %conv1_ref.1) | copy-start | bytes 13828
  1.4 7.8 %collective-permute-start = (f32[8,384]{1,0:T(8,128)S(1)}, f32[8,384]{1,0:T(8,128)S(1)}, u32[]{:S(2)}, u32[]{:S(2)}) collective-permute-start(f32[8,384]{1,0:T(8,128)S(1)} %slice.3), channel_id=1, source_target_pairs={{0,1},{1,2},{2,3},{3,4},{4,5},{5,6},{6,7},{7,8},{8,9},{9,10},{10,1... | collective-permute-start | bytes 36872 | tf_op jit(solution)/shard_map/ppermute | solution.py:430
  5.0 15.1 %collective-permute-start.3 = (bf16[1024,128]{1,0:T(8,128)(2,1)}, bf16[1024,128]{1,0:T(8,128)(2,1)S(1)}, u32[]{:S(2)}, u32[]{:S(2)}) collective-permute-start(bf16[1024,128]{1,0:T(8,128)(2,1)} %refs_2_.1), channel_id=1, source_target_pairs={{0,16},{4,20},{8,24},{12,28},{16,0},{20,4},{24,8},{28,12},{1,17},{... | collective-permute-start | bytes 786440 | tf_op jit(solution)/shard_map/ppermute | solution.py:434
  6.6 16.0 %collective-permute-start.2 = (bf16[1024,128]{1,0:T(8,128)(2,1)}, bf16[1024,128]{1,0:T(8,128)(2,1)}, u32[]{:S(2)}, u32[]{:S(2)}) collective-permute-start(bf16[1024,128]{1,0:T(8,128)(2,1)} %refs_2_.1), channel_id=1, source_target_pairs={{0,8},{4,12},{8,0},{12,4},{16,24},{20,28},{24,16},{28,20},{1,9},{5... | collective-permute-start | bytes 786440 | tf_op jit(solution)/shard_map/ppermute | solution.py:434
  7.2 19.1 %collective-permute-start.4 = (bf16[1024,128]{1,0:T(8,128)(2,1)}, bf16[1024,128]{1,0:T(8,128)(2,1)}, u32[]{:S(2)}, u32[]{:S(2)}) collective-permute-start(bf16[1024,128]{1,0:T(8,128)(2,1)} %refs_2_.1), channel_id=1, source_target_pairs={{0,24},{4,28},{8,16},{12,20},{16,8},{20,12},{24,0},{28,4},{1,25},{... | collective-permute-start | bytes 786440 | tf_op jit(solution)/shard_map/ppermute | solution.py:434
  9.3 0.6 copy-start.10
  15.4 10.9 %all-to-all-start = ((bf16[32,8,128]{2,1,0:T(8,128)(2,1)}), bf16[32,8,128]{2,1,0:T(8,128)(2,1)S(1)}, u32[]{:S(2)}, u32[]{:S(2)}) async-start(bf16[32,8,128]{2,1,0:T(8,128)(2,1)} %get-tuple-element.21), calls=%async_computation | async-start | bytes 131072 | tf_op jit(solution)/shard_map/all_to_all | solution.py:472
  19.8 16.8 %collective-permute-start.8 = (bf16[128,768]{1,0:T(8,128)(2,1)}, bf16[128,768]{1,0:T(8,128)(2,1)S(1)}, u32[]{:S(2)}, u32[]{:S(2)}) collective-permute-start(bf16[128,768]{1,0:T(8,128)(2,1)} %get-tuple-element.27), channel_id=1, source_target_pairs={{0,8},{4,12},{8,0},{12,4},{16,24},{20,28},{24,16},{28,20},{1,9},{5... | collective-permute-start | bytes 589832 | tf_op jit(solution)/shard_map/ppermute | solution.py:434
  20.2 0.7 copy-start.7
  20.9 17.2 %collective-permute-start.9 = (bf16[128,768]{1,0:T(8,128)(2,1)}, bf16[128,768]{1,0:T(8,128)(2,1)S(1)}, u32[]{:S(2)}, u32[]{:S(2)}) collective-permute-start(bf16[128,768]{1,0:T(8,128)(2,1)} %get-tuple-element.28), channel_id=1, source_target_pairs={{0,16},{4,20},{8,24},{12,28},{16,0},{20,4},{24,8},{28,12},{1,17},{... | collective-permute-start | bytes 589832 | tf_op jit(solution)/shard_map/ppermute | solution.py:434
  22.6 21.1 %copy-start = (bf16[128,768]{1,0:T(8,128)(2,1)S(1)}, bf16[128,768]{1,0:T(8,128)(2,1)}, u32[]{:S(2)}) copy-start(bf16[128,768]{1,0:T(8,128)(2,1)} %get-tuple-element.26.refs_4_) | copy-start | bytes 589828
  22.6 21.1 %copy-start.1 = (s32[8]{0:T(128)S(1)}, s32[8]{0:T(128)}, u32[]{:S(2)}) copy-start(s32[8]{0:T(128)} %slots_ref.7) | copy-start | bytes 100
  22.6 21.1 %copy-start.2 = (s32[8]{0:T(128)S(1)}, s32[8]{0:T(128)}, u32[]{:S(2)}) copy-start(s32[8]{0:T(128)} %starts_ref.5) | copy-start | bytes 100
  22.6 21.1 %copy-start.3 = (s32[8]{0:T(128)S(1)}, s32[8]{0:T(128)}, u32[]{:S(2)}) copy-start(s32[8]{0:T(128)} %lengths_ref.5) | copy-start | bytes 100
  22.6 15.4 %collective-permute-start.10 = (bf16[128,768]{1,0:T(8,128)(2,1)}, bf16[128,768]{1,0:T(8,128)(2,1)S(1)}, u32[]{:S(2)}, u32[]{:S(2)}) collective-permute-start(bf16[128,768]{1,0:T(8,128)(2,1)} %get-tuple-element.29), channel_id=1, source_target_pairs={{0,24},{4,28},{8,16},{12,20},{16,8},{20,12},{24,0},{28,4},{1,25},{... | collective-permute-start | bytes 589832 | tf_op jit(solution)/shard_map/ppermute | solution.py:434
  26.2 1.3 %copy-start.5 = (bf16[2304,256]{1,0:T(8,128)(2,1)S(1)}, bf16[2304,256]{1,0:T(8,128)(2,1)}, u32[]{:S(2)}) copy-start(bf16[2304,256]{1,0:T(8,128)(2,1)} %conv2_ref.1) | copy-start | bytes 3538948
  27.5 0.9 %copy-start.6 = (bf16[1024,128]{1,0:T(8,128)(2,1)S(1)}, bf16[1024,128]{1,0:T(8,128)(2,1)}, u32[]{:S(2)}) copy-start(bf16[1024,128]{1,0:T(8,128)(2,1)} %refs_2_.1) | copy-start | bytes 786436
  28.5 0.9 %copy-start.8 = (bf16[1024,128]{1,0:T(8,128)(2,1)S(1)}, bf16[1024,128]{1,0:T(8,128)(2,1)}, u32[]{:S(2)}) copy-start(bf16[1024,128]{1,0:T(8,128)(2,1)} %copy-done.7) | copy-start | bytes 786436
  34.5 6.1 %collective-permute-start.5 = (bf16[64,1024]{1,0:T(8,128)(2,1)S(1)}, bf16[64,1024]{1,0:T(8,128)(2,1)S(1)}, u32[]{:S(2)}, u32[]{:S(2)}) collective-permute-start(bf16[64,1024]{1,0:T(8,128)(2,1)S(1)} %get-tuple-element.23), channel_id=1, source_target_pairs={{0,8},{4,12},{8,0},{12,4},{16,24},{20,28},{24,16},{28,20},{1,9},{5... | collective-permute-start | bytes 393224 | tf_op jit(solution)/shard_map/ppermute | solution.py:434
  36.0 7.8 %collective-permute-start.6 = (bf16[64,1024]{1,0:T(8,128)(2,1)S(1)}, bf16[64,1024]{1,0:T(8,128)(2,1)S(1)}, u32[]{:S(2)}, u32[]{:S(2)}) collective-permute-start(bf16[64,1024]{1,0:T(8,128)(2,1)S(1)} %get-tuple-element.24), channel_id=1, source_target_pairs={{0,16},{4,20},{8,24},{12,28},{16,0},{20,4},{24,8},{28,12},{1,17},{... | collective-permute-start | bytes 393224 | tf_op jit(solution)/shard_map/ppermute | solution.py:434
  36.6 7.1 %collective-permute-start.7 = (bf16[64,1024]{1,0:T(8,128)(2,1)S(1)}, bf16[64,1024]{1,0:T(8,128)(2,1)S(1)}, u32[]{:S(2)}, u32[]{:S(2)}) collective-permute-start(bf16[64,1024]{1,0:T(8,128)(2,1)S(1)} %get-tuple-element.25), channel_id=1, source_target_pairs={{0,24},{4,28},{8,16},{12,20},{16,8},{20,12},{24,0},{28,4},{1,25},{... | collective-permute-start | bytes 393224 | tf_op jit(solution)/shard_map/ppermute | solution.py:434
  38.1 31.8 %collective-permute-start.19 = (bf16[4,1024,128]{2,1,0:T(8,128)(2,1)S(1)}, bf16[4,1024,128]{2,1,0:T(8,128)(2,1)S(1)}, u32[]{:S(2)}, u32[]{:S(2)}) collective-permute-start(bf16[4,1024,128]{2,1,0:T(8,128)(2,1)S(1)} %get-tuple-element.37.refs_4_), channel_id=1, source_target_pairs={{0,4},{4,0},{8,12},{12,8},{16,20},{20,16},{24,28},{28,24},{1,5},{5... | collective-permute-start | bytes 3145736 | tf_op jit(solution)/shard_map/ppermute | solution.py:438
  45.6 9.5 %collective-permute-start.14 = (bf16[4,128,768]{2,1,0:T(8,128)(2,1)S(1)}, bf16[4,128,768]{2,1,0:T(8,128)(2,1)S(1)}, u32[]{:S(2)}, u32[]{:S(2)}) collective-permute-start(bf16[4,128,768]{2,1,0:T(8,128)(2,1)S(1)} %get-tuple-element.32.refs_4_), channel_id=1, source_target_pairs={{0,4},{4,0},{8,12},{12,8},{16,20},{20,16},{24,28},{28,24},{1,5},{5... | collective-permute-start | bytes 2359304 | tf_op jit(solution)/shard_map/ppermute | solution.py:438
  45.7 7.3 %collective-permute-start.13 = (bf16[64,1024]{1,0:T(8,128)(2,1)S(1)}, bf16[64,1024]{1,0:T(8,128)(2,1)S(1)}, u32[]{:S(2)}, u32[]{:S(2)}) collective-permute-start(bf16[64,1024]{1,0:T(8,128)(2,1)S(1)} %get-tuple-element.31.refs_0_), channel_id=1, source_target_pairs={{0,24},{4,28},{8,16},{12,20},{16,8},{20,12},{24,0},{28,4},{1,25},{... | collective-permute-start | bytes 393224 | tf_op jit(solution)/shard_map/ppermute | solution.py:434
  46.7 8.4 %collective-permute-start.12 = (bf16[64,1024]{1,0:T(8,128)(2,1)S(1)}, bf16[64,1024]{1,0:T(8,128)(2,1)S(1)}, u32[]{:S(2)}, u32[]{:S(2)}) collective-permute-start(bf16[64,1024]{1,0:T(8,128)(2,1)S(1)} %get-tuple-element.31.refs_0_), channel_id=1, source_target_pairs={{0,16},{4,20},{8,24},{12,28},{16,0},{20,4},{24,8},{28,12},{1,17},{... | collective-permute-start | bytes 393224 | tf_op jit(solution)/shard_map/ppermute | solution.py:434
  47.9 7.2 %collective-permute-start.11 = (bf16[64,1024]{1,0:T(8,128)(2,1)S(1)}, bf16[64,1024]{1,0:T(8,128)(2,1)S(1)}, u32[]{:S(2)}, u32[]{:S(2)}) collective-permute-start(bf16[64,1024]{1,0:T(8,128)(2,1)S(1)} %get-tuple-element.31.refs_0_), channel_id=1, source_target_pairs={{0,8},{4,12},{8,0},{12,4},{16,24},{20,28},{24,16},{28,20},{1,9},{5... | collective-permute-start | bytes 393224 | tf_op jit(solution)/shard_map/ppermute | solution.py:434
  56.9 15.7 %collective-permute-start.15 = (bf16[64,1280]{1,0:T(8,128)(2,1)S(1)}, bf16[64,1280]{1,0:T(8,128)(2,1)S(1)}, u32[]{:S(2)}, u32[]{:S(2)}) collective-permute-start(bf16[64,1280]{1,0:T(8,128)(2,1)S(1)} %get-tuple-element.33), channel_id=1, source_target_pairs={{0,0},{1,8},{2,16},{3,24},{4,4},{5,12},{6,20},{7,28},{8,1},{9,9},{... | collective-permute-start | bytes 491528 | tf_op jit(solution)/shard_map/ppermute | solution.py:446
  59.7 5.0 %collective-permute-start.16 = (bf16[64,256]{1,0:T(8,128)(2,1)S(1)}, bf16[64,256]{1,0:T(8,128)(2,1)S(1)}, u32[]{:S(2)}, u32[]{:S(2)}) collective-permute-start(bf16[64,256]{1,0:T(8,128)(2,1)S(1)} %get-tuple-element.34), channel_id=1, source_target_pairs={{0,1},{1,9},{2,17},{3,25},{4,5},{5,13},{6,21},{7,29},{8,0},{9,8},{... | collective-permute-start | bytes 98312 | tf_op jit(solution)/shard_map/ppermute | solution.py:446
  59.8 6.6 %collective-permute-start.17 = (bf16[64,256]{1,0:T(8,128)(2,1)S(1)}, bf16[64,256]{1,0:T(8,128)(2,1)S(1)}, u32[]{:S(2)}, u32[]{:S(2)}) collective-permute-start(bf16[64,256]{1,0:T(8,128)(2,1)S(1)} %get-tuple-element.35), channel_id=1, source_target_pairs={{0,2},{1,10},{2,18},{3,26},{4,6},{5,14},{6,22},{7,30},{8,3},{9,11}... | collective-permute-start | bytes 98312 | tf_op jit(solution)/shard_map/ppermute | solution.py:446
  64.7 5.2 %collective-permute-start.18 = (bf16[64,256]{1,0:T(8,128)(2,1)S(1)}, bf16[64,256]{1,0:T(8,128)(2,1)S(1)}, u32[]{:S(2)}, u32[]{:S(2)}) collective-permute-start(bf16[64,256]{1,0:T(8,128)(2,1)S(1)} %get-tuple-element.36), channel_id=1, source_target_pairs={{0,3},{1,11},{2,19},{3,27},{4,7},{5,15},{6,23},{7,31},{8,2},{9,10}... | collective-permute-start | bytes 98312 | tf_op jit(solution)/shard_map/ppermute | solution.py:446
where the time goes:
time: 74.9 us; the launch traced here: 74.5 us
  starting transfers between devices  30.2 us (40%)
  waiting for transfers between devices  22.2 us (30%)
  Pallas kernels  16.1 us (21%)
  local copies, waits for them, and re-layouts  5.19 us (7%)
  between operations  0.79 us (1%)
    ppermute x12, starting transfers between devices, to_part(): return lax.ppermute(block, 'dp', pairs)  14.3 us
    ppermute x12, waiting for transfers between devices, to_part(): return lax.ppermute(block, 'dp', pairs)  11.5 us
    ppermute x4, waiting for transfers between devices, to_owner(): return lax.ppermute(block, ('dp', 'seq'), pairs)  8 us
    ppermute x4, starting transfers between devices, to_owner(): return lax.ppermute(block, ('dp', 'seq'), pairs)  7.73 us
    pallas_call x1, Pallas kernels, on_device(): pl.pallas_call(functools.partial(mel_kernel, parts, group), out_shape=tup...  5.5 us
    pallas_call x1, Pallas kernels, on_device(): pl.pallas_call(functools.partial(conv_kernel, parts, width, windows), out...  5.09 us
    unnamed x22, local copies, waits for them, and re-layouts  4.48 us
    all_to_all x1, starting transfers between devices, on_device(): lax.all_to_all(mel, ('dp', 'seq'), split_axis=0, concat_axis=0, tiled=True)  4.46 us
  transfers between devices with their start and end apart: 21, of which 9 were waited for; matrix products, arithmetic and copies ran while one was open for 1% of the time, Pallas kernels for 19%

commit v1 on v0

v1 whole, which is shorter than its diff:
```python
import functools
import math

import jax
import jax.numpy as jnp
import numpy as np
from jax import lax
from jax.experimental import pallas as pl
from jax.experimental.pallas import tpu as pltpu
from jax.sharding import PartitionSpec as P

HEADS = 8
HEAD_DIM = 128
MELS = 80
BANDS = MELS // 4
N_FFT = 512
HOP = 160
W = 8
RIM = 1024
SPAN = 4 * HOP
JS = W + 1
LANES = 128
SAMPLE_RATE = 16000.0
EPS_LOG = 1e-06
EPS_NORM = 1e-05
MASKED = -1e30
F32 = jnp.float32
BF16 = jnp.bfloat16
MIB = 1 << 20


def mel_table(size, bands):
    count = size // 2 + 1
    highest = 2595.0 * math.log10(1.0 + SAMPLE_RATE / 1400.0)
    points = np.linspace(0.0, highest, bands + 2)
    edges = 700.0 * (10.0 ** (points / 2595.0) - 1.0)
    edges[0] = 0.0
    edges[-1] = SAMPLE_RATE / 2.0
    frequency = np.arange(count) * (SAMPLE_RATE / size)
    lower = edges[:-2][None, :]
    middle = edges[1:-1][None, :]
    upper = edges[2:][None, :]
    rising = (frequency[:, None] - lower) / (middle - lower)
    falling = (upper - frequency[:, None]) / (upper - middle)
    return np.maximum(0.0, np.minimum(rising, falling)).astype(np.float32)


def spectrum_table(size):
    sample = np.arange(size)
    phase = sample[:, None] * np.arange(size // 2)[None, :] % size
    angle = phase * (2.0 * math.pi / size)
    window = 0.5 - 0.5 * np.cos(sample * (2.0 * math.pi / size))
    both = np.concatenate([np.cos(angle), np.sin(angle)], axis=1) * window[:, None]
    filters = np.zeros((size, LANES))
    filters[: size // 2, :MELS] = mel_table(size, MELS)[: size // 2]
    return np.concatenate([both, filters], axis=1).astype(np.float32)


def vmem():
    return pl.BlockSpec(memory_space=pltpu.VMEM)


def smem():
    return pl.BlockSpec(memory_space=pltpu.SMEM)


def anywhere():
    return pl.BlockSpec(memory_space=pl.ANY)


def params(mib):
    return pltpu.CompilerParams(vmem_limit_bytes=mib * MIB)


def cost(flops, moved):
    return pl.CostEstimate(flops=int(flops), bytes_accessed=int(moved), transcendentals=0)


def place(parts):
    mine = lax.axis_index("dp")
    copies = lax.axis_size("dp") // parts
    return mine // copies, mine % copies


def start_all(copies):
    for copy in copies:
        copy.start()


def wait_all(copies):
    for copy in copies:
        copy.wait()


def iota(rows, columns, axis):
    return lax.broadcasted_iota(jnp.int32, (rows, columns), axis)


def quotient(index, step, count):
    result = jnp.zeros_like(index)
    for i in range(1, count):
        result += (index >= i * step).astype(jnp.int32)
    return result


def one_hot(target, count):
    return (iota(target.shape[0], count, 1) == target).astype(F32).astype(BF16)


def frame_order(parts, copies):
    count = parts * copies * W
    row = iota(count, 1, 0)
    k = quotient(row, W, parts * copies)
    p = quotient(k, copies, parts)
    return one_hot((k - p * copies) * W * parts + (row - k * W) * parts + p, count)


def row_order(parts, streams):
    count = W * parts * streams
    row = iota(count, 1, 0)
    r = quotient(row, W * parts, streams)
    rest = row - r * W * parts
    return one_hot(rest * streams + r, count)


def samples(index, windows, group):
    return (index + quotient(index, W, windows) * (group - 1) * W) * SPAN


def mix_columns(group, qkv_ref, mix_out, sems):
    features = qkv_ref.shape[1] // 3
    width = features // group
    first = pl.multiple_of(lax.axis_index("seq") * width, LANES)
    return [
        pltpu.make_async_copy(
            qkv_ref.at[:, pl.ds(kind * features + first, width)],
            mix_out.at[:, pl.ds(kind * width, width)],
            sems.at[kind],
        )
        for kind in range(3)
    ]


def banded_weights(width, conv1_ref, banded_out):
    taps, channels = conv1_ref.shape
    row = lax.broadcasted_iota(jnp.int32, (LANES, taps), 0)
    tap = lax.broadcasted_iota(jnp.int32, (LANES, taps), 1)
    line = (tap >= 3).astype(jnp.int32) + (tap >= 6).astype(jnp.int32)
    target = line * (width - 3) + tap + 1
    weight = conv1_ref[...]
    for g in range(banded_out.shape[1] // channels):
        select = (row == target + 2 * g).astype(F32).astype(BF16)
        banded_out[:, g * channels : (g + 1) * channels] = jnp.dot(
            select, weight, preferred_element_type=F32
        ).astype(BF16)


def mel_kernel(parts, group, slots_ref, rim_ref, audio_ref, table_ref, qkv_ref, *refs):
    outs_refs, (mix_out, ext, table, blocks, sems) = refs[:parts], refs[parts:]
    load_audio = pltpu.make_async_copy(audio_ref, ext.at[:, pl.ds(RIM, audio_ref.shape[1])], sems.at[3])
    load_table = pltpu.make_async_copy(table_ref, table, sems.at[4])
    load_audio.start()
    load_table.start()
    pieces = mix_columns(group, qkv_ref, mix_out, sems)
    start_all(pieces)
    streams = audio_ref.shape[0]
    rows = JS * streams
    ext[:, :RIM] = rim_ref[...]
    column = iota(1, rows, 1)
    early = quotient(column, streams, JS)
    target = jnp.zeros((1, rows), jnp.int32)
    for u in range(streams):
        target = jnp.where(column - early * streams == u, early * streams + slots_ref[u], target)
    routing = (target == iota(rows, rows, 0)).astype(F32).astype(BF16)
    load_audio.wait()
    phases = []
    for phase in range(4):
        start = HOP * phase + 32
        base, shift = start // LANES * LANES, start % LANES
        length = N_FFT + (LANES if shift else 0)
        block = jnp.concatenate(
            [ext[:, SPAN * j + base : SPAN * j + base + length] for j in range(JS)], axis=0
        )
        if shift:
            block = pltpu.roll(block, length - shift, 1)[:, :N_FFT]
        phases.append(block)
    frames = jnp.concatenate(phases, axis=0)
    load_table.wait()
    spectrum = jnp.dot(
        frames, table[:, :N_FFT], precision=lax.Precision.HIGHEST, preferred_element_type=F32
    )
    half = N_FFT // 2
    real, imag = spectrum[:, :half], spectrum[:, half:]
    power = real * real + imag * imag
    mel_power = jnp.dot(
        power, table[:half, N_FFT:], precision=lax.Precision.HIGHEST, preferred_element_type=F32
    )
    log_mel = jnp.log(mel_power + EPS_LOG)
    share = BANDS // parts
    width = 4 * share + 4
    lane = iota(rows, LANES, 1)
    by_phase = [log_mel[phase * rows : (phase + 1) * rows] for phase in range(4)]

    def next_four(frames):
        return jnp.concatenate([frames[streams:], jnp.zeros((streams, LANES), F32)], axis=0)

    taps = [by_phase[1], by_phase[2], by_phase[3], next_four(by_phase[0]), next_four(by_phase[1])]
    for part in range(parts):
        first = 4 * share * part - 4
        block = jnp.zeros((rows, LANES), F32)
        for delta, frames in enumerate(taps):
            band = lane - width * delta + first
            here = (lane >= width * delta) & (lane < width * (delta + 1)) & (band >= 0) & (band < MELS)
            shift = (width * delta - first) % LANES
            block = jnp.where(here, pltpu.roll(frames, shift, 1) if shift else frames, block)
        blocks[part] = jnp.dot(routing, block.astype(BF16), preferred_element_type=F32).astype(BF16)
    mine, _ = place(parts)
    for step in range(parts):
        outs_refs[step][...] = blocks[mine ^ step]
    wait_all(pieces)


def stacked(parts, pieces, stack_out, sems, base):
    part, _ = place(parts)
    return [
        pltpu.make_async_copy(pieces[step], stack_out.at[part ^ step], sems.at[base + step])
        for step in range(parts)
    ]


def conv_kernel(parts, width, conv1_ref, conv2_ref, *refs):
    part, copy_index = place(parts)
    mine = lax.axis_index("dp")
    windows = lax.axis_size("dp")
    copies = windows // parts
    mel_refs, refs = refs[:parts], refs[parts:]
    proj_refs, refs = refs[:copies], refs[copies:]
    outs_refs, refs = refs[:windows], refs[windows:]
    mel, banded_ref, even, odd, second, conv2, proj, partial, sems = refs
    load_conv2 = pltpu.make_async_copy(conv2_ref, conv2, sems.at[0])
    load_conv2.start()
    loads = []
    for step in range(copies):
        slot = copy_index ^ step
        loads.append(pltpu.make_async_copy(proj_refs[step], proj.at[slot], sems.at[1 + step]))
    start_all(loads)
    banded_weights(width, conv1_ref, banded_ref)
    streams = mel_refs[0].shape[0] // JS
    n = parts * streams
    for step in range(parts):
        mel[part ^ step] = mel_refs[step][...].astype(F32)
    evens = jnp.concatenate(
        [mel[p, j * streams : (j + 1) * streams, :] for j in range(JS) for p in range(parts)], axis=0
    )
    odds = pltpu.roll(evens[: W * n], LANES - 2 * width, 1).astype(BF16)
    evens = evens.astype(BF16)
    channels = conv2.shape[1]
    outs = banded_ref.shape[1] // channels
    for g in range(outs):
        lanes = slice(g * channels, (g + 1) * channels)
        weight = banded_ref[:, lanes]
        even[:, lanes] = jax.nn.relu(jnp.dot(evens, weight, preferred_element_type=F32)).astype(BF16)
        odd[:, lanes] = jax.nn.relu(jnp.dot(odds, weight, preferred_element_type=F32)).astype(BF16)

    load_conv2.wait()
    order = row_order(parts, streams)
    for h in range((outs - 1) // 2):
        lanes = slice(2 * h * channels, (2 * h + 3) * channels)
        depth = 3 * channels
        total = jnp.dot(even[: W * n, lanes], conv2[:depth], preferred_element_type=F32)
        total += jnp.dot(odd[:, lanes], conv2[depth : 2 * depth], preferred_element_type=F32)
        total += jnp.dot(even[n:, lanes], conv2[2 * depth :], preferred_element_type=F32)
        second[:, h * channels : (h + 1) * channels] = jnp.dot(
            order, jax.nn.relu(total).astype(BF16), preferred_element_type=F32
        ).astype(BF16)
    wait_all(loads)
    weights = proj[...].reshape(second.shape[1], proj.shape[2])
    partial[...] = jnp.dot(second[...], weights, preferred_element_type=F32)
    rows = W * parts
    for step in range(windows):
        at = pl.multiple_of((mine ^ step) * rows, rows)
        outs_refs[step][...] = partial[pl.ds(at, rows), :].astype(BF16)


def bounds(row, slots_ref, starts_ref, lengths_ref):
    begin, span = jnp.int32(0), jnp.int32(0)
    for u in range(slots_ref.shape[0]):
        chosen = slots_ref[u] == row
        begin = begin + jnp.where(chosen, starts_ref[u], 0)
        span = span + jnp.where(chosen, lengths_ref[u], 0)
    return begin, begin + span


def norm_kernel(parts, group, slots_ref, starts_ref, lengths_ref, *refs):
    _, copy_index = place(parts)
    windows = lax.axis_size("dp")
    copies = windows // parts
    part_refs, refs = refs[:windows], refs[windows:]
    piece_refs, refs = refs[:parts], refs[parts:]
    rows_out, normed_out, stack_out, encoded, sems = refs
    moves = stacked(parts, piece_refs, stack_out, sems, 0)
    start_all(moves)
    begin, end = bounds(lax.axis_index("dp"), slots_ref, starts_ref, lengths_ref)
    rows = W * parts
    for copy in range(copies):
        total = part_refs[copy][...].astype(F32)
        for step in range(1, parts):
            total += part_refs[step * copies + copy][...].astype(F32)
        at = pl.multiple_of((copy_index ^ copy) * rows, rows)
        encoded[pl.ds(at, rows), :] = total.astype(BF16)
    values = jnp.dot(frame_order(parts, copies), encoded[...], preferred_element_type=F32)
    mean = jnp.mean(values, axis=-1, keepdims=True)
    centered = values - mean
    variance = jnp.mean(centered * centered, axis=-1, keepdims=True)
    normed_out[...] = (centered * lax.rsqrt(variance + EPS_NORM)).astype(BF16)
    sample = samples(iota(windows * W, 1, 0), windows, group) + lax.axis_index("seq") * (W * SPAN)
    valid = (sample >= begin) & (sample < end)
    rows_out[...] = jnp.where(valid, values, 0.0).astype(BF16)
    wait_all(moves)


def attention_kernel(parts, windows, group, slots_ref, starts_ref, lengths_ref, *refs):
    _, copy_index = place(parts)
    plane = lax.axis_index("seq")
    copies = windows // parts
    normed_refs, refs = refs[:group], refs[group:]
    stack_refs, refs = refs[:copies], refs[copies:]
    weight_refs, refs = refs[:parts], refs[parts:]
    outs_refs, (stack_out, pieces, sems) = refs[:group], refs[group:]
    moves = stacked(parts, weight_refs, stack_out, sems, 0)
    start_all(moves)
    begin, end = bounds(lax.axis_index("dp"), slots_ref, starts_ref, lengths_ref)
    masks = []
    for step in range(group):
        sample = samples(iota(1, windows * W, 1), windows, group) + (plane ^ step) * (W * SPAN)
        masks.append(((sample >= begin) & (sample < end)).astype(F32))
    valid = jnp.concatenate(masks, axis=1) > 0.5
    local = normed_refs[0].shape[0]
    depth = pieces.shape[2]
    for step in range(group):
        for piece in range(windows):
            pieces[piece, step * local : (step + 1) * local, :] = normed_refs[step][
                :, piece * depth : (piece + 1) * depth
            ]
    mixed = 0.0
    for step in range(copies):
        slot = copy_index ^ step
        normed = jnp.concatenate([pieces[piece * copies + slot] for piece in range(parts)], axis=1)
        weights = stack_refs[step][...].reshape(parts * depth, stack_refs[step].shape[2])
        mixed += jnp.dot(normed, weights, preferred_element_type=F32)
    mixed = mixed.astype(BF16)
    width = mixed.shape[1] // 3
    scale = HEAD_DIM ** (-0.5)
    for head in range(width // HEAD_DIM):
        at = head * HEAD_DIM
        query = mixed[:, at : at + HEAD_DIM]
        key = mixed[:, width + at : width + at + HEAD_DIM]
        value = mixed[:, 2 * width + at : 2 * width + at + HEAD_DIM]
        scores = lax.dot_general(query, key, (((1,), (1,)), ((), ())), preferred_element_type=F32) * scale
        masked = jnp.where(valid, scores, MASKED)
        peak = jnp.max(masked, axis=1, keepdims=True)
        weight = jnp.where(valid, jnp.exp(masked - peak), 0.0)
        total = jnp.sum(weight, axis=1, keepdims=True)
        summed = jnp.dot(weight.astype(BF16), value, preferred_element_type=F32)
        context = (summed / total).astype(BF16)
        for step in range(group):
            outs_refs[step][:, at : at + HEAD_DIM] = context[step * local : (step + 1) * local]
    wait_all(moves)


def output_kernel(parts, windows, group, slots_ref, starts_ref, lengths_ref, *refs):
    context_refs, refs = refs[:group], refs[group:]
    stack_refs, refs = refs[: windows // parts], refs[windows // parts :]
    out_ref, context, pieces = refs
    _, copy_index = place(parts)
    copies = windows // parts
    plane = lax.axis_index("seq")
    begin, end = bounds(lax.axis_index("dp"), slots_ref, starts_ref, lengths_ref)
    head_width = context_refs[0].shape[1]
    for step in range(group):
        at = pl.multiple_of((plane ^ step) * head_width, LANES)
        context[:, pl.ds(at, head_width)] = context_refs[step][...]
    ordered = context[...]
    sample = samples(iota(windows * W, 1, 0), windows, group) + plane * (W * SPAN)
    valid = (sample >= begin) & (sample < end)
    for step in range(copies):
        slot = copy_index ^ step
        for piece in range(parts):
            pieces[piece * copies + slot] = jnp.dot(
                ordered, stack_refs[step][piece], preferred_element_type=F32
            )
    result = jnp.concatenate([pieces[d] for d in range(windows)], axis=1)
    out_ref[...] = jnp.where(valid, result, 0.0).astype(BF16)


def on_device(
    audio, starts, lengths, slots, conv1_weight, conv2_weight, proj_weight, qkv_weight, out_weight
):
    streams = audio.shape[0]
    windows = lax.axis_size("dp")
    group = lax.axis_size("seq")
    parts = math.gcd(windows, BANDS)
    copies = windows // parts
    assert streams == windows and all(count & (count - 1) == 0 for count in (parts, copies, group))
    share = BANDS // parts
    width = 4 * share + 4
    channels = conv1_weight.shape[1]
    features = proj_weight.shape[1]
    head_width = features // group
    local = windows * W
    rows = JS * streams
    n = parts * streams
    outs = 2 * share + 1
    scale = max(1, windows * group // 32)

    route = [(i, i + 1) for i in range(windows * group - 1)]
    rim = lax.ppermute(audio[:, audio.shape[1] - RIM :], ("dp", "seq"), route)

    def to_part(block, step):
        pairs = [(p * copies + c, (p ^ step) * copies + c) for p in range(parts) for c in range(copies)]
        return lax.ppermute(block, "dp", pairs)

    def to_copy(block, step):
        pairs = [(p * copies + c, p * copies + (c ^ step)) for p in range(parts) for c in range(copies)]
        return lax.ppermute(block, "dp", pairs)

    def to_window(block, step):
        return lax.ppermute(block, "dp", [(i, i ^ step) for i in range(windows)])

    def to_plane(block, step):
        return lax.ppermute(block, "seq", [(i, i ^ step) for i in range(group)])

    proj_all = [proj_weight] + [to_copy(proj_weight, step) for step in range(1, copies)]

    table = jnp.asarray(spectrum_table(N_FFT))
    mix_piece = jax.ShapeDtypeStruct((qkv_weight.shape[0], 3 * head_width), BF16)
    *mel_all, mix = pl.pallas_call(
        functools.partial(mel_kernel, parts, group),
        out_shape=tuple([jax.ShapeDtypeStruct((rows, LANES), BF16)] * parts + [mix_piece]),
        in_specs=[smem(), vmem()] + [anywhere()] * 3,
        out_specs=tuple([vmem()] * (parts + 1)),
        scratch_shapes=[
            pltpu.VMEM((streams, RIM + audio.shape[1]), F32),
            pltpu.VMEM(table.shape, F32),
            pltpu.VMEM((parts, rows, LANES), BF16),
            pltpu.SemaphoreType.DMA((5,)),
        ],
        compiler_params=params(60),
        cost_estimate=cost(2e9, 2e6),
        name="log_mel",
    )(slots, rim, audio, table, qkv_weight)
    mel_all = [mel_all[0]] + [to_part(mel_all[step], step) for step in range(1, parts)]
    mix_all = [mix] + [to_part(mix, step) for step in range(1, parts)]

    block = jax.ShapeDtypeStruct((local, features), BF16)
    partials = pl.pallas_call(
        functools.partial(conv_kernel, parts, width),
        out_shape=tuple([jax.ShapeDtypeStruct((W * parts, features), BF16)] * windows),
        in_specs=[vmem()] + [anywhere()] + [vmem()] * parts + [anywhere()] * copies,
        out_specs=tuple([vmem()] * windows),
        scratch_shapes=[
            pltpu.VMEM((parts, rows, LANES), F32),
            pltpu.VMEM((LANES, outs * channels), BF16),
            pltpu.VMEM((JS * n, outs * channels), BF16),
            pltpu.VMEM((W * n, outs * channels), BF16),
            pltpu.VMEM((W * n, share * channels), BF16),
            pltpu.VMEM(conv2_weight.shape, BF16),
            pltpu.VMEM((copies,) + proj_weight.shape, BF16),
            pltpu.VMEM((W * n, features), F32),
            pltpu.SemaphoreType.DMA((1 + copies,)),
        ],
        compiler_params=params(min(40 + 4 * scale, 56)),
        cost_estimate=cost(2e9, 4e6),
        name="conv",
    )(conv1_weight, conv2_weight, *mel_all, *proj_all)
    partials = [partials[0]] + [to_window(partials[step], step) for step in range(1, windows)]

    regrouped, normed, stack = pl.pallas_call(
        functools.partial(norm_kernel, parts, group),
        out_shape=(block, block, jax.ShapeDtypeStruct((parts,) + mix_piece.shape, BF16)),
        in_specs=[smem()] * 3 + [vmem()] * windows + [anywhere()] * parts,
        out_specs=(vmem(), vmem(), vmem()),
        scratch_shapes=[pltpu.VMEM((local, features), BF16), pltpu.SemaphoreType.DMA((parts,))],
        compiler_params=params(min(12 * scale, 32)),
        cost_estimate=cost(1e8, 1e6),
        name="layer_norm",
    )(slots, starts, lengths, *partials, *mix_all)
    mix_stacks = [stack] + [to_copy(stack, step) for step in range(1, copies)]
    normed, out_here = lax.optimization_barrier((normed, out_weight))
    normed = [normed] + [to_plane(normed, step) for step in range(1, group)]
    out_all = [out_here] + [to_part(out_here, step) for step in range(1, parts)]

    *context, stack = pl.pallas_call(
        functools.partial(attention_kernel, parts, windows, group),
        out_shape=tuple(
            [jax.ShapeDtypeStruct((local, head_width), BF16)] * group
            + [jax.ShapeDtypeStruct((parts,) + out_weight.shape, BF16)]
        ),
        in_specs=[smem()] * 3 + [vmem()] * (group + copies) + [anywhere()] * parts,
        out_specs=tuple([vmem()] * (group + 1)),
        scratch_shapes=[
            pltpu.VMEM((windows, group * local, qkv_weight.shape[0]), BF16),
            pltpu.SemaphoreType.DMA((parts,)),
        ],
        compiler_params=params(min(16 * scale, 48)),
        cost_estimate=cost(1e9, 2e6),
        name="attention",
    )(slots, starts, lengths, *normed, *mix_stacks, *out_all)
    context = [context[0]] + [to_plane(context[step], step) for step in range(1, group)]
    out_stacks = [stack] + [to_copy(stack, step) for step in range(1, copies)]

    attended = pl.pallas_call(
        functools.partial(output_kernel, parts, windows, group),
        out_shape=block,
        in_specs=[smem()] * 3 + [vmem()] * (group + copies),
        out_specs=vmem(),
        scratch_shapes=[
            pltpu.VMEM((local, features), BF16),
            pltpu.VMEM((windows, local, out_weight.shape[1]), F32),
        ],
        compiler_params=params(min(12 * scale, 32)),
        cost_estimate=cost(1e8, 3e6),
        name="output",
    )(slots, starts, lengths, *context, *out_stacks)
    shape = (1, windows, 1, W, features)
    return (regrouped.reshape(shape), attended.reshape(shape))


def solution(mesh):
    in_specs = (
        P(None, ("dp", "seq")),
        P(),
        P(),
        P(),
        P(),
        P(),
        P("dp", None),
        P("dp", None),
        P(None, "dp"),
    )
    out_specs = (P("dp", None, "seq", None, None), P("dp", None, "seq", None, None))
    return jax.shard_map(
        on_device, mesh=mesh, in_specs=in_specs, out_specs=out_specs, check_vma=False
    )
```

time: 74.9 us -> 76.9 us (1.027)
  the two profiles are of different devices: /device:TPU:2 before, /device:TPU:0 now
where the time goes in v1:
time: 76.9 us; the launch traced here: 76.5 us
  starting transfers between devices  31.5 us (41%)
  waiting for transfers between devices  23.8 us (31%)
  Pallas kernels  18.4 us (24%)
  local copies, waits for them, and re-layouts  2.12 us (3%)
  between operations  0.77 us (1%)
    ppermute x6, waiting for transfers between devices, to_plane(): return lax.ppermute(block, 'seq', [(i, i ^ step) for i in range(group)])  17.5 us
    ppermute x9, starting transfers between devices, to_part(): return lax.ppermute(block, 'dp', pairs)  14 us
    pallas_call x1, Pallas kernels, on_device(): pl.pallas_call(functools.partial(conv_kernel, parts, width), out_shape=tu...  7 us
    ppermute x7, starting transfers between devices, to_window(): return lax.ppermute(block, 'dp', [(i, i ^ step) for i in range(windows)])  6.33 us
    ppermute x6, starting transfers between devices, to_plane(): return lax.ppermute(block, 'seq', [(i, i ^ step) for i in range(group)])  5.75 us
    pallas_call x1, Pallas kernels, on_device(): pl.pallas_call(functools.partial(mel_kernel, parts, group), out_shape=tup...  5.01 us
    ppermute x1, starting transfers between devices, on_device(): rim = lax.ppermute(audio[:, audio.shape[1] - RIM:], ('dp', 'seq'), route)  4.63 us
    ppermute x7, waiting for transfers between devices, to_window(): return lax.ppermute(block, 'dp', [(i, i ^ step) for i in range(windows)])  3.91 us
  transfers between devices with their start and end apart: 26, of which 11 were waited for; matrix products, arithmetic and copies ran while one was open for 1% of the time, Pallas kernels for 16%

profile of v1, /device:TPU:0, one launch (start us, length us, event | category | flops | bytes accessed | tf_op | source)
XLA Modules:
  0.0 76.5 jit_solution(15814522256792020586)
XLA Ops:
  0.6 0.5 collective-permute-start.4
  1.1 0.8 slice.3
  1.9 4.6 %collective-permute-start = (f32[8,1024]{1,0:T(8,128)S(1)}, f32[8,1024]{1,0:T(8,128)S(1)}, u32[]{:S(2)}, u32[]{:S(2)}) collective-permute-start(f32[8,1024]{1,0:T(8,128)S(1)} %slice.3), channel_id=1, source_target_pairs={{0,1},{1,2},{2,3},{3,4},{4,5},{5,6},{6,7},{7,8},{8,9},{9,10},{10,1... | collective-permute-start | bytes 98312 | tf_op jit(solution)/shard_map/ppermute | solution.py:417
  6.6 1.6 %collective-permute-done.rim_ref = f32[8,1024]{1,0:T(8,128)S(1)} collective-permute-done((f32[8,1024]{1,0:T(8,128)S(1)}, f32[8,1024]{1,0:T(8,128)S(1)}, u32[]{:S(2)}, u32[]{:S(2)}) %collective-permute-start) | collective-permute-done | bytes 32800 | tf_op jit(solution)/shard_map/ppermute | solution.py:417
  8.1 0.6 copy-done.9
  8.7 5.0 %log_mel.1 = (bf16[72,128]{1,0:T(8,128)(2,1)}, bf16[72,128]{1,0:T(8,128)(2,1)}, bf16[72,128]{1,0:T(8,128)(2,1)}, bf16[72,128]{1,0:T(8,128)(2,1)}, bf16[128,768]{1,0:T(8,128)(2,1)}) custom-call(s32[8]{0:T(128)} %slots_ref.7, f32[8,1024]{1,0:T(8,128)} %copy-done.9, f32[8,5120]{1,0:T(8,128)} %audio_ref.1, f32[512,640]{1,0:T(8,128)} %constant.2.clone.table_ref, ...), custom_call_target="tpu_custom_call" | custom-call | flops 2000000000 | bytes 2000000 | tf_op jit(solution)/shard_map/log_mel/pallas_call | solution.py:437
  13.8 4.4 %collective-permute-start.1 = (bf16[72,128]{1,0:T(8,128)(2,1)}, bf16[72,128]{1,0:T(8,128)(2,1)S(1)}, u32[]{:S(2)}, u32[]{:S(2)}) collective-permute-start(bf16[72,128]{1,0:T(8,128)(2,1)} %get-tuple-element.26), channel_id=1, source_target_pairs={{0,8},{4,12},{8,0},{12,4},{16,24},{20,28},{24,16},{28,20},{1,9},{5... | collective-permute-start | bytes 55304 | tf_op jit(solution)/shard_map/ppermute | solution.py:421
  18.2 1.6 %collective-permute-start.2 = (bf16[72,128]{1,0:T(8,128)(2,1)}, bf16[72,128]{1,0:T(8,128)(2,1)S(1)}, u32[]{:S(2)}, u32[]{:S(2)}) collective-permute-start(bf16[72,128]{1,0:T(8,128)(2,1)} %get-tuple-element.27), channel_id=1, source_target_pairs={{0,16},{4,20},{8,24},{12,28},{16,0},{20,4},{24,8},{28,12},{1,17},{... | collective-permute-start | bytes 55304 | tf_op jit(solution)/shard_map/ppermute | solution.py:421
  19.8 0.9 %collective-permute-start.3 = (bf16[72,128]{1,0:T(8,128)(2,1)}, bf16[72,128]{1,0:T(8,128)(2,1)S(1)}, u32[]{:S(2)}, u32[]{:S(2)}) collective-permute-start(bf16[72,128]{1,0:T(8,128)(2,1)} %get-tuple-element.28), channel_id=1, source_target_pairs={{0,24},{4,28},{8,16},{12,20},{16,8},{20,12},{24,0},{28,4},{1,25},{... | collective-permute-start | bytes 55304 | tf_op jit(solution)/shard_map/ppermute | solution.py:421
  20.7 2.1 %collective-permute-start.14 = (bf16[128,768]{1,0:T(8,128)(2,1)}, bf16[128,768]{1,0:T(8,128)(2,1)S(1)}, u32[]{:S(2)}, u32[]{:S(2)}) collective-permute-start(bf16[128,768]{1,0:T(8,128)(2,1)} %get-tuple-element.37.refs_8_), channel_id=1, source_target_pairs={{0,24},{4,28},{8,16},{12,20},{16,8},{20,12},{24,0},{28,4},{1,25},{... | collective-permute-start | bytes 589832 | tf_op jit(solution)/shard_map/ppermute | solution.py:421
  22.7 0.0 collective-permute-done.1.refs_1_
  22.7 0.4 collective-permute-start.13
  23.2 1.1 %collective-permute-start.12 = (bf16[128,768]{1,0:T(8,128)(2,1)}, bf16[128,768]{1,0:T(8,128)(2,1)S(1)}, u32[]{:S(2)}, u32[]{:S(2)}) collective-permute-start(bf16[128,768]{1,0:T(8,128)(2,1)} %get-tuple-element.37.refs_8_), channel_id=1, source_target_pairs={{0,8},{4,12},{8,0},{12,4},{16,24},{20,28},{24,16},{28,20},{1,9},{5... | collective-permute-start | bytes 589832 | tf_op jit(solution)/shard_map/ppermute | solution.py:421
  24.2 0.8 %collective-permute-done.3.refs_3_ = bf16[72,128]{1,0:T(8,128)(2,1)S(1)} collective-permute-done((bf16[72,128]{1,0:T(8,128)(2,1)}, bf16[72,128]{1,0:T(8,128)(2,1)S(1)}, u32[]{:S(2)}, u32[]{:S(2)}) %collective-permute-start.3) | collective-permute-done | bytes 18464 | tf_op jit(solution)/shard_map/ppermute | solution.py:421
  25.0 0.0 collective-permute-done.4.refs_5_
  25.0 0.0 copy-start.8
  25.0 0.7 copy-done.8
  25.8 7.0 %conv.1 = (bf16[32,1024]{1,0:T(8,128)(2,1)S(1)}, bf16[32,1024]{1,0:T(8,128)(2,1)S(1)}, bf16[32,1024]{1,0:T(8,128)(2,1)S(1)}, bf16[32,1024]{1,0:T(8,128)(2,1)S(1)...) custom-call(bf16[9,256]{1,0:T(8,128)(2,1)S(1)} %copy-done.7, ...), custom_call_target="tpu_custom_call" | custom-call | flops 2000000000 | bytes 4000000 | tf_op jit(solution)/shard_map/conv/pallas_call | solution.py:456
  32.8 0.0 copy-start.6
  32.8 0.1 collective-permute-start.5
  32.9 1.5 %collective-permute-start.6 = (bf16[32,1024]{1,0:T(8,128)(2,1)S(1)}, bf16[32,1024]{1,0:T(8,128)(2,1)S(1)}, u32[]{:S(2)}, u32[]{:S(2)}) collective-permute-start(bf16[32,1024]{1,0:T(8,128)(2,1)S(1)} %get-tuple-element.31), channel_id=1, source_target_pairs={{0,8},{4,12},{8,0},{12,4},{16,24},{20,28},{24,16},{28,20},{1,9},{5... | collective-permute-start | bytes 196616 | tf_op jit(solution)/shard_map/ppermute | solution.py:428
  34.4 0.0 collective-permute-done.14.refs_11_
  34.4 0.4 collective-permute-start.7
  34.7 1.2 %collective-permute-start.8 = (bf16[32,1024]{1,0:T(8,128)(2,1)S(1)}, bf16[32,1024]{1,0:T(8,128)(2,1)S(1)}, u32[]{:S(2)}, u32[]{:S(2)}) collective-permute-start(bf16[32,1024]{1,0:T(8,128)(2,1)S(1)} %get-tuple-element.33), channel_id=1, source_target_pairs={{0,16},{4,20},{8,24},{12,28},{16,0},{20,4},{24,8},{28,12},{1,17},{... | collective-permute-start | bytes 196616 | tf_op jit(solution)/shard_map/ppermute | solution.py:428
  35.9 0.5 collective-permute-start.9
  36.4 1.3 %collective-permute-start.10 = (bf16[32,1024]{1,0:T(8,128)(2,1)S(1)}, bf16[32,1024]{1,0:T(8,128)(2,1)S(1)}, u32[]{:S(2)}, u32[]{:S(2)}) collective-permute-start(bf16[32,1024]{1,0:T(8,128)(2,1)S(1)} %get-tuple-element.35), channel_id=1, source_target_pairs={{0,24},{4,28},{8,16},{12,20},{16,8},{20,12},{24,0},{28,4},{1,25},{... | collective-permute-start | bytes 196616 | tf_op jit(solution)/shard_map/ppermute | solution.py:428
  37.7 1.4 %collective-permute-start.11 = (bf16[32,1024]{1,0:T(8,128)(2,1)S(1)}, bf16[32,1024]{1,0:T(8,128)(2,1)S(1)}, u32[]{:S(2)}, u32[]{:S(2)}) collective-permute-start(bf16[32,1024]{1,0:T(8,128)(2,1)S(1)} %get-tuple-element.36), channel_id=1, source_target_pairs={{0,28},{4,24},{8,20},{12,16},{16,12},{20,8},{24,4},{28,0},{1,29},{... | collective-permute-start | bytes 196616 | tf_op jit(solution)/shard_map/ppermute | solution.py:428
  39.1 0.1 collective-permute-done.8.refs_4_
  39.3 1.0 %collective-permute-done.9.refs_5_ = bf16[32,1024]{1,0:T(8,128)(2,1)S(1)} collective-permute-done((bf16[32,1024]{1,0:T(8,128)(2,1)S(1)}, bf16[32,1024]{1,0:T(8,128)(2,1)S(1)}, u32[]{:S(2)}, u32[]{:S(2)}) %collective-permute-start.9) | collective-permute-done | bytes 65568 | tf_op jit(solution)/shard_map/ppermute | solution.py:428
  40.3 1.8 %collective-permute-done.10.refs_6_ = bf16[32,1024]{1,0:T(8,128)(2,1)S(1)} collective-permute-done((bf16[32,1024]{1,0:T(8,128)(2,1)S(1)}, bf16[32,1024]{1,0:T(8,128)(2,1)S(1)}, u32[]{:S(2)}, u32[]{:S(2)}) %collective-permute-start.10) | collective-permute-done | bytes 65568 | tf_op jit(solution)/shard_map/ppermute | solution.py:428
  42.1 0.9 %collective-permute-done.11.refs_7_ = bf16[32,1024]{1,0:T(8,128)(2,1)S(1)} collective-permute-done((bf16[32,1024]{1,0:T(8,128)(2,1)S(1)}, bf16[32,1024]{1,0:T(8,128)(2,1)S(1)}, u32[]{:S(2)}, u32[]{:S(2)}) %collective-permute-start.11) | collective-permute-done | bytes 65568 | tf_op jit(solution)/shard_map/ppermute | solution.py:428
  43.1 2.7 %layer_norm.1 = (bf16[64,1024]{1,0:T(8,128)(2,1)}, bf16[64,1024]{1,0:T(8,128)(2,1)S(1)}, bf16[4,128,768]{2,1,0:T(8,128)(2,1)S(1)}) custom-call(s32[8]{0:T(128)S(1)} %copy-done.1, s32[8]{0:T(128)S(1)} %copy-done.2, s32[8]{0:T(128)S(1)} %copy-done.3, bf16[32,1024]{1,0:T(8,128)(2,1)S(1)} %get-tuple-element.29.refs_0_, ...), custom_call_target="tpu_custom_call" | custom-call | flops 100000000 | bytes 1000000 | tf_op jit(solution)/shard_map/layer_norm/pallas_call | solution.py:478
  45.8 0.1 collective-permute-start.18
  45.9 1.3 %collective-permute-start.17 = (bf16[64,1024]{1,0:T(8,128)(2,1)S(1)}, bf16[64,1024]{1,0:T(8,128)(2,1)S(1)}, u32[]{:S(2)}, u32[]{:S(2)}) collective-permute-start(bf16[64,1024]{1,0:T(8,128)(2,1)S(1)} %get-tuple-element.40.refs_0_), channel_id=1, source_target_pairs={{0,3},{1,2},{2,1},{3,0},{4,7},{5,6},{6,5},{7,4},{8,11},{9,10},{10,... | collective-permute-start | bytes 393224 | tf_op jit(solution)/shard_map/ppermute | solution.py:431
  47.2 1.3 %collective-permute-start.21 = (bf16[1024,128]{1,0:T(8,128)(2,1)S(1)}, bf16[1024,128]{1,0:T(8,128)(2,1)S(1)}, u32[]{:S(2)}, u32[]{:S(2)}) collective-permute-start(bf16[1024,128]{1,0:T(8,128)(2,1)S(1)} %copy-done.6), channel_id=1, source_target_pairs={{0,24},{4,28},{8,16},{12,20},{16,8},{20,12},{24,0},{28,4},{1,25},{... | collective-permute-start | bytes 786440 | tf_op jit(solution)/shard_map/ppermute | solution.py:421
  48.6 0.7 collective-permute-start.20
  49.3 4.8 %collective-permute-done.17.refs_3_ = bf16[64,1024]{1,0:T(8,128)(2,1)S(1)} collective-permute-done((bf16[64,1024]{1,0:T(8,128)(2,1)S(1)}, bf16[64,1024]{1,0:T(8,128)(2,1)S(1)}, u32[]{:S(2)}, u32[]{:S(2)}) %collective-permute-start.17) | collective-permute-done | bytes 131104 | tf_op jit(solution)/shard_map/ppermute | solution.py:431
  54.1 1.5 %collective-permute-start.19 = (bf16[1024,128]{1,0:T(8,128)(2,1)S(1)}, bf16[1024,128]{1,0:T(8,128)(2,1)S(1)}, u32[]{:S(2)}, u32[]{:S(2)}) collective-permute-start(bf16[1024,128]{1,0:T(8,128)(2,1)S(1)} %copy-done.6), channel_id=1, source_target_pairs={{0,8},{4,12},{8,0},{12,4},{16,24},{20,28},{24,16},{28,20},{1,9},{5... | collective-permute-start | bytes 786440 | tf_op jit(solution)/shard_map/ppermute | solution.py:421
  55.7 3.5 %collective-permute-done.16.refs_2_ = bf16[64,1024]{1,0:T(8,128)(2,1)S(1)} collective-permute-done((bf16[64,1024]{1,0:T(8,128)(2,1)S(1)}, bf16[64,1024]{1,0:T(8,128)(2,1)S(1)}, u32[]{:S(2)}, u32[]{:S(2)}) %collective-permute-start.16) | collective-permute-done | bytes 131104 | tf_op jit(solution)/shard_map/ppermute | solution.py:431
  59.2 5.4 %collective-permute-done.15.refs_1_ = bf16[64,1024]{1,0:T(8,128)(2,1)S(1)} collective-permute-done((bf16[64,1024]{1,0:T(8,128)(2,1)S(1)}, bf16[64,1024]{1,0:T(8,128)(2,1)S(1)}, u32[]{:S(2)}, u32[]{:S(2)}) %collective-permute-start.15) | collective-permute-done | bytes 131104 | tf_op jit(solution)/shard_map/ppermute | solution.py:431
  64.7 1.9 %attention.1 = (bf16[64,256]{1,0:T(8,128)(2,1)S(1)}, bf16[64,256]{1,0:T(8,128)(2,1)S(1)}, bf16[64,256]{1,0:T(8,128)(2,1)S(1)}, bf16[64,256]{1,0:T(8,128)(2,1)S(1)}, bf16[4,1024,128]{2,1,0:T(8,128)(2,1)S(1)}) custom-call(s32[8]{0:T(128)S(1)} %copy-done.1, s32[8]{0:T(128)S(1)} %copy-done.2, s32[8]{0:T(128)S(1)} %copy-done.3, ...), custom_call_target="tpu_custom_call" | custom-call | flops 1000000000 | bytes 2000000 | tf_op jit(solution)/shard_map/attention/pallas_call | solution.py:493
  66.6 0.1 collective-permute-start.25
  66.7 0.3 collective-permute-start.22
  67.1 2.1 %collective-permute-start.23 = (bf16[64,256]{1,0:T(8,128)(2,1)S(1)}, bf16[64,256]{1,0:T(8,128)(2,1)S(1)}, u32[]{:S(2)}, u32[]{:S(2)}) collective-permute-start(bf16[64,256]{1,0:T(8,128)(2,1)S(1)} %get-tuple-element.45), channel_id=1, source_target_pairs={{0,2},{1,3},{2,0},{3,1},{4,6},{5,7},{6,4},{7,5},{8,10},{9,11},{10,... | collective-permute-start | bytes 98312 | tf_op jit(solution)/shard_map/ppermute | solution.py:431
  69.1 2.0 %collective-permute-start.24 = (bf16[64,256]{1,0:T(8,128)(2,1)S(1)}, bf16[64,256]{1,0:T(8,128)(2,1)S(1)}, u32[]{:S(2)}, u32[]{:S(2)}) collective-permute-start(bf16[64,256]{1,0:T(8,128)(2,1)S(1)} %get-tuple-element.46), channel_id=1, source_target_pairs={{0,3},{1,2},{2,1},{3,0},{4,7},{5,6},{6,5},{7,4},{8,11},{9,10},{10,... | collective-permute-start | bytes 98312 | tf_op jit(solution)/shard_map/ppermute | solution.py:431
  71.2 1.3 %collective-permute-done.23.refs_2_ = bf16[64,256]{1,0:T(8,128)(2,1)S(1)} collective-permute-done((bf16[64,256]{1,0:T(8,128)(2,1)S(1)}, bf16[64,256]{1,0:T(8,128)(2,1)S(1)}, u32[]{:S(2)}, u32[]{:S(2)}) %collective-permute-start.23) | collective-permute-done | bytes 32800 | tf_op jit(solution)/shard_map/ppermute | solution.py:431
  72.5 2.4 %collective-permute-done.24.refs_3_ = bf16[64,256]{1,0:T(8,128)(2,1)S(1)} collective-permute-done((bf16[64,256]{1,0:T(8,128)(2,1)S(1)}, bf16[64,256]{1,0:T(8,128)(2,1)S(1)}, u32[]{:S(2)}, u32[]{:S(2)}) %collective-permute-start.24) | collective-permute-done | bytes 32800 | tf_op jit(solution)/shard_map/ppermute | solution.py:431
  74.9 1.7 %output.1 = bf16[64,1024]{1,0:T(8,128)(2,1)} custom-call(s32[8]{0:T(128)S(1)} %copy-done.1, s32[8]{0:T(128)S(1)} %copy-done.2, s32[8]{0:T(128)S(1)} %copy-done.3, bf16[64,256]{1,0:T(8,128)(2,1)S(1)} %get-tuple-element.43.refs_0_, bf16[64,256]{1,0:T(8,128)(2,1)S(1)} %collective-permute-done.22.refs_1_, bf16[64,256]{1,0:T(8,128)(2,1)S(1)} %collective-permute-done.23.refs_2_, ...), custom_call_target="tpu_custom_call" | custom-call | flops 100000000 | bytes 3000000 | tf_op jit(solution)/shard_map/output/pallas_call | solution.py:512
  (30 shorter events, 0.1 us)
Async XLA Ops:
  0.6 24.4 %collective-permute-start.4 = (bf16[640,1024]{1,0:T(8,128)(2,1)}, bf16[640,1024]{1,0:T(8,128)(2,1)S(1)}, u32[]{:S(2)}, u32[]{:S(2)}) collective-permute-start(bf16[640,1024]{1,0:T(8,128)(2,1)} %refs_4_.1), channel_id=1, source_target_pairs={{0,4},{4,0},{8,12},{12,8},{16,20},{20,16},{24,28},{28,24},{1,5},{5... | collective-permute-start | bytes 3932168 | tf_op jit(solution)/shard_map/ppermute | solution.py:425
  1.9 23.1 %copy-start.4 = (bf16[640,1024]{1,0:T(8,128)(2,1)S(1)}, bf16[640,1024]{1,0:T(8,128)(2,1)}, u32[]{:S(2)}) copy-start(bf16[640,1024]{1,0:T(8,128)(2,1)} %refs_4_.1) | copy-start | bytes 3932164
  1.9 23.1 %copy-start.5 = (bf16[2304,256]{1,0:T(8,128)(2,1)S(1)}, bf16[2304,256]{1,0:T(8,128)(2,1)}, u32[]{:S(2)}) copy-start(bf16[2304,256]{1,0:T(8,128)(2,1)} %conv2_ref.1) | copy-start | bytes 3538948
  1.9 23.1 %copy-start.7 = (bf16[9,256]{1,0:T(8,128)(2,1)S(1)}, bf16[9,256]{1,0:T(8,128)(2,1)}, u32[]{:S(2)}) copy-start(bf16[9,256]{1,0:T(8,128)(2,1)} %conv1_ref.1) | copy-start | bytes 13828
  1.9 6.2 %collective-permute-start = (f32[8,1024]{1,0:T(8,128)S(1)}, f32[8,1024]{1,0:T(8,128)S(1)}, u32[]{:S(2)}, u32[]{:S(2)}) collective-permute-start(f32[8,1024]{1,0:T(8,128)S(1)} %slice.3), channel_id=1, source_target_pairs={{0,1},{1,2},{2,3},{3,4},{4,5},{5,6},{6,7},{7,8},{8,9},{9,10},{10,1... | collective-permute-start | bytes 98312 | tf_op jit(solution)/shard_map/ppermute | solution.py:417
  8.1 0.6 copy-start.9
  13.8 9.0 %collective-permute-start.1 = (bf16[72,128]{1,0:T(8,128)(2,1)}, bf16[72,128]{1,0:T(8,128)(2,1)S(1)}, u32[]{:S(2)}, u32[]{:S(2)}) collective-permute-start(bf16[72,128]{1,0:T(8,128)(2,1)} %get-tuple-element.26), channel_id=1, source_target_pairs={{0,8},{4,12},{8,0},{12,4},{16,24},{20,28},{24,16},{28,20},{1,9},{5... | collective-permute-start | bytes 55304 | tf_op jit(solution)/shard_map/ppermute | solution.py:421
  18.2 5.0 %collective-permute-start.2 = (bf16[72,128]{1,0:T(8,128)(2,1)}, bf16[72,128]{1,0:T(8,128)(2,1)S(1)}, u32[]{:S(2)}, u32[]{:S(2)}) collective-permute-start(bf16[72,128]{1,0:T(8,128)(2,1)} %get-tuple-element.27), channel_id=1, source_target_pairs={{0,16},{4,20},{8,24},{12,28},{16,0},{20,4},{24,8},{28,12},{1,17},{... | collective-permute-start | bytes 55304 | tf_op jit(solution)/shard_map/ppermute | solution.py:421
  19.8 5.2 %collective-permute-start.3 = (bf16[72,128]{1,0:T(8,128)(2,1)}, bf16[72,128]{1,0:T(8,128)(2,1)S(1)}, u32[]{:S(2)}, u32[]{:S(2)}) collective-permute-start(bf16[72,128]{1,0:T(8,128)(2,1)} %get-tuple-element.28), channel_id=1, source_target_pairs={{0,24},{4,28},{8,16},{12,20},{16,8},{20,12},{24,0},{28,4},{1,25},{... | collective-permute-start | bytes 55304 | tf_op jit(solution)/shard_map/ppermute | solution.py:421
  20.7 13.7 %collective-permute-start.14 = (bf16[128,768]{1,0:T(8,128)(2,1)}, bf16[128,768]{1,0:T(8,128)(2,1)S(1)}, u32[]{:S(2)}, u32[]{:S(2)}) collective-permute-start(bf16[128,768]{1,0:T(8,128)(2,1)} %get-tuple-element.37.refs_8_), channel_id=1, source_target_pairs={{0,24},{4,28},{8,16},{12,20},{16,8},{20,12},{24,0},{28,4},{1,25},{... | collective-permute-start | bytes 589832 | tf_op jit(solution)/shard_map/ppermute | solution.py:421
  22.7 12.0 %collective-permute-start.13 = (bf16[128,768]{1,0:T(8,128)(2,1)}, bf16[128,768]{1,0:T(8,128)(2,1)S(1)}, u32[]{:S(2)}, u32[]{:S(2)}) collective-permute-start(bf16[128,768]{1,0:T(8,128)(2,1)} %get-tuple-element.37.refs_8_), channel_id=1, source_target_pairs={{0,16},{4,20},{8,24},{12,28},{16,0},{20,4},{24,8},{28,12},{1,17},{... | collective-permute-start | bytes 589832 | tf_op jit(solution)/shard_map/ppermute | solution.py:421
  23.2 12.7 %collective-permute-start.12 = (bf16[128,768]{1,0:T(8,128)(2,1)}, bf16[128,768]{1,0:T(8,128)(2,1)S(1)}, u32[]{:S(2)}, u32[]{:S(2)}) collective-permute-start(bf16[128,768]{1,0:T(8,128)(2,1)} %get-tuple-element.37.refs_8_), channel_id=1, source_target_pairs={{0,8},{4,12},{8,0},{12,4},{16,24},{20,28},{24,16},{28,20},{1,9},{5... | collective-permute-start | bytes 589832 | tf_op jit(solution)/shard_map/ppermute | solution.py:421
  25.0 0.7 copy-start.8
  25.8 17.3 %copy-start = (bf16[128,768]{1,0:T(8,128)(2,1)S(1)}, bf16[128,768]{1,0:T(8,128)(2,1)}, u32[]{:S(2)}) copy-start(bf16[128,768]{1,0:T(8,128)(2,1)} %get-tuple-element.37.refs_8_) | copy-start | bytes 589828
  25.8 17.3 %copy-start.1 = (s32[8]{0:T(128)S(1)}, s32[8]{0:T(128)}, u32[]{:S(2)}) copy-start(s32[8]{0:T(128)} %slots_ref.7) | copy-start | bytes 100
  25.8 17.3 %copy-start.2 = (s32[8]{0:T(128)S(1)}, s32[8]{0:T(128)}, u32[]{:S(2)}) copy-start(s32[8]{0:T(128)} %starts_ref.5) | copy-start | bytes 100
  25.8 17.3 %copy-start.3 = (s32[8]{0:T(128)S(1)}, s32[8]{0:T(128)}, u32[]{:S(2)}) copy-start(s32[8]{0:T(128)} %lengths_ref.5) | copy-start | bytes 100
  32.8 14.5 %copy-start.6 = (bf16[1024,128]{1,0:T(8,128)(2,1)S(1)}, bf16[1024,128]{1,0:T(8,128)(2,1)}, u32[]{:S(2)}) copy-start(bf16[1024,128]{1,0:T(8,128)(2,1)} %refs_6_) | copy-start | bytes 786436
  32.8 3.7 %collective-permute-start.5 = (bf16[32,1024]{1,0:T(8,128)(2,1)S(1)}, bf16[32,1024]{1,0:T(8,128)(2,1)S(1)}, u32[]{:S(2)}, u32[]{:S(2)}) collective-permute-start(bf16[32,1024]{1,0:T(8,128)(2,1)S(1)} %get-tuple-element.30), channel_id=1, source_target_pairs={{0,4},{4,0},{8,12},{12,8},{16,20},{20,16},{24,28},{28,24},{1,5},{5... | collective-permute-start | bytes 196616 | tf_op jit(solution)/shard_map/ppermute | solution.py:428
  32.9 4.9 %collective-permute-start.6 = (bf16[32,1024]{1,0:T(8,128)(2,1)S(1)}, bf16[32,1024]{1,0:T(8,128)(2,1)S(1)}, u32[]{:S(2)}, u32[]{:S(2)}) collective-permute-start(bf16[32,1024]{1,0:T(8,128)(2,1)S(1)} %get-tuple-element.31), channel_id=1, source_target_pairs={{0,8},{4,12},{8,0},{12,4},{16,24},{20,28},{24,16},{28,20},{1,9},{5... | collective-permute-start | bytes 196616 | tf_op jit(solution)/shard_map/ppermute | solution.py:428
  34.4 4.8 %collective-permute-start.7 = (bf16[32,1024]{1,0:T(8,128)(2,1)S(1)}, bf16[32,1024]{1,0:T(8,128)(2,1)S(1)}, u32[]{:S(2)}, u32[]{:S(2)}) collective-permute-start(bf16[32,1024]{1,0:T(8,128)(2,1)S(1)} %get-tuple-element.32), channel_id=1, source_target_pairs={{0,12},{4,8},{8,4},{12,0},{16,28},{20,24},{24,20},{28,16},{1,13},{... | collective-permute-start | bytes 196616 | tf_op jit(solution)/shard_map/ppermute | solution.py:428
  34.7 4.6 %collective-permute-start.8 = (bf16[32,1024]{1,0:T(8,128)(2,1)S(1)}, bf16[32,1024]{1,0:T(8,128)(2,1)S(1)}, u32[]{:S(2)}, u32[]{:S(2)}) collective-permute-start(bf16[32,1024]{1,0:T(8,128)(2,1)S(1)} %get-tuple-element.33), channel_id=1, source_target_pairs={{0,16},{4,20},{8,24},{12,28},{16,0},{20,4},{24,8},{28,12},{1,17},{... | collective-permute-start | bytes 196616 | tf_op jit(solution)/shard_map/ppermute | solution.py:428
  35.9 4.3 %collective-permute-start.9 = (bf16[32,1024]{1,0:T(8,128)(2,1)S(1)}, bf16[32,1024]{1,0:T(8,128)(2,1)S(1)}, u32[]{:S(2)}, u32[]{:S(2)}) collective-permute-start(bf16[32,1024]{1,0:T(8,128)(2,1)S(1)} %get-tuple-element.34), channel_id=1, source_target_pairs={{0,20},{4,16},{8,28},{12,24},{16,4},{20,0},{24,12},{28,8},{1,21},{... | collective-permute-start | bytes 196616 | tf_op jit(solution)/shard_map/ppermute | solution.py:428
  36.4 5.7 %collective-permute-start.10 = (bf16[32,1024]{1,0:T(8,128)(2,1)S(1)}, bf16[32,1024]{1,0:T(8,128)(2,1)S(1)}, u32[]{:S(2)}, u32[]{:S(2)}) collective-permute-start(bf16[32,1024]{1,0:T(8,128)(2,1)S(1)} %get-tuple-element.35), channel_id=1, source_target_pairs={{0,24},{4,28},{8,16},{12,20},{16,8},{20,12},{24,0},{28,4},{1,25},{... | collective-permute-start | bytes 196616 | tf_op jit(solution)/shard_map/ppermute | solution.py:428
  37.7 5.3 %collective-permute-start.11 = (bf16[32,1024]{1,0:T(8,128)(2,1)S(1)}, bf16[32,1024]{1,0:T(8,128)(2,1)S(1)}, u32[]{:S(2)}, u32[]{:S(2)}) collective-permute-start(bf16[32,1024]{1,0:T(8,128)(2,1)S(1)} %get-tuple-element.36), channel_id=1, source_target_pairs={{0,28},{4,24},{8,20},{12,16},{16,12},{20,8},{24,4},{28,0},{1,29},{... | collective-permute-start | bytes 196616 | tf_op jit(solution)/shard_map/ppermute | solution.py:428
  45.8 18.9 %collective-permute-start.18 = (bf16[4,128,768]{2,1,0:T(8,128)(2,1)S(1)}, bf16[4,128,768]{2,1,0:T(8,128)(2,1)S(1)}, u32[]{:S(2)}, u32[]{:S(2)}) collective-permute-start(bf16[4,128,768]{2,1,0:T(8,128)(2,1)S(1)} %get-tuple-element.41.refs_4_), channel_id=1, source_target_pairs={{0,4},{4,0},{8,12},{12,8},{16,20},{20,16},{24,28},{28,24},{1,5},{5... | collective-permute-start | bytes 2359304 | tf_op jit(solution)/shard_map/ppermute | solution.py:425
  45.9 8.2 %collective-permute-start.17 = (bf16[64,1024]{1,0:T(8,128)(2,1)S(1)}, bf16[64,1024]{1,0:T(8,128)(2,1)S(1)}, u32[]{:S(2)}, u32[]{:S(2)}) collective-permute-start(bf16[64,1024]{1,0:T(8,128)(2,1)S(1)} %get-tuple-element.40.refs_0_), channel_id=1, source_target_pairs={{0,3},{1,2},{2,1},{3,0},{4,7},{5,6},{6,5},{7,4},{8,11},{9,10},{10,... | collective-permute-start | bytes 393224 | tf_op jit(solution)/shard_map/ppermute | solution.py:431
  47.2 12.0 %collective-permute-start.16 = (bf16[64,1024]{1,0:T(8,128)(2,1)S(1)}, bf16[64,1024]{1,0:T(8,128)(2,1)S(1)}, u32[]{:S(2)}, u32[]{:S(2)}) collective-permute-start(bf16[64,1024]{1,0:T(8,128)(2,1)S(1)} %get-tuple-element.40.refs_0_), channel_id=1, source_target_pairs={{0,2},{1,3},{2,0},{3,1},{4,6},{5,7},{6,4},{7,5},{8,10},{9,11},{10,... | collective-permute-start | bytes 393224 | tf_op jit(solution)/shard_map/ppermute | solution.py:431
  47.2 17.4 %collective-permute-start.21 = (bf16[1024,128]{1,0:T(8,128)(2,1)S(1)}, bf16[1024,128]{1,0:T(8,128)(2,1)S(1)}, u32[]{:S(2)}, u32[]{:S(2)}) collective-permute-start(bf16[1024,128]{1,0:T(8,128)(2,1)S(1)} %copy-done.6), channel_id=1, source_target_pairs={{0,24},{4,28},{8,16},{12,20},{16,8},{20,12},{24,0},{28,4},{1,25},{... | collective-permute-start | bytes 786440 | tf_op jit(solution)/shard_map/ppermute | solution.py:421
  48.6 16.1 %collective-permute-start.20 = (bf16[1024,128]{1,0:T(8,128)(2,1)S(1)}, bf16[1024,128]{1,0:T(8,128)(2,1)S(1)}, u32[]{:S(2)}, u32[]{:S(2)}) collective-permute-start(bf16[1024,128]{1,0:T(8,128)(2,1)S(1)} %copy-done.6), channel_id=1, source_target_pairs={{0,16},{4,20},{8,24},{12,28},{16,0},{20,4},{24,8},{28,12},{1,17},{... | collective-permute-start | bytes 786440 | tf_op jit(solution)/shard_map/ppermute | solution.py:421
  54.1 10.5 %collective-permute-start.19 = (bf16[1024,128]{1,0:T(8,128)(2,1)S(1)}, bf16[1024,128]{1,0:T(8,128)(2,1)S(1)}, u32[]{:S(2)}, u32[]{:S(2)}) collective-permute-start(bf16[1024,128]{1,0:T(8,128)(2,1)S(1)} %copy-done.6), channel_id=1, source_target_pairs={{0,8},{4,12},{8,0},{12,4},{16,24},{20,28},{24,16},{28,20},{1,9},{5... | collective-permute-start | bytes 786440 | tf_op jit(solution)/shard_map/ppermute | solution.py:421
  59.2 5.4 %collective-permute-start.15 = (bf16[64,1024]{1,0:T(8,128)(2,1)S(1)}, bf16[64,1024]{1,0:T(8,128)(2,1)S(1)}, u32[]{:S(2)}, u32[]{:S(2)}) collective-permute-start(bf16[64,1024]{1,0:T(8,128)(2,1)S(1)} %get-tuple-element.40.refs_0_), channel_id=1, source_target_pairs={{0,1},{1,0},{2,3},{3,2},{4,5},{5,4},{6,7},{7,6},{8,9},{9,8},{10,11... | collective-permute-start | bytes 393224 | tf_op jit(solution)/shard_map/ppermute | solution.py:431
  66.6 8.2 %collective-permute-start.25 = (bf16[4,1024,128]{2,1,0:T(8,128)(2,1)S(1)}, bf16[4,1024,128]{2,1,0:T(8,128)(2,1)S(1)}, u32[]{:S(2)}, u32[]{:S(2)}) collective-permute-start(bf16[4,1024,128]{2,1,0:T(8,128)(2,1)S(1)} %get-tuple-element.47.refs_4_), channel_id=1, source_target_pairs={{0,4},{4,0},{8,12},{12,8},{16,20},{20,16},{24,28},{28,24},{1,5},{5... | collective-permute-start | bytes 3145736 | tf_op jit(solution)/shard_map/ppermute | solution.py:425
  66.7 4.5 %collective-permute-start.22 = (bf16[64,256]{1,0:T(8,128)(2,1)S(1)}, bf16[64,256]{1,0:T(8,128)(2,1)S(1)}, u32[]{:S(2)}, u32[]{:S(2)}) collective-permute-start(bf16[64,256]{1,0:T(8,128)(2,1)S(1)} %get-tuple-element.44), channel_id=1, source_target_pairs={{0,1},{1,0},{2,3},{3,2},{4,5},{5,4},{6,7},{7,6},{8,9},{9,8},{10,11... | collective-permute-start | bytes 98312 | tf_op jit(solution)/shard_map/ppermute | solution.py:431
  67.1 5.4 %collective-permute-start.23 = (bf16[64,256]{1,0:T(8,128)(2,1)S(1)}, bf16[64,256]{1,0:T(8,128)(2,1)S(1)}, u32[]{:S(2)}, u32[]{:S(2)}) collective-permute-start(bf16[64,256]{1,0:T(8,128)(2,1)S(1)} %get-tuple-element.45), channel_id=1, source_target_pairs={{0,2},{1,3},{2,0},{3,1},{4,6},{5,7},{6,4},{7,5},{8,10},{9,11},{10,... | collective-permute-start | bytes 98312 | tf_op jit(solution)/shard_map/ppermute | solution.py:431
  69.1 5.7 %collective-permute-start.24 = (bf16[64,256]{1,0:T(8,128)(2,1)S(1)}, bf16[64,256]{1,0:T(8,128)(2,1)S(1)}, u32[]{:S(2)}, u32[]{:S(2)}) collective-permute-start(bf16[64,256]{1,0:T(8,128)(2,1)S(1)} %get-tuple-element.46), channel_id=1, source_target_pairs={{0,3},{1,2},{2,1},{3,0},{4,7},{5,6},{6,5},{7,4},{8,11},{9,10},{10,... | collective-permute-start | bytes 98312 | tf_op jit(solution)/shard_map/ppermute | solution.py:431

commit v2 on v1

--- a/solution.py
+++ b/solution.py
@@ -235,14 +235,16 @@
     copies = windows // parts
     mel_refs, refs = refs[:parts], refs[parts:]
     proj_refs, refs = refs[:copies], refs[copies:]
+    weight_refs, refs = refs[:parts], refs[parts:]
     outs_refs, refs = refs[:windows], refs[windows:]
-    mel, banded_ref, even, odd, second, conv2, proj, partial, sems = refs
+    stack_out, mel, banded_ref, even, odd, second, conv2, proj, partial, sems = refs
     load_conv2 = pltpu.make_async_copy(conv2_ref, conv2, sems.at[0])
     load_conv2.start()
     loads = []
     for step in range(copies):
         slot = copy_index ^ step
         loads.append(pltpu.make_async_copy(proj_refs[step], proj.at[slot], sems.at[1 + step]))
+    loads += stacked(parts, weight_refs, stack_out, sems, 1 + copies)
     start_all(loads)
     banded_weights(width, conv1_ref, banded_ref)
     streams = mel_refs[0].shape[0] // JS
@@ -325,10 +327,7 @@
     copies = windows // parts
     normed_refs, refs = refs[:group], refs[group:]
     stack_refs, refs = refs[:copies], refs[copies:]
-    weight_refs, refs = refs[:parts], refs[parts:]
-    outs_refs, (stack_out, pieces, sems) = refs[:group], refs[group:]
-    moves = stacked(parts, weight_refs, stack_out, sems, 0)
-    start_all(moves)
+    outs_refs, (pieces,) = refs[:group], refs[group:]
     begin, end = bounds(lax.axis_index("dp"), slots_ref, starts_ref, lengths_ref)
     masks = []
     for step in range(group):
@@ -365,7 +364,6 @@
         context = (summed / total).astype(BF16)
         for step in range(group):
             outs_refs[step][:, at : at + HEAD_DIM] = context[step * local : (step + 1) * local]
-    wait_all(moves)
 
 
 def output_kernel(parts, windows, group, slots_ref, starts_ref, lengths_ref, *refs):
@@ -453,11 +451,15 @@
     mix_all = [mix] + [to_part(mix, step) for step in range(1, parts)]
 
     block = jax.ShapeDtypeStruct((local, features), BF16)
-    partials = pl.pallas_call(
+    out_all = [out_weight] + [to_part(out_weight, step) for step in range(1, parts)]
+    *partials, stack = pl.pallas_call(
         functools.partial(conv_kernel, parts, width),
-        out_shape=tuple([jax.ShapeDtypeStruct((W * parts, features), BF16)] * windows),
-        in_specs=[vmem()] + [anywhere()] + [vmem()] * parts + [anywhere()] * copies,
-        out_specs=tuple([vmem()] * windows),
+        out_shape=tuple(
+            [jax.ShapeDtypeStruct((W * parts, features), BF16)] * windows
+            + [jax.ShapeDtypeStruct((parts,) + out_weight.shape, BF16)]
+        ),
+        in_specs=[vmem()] + [anywhere()] + [vmem()] * parts + [anywhere()] * (copies + parts),
+        out_specs=tuple([vmem()] * (windows + 1)),
         scratch_shapes=[
             pltpu.VMEM((parts, rows, LANES), F32),
             pltpu.VMEM((LANES, outs * channels), BF16),
@@ -467,12 +469,13 @@
             pltpu.VMEM(conv2_weight.shape, BF16),
             pltpu.VMEM((copies,) + proj_weight.shape, BF16),
             pltpu.VMEM((W * n, features), F32),
-            pltpu.SemaphoreType.DMA((1 + copies,)),
+            pltpu.SemaphoreType.DMA((1 + copies + parts,)),
         ],
         compiler_params=params(min(40 + 4 * scale, 56)),
         cost_estimate=cost(2e9, 4e6),
         name="conv",
-    )(conv1_weight, conv2_weight, *mel_all, *proj_all)
+    )(conv1_weight, conv2_weight, *mel_all, *proj_all, *out_all)
+    out_stacks = [stack] + [to_copy(stack, step) for step in range(1, copies)]
     partials = [partials[0]] + [to_window(partials[step], step) for step in range(1, windows)]
 
     regrouped, normed, stack = pl.pallas_call(
@@ -486,28 +489,19 @@
         name="layer_norm",
     )(slots, starts, lengths, *partials, *mix_all)
     mix_stacks = [stack] + [to_copy(stack, step) for step in range(1, copies)]
-    normed, out_here = lax.optimization_barrier((normed, out_weight))
     normed = [normed] + [to_plane(normed, step) for step in range(1, group)]
-    out_all = [out_here] + [to_part(out_here, step) for step in range(1, parts)]
-
-    *context, stack = pl.pallas_call(
+
+    context = pl.pallas_call(
         functools.partial(attention_kernel, parts, windows, group),
-        out_shape=tuple(
-            [jax.ShapeDtypeStruct((local, head_width), BF16)] * group
-            + [jax.ShapeDtypeStruct((parts,) + out_weight.shape, BF16)]
-        ),
-        in_specs=[smem()] * 3 + [vmem()] * (group + copies) + [anywhere()] * parts,
-        out_specs=tuple([vmem()] * (group + 1)),
-        scratch_shapes=[
-            pltpu.VMEM((windows, group * local, qkv_weight.shape[0]), BF16),
-            pltpu.SemaphoreType.DMA((parts,)),
-        ],
+        out_shape=tuple([jax.ShapeDtypeStruct((local, head_width), BF16)] * group),
+        in_specs=[smem()] * 3 + [vmem()] * (group + copies),
+        out_specs=tuple([vmem()] * group),
+        scratch_shapes=[pltpu.VMEM((windows, group * local, qkv_weight.shape[0]), BF16)],
         compiler_params=params(min(16 * scale, 48)),
         cost_estimate=cost(1e9, 2e6),
         name="attention",
-    )(slots, starts, lengths, *normed, *mix_stacks, *out_all)
+    )(slots, starts, lengths, *normed, *mix_stacks)
     context = [context[0]] + [to_plane(context[step], step) for step in range(1, group)]
-    out_stacks = [stack] + [to_copy(stack, step) for step in range(1, copies)]
 
     attended = pl.pallas_call(
         functools.partial(output_kernel, parts, windows, group),

time: 76.9 us -> 83.6 us (1.087)
  starting transfers between devices: 31.5 us -> 36.2 us
  waiting for transfers between devices: 23.8 us -> 25.9 us
    ppermute x9, waiting for transfers between devices: 0.79 us -> 8.14 us  [to_part(): return lax.ppermute(block, 'dp', pairs)]
    ppermute x6, starting transfers between devices: 5.75 us -> 9.59 us  [to_plane(): return lax.ppermute(block, 'seq', [(i, i ^ step) for i in range(group)])]
    ppermute x6, waiting for transfers between devices: 17.5 us -> 14 us  [to_plane(): return lax.ppermute(block, 'seq', [(i, i ^ step) for i in range(group)])]
    ppermute x1, waiting for transfers between devices: 1.58 us -> 0.01 us  [on_device(): rim = lax.ppermute(audio[:, audio.shape[1] - RIM:], ('dp', 'seq'), route)]
    ppermute x7, starting transfers between devices: 6.33 us -> 7.58 us  [to_window(): return lax.ppermute(block, 'dp', [(i, i ^ step) for i in range(windows)])]
  transfers between devices with their start and end apart: 26 -> 26, of which waited for: 11 -> 10; matrix products, arithmetic and copies ran while one was open for 1% -> 1% of each run, Pallas kernels for 16% -> 20%
where the time goes in v2:
time: 83.6 us; the launch traced here: 83.3 us
  starting transfers between devices  36.2 us (43%)
  waiting for transfers between devices  25.9 us (31%)
  Pallas kernels  18.3 us (22%)
  local copies, waits for them, and re-layouts  2.12 us (3%)
    ppermute x6, waiting for transfers between devices, to_plane(): return lax.ppermute(block, 'seq', [(i, i ^ step) for i in range(group)])  14 us
    ppermute x9, starting transfers between devices, to_part(): return lax.ppermute(block, 'dp', pairs)  13.7 us
    ppermute x6, starting transfers between devices, to_plane(): return lax.ppermute(block, 'seq', [(i, i ^ step) for i in range(group)])  9.59 us
    ppermute x9, waiting for transfers between devices, to_part(): return lax.ppermute(block, 'dp', pairs)  8.14 us
    ppermute x7, starting transfers between devices, to_window(): return lax.ppermute(block, 'dp', [(i, i ^ step) for i in range(windows)])  7.58 us
    pallas_call x1, Pallas kernels, on_device(): pl.pallas_call(functools.partial(conv_kernel, parts, width), out_shape=tu...  7.08 us
    pallas_call x1, Pallas kernels, on_device(): pl.pallas_call(functools.partial(mel_kernel, parts, group), out_shape=tup...  5.03 us
    ppermute x1, starting transfers between devices, on_device(): rim = lax.ppermute(audio[:, audio.shape[1] - RIM:], ('dp', 'seq'), route)  4.76 us
  transfers between devices with their start and end apart: 26, of which 10 were waited for; matrix products, arithmetic and copies ran while one was open for 1% of the time, Pallas kernels for 20%

profile of v2, /device:TPU:0, one launch (start us, length us, event | category | flops | bytes accessed | tf_op | source)
XLA Modules:
  0.0 83.3 jit_solution(15138563630634135735)
XLA Ops:
  0.6 0.5 collective-permute-start.4
  1.1 0.8 slice.3
  1.9 0.0 copy-start.7
  1.9 4.8 %collective-permute-start = (f32[8,1024]{1,0:T(8,128)S(1)}, f32[8,1024]{1,0:T(8,128)S(1)}, u32[]{:S(2)}, u32[]{:S(2)}) collective-permute-start(f32[8,1024]{1,0:T(8,128)S(1)} %slice.3), channel_id=1, source_target_pairs={{0,1},{1,2},{2,3},{3,4},{4,5},{5,6},{6,7},{7,8},{8,9},{9,10},{10,1... | collective-permute-start | bytes 98312 | tf_op jit(solution)/shard_map/ppermute | solution.py:415
  6.7 1.6 %collective-permute-start.5 = (bf16[1024,128]{1,0:T(8,128)(2,1)}, bf16[1024,128]{1,0:T(8,128)(2,1)}, u32[]{:S(2)}, u32[]{:S(2)}) collective-permute-start(bf16[1024,128]{1,0:T(8,128)(2,1)} %refs_6_.1), channel_id=1, source_target_pairs={{0,8},{4,12},{8,0},{12,4},{16,24},{20,28},{24,16},{28,20},{1,9},{5... | collective-permute-start | bytes 786440 | tf_op jit(solution)/shard_map/ppermute | solution.py:419
  8.3 1.5 %collective-permute-start.6 = (bf16[1024,128]{1,0:T(8,128)(2,1)}, bf16[1024,128]{1,0:T(8,128)(2,1)}, u32[]{:S(2)}, u32[]{:S(2)}) collective-permute-start(bf16[1024,128]{1,0:T(8,128)(2,1)} %refs_6_.1), channel_id=1, source_target_pairs={{0,16},{4,20},{8,24},{12,28},{16,0},{20,4},{24,8},{28,12},{1,17},{... | collective-permute-start | bytes 786440 | tf_op jit(solution)/shard_map/ppermute | solution.py:419
  9.8 0.5 collective-permute-start.7
  10.3 0.6 copy-done.9
  10.9 5.0 %log_mel.1 = (bf16[72,128]{1,0:T(8,128)(2,1)}, bf16[72,128]{1,0:T(8,128)(2,1)}, bf16[72,128]{1,0:T(8,128)(2,1)}, bf16[72,128]{1,0:T(8,128)(2,1)}, bf16[128,768]{1,0:T(8,128)(2,1)}) custom-call(s32[8]{0:T(128)} %slots_ref.7, f32[8,1024]{1,0:T(8,128)} %copy-done.9, f32[8,5120]{1,0:T(8,128)} %audio_ref.1, f32[512,640]{1,0:T(8,128)} %constant.2.clone.table_ref, ...), custom_call_target="tpu_custom_call" | custom-call | flops 2000000000 | bytes 2000000 | tf_op jit(solution)/shard_map/log_mel/pallas_call | solution.py:435
  15.9 2.5 %collective-permute-start.1 = (bf16[72,128]{1,0:T(8,128)(2,1)}, bf16[72,128]{1,0:T(8,128)(2,1)S(1)}, u32[]{:S(2)}, u32[]{:S(2)}) collective-permute-start(bf16[72,128]{1,0:T(8,128)(2,1)} %get-tuple-element.24), channel_id=1, source_target_pairs={{0,8},{4,12},{8,0},{12,4},{16,24},{20,28},{24,16},{28,20},{1,9},{5... | collective-permute-start | bytes 55304 | tf_op jit(solution)/shard_map/ppermute | solution.py:419
  18.5 3.4 %collective-permute-done.1.refs_1_ = bf16[72,128]{1,0:T(8,128)(2,1)S(1)} collective-permute-done((bf16[72,128]{1,0:T(8,128)(2,1)}, bf16[72,128]{1,0:T(8,128)(2,1)S(1)}, u32[]{:S(2)}, u32[]{:S(2)}) %collective-permute-start.1) | collective-permute-done | bytes 18464 | tf_op jit(solution)/shard_map/ppermute | solution.py:419
  21.8 1.7 %collective-permute-start.2 = (bf16[72,128]{1,0:T(8,128)(2,1)}, bf16[72,128]{1,0:T(8,128)(2,1)S(1)}, u32[]{:S(2)}, u32[]{:S(2)}) collective-permute-start(bf16[72,128]{1,0:T(8,128)(2,1)} %get-tuple-element.25), channel_id=1, source_target_pairs={{0,16},{4,20},{8,24},{12,28},{16,0},{20,4},{24,8},{28,12},{1,17},{... | collective-permute-start | bytes 55304 | tf_op jit(solution)/shard_map/ppermute | solution.py:419
  23.5 2.3 %collective-permute-done.2.refs_2_ = bf16[72,128]{1,0:T(8,128)(2,1)S(1)} collective-permute-done((bf16[72,128]{1,0:T(8,128)(2,1)}, bf16[72,128]{1,0:T(8,128)(2,1)S(1)}, u32[]{:S(2)}, u32[]{:S(2)}) %collective-permute-start.2) | collective-permute-done | bytes 18464 | tf_op jit(solution)/shard_map/ppermute | solution.py:419
  25.8 2.4 %collective-permute-start.3 = (bf16[72,128]{1,0:T(8,128)(2,1)}, bf16[72,128]{1,0:T(8,128)(2,1)S(1)}, u32[]{:S(2)}, u32[]{:S(2)}) collective-permute-start(bf16[72,128]{1,0:T(8,128)(2,1)} %get-tuple-element.26), channel_id=1, source_target_pairs={{0,24},{4,28},{8,16},{12,20},{16,8},{20,12},{24,0},{28,4},{1,25},{... | collective-permute-start | bytes 55304 | tf_op jit(solution)/shard_map/ppermute | solution.py:419
  28.2 2.5 %collective-permute-done.3.refs_3_ = bf16[72,128]{1,0:T(8,128)(2,1)S(1)} collective-permute-done((bf16[72,128]{1,0:T(8,128)(2,1)}, bf16[72,128]{1,0:T(8,128)(2,1)S(1)}, u32[]{:S(2)}, u32[]{:S(2)}) %collective-permute-start.3) | collective-permute-done | bytes 18464 | tf_op jit(solution)/shard_map/ppermute | solution.py:419
  30.6 1.4 %collective-permute-start.15 = (bf16[128,768]{1,0:T(8,128)(2,1)}, bf16[128,768]{1,0:T(8,128)(2,1)S(1)}, u32[]{:S(2)}, u32[]{:S(2)}) collective-permute-start(bf16[128,768]{1,0:T(8,128)(2,1)} %get-tuple-element.35.refs_8_), channel_id=1, source_target_pairs={{0,8},{4,12},{8,0},{12,4},{16,24},{20,28},{24,16},{28,20},{1,9},{5... | collective-permute-start | bytes 589832 | tf_op jit(solution)/shard_map/ppermute | solution.py:419
  32.1 0.0 collective-permute-done.5.refs_7_
  32.1 1.6 %collective-permute-start.16 = (bf16[128,768]{1,0:T(8,128)(2,1)}, bf16[128,768]{1,0:T(8,128)(2,1)S(1)}, u32[]{:S(2)}, u32[]{:S(2)}) collective-permute-start(bf16[128,768]{1,0:T(8,128)(2,1)} %get-tuple-element.35.refs_8_), channel_id=1, source_target_pairs={{0,16},{4,20},{8,24},{12,28},{16,0},{20,4},{24,8},{28,12},{1,17},{... | collective-permute-start | bytes 589832 | tf_op jit(solution)/shard_map/ppermute | solution.py:419
  33.7 0.0 collective-permute-done.6.refs_8_
  33.7 0.5 collective-permute-start.17
  34.2 0.0 copy-start.8
  34.2 0.7 copy-done.8
  34.9 7.1 %conv.1 = (bf16[32,1024]{1,0:T(8,128)(2,1)S(1)}, bf16[32,1024]{1,0:T(8,128)(2,1)S(1)}, bf16[32,1024]{1,0:T(8,128)(2,1)S(1)}, bf16[32,1024]{1,0:T(8,128)(2,1)S(1)...) custom-call(bf16[9,256]{1,0:T(8,128)(2,1)S(1)} %copy-done.7, ...), custom_call_target="tpu_custom_call" | custom-call | flops 2000000000 | bytes 4000000 | tf_op jit(solution)/shard_map/conv/pallas_call | solution.py:455
  42.0 0.1 collective-permute-start.10
  42.1 1.9 %collective-permute-start.11 = (bf16[32,1024]{1,0:T(8,128)(2,1)S(1)}, bf16[32,1024]{1,0:T(8,128)(2,1)S(1)}, u32[]{:S(2)}, u32[]{:S(2)}) collective-permute-start(bf16[32,1024]{1,0:T(8,128)(2,1)S(1)} %get-tuple-element.31), channel_id=1, source_target_pairs={{0,16},{4,20},{8,24},{12,28},{16,0},{20,4},{24,8},{28,12},{1,17},{... | collective-permute-start | bytes 196616 | tf_op jit(solution)/shard_map/ppermute | solution.py:426
  44.0 1.0 %collective-permute-start.12 = (bf16[32,1024]{1,0:T(8,128)(2,1)S(1)}, bf16[32,1024]{1,0:T(8,128)(2,1)S(1)}, u32[]{:S(2)}, u32[]{:S(2)}) collective-permute-start(bf16[32,1024]{1,0:T(8,128)(2,1)S(1)} %get-tuple-element.32), channel_id=1, source_target_pairs={{0,20},{4,16},{8,28},{12,24},{16,4},{20,0},{24,12},{28,8},{1,21},{... | collective-permute-start | bytes 196616 | tf_op jit(solution)/shard_map/ppermute | solution.py:426
  45.0 0.0 collective-permute-start.25
  45.0 1.9 %collective-permute-start.13 = (bf16[32,1024]{1,0:T(8,128)(2,1)S(1)}, bf16[32,1024]{1,0:T(8,128)(2,1)S(1)}, u32[]{:S(2)}, u32[]{:S(2)}) collective-permute-start(bf16[32,1024]{1,0:T(8,128)(2,1)S(1)} %get-tuple-element.33), channel_id=1, source_target_pairs={{0,24},{4,28},{8,16},{12,20},{16,8},{20,12},{24,0},{28,4},{1,25},{... | collective-permute-start | bytes 196616 | tf_op jit(solution)/shard_map/ppermute | solution.py:426
  47.0 0.8 collective-permute-start.14
  47.8 0.7 collective-permute-start.8
  48.5 1.2 %collective-permute-start.9 = (bf16[32,1024]{1,0:T(8,128)(2,1)S(1)}, bf16[32,1024]{1,0:T(8,128)(2,1)S(1)}, u32[]{:S(2)}, u32[]{:S(2)}) collective-permute-start(bf16[32,1024]{1,0:T(8,128)(2,1)S(1)} %get-tuple-element.29), channel_id=1, source_target_pairs={{0,8},{4,12},{8,0},{12,4},{16,24},{20,28},{24,16},{28,20},{1,9},{5... | collective-permute-start | bytes 196616 | tf_op jit(solution)/shard_map/ppermute | solution.py:426
  49.6 0.8 collective-permute-done.13.refs_6_
  50.4 1.5 %collective-permute-done.14.refs_7_ = bf16[32,1024]{1,0:T(8,128)(2,1)S(1)} collective-permute-done((bf16[32,1024]{1,0:T(8,128)(2,1)S(1)}, bf16[32,1024]{1,0:T(8,128)(2,1)S(1)}, u32[]{:S(2)}, u32[]{:S(2)}) %collective-permute-start.14) | collective-permute-done | bytes 65568 | tf_op jit(solution)/shard_map/ppermute | solution.py:426
  51.9 1.4 %collective-permute-done.9.refs_2_ = bf16[32,1024]{1,0:T(8,128)(2,1)S(1)} collective-permute-done((bf16[32,1024]{1,0:T(8,128)(2,1)S(1)}, bf16[32,1024]{1,0:T(8,128)(2,1)S(1)}, u32[]{:S(2)}, u32[]{:S(2)}) %collective-permute-start.9) | collective-permute-done | bytes 65568 | tf_op jit(solution)/shard_map/ppermute | solution.py:426
  53.4 2.7 %layer_norm.1 = (bf16[64,1024]{1,0:T(8,128)(2,1)}, bf16[64,1024]{1,0:T(8,128)(2,1)S(1)}, bf16[4,128,768]{2,1,0:T(8,128)(2,1)S(1)}) custom-call(s32[8]{0:T(128)S(1)} %copy-done.1, s32[8]{0:T(128)S(1)} %copy-done.2, s32[8]{0:T(128)S(1)} %copy-done.3, bf16[32,1024]{1,0:T(8,128)(2,1)S(1)} %get-tuple-element.27.refs_0_, ...), custom_call_target="tpu_custom_call" | custom-call | flops 100000000 | bytes 1000000 | tf_op jit(solution)/shard_map/layer_norm/pallas_call | solution.py:481
  56.1 0.1 collective-permute-start.21
  56.2 1.2 %collective-permute-start.18 = (bf16[64,1024]{1,0:T(8,128)(2,1)S(1)}, bf16[64,1024]{1,0:T(8,128)(2,1)S(1)}, u32[]{:S(2)}, u32[]{:S(2)}) collective-permute-start(bf16[64,1024]{1,0:T(8,128)(2,1)S(1)} %get-tuple-element.37.refs_0_), channel_id=1, source_target_pairs={{0,1},{1,0},{2,3},{3,2},{4,5},{5,4},{6,7},{7,6},{8,9},{9,8},{10,11... | collective-permute-start | bytes 393224 | tf_op jit(solution)/shard_map/ppermute | solution.py:429
  57.4 1.4 %collective-permute-start.19 = (bf16[64,1024]{1,0:T(8,128)(2,1)S(1)}, bf16[64,1024]{1,0:T(8,128)(2,1)S(1)}, u32[]{:S(2)}, u32[]{:S(2)}) collective-permute-start(bf16[64,1024]{1,0:T(8,128)(2,1)S(1)} %get-tuple-element.37.refs_0_), channel_id=1, source_target_pairs={{0,2},{1,3},{2,0},{3,1},{4,6},{5,7},{6,4},{7,5},{8,10},{9,11},{10,... | collective-permute-start | bytes 393224 | tf_op jit(solution)/shard_map/ppermute | solution.py:429
  58.8 1.8 %collective-permute-start.20 = (bf16[64,1024]{1,0:T(8,128)(2,1)S(1)}, bf16[64,1024]{1,0:T(8,128)(2,1)S(1)}, u32[]{:S(2)}, u32[]{:S(2)}) collective-permute-start(bf16[64,1024]{1,0:T(8,128)(2,1)S(1)} %get-tuple-element.37.refs_0_), channel_id=1, source_target_pairs={{0,3},{1,2},{2,1},{3,0},{4,7},{5,6},{6,5},{7,4},{8,11},{9,10},{10,... | collective-permute-start | bytes 393224 | tf_op jit(solution)/shard_map/ppermute | solution.py:429
  60.6 3.8 %collective-permute-done.18.refs_1_ = bf16[64,1024]{1,0:T(8,128)(2,1)S(1)} collective-permute-done((bf16[64,1024]{1,0:T(8,128)(2,1)S(1)}, bf16[64,1024]{1,0:T(8,128)(2,1)S(1)}, u32[]{:S(2)}, u32[]{:S(2)}) %collective-permute-start.18) | collective-permute-done | bytes 131104 | tf_op jit(solution)/shard_map/ppermute | solution.py:429
  64.4 5.9 %collective-permute-done.19.refs_2_ = bf16[64,1024]{1,0:T(8,128)(2,1)S(1)} collective-permute-done((bf16[64,1024]{1,0:T(8,128)(2,1)S(1)}, bf16[64,1024]{1,0:T(8,128)(2,1)S(1)}, u32[]{:S(2)}, u32[]{:S(2)}) %collective-permute-start.19) | collective-permute-done | bytes 131104 | tf_op jit(solution)/shard_map/ppermute | solution.py:429
  70.3 1.8 %attention.1 = (bf16[64,256]{1,0:T(8,128)(2,1)S(1)}, bf16[64,256]{1,0:T(8,128)(2,1)S(1)}, bf16[64,256]{1,0:T(8,128)(2,1)S(1)}, bf16[64,256]{1,0:T(8,128)(2,1)S(1)}) custom-call(s32[8]{0:T(128)S(1)} %copy-done.1, s32[8]{0:T(128)S(1)} %copy-done.2, s32[8]{0:T(128)S(1)} %copy-done.3, bf16[64,1024]{1,0:T(8,128)(2,1)S(1)} %get-tuple-element.37.refs_0_, ...), custom_call_target="tpu_custom_call" | custom-call | flops 1000000000 | bytes 2000000 | tf_op jit(solution)/shard_map/attention/pallas_call | solution.py:494
  72.1 2.7 %collective-permute-start.22 = (bf16[64,256]{1,0:T(8,128)(2,1)S(1)}, bf16[64,256]{1,0:T(8,128)(2,1)S(1)}, u32[]{:S(2)}, u32[]{:S(2)}) collective-permute-start(bf16[64,256]{1,0:T(8,128)(2,1)S(1)} %get-tuple-element.40), channel_id=1, source_target_pairs={{0,1},{1,0},{2,3},{3,2},{4,5},{5,4},{6,7},{7,6},{8,9},{9,8},{10,11... | collective-permute-start | bytes 98312 | tf_op jit(solution)/shard_map/ppermute | solution.py:429
  74.8 1.1 %collective-permute-start.23 = (bf16[64,256]{1,0:T(8,128)(2,1)S(1)}, bf16[64,256]{1,0:T(8,128)(2,1)S(1)}, u32[]{:S(2)}, u32[]{:S(2)}) collective-permute-start(bf16[64,256]{1,0:T(8,128)(2,1)S(1)} %get-tuple-element.41), channel_id=1, source_target_pairs={{0,2},{1,3},{2,0},{3,1},{4,6},{5,7},{6,4},{7,5},{8,10},{9,11},{10,... | collective-permute-start | bytes 98312 | tf_op jit(solution)/shard_map/ppermute | solution.py:429
  75.9 1.4 %collective-permute-start.24 = (bf16[64,256]{1,0:T(8,128)(2,1)S(1)}, bf16[64,256]{1,0:T(8,128)(2,1)S(1)}, u32[]{:S(2)}, u32[]{:S(2)}) collective-permute-start(bf16[64,256]{1,0:T(8,128)(2,1)S(1)} %get-tuple-element.42), channel_id=1, source_target_pairs={{0,3},{1,2},{2,1},{3,0},{4,7},{5,6},{6,5},{7,4},{8,11},{9,10},{10,... | collective-permute-start | bytes 98312 | tf_op jit(solution)/shard_map/ppermute | solution.py:429
  77.3 2.9 %collective-permute-done.23.refs_2_ = bf16[64,256]{1,0:T(8,128)(2,1)S(1)} collective-permute-done((bf16[64,256]{1,0:T(8,128)(2,1)S(1)}, bf16[64,256]{1,0:T(8,128)(2,1)S(1)}, u32[]{:S(2)}, u32[]{:S(2)}) %collective-permute-start.23) | collective-permute-done | bytes 32800 | tf_op jit(solution)/shard_map/ppermute | solution.py:429
  80.2 1.4 %collective-permute-done.24.refs_3_ = bf16[64,256]{1,0:T(8,128)(2,1)S(1)} collective-permute-done((bf16[64,256]{1,0:T(8,128)(2,1)S(1)}, bf16[64,256]{1,0:T(8,128)(2,1)S(1)}, u32[]{:S(2)}, u32[]{:S(2)}) %collective-permute-start.24) | collective-permute-done | bytes 32800 | tf_op jit(solution)/shard_map/ppermute | solution.py:429
  81.6 1.7 %output.1 = bf16[64,1024]{1,0:T(8,128)(2,1)} custom-call(s32[8]{0:T(128)S(1)} %copy-done.1, s32[8]{0:T(128)S(1)} %copy-done.2, s32[8]{0:T(128)S(1)} %copy-done.3, bf16[64,256]{1,0:T(8,128)(2,1)S(1)} %get-tuple-element.39.refs_0_, bf16[64,256]{1,0:T(8,128)(2,1)S(1)} %collective-permute-done.22.refs_1_, bf16[64,256]{1,0:T(8,128)(2,1)S(1)} %collective-permute-done.23.refs_2_, ...), custom_call_target="tpu_custom_call" | custom-call | flops 100000000 | bytes 3000000 | tf_op jit(solution)/shard_map/output/pallas_call | solution.py:506
  (30 shorter events, 0.1 us)
Async XLA Ops:
  0.6 33.5 %collective-permute-start.4 = (bf16[640,1024]{1,0:T(8,128)(2,1)}, bf16[640,1024]{1,0:T(8,128)(2,1)S(1)}, u32[]{:S(2)}, u32[]{:S(2)}) collective-permute-start(bf16[640,1024]{1,0:T(8,128)(2,1)} %refs_4_.1), channel_id=1, source_target_pairs={{0,4},{4,0},{8,12},{12,8},{16,20},{20,16},{24,28},{28,24},{1,5},{5... | collective-permute-start | bytes 3932168 | tf_op jit(solution)/shard_map/ppermute | solution.py:423
  1.9 32.2 %copy-start.4 = (bf16[640,1024]{1,0:T(8,128)(2,1)S(1)}, bf16[640,1024]{1,0:T(8,128)(2,1)}, u32[]{:S(2)}) copy-start(bf16[640,1024]{1,0:T(8,128)(2,1)} %refs_4_.1) | copy-start | bytes 3932164
  1.9 32.2 %copy-start.5 = (bf16[2304,256]{1,0:T(8,128)(2,1)S(1)}, bf16[2304,256]{1,0:T(8,128)(2,1)}, u32[]{:S(2)}) copy-start(bf16[2304,256]{1,0:T(8,128)(2,1)} %conv2_ref.1) | copy-start | bytes 3538948
  1.9 32.3 %copy-start.6 = (bf16[1024,128]{1,0:T(8,128)(2,1)S(1)}, bf16[1024,128]{1,0:T(8,128)(2,1)}, u32[]{:S(2)}) copy-start(bf16[1024,128]{1,0:T(8,128)(2,1)} %refs_6_.1) | copy-start | bytes 786436
  1.9 32.3 %copy-start.7 = (bf16[9,256]{1,0:T(8,128)(2,1)S(1)}, bf16[9,256]{1,0:T(8,128)(2,1)}, u32[]{:S(2)}) copy-start(bf16[9,256]{1,0:T(8,128)(2,1)} %conv1_ref.1) | copy-start | bytes 13828
  1.9 8.3 %collective-permute-start = (f32[8,1024]{1,0:T(8,128)S(1)}, f32[8,1024]{1,0:T(8,128)S(1)}, u32[]{:S(2)}, u32[]{:S(2)}) collective-permute-start(f32[8,1024]{1,0:T(8,128)S(1)} %slice.3), channel_id=1, source_target_pairs={{0,1},{1,2},{2,3},{3,4},{4,5},{5,6},{6,7},{7,8},{8,9},{9,10},{10,1... | collective-permute-start | bytes 98312 | tf_op jit(solution)/shard_map/ppermute | solution.py:415
  6.7 25.4 %collective-permute-start.5 = (bf16[1024,128]{1,0:T(8,128)(2,1)}, bf16[1024,128]{1,0:T(8,128)(2,1)}, u32[]{:S(2)}, u32[]{:S(2)}) collective-permute-start(bf16[1024,128]{1,0:T(8,128)(2,1)} %refs_6_.1), channel_id=1, source_target_pairs={{0,8},{4,12},{8,0},{12,4},{16,24},{20,28},{24,16},{28,20},{1,9},{5... | collective-permute-start | bytes 786440 | tf_op jit(solution)/shard_map/ppermute | solution.py:419
  8.3 25.4 %collective-permute-start.6 = (bf16[1024,128]{1,0:T(8,128)(2,1)}, bf16[1024,128]{1,0:T(8,128)(2,1)}, u32[]{:S(2)}, u32[]{:S(2)}) collective-permute-start(bf16[1024,128]{1,0:T(8,128)(2,1)} %refs_6_.1), channel_id=1, source_target_pairs={{0,16},{4,20},{8,24},{12,28},{16,0},{20,4},{24,8},{28,12},{1,17},{... | collective-permute-start | bytes 786440 | tf_op jit(solution)/shard_map/ppermute | solution.py:419
  9.8 24.4 %collective-permute-start.7 = (bf16[1024,128]{1,0:T(8,128)(2,1)}, bf16[1024,128]{1,0:T(8,128)(2,1)}, u32[]{:S(2)}, u32[]{:S(2)}) collective-permute-start(bf16[1024,128]{1,0:T(8,128)(2,1)} %refs_6_.1), channel_id=1, source_target_pairs={{0,24},{4,28},{8,16},{12,20},{16,8},{20,12},{24,0},{28,4},{1,25},{... | collective-permute-start | bytes 786440 | tf_op jit(solution)/shard_map/ppermute | solution.py:419
  10.3 0.6 copy-start.9
  15.9 5.9 %collective-permute-start.1 = (bf16[72,128]{1,0:T(8,128)(2,1)}, bf16[72,128]{1,0:T(8,128)(2,1)S(1)}, u32[]{:S(2)}, u32[]{:S(2)}) collective-permute-start(bf16[72,128]{1,0:T(8,128)(2,1)} %get-tuple-element.24), channel_id=1, source_target_pairs={{0,8},{4,12},{8,0},{12,4},{16,24},{20,28},{24,16},{28,20},{1,9},{5... | collective-permute-start | bytes 55304 | tf_op jit(solution)/shard_map/ppermute | solution.py:419
  21.8 4.0 %collective-permute-start.2 = (bf16[72,128]{1,0:T(8,128)(2,1)}, bf16[72,128]{1,0:T(8,128)(2,1)S(1)}, u32[]{:S(2)}, u32[]{:S(2)}) collective-permute-start(bf16[72,128]{1,0:T(8,128)(2,1)} %get-tuple-element.25), channel_id=1, source_target_pairs={{0,16},{4,20},{8,24},{12,28},{16,0},{20,4},{24,8},{28,12},{1,17},{... | collective-permute-start | bytes 55304 | tf_op jit(solution)/shard_map/ppermute | solution.py:419
  25.8 4.9 %collective-permute-start.3 = (bf16[72,128]{1,0:T(8,128)(2,1)}, bf16[72,128]{1,0:T(8,128)(2,1)S(1)}, u32[]{:S(2)}, u32[]{:S(2)}) collective-permute-start(bf16[72,128]{1,0:T(8,128)(2,1)} %get-tuple-element.26), channel_id=1, source_target_pairs={{0,24},{4,28},{8,16},{12,20},{16,8},{20,12},{24,0},{28,4},{1,25},{... | collective-permute-start | bytes 55304 | tf_op jit(solution)/shard_map/ppermute | solution.py:419
  30.6 13.4 %collective-permute-start.15 = (bf16[128,768]{1,0:T(8,128)(2,1)}, bf16[128,768]{1,0:T(8,128)(2,1)S(1)}, u32[]{:S(2)}, u32[]{:S(2)}) collective-permute-start(bf16[128,768]{1,0:T(8,128)(2,1)} %get-tuple-element.35.refs_8_), channel_id=1, source_target_pairs={{0,8},{4,12},{8,0},{12,4},{16,24},{20,28},{24,16},{28,20},{1,9},{5... | collective-permute-start | bytes 589832 | tf_op jit(solution)/shard_map/ppermute | solution.py:419
  32.1 12.9 %collective-permute-start.16 = (bf16[128,768]{1,0:T(8,128)(2,1)}, bf16[128,768]{1,0:T(8,128)(2,1)S(1)}, u32[]{:S(2)}, u32[]{:S(2)}) collective-permute-start(bf16[128,768]{1,0:T(8,128)(2,1)} %get-tuple-element.35.refs_8_), channel_id=1, source_target_pairs={{0,16},{4,20},{8,24},{12,28},{16,0},{20,4},{24,8},{28,12},{1,17},{... | collective-permute-start | bytes 589832 | tf_op jit(solution)/shard_map/ppermute | solution.py:419
  33.7 11.3 %collective-permute-start.17 = (bf16[128,768]{1,0:T(8,128)(2,1)}, bf16[128,768]{1,0:T(8,128)(2,1)S(1)}, u32[]{:S(2)}, u32[]{:S(2)}) collective-permute-start(bf16[128,768]{1,0:T(8,128)(2,1)} %get-tuple-element.35.refs_8_), channel_id=1, source_target_pairs={{0,24},{4,28},{8,16},{12,20},{16,8},{20,12},{24,0},{28,4},{1,25},{... | collective-permute-start | bytes 589832 | tf_op jit(solution)/shard_map/ppermute | solution.py:419
  34.2 0.7 copy-start.8
  34.9 18.4 %copy-start = (bf16[128,768]{1,0:T(8,128)(2,1)S(1)}, bf16[128,768]{1,0:T(8,128)(2,1)}, u32[]{:S(2)}) copy-start(bf16[128,768]{1,0:T(8,128)(2,1)} %get-tuple-element.35.refs_8_) | copy-start | bytes 589828
  34.9 18.4 %copy-start.1 = (s32[8]{0:T(128)S(1)}, s32[8]{0:T(128)}, u32[]{:S(2)}) copy-start(s32[8]{0:T(128)} %slots_ref.7) | copy-start | bytes 100
  34.9 18.4 %copy-start.2 = (s32[8]{0:T(128)S(1)}, s32[8]{0:T(128)}, u32[]{:S(2)}) copy-start(s32[8]{0:T(128)} %starts_ref.5) | copy-start | bytes 100
  34.9 18.4 %copy-start.3 = (s32[8]{0:T(128)S(1)}, s32[8]{0:T(128)}, u32[]{:S(2)}) copy-start(s32[8]{0:T(128)} %lengths_ref.5) | copy-start | bytes 100
  42.0 4.9 %collective-permute-start.10 = (bf16[32,1024]{1,0:T(8,128)(2,1)S(1)}, bf16[32,1024]{1,0:T(8,128)(2,1)S(1)}, u32[]{:S(2)}, u32[]{:S(2)}) collective-permute-start(bf16[32,1024]{1,0:T(8,128)(2,1)S(1)} %get-tuple-element.30), channel_id=1, source_target_pairs={{0,12},{4,8},{8,4},{12,0},{16,28},{20,24},{24,20},{28,16},{1,13},{... | collective-permute-start | bytes 196616 | tf_op jit(solution)/shard_map/ppermute | solution.py:426
  42.1 5.7 %collective-permute-start.11 = (bf16[32,1024]{1,0:T(8,128)(2,1)S(1)}, bf16[32,1024]{1,0:T(8,128)(2,1)S(1)}, u32[]{:S(2)}, u32[]{:S(2)}) collective-permute-start(bf16[32,1024]{1,0:T(8,128)(2,1)S(1)} %get-tuple-element.31), channel_id=1, source_target_pairs={{0,16},{4,20},{8,24},{12,28},{16,0},{20,4},{24,8},{28,12},{1,17},{... | collective-permute-start | bytes 196616 | tf_op jit(solution)/shard_map/ppermute | solution.py:426
  44.0 4.5 %collective-permute-start.12 = (bf16[32,1024]{1,0:T(8,128)(2,1)S(1)}, bf16[32,1024]{1,0:T(8,128)(2,1)S(1)}, u32[]{:S(2)}, u32[]{:S(2)}) collective-permute-start(bf16[32,1024]{1,0:T(8,128)(2,1)S(1)} %get-tuple-element.32), channel_id=1, source_target_pairs={{0,20},{4,16},{8,28},{12,24},{16,4},{20,0},{24,12},{28,8},{1,21},{... | collective-permute-start | bytes 196616 | tf_op jit(solution)/shard_map/ppermute | solution.py:426
  45.0 36.6 %collective-permute-start.25 = (bf16[4,1024,128]{2,1,0:T(8,128)(2,1)S(1)}, bf16[4,1024,128]{2,1,0:T(8,128)(2,1)S(1)}, u32[]{:S(2)}, u32[]{:S(2)}) collective-permute-start(bf16[4,1024,128]{2,1,0:T(8,128)(2,1)S(1)} %get-tuple-element.43.refs_4_), channel_id=1, source_target_pairs={{0,4},{4,0},{8,12},{12,8},{16,20},{20,16},{24,28},{28,24},{1,5},{5... | collective-permute-start | bytes 3145736 | tf_op jit(solution)/shard_map/ppermute | solution.py:423
  45.0 5.4 %collective-permute-start.13 = (bf16[32,1024]{1,0:T(8,128)(2,1)S(1)}, bf16[32,1024]{1,0:T(8,128)(2,1)S(1)}, u32[]{:S(2)}, u32[]{:S(2)}) collective-permute-start(bf16[32,1024]{1,0:T(8,128)(2,1)S(1)} %get-tuple-element.33), channel_id=1, source_target_pairs={{0,24},{4,28},{8,16},{12,20},{16,8},{20,12},{24,0},{28,4},{1,25},{... | collective-permute-start | bytes 196616 | tf_op jit(solution)/shard_map/ppermute | solution.py:426
  47.0 5.0 %collective-permute-start.14 = (bf16[32,1024]{1,0:T(8,128)(2,1)S(1)}, bf16[32,1024]{1,0:T(8,128)(2,1)S(1)}, u32[]{:S(2)}, u32[]{:S(2)}) collective-permute-start(bf16[32,1024]{1,0:T(8,128)(2,1)S(1)} %get-tuple-element.34), channel_id=1, source_target_pairs={{0,28},{4,24},{8,20},{12,16},{16,12},{20,8},{24,4},{28,0},{1,29},{... | collective-permute-start | bytes 196616 | tf_op jit(solution)/shard_map/ppermute | solution.py:426
  47.8 4.1 %collective-permute-start.8 = (bf16[32,1024]{1,0:T(8,128)(2,1)S(1)}, bf16[32,1024]{1,0:T(8,128)(2,1)S(1)}, u32[]{:S(2)}, u32[]{:S(2)}) collective-permute-start(bf16[32,1024]{1,0:T(8,128)(2,1)S(1)} %get-tuple-element.28), channel_id=1, source_target_pairs={{0,4},{4,0},{8,12},{12,8},{16,20},{20,16},{24,28},{28,24},{1,5},{5... | collective-permute-start | bytes 196616 | tf_op jit(solution)/shard_map/ppermute | solution.py:426
  48.5 4.9 %collective-permute-start.9 = (bf16[32,1024]{1,0:T(8,128)(2,1)S(1)}, bf16[32,1024]{1,0:T(8,128)(2,1)S(1)}, u32[]{:S(2)}, u32[]{:S(2)}) collective-permute-start(bf16[32,1024]{1,0:T(8,128)(2,1)S(1)} %get-tuple-element.29), channel_id=1, source_target_pairs={{0,8},{4,12},{8,0},{12,4},{16,24},{20,28},{24,16},{28,20},{1,9},{5... | collective-permute-start | bytes 196616 | tf_op jit(solution)/shard_map/ppermute | solution.py:426
  56.1 14.2 %collective-permute-start.21 = (bf16[4,128,768]{2,1,0:T(8,128)(2,1)S(1)}, bf16[4,128,768]{2,1,0:T(8,128)(2,1)S(1)}, u32[]{:S(2)}, u32[]{:S(2)}) collective-permute-start(bf16[4,128,768]{2,1,0:T(8,128)(2,1)S(1)} %get-tuple-element.38.refs_4_), channel_id=1, source_target_pairs={{0,4},{4,0},{8,12},{12,8},{16,20},{20,16},{24,28},{28,24},{1,5},{5... | collective-permute-start | bytes 2359304 | tf_op jit(solution)/shard_map/ppermute | solution.py:423
  56.2 8.3 %collective-permute-start.18 = (bf16[64,1024]{1,0:T(8,128)(2,1)S(1)}, bf16[64,1024]{1,0:T(8,128)(2,1)S(1)}, u32[]{:S(2)}, u32[]{:S(2)}) collective-permute-start(bf16[64,1024]{1,0:T(8,128)(2,1)S(1)} %get-tuple-element.37.refs_0_), channel_id=1, source_target_pairs={{0,1},{1,0},{2,3},{3,2},{4,5},{5,4},{6,7},{7,6},{8,9},{9,8},{10,11... | collective-permute-start | bytes 393224 | tf_op jit(solution)/shard_map/ppermute | solution.py:429
  57.4 12.9 %collective-permute-start.19 = (bf16[64,1024]{1,0:T(8,128)(2,1)S(1)}, bf16[64,1024]{1,0:T(8,128)(2,1)S(1)}, u32[]{:S(2)}, u32[]{:S(2)}) collective-permute-start(bf16[64,1024]{1,0:T(8,128)(2,1)S(1)} %get-tuple-element.37.refs_0_), channel_id=1, source_target_pairs={{0,2},{1,3},{2,0},{3,1},{4,6},{5,7},{6,4},{7,5},{8,10},{9,11},{10,... | collective-permute-start | bytes 393224 | tf_op jit(solution)/shard_map/ppermute | solution.py:429
  58.8 11.5 %collective-permute-start.20 = (bf16[64,1024]{1,0:T(8,128)(2,1)S(1)}, bf16[64,1024]{1,0:T(8,128)(2,1)S(1)}, u32[]{:S(2)}, u32[]{:S(2)}) collective-permute-start(bf16[64,1024]{1,0:T(8,128)(2,1)S(1)} %get-tuple-element.37.refs_0_), channel_id=1, source_target_pairs={{0,3},{1,2},{2,1},{3,0},{4,7},{5,6},{6,5},{7,4},{8,11},{9,10},{10,... | collective-permute-start | bytes 393224 | tf_op jit(solution)/shard_map/ppermute | solution.py:429
  72.1 5.1 %collective-permute-start.22 = (bf16[64,256]{1,0:T(8,128)(2,1)S(1)}, bf16[64,256]{1,0:T(8,128)(2,1)S(1)}, u32[]{:S(2)}, u32[]{:S(2)}) collective-permute-start(bf16[64,256]{1,0:T(8,128)(2,1)S(1)} %get-tuple-element.40), channel_id=1, source_target_pairs={{0,1},{1,0},{2,3},{3,2},{4,5},{5,4},{6,7},{7,6},{8,9},{9,8},{10,11... | collective-permute-start | bytes 98312 | tf_op jit(solution)/shard_map/ppermute | solution.py:429
  74.8 5.4 %collective-permute-start.23 = (bf16[64,256]{1,0:T(8,128)(2,1)S(1)}, bf16[64,256]{1,0:T(8,128)(2,1)S(1)}, u32[]{:S(2)}, u32[]{:S(2)}) collective-permute-start(bf16[64,256]{1,0:T(8,128)(2,1)S(1)} %get-tuple-element.41), channel_id=1, source_target_pairs={{0,2},{1,3},{2,0},{3,1},{4,6},{5,7},{6,4},{7,5},{8,10},{9,11},{10,... | collective-permute-start | bytes 98312 | tf_op jit(solution)/shard_map/ppermute | solution.py:429
  75.9 5.7 %collective-permute-start.24 = (bf16[64,256]{1,0:T(8,128)(2,1)S(1)}, bf16[64,256]{1,0:T(8,128)(2,1)S(1)}, u32[]{:S(2)}, u32[]{:S(2)}) collective-permute-start(bf16[64,256]{1,0:T(8,128)(2,1)S(1)} %get-tuple-element.42), channel_id=1, source_target_pairs={{0,3},{1,2},{2,1},{3,0},{4,7},{5,6},{6,5},{7,4},{8,11},{9,10},{10,... | collective-permute-start | bytes 98312 | tf_op jit(solution)/shard_map/ppermute | solution.py:429

commit v3 on v1

--- a/solution.py
+++ b/solution.py
@@ -113,14 +113,6 @@
     k = quotient(row, W, parts * copies)
     p = quotient(k, copies, parts)
     return one_hot((k - p * copies) * W * parts + (row - k * W) * parts + p, count)
-
-
-def row_order(parts, streams):
-    count = W * parts * streams
-    row = iota(count, 1, 0)
-    r = quotient(row, W * parts, streams)
-    rest = row - r * W * parts
-    return one_hot(rest * streams + r, count)
 
 
 def samples(index, windows, group):
@@ -263,23 +255,22 @@
         odd[:, lanes] = jax.nn.relu(jnp.dot(odds, weight, preferred_element_type=F32)).astype(BF16)
 
     load_conv2.wait()
-    order = row_order(parts, streams)
     for h in range((outs - 1) // 2):
         lanes = slice(2 * h * channels, (2 * h + 3) * channels)
         depth = 3 * channels
         total = jnp.dot(even[: W * n, lanes], conv2[:depth], preferred_element_type=F32)
         total += jnp.dot(odd[:, lanes], conv2[depth : 2 * depth], preferred_element_type=F32)
         total += jnp.dot(even[n:, lanes], conv2[2 * depth :], preferred_element_type=F32)
-        second[:, h * channels : (h + 1) * channels] = jnp.dot(
-            order, jax.nn.relu(total).astype(BF16), preferred_element_type=F32
-        ).astype(BF16)
+        second[:, h * channels : (h + 1) * channels] = jax.nn.relu(total).astype(BF16)
     wait_all(loads)
     weights = proj[...].reshape(second.shape[1], proj.shape[2])
-    partial[...] = jnp.dot(second[...], weights, preferred_element_type=F32)
-    rows = W * parts
+    sums = jnp.dot(second[...], weights, preferred_element_type=F32)
+    for block in range(partial.shape[0]):
+        partial[block] = sums[:, block * LANES : (block + 1) * LANES]
     for step in range(windows):
-        at = pl.multiple_of((mine ^ step) * rows, rows)
-        outs_refs[step][...] = partial[pl.ds(at, rows), :].astype(BF16)
+        for block in range(partial.shape[0]):
+            rows = partial[block, pl.ds(mine ^ step, W * parts, stride=streams), :]
+            outs_refs[step][:, block * LANES : (block + 1) * LANES] = rows.astype(BF16)
 
 
 def bounds(row, slots_ref, starts_ref, lengths_ref):
@@ -446,9 +437,11 @@
             pltpu.SemaphoreType.DMA((5,)),
         ],
         compiler_params=params(60),
-        cost_estimate=cost(2e9, 2e6),
+        cost_estimate=cost(1e10, 2e6),
         name="log_mel",
     )(slots, rim, audio, table, qkv_weight)
+    near = [to_part(out_weight, step) for step in range(1, parts - 1)]
+    mel_all, proj_all, near = lax.optimization_barrier((mel_all, proj_all, near))
     mel_all = [mel_all[0]] + [to_part(mel_all[step], step) for step in range(1, parts)]
     mix_all = [mix] + [to_part(mix, step) for step in range(1, parts)]
 
@@ -466,7 +459,7 @@
             pltpu.VMEM((W * n, share * channels), BF16),
             pltpu.VMEM(conv2_weight.shape, BF16),
             pltpu.VMEM((copies,) + proj_weight.shape, BF16),
-            pltpu.VMEM((W * n, features), F32),
+            pltpu.VMEM((features // LANES, W * n, LANES), F32),
             pltpu.SemaphoreType.DMA((1 + copies,)),
         ],
         compiler_params=params(min(40 + 4 * scale, 56)),
@@ -488,7 +481,7 @@
     mix_stacks = [stack] + [to_copy(stack, step) for step in range(1, copies)]
     normed, out_here = lax.optimization_barrier((normed, out_weight))
     normed = [normed] + [to_plane(normed, step) for step in range(1, group)]
-    out_all = [out_here] + [to_part(out_here, step) for step in range(1, parts)]
+    out_all = [out_here] + near + [to_part(out_here, parts - 1)]
 
     *context, stack = pl.pallas_call(
         functools.partial(attention_kernel, parts, windows, group),

time: 76.9 us -> 72 us (0.936)
  waiting for transfers between devices: 23.8 us -> 19.3 us
  Pallas kernels: 18.4 us -> 16.4 us
  starting transfers between devices: 31.5 us -> 33 us
    ppermute x6, waiting for transfers between devices: 17.5 us -> 13.4 us  [to_plane(): return lax.ppermute(block, 'seq', [(i, i ^ step) for i in range(group)])]
    ppermute x6, starting transfers between devices: 5.75 us -> 8.83 us  [to_plane(): return lax.ppermute(block, 'seq', [(i, i ^ step) for i in range(group)])]
    pallas_call x1, Pallas kernels: 7 us -> 5.04 us  [on_device(): pl.pallas_call(functools.partial(conv_kernel, parts, width), out_shape=tu...]
    ppermute x1, waiting for transfers between devices: 1.58 us -> 0.01 us  [on_device(): rim = lax.ppermute(audio[:, audio.shape[1] - RIM:], ('dp', 'seq'), route)]
    ppermute x9, starting transfers between devices: 14 us -> 12.5 us  [to_part(): return lax.ppermute(block, 'dp', pairs)]
    ppermute x9, waiting for transfers between devices: 0.79 us -> 2.05 us  [to_part(): return lax.ppermute(block, 'dp', pairs)]
  transfers between devices with their start and end apart: 26 -> 26, of which waited for: 11 -> 10; matrix products, arithmetic and copies ran while one was open for 1% -> 1% of each run, Pallas kernels for 16% -> 14%
where the time goes in v3:
time: 72 us; the launch traced here: 71.6 us
  starting transfers between devices  33 us (46%)
  waiting for transfers between devices  19.3 us (27%)
  Pallas kernels  16.4 us (23%)
  local copies, waits for them, and re-layouts  2.12 us (3%)
  between operations  0.76 us (1%)
    ppermute x6, waiting for transfers between devices, to_plane(): return lax.ppermute(block, 'seq', [(i, i ^ step) for i in range(group)])  13.4 us
    ppermute x9, starting transfers between devices, to_part(): return lax.ppermute(block, 'dp', pairs)  12.5 us
    ppermute x6, starting transfers between devices, to_plane(): return lax.ppermute(block, 'seq', [(i, i ^ step) for i in range(group)])  8.83 us
    ppermute x7, starting transfers between devices, to_window(): return lax.ppermute(block, 'dp', [(i, i ^ step) for i in range(windows)])  6.33 us
    pallas_call x1, Pallas kernels, on_device(): pl.pallas_call(functools.partial(conv_kernel, parts, width), out_shape=tu...  5.04 us
    pallas_call x1, Pallas kernels, on_device(): pl.pallas_call(functools.partial(mel_kernel, parts, group), out_shape=tup...  5.02 us
    ppermute x1, starting transfers between devices, on_device(): rim = lax.ppermute(audio[:, audio.shape[1] - RIM:], ('dp', 'seq'), route)  4.63 us
    ppermute x7, waiting for transfers between devices, to_window(): return lax.ppermute(block, 'dp', [(i, i ^ step) for i in range(windows)])  3.92 us
  transfers between devices with their start and end apart: 26, of which 10 were waited for; matrix products, arithmetic and copies ran while one was open for 1% of the time, Pallas kernels for 14%

profile of v3, /device:TPU:0, one launch (start us, length us, event | category | flops | bytes accessed | tf_op | source)
XLA Modules:
  0.0 71.6 jit_solution(11474747523248537153)
XLA Ops:
  0.6 0.5 collective-permute-start.1
  1.1 0.8 %slice.3 = f32[8,1024]{1,0:T(8,128)S(1)} slice(f32[8,5120]{1,0:T(8,128)} %audio_ref.1), slice={[0:8], [4096:5120]} | slice | bytes 65536 | tf_op jit(solution)/shard_map/slice | solution.py:408
  1.9 4.6 %collective-permute-start = (f32[8,1024]{1,0:T(8,128)S(1)}, f32[8,1024]{1,0:T(8,128)S(1)}, u32[]{:S(2)}, u32[]{:S(2)}) collective-permute-start(f32[8,1024]{1,0:T(8,128)S(1)} %slice.3), channel_id=1, source_target_pairs={{0,1},{1,2},{2,3},{3,4},{4,5},{5,6},{6,7},{7,8},{8,9},{9,10},{10,1... | collective-permute-start | bytes 98312 | tf_op jit(solution)/shard_map/ppermute | solution.py:408
  6.6 1.6 %collective-permute-start.2 = (bf16[1024,128]{1,0:T(8,128)(2,1)}, bf16[1024,128]{1,0:T(8,128)(2,1)S(1)}, u32[]{:S(2)}, u32[]{:S(2)}) collective-permute-start(bf16[1024,128]{1,0:T(8,128)(2,1)} %refs_6_), channel_id=1, source_target_pairs={{0,8},{4,12},{8,0},{12,4},{16,24},{20,28},{24,16},{28,20},{1,9},{5... | collective-permute-start | bytes 786440 | tf_op jit(solution)/shard_map/ppermute | solution.py:412
  8.1 1.5 %collective-permute-start.3 = (bf16[1024,128]{1,0:T(8,128)(2,1)}, bf16[1024,128]{1,0:T(8,128)(2,1)}, u32[]{:S(2)}, u32[]{:S(2)}) collective-permute-start(bf16[1024,128]{1,0:T(8,128)(2,1)} %refs_6_), channel_id=1, source_target_pairs={{0,16},{4,20},{8,24},{12,28},{16,0},{20,4},{24,8},{28,12},{1,17},{... | collective-permute-start | bytes 786440 | tf_op jit(solution)/shard_map/ppermute | solution.py:412
  9.6 0.0 collective-permute-done.rim_ref
  9.6 0.6 copy-done.9
  10.2 5.0 %log_mel.1 = (bf16[72,128]{1,0:T(8,128)(2,1)}, bf16[72,128]{1,0:T(8,128)(2,1)}, bf16[72,128]{1,0:T(8,128)(2,1)}, bf16[72,128]{1,0:T(8,128)(2,1)}, bf16[128,768]{1,0:T(8,128)(2,1)}) custom-call(s32[8]{0:T(128)} %slots_ref.7, f32[8,1024]{1,0:T(8,128)} %copy-done.9, f32[8,5120]{1,0:T(8,128)} %audio_ref.1, f32[512,640]{1,0:T(8,128)} %constant.2.clone.table_ref, ...), custom_call_target="tpu_custom_call" | custom-call | flops 10000000000 | bytes 2000000 | tf_op jit(solution)/shard_map/log_mel/pallas_call | solution.py:428
  15.3 0.3 collective-permute-done.2.refs_7_
  15.6 1.0 %collective-permute-done.3.refs_8_ = bf16[1024,128]{1,0:T(8,128)(2,1)} collective-permute-done((bf16[1024,128]{1,0:T(8,128)(2,1)}, bf16[1024,128]{1,0:T(8,128)(2,1)}, u32[]{:S(2)}, u32[]{:S(2)}) %collective-permute-start.3) | collective-permute-done | bytes 262176 | tf_op jit(solution)/shard_map/ppermute | solution.py:412
  16.6 1.8 %collective-permute-start.4 = (bf16[72,128]{1,0:T(8,128)(2,1)}, bf16[72,128]{1,0:T(8,128)(2,1)S(1)}, u32[]{:S(2)}, u32[]{:S(2)}) collective-permute-start(bf16[72,128]{1,0:T(8,128)(2,1)} %get-tuple-element.38), channel_id=1, source_target_pairs={{0,8},{4,12},{8,0},{12,4},{16,24},{20,28},{24,16},{28,20},{1,9},{5... | collective-permute-start | bytes 55304 | tf_op jit(solution)/shard_map/ppermute | solution.py:412
  18.3 1.6 %collective-permute-start.5 = (bf16[72,128]{1,0:T(8,128)(2,1)}, bf16[72,128]{1,0:T(8,128)(2,1)S(1)}, u32[]{:S(2)}, u32[]{:S(2)}) collective-permute-start(bf16[72,128]{1,0:T(8,128)(2,1)} %get-tuple-element.39), channel_id=1, source_target_pairs={{0,16},{4,20},{8,24},{12,28},{16,0},{20,4},{24,8},{28,12},{1,17},{... | collective-permute-start | bytes 55304 | tf_op jit(solution)/shard_map/ppermute | solution.py:412
  19.9 0.9 %collective-permute-start.6 = (bf16[72,128]{1,0:T(8,128)(2,1)}, bf16[72,128]{1,0:T(8,128)(2,1)S(1)}, u32[]{:S(2)}, u32[]{:S(2)}) collective-permute-start(bf16[72,128]{1,0:T(8,128)(2,1)} %get-tuple-element.40), channel_id=1, source_target_pairs={{0,24},{4,28},{8,16},{12,20},{16,8},{20,12},{24,0},{28,4},{1,25},{... | collective-permute-start | bytes 55304 | tf_op jit(solution)/shard_map/ppermute | solution.py:412
  20.9 2.1 %collective-permute-start.16 = (bf16[128,768]{1,0:T(8,128)(2,1)}, bf16[128,768]{1,0:T(8,128)(2,1)S(1)}, u32[]{:S(2)}, u32[]{:S(2)}) collective-permute-start(bf16[128,768]{1,0:T(8,128)(2,1)} %get-tuple-element.51.refs_8_), channel_id=1, source_target_pairs={{0,24},{4,28},{8,16},{12,20},{16,8},{20,12},{24,0},{28,4},{1,25},{... | collective-permute-start | bytes 589832 | tf_op jit(solution)/shard_map/ppermute | solution.py:412
  22.9 0.4 collective-permute-start.15
  23.4 1.0 %collective-permute-start.14 = (bf16[128,768]{1,0:T(8,128)(2,1)}, bf16[128,768]{1,0:T(8,128)(2,1)S(1)}, u32[]{:S(2)}, u32[]{:S(2)}) collective-permute-start(bf16[128,768]{1,0:T(8,128)(2,1)} %get-tuple-element.51.refs_8_), channel_id=1, source_target_pairs={{0,8},{4,12},{8,0},{12,4},{16,24},{20,28},{24,16},{28,20},{1,9},{5... | collective-permute-start | bytes 589832 | tf_op jit(solution)/shard_map/ppermute | solution.py:412
  24.4 0.7 %collective-permute-done.6.refs_3_ = bf16[72,128]{1,0:T(8,128)(2,1)S(1)} collective-permute-done((bf16[72,128]{1,0:T(8,128)(2,1)}, bf16[72,128]{1,0:T(8,128)(2,1)S(1)}, u32[]{:S(2)}, u32[]{:S(2)}) %collective-permute-start.6) | collective-permute-done | bytes 18464 | tf_op jit(solution)/shard_map/ppermute | solution.py:412
  25.2 0.0 copy-start.8
  25.2 0.7 copy-done.8
  25.9 5.0 %conv.1 = (bf16[32,1024]{1,0:T(8,128)(2,1)S(1)}, bf16[32,1024]{1,0:T(8,128)(2,1)S(1)}, bf16[32,1024]{1,0:T(8,128)(2,1)S(1)}, bf16[32,1024]{1,0:T(8,128)(2,1)S(1)...) custom-call(bf16[9,256]{1,0:T(8,128)(2,1)S(1)} %copy-done.7, ...), custom_call_target="tpu_custom_call" | custom-call | flops 2000000000 | bytes 4000000 | tf_op jit(solution)/shard_map/conv/pallas_call | solution.py:449
  30.9 0.0 copy-start.6
  31.0 0.1 collective-permute-start.7
  31.0 1.5 %collective-permute-start.8 = (bf16[32,1024]{1,0:T(8,128)(2,1)S(1)}, bf16[32,1024]{1,0:T(8,128)(2,1)S(1)}, u32[]{:S(2)}, u32[]{:S(2)}) collective-permute-start(bf16[32,1024]{1,0:T(8,128)(2,1)S(1)} %get-tuple-element.45), channel_id=1, source_target_pairs={{0,8},{4,12},{8,0},{12,4},{16,24},{20,28},{24,16},{28,20},{1,9},{5... | collective-permute-start | bytes 196616 | tf_op jit(solution)/shard_map/ppermute | solution.py:419
  32.6 0.3 collective-permute-start.9
  32.9 1.3 %collective-permute-start.10 = (bf16[32,1024]{1,0:T(8,128)(2,1)S(1)}, bf16[32,1024]{1,0:T(8,128)(2,1)S(1)}, u32[]{:S(2)}, u32[]{:S(2)}) collective-permute-start(bf16[32,1024]{1,0:T(8,128)(2,1)S(1)} %get-tuple-element.47), channel_id=1, source_target_pairs={{0,16},{4,20},{8,24},{12,28},{16,0},{20,4},{24,8},{28,12},{1,17},{... | collective-permute-start | bytes 196616 | tf_op jit(solution)/shard_map/ppermute | solution.py:419
  34.2 0.4 collective-permute-start.11
  34.6 1.3 %collective-permute-start.12 = (bf16[32,1024]{1,0:T(8,128)(2,1)S(1)}, bf16[32,1024]{1,0:T(8,128)(2,1)S(1)}, u32[]{:S(2)}, u32[]{:S(2)}) collective-permute-start(bf16[32,1024]{1,0:T(8,128)(2,1)S(1)} %get-tuple-element.49), channel_id=1, source_target_pairs={{0,24},{4,28},{8,16},{12,20},{16,8},{20,12},{24,0},{28,4},{1,25},{... | collective-permute-start | bytes 196616 | tf_op jit(solution)/shard_map/ppermute | solution.py:419
  35.9 1.4 %collective-permute-start.13 = (bf16[32,1024]{1,0:T(8,128)(2,1)S(1)}, bf16[32,1024]{1,0:T(8,128)(2,1)S(1)}, u32[]{:S(2)}, u32[]{:S(2)}) collective-permute-start(bf16[32,1024]{1,0:T(8,128)(2,1)S(1)} %get-tuple-element.50), channel_id=1, source_target_pairs={{0,28},{4,24},{8,20},{12,16},{16,12},{20,8},{24,4},{28,0},{1,29},{... | collective-permute-start | bytes 196616 | tf_op jit(solution)/shard_map/ppermute | solution.py:419
  37.3 0.0 collective-permute-done.10.refs_4_
  37.3 1.1 %collective-permute-done.11.refs_5_ = bf16[32,1024]{1,0:T(8,128)(2,1)S(1)} collective-permute-done((bf16[32,1024]{1,0:T(8,128)(2,1)S(1)}, bf16[32,1024]{1,0:T(8,128)(2,1)S(1)}, u32[]{:S(2)}, u32[]{:S(2)}) %collective-permute-start.11) | collective-permute-done | bytes 65568 | tf_op jit(solution)/shard_map/ppermute | solution.py:419
  38.5 1.8 %collective-permute-done.12.refs_6_ = bf16[32,1024]{1,0:T(8,128)(2,1)S(1)} collective-permute-done((bf16[32,1024]{1,0:T(8,128)(2,1)S(1)}, bf16[32,1024]{1,0:T(8,128)(2,1)S(1)}, u32[]{:S(2)}, u32[]{:S(2)}) %collective-permute-start.12) | collective-permute-done | bytes 65568 | tf_op jit(solution)/shard_map/ppermute | solution.py:419
  40.3 1.0 %collective-permute-done.13.refs_7_ = bf16[32,1024]{1,0:T(8,128)(2,1)S(1)} collective-permute-done((bf16[32,1024]{1,0:T(8,128)(2,1)S(1)}, bf16[32,1024]{1,0:T(8,128)(2,1)S(1)}, u32[]{:S(2)}, u32[]{:S(2)}) %collective-permute-start.13) | collective-permute-done | bytes 65568 | tf_op jit(solution)/shard_map/ppermute | solution.py:419
  41.3 2.7 %layer_norm.1 = (bf16[64,1024]{1,0:T(8,128)(2,1)}, bf16[64,1024]{1,0:T(8,128)(2,1)S(1)}, bf16[4,128,768]{2,1,0:T(8,128)(2,1)S(1)}) custom-call(s32[8]{0:T(128)S(1)} %copy-done.1, s32[8]{0:T(128)S(1)} %copy-done.2, s32[8]{0:T(128)S(1)} %copy-done.3, bf16[32,1024]{1,0:T(8,128)(2,1)S(1)} %get-tuple-element.43.refs_0_, ...), custom_call_target="tpu_custom_call" | custom-call | flops 100000000 | bytes 1000000 | tf_op jit(solution)/shard_map/layer_norm/pallas_call | solution.py:471
  44.0 0.1 collective-permute-start.20
  44.1 1.6 %collective-permute-start.21 = (bf16[1024,128]{1,0:T(8,128)(2,1)S(1)}, bf16[1024,128]{1,0:T(8,128)(2,1)S(1)}, u32[]{:S(2)}, u32[]{:S(2)}) collective-permute-start(bf16[1024,128]{1,0:T(8,128)(2,1)S(1)} %copy-done.6), channel_id=1, source_target_pairs={{0,24},{4,28},{8,16},{12,20},{16,8},{20,12},{24,0},{28,4},{1,25},{... | collective-permute-start | bytes 786440 | tf_op jit(solution)/shard_map/ppermute | solution.py:412
  45.7 1.5 %collective-permute-start.19 = (bf16[64,1024]{1,0:T(8,128)(2,1)S(1)}, bf16[64,1024]{1,0:T(8,128)(2,1)S(1)}, u32[]{:S(2)}, u32[]{:S(2)}) collective-permute-start(bf16[64,1024]{1,0:T(8,128)(2,1)S(1)} %get-tuple-element.54.refs_0_), channel_id=1, source_target_pairs={{0,3},{1,2},{2,1},{3,0},{4,7},{5,6},{6,5},{7,4},{8,11},{9,10},{10,... | collective-permute-start | bytes 393224 | tf_op jit(solution)/shard_map/ppermute | solution.py:422
  47.2 0.0 collective-permute-start.18
  47.2 2.9 %collective-permute-start.17 = (bf16[64,1024]{1,0:T(8,128)(2,1)S(1)}, bf16[64,1024]{1,0:T(8,128)(2,1)S(1)}, u32[]{:S(2)}, u32[]{:S(2)}) collective-permute-start(bf16[64,1024]{1,0:T(8,128)(2,1)S(1)} %get-tuple-element.54.refs_0_), channel_id=1, source_target_pairs={{0,1},{1,0},{2,3},{3,2},{4,5},{5,4},{6,7},{7,6},{8,9},{9,8},{10,11... | collective-permute-start | bytes 393224 | tf_op jit(solution)/shard_map/ppermute | solution.py:422
  50.1 3.9 %collective-permute-done.19.refs_3_ = bf16[64,1024]{1,0:T(8,128)(2,1)S(1)} collective-permute-done((bf16[64,1024]{1,0:T(8,128)(2,1)S(1)}, bf16[64,1024]{1,0:T(8,128)(2,1)S(1)}, u32[]{:S(2)}, u32[]{:S(2)}) %collective-permute-start.19) | collective-permute-done | bytes 131104 | tf_op jit(solution)/shard_map/ppermute | solution.py:422
  53.9 5.1 %collective-permute-done.18.refs_2_ = bf16[64,1024]{1,0:T(8,128)(2,1)S(1)} collective-permute-done((bf16[64,1024]{1,0:T(8,128)(2,1)S(1)}, bf16[64,1024]{1,0:T(8,128)(2,1)S(1)}, u32[]{:S(2)}, u32[]{:S(2)}) %collective-permute-start.18) | collective-permute-done | bytes 131104 | tf_op jit(solution)/shard_map/ppermute | solution.py:422
  59.1 1.9 %attention.1 = (bf16[64,256]{1,0:T(8,128)(2,1)S(1)}, bf16[64,256]{1,0:T(8,128)(2,1)S(1)}, bf16[64,256]{1,0:T(8,128)(2,1)S(1)}, bf16[64,256]{1,0:T(8,128)(2,1)S(1)}, bf16[4,1024,128]{2,1,0:T(8,128)(2,1)S(1)}) custom-call(s32[8]{0:T(128)S(1)} %copy-done.1, s32[8]{0:T(128)S(1)} %copy-done.2, s32[8]{0:T(128)S(1)} %copy-done.3, ...), custom_call_target="tpu_custom_call" | custom-call | flops 1000000000 | bytes 2000000 | tf_op jit(solution)/shard_map/attention/pallas_call | solution.py:486
  61.0 0.1 collective-permute-start.25
  61.1 0.1 collective-permute-start.22
  61.2 3.0 %collective-permute-start.23 = (bf16[64,256]{1,0:T(8,128)(2,1)S(1)}, bf16[64,256]{1,0:T(8,128)(2,1)S(1)}, u32[]{:S(2)}, u32[]{:S(2)}) collective-permute-start(bf16[64,256]{1,0:T(8,128)(2,1)S(1)} %get-tuple-element.61), channel_id=1, source_target_pairs={{0,2},{1,3},{2,0},{3,1},{4,6},{5,7},{6,4},{7,5},{8,10},{9,11},{10,... | collective-permute-start | bytes 98312 | tf_op jit(solution)/shard_map/ppermute | solution.py:422
  64.2 1.3 %collective-permute-start.24 = (bf16[64,256]{1,0:T(8,128)(2,1)S(1)}, bf16[64,256]{1,0:T(8,128)(2,1)S(1)}, u32[]{:S(2)}, u32[]{:S(2)}) collective-permute-start(bf16[64,256]{1,0:T(8,128)(2,1)S(1)} %get-tuple-element.62), channel_id=1, source_target_pairs={{0,3},{1,2},{2,1},{3,0},{4,7},{5,6},{6,5},{7,4},{8,11},{9,10},{10,... | collective-permute-start | bytes 98312 | tf_op jit(solution)/shard_map/ppermute | solution.py:422
  65.6 0.5 collective-permute-done.23.refs_2_
  66.1 3.8 %collective-permute-done.24.refs_3_ = bf16[64,256]{1,0:T(8,128)(2,1)S(1)} collective-permute-done((bf16[64,256]{1,0:T(8,128)(2,1)S(1)}, bf16[64,256]{1,0:T(8,128)(2,1)S(1)}, u32[]{:S(2)}, u32[]{:S(2)}) %collective-permute-start.24) | collective-permute-done | bytes 32800 | tf_op jit(solution)/shard_map/ppermute | solution.py:422
  69.9 1.7 %output.1 = bf16[64,1024]{1,0:T(8,128)(2,1)} custom-call(s32[8]{0:T(128)S(1)} %copy-done.1, s32[8]{0:T(128)S(1)} %copy-done.2, s32[8]{0:T(128)S(1)} %copy-done.3, bf16[64,256]{1,0:T(8,128)(2,1)S(1)} %get-tuple-element.59.refs_0_, bf16[64,256]{1,0:T(8,128)(2,1)S(1)} %collective-permute-done.22.refs_1_, bf16[64,256]{1,0:T(8,128)(2,1)S(1)} %collective-permute-done.23.refs_2_, ...), custom_call_target="tpu_custom_call" | custom-call | flops 100000000 | bytes 3000000 | tf_op jit(solution)/shard_map/output/pallas_call | solution.py:505
  (30 shorter events, 0.1 us)
Async XLA Ops:
  0.6 15.9 %collective-permute-start.1 = (bf16[640,1024]{1,0:T(8,128)(2,1)}, bf16[640,1024]{1,0:T(8,128)(2,1)S(1)}, u32[]{:S(2)}, u32[]{:S(2)}) collective-permute-start(bf16[640,1024]{1,0:T(8,128)(2,1)} %refs_4_), channel_id=1, source_target_pairs={{0,4},{4,0},{8,12},{12,8},{16,20},{20,16},{24,28},{28,24},{1,5},{5... | collective-permute-start | bytes 3932168 | tf_op jit(solution)/shard_map/ppermute | solution.py:416
  1.9 23.3 %copy-start.4 = (bf16[640,1024]{1,0:T(8,128)(2,1)S(1)}, bf16[640,1024]{1,0:T(8,128)(2,1)}, u32[]{:S(2)}) copy-start(bf16[640,1024]{1,0:T(8,128)(2,1)} %refs_4_) | copy-start | bytes 3932164
  1.9 23.3 %copy-start.5 = (bf16[2304,256]{1,0:T(8,128)(2,1)S(1)}, bf16[2304,256]{1,0:T(8,128)(2,1)}, u32[]{:S(2)}) copy-start(bf16[2304,256]{1,0:T(8,128)(2,1)} %conv2_ref.1) | copy-start | bytes 3538948
  1.9 23.3 %copy-start.7 = (bf16[9,256]{1,0:T(8,128)(2,1)S(1)}, bf16[9,256]{1,0:T(8,128)(2,1)}, u32[]{:S(2)}) copy-start(bf16[9,256]{1,0:T(8,128)(2,1)} %conv1_ref.1) | copy-start | bytes 13828
  1.9 7.7 %collective-permute-start = (f32[8,1024]{1,0:T(8,128)S(1)}, f32[8,1024]{1,0:T(8,128)S(1)}, u32[]{:S(2)}, u32[]{:S(2)}) collective-permute-start(f32[8,1024]{1,0:T(8,128)S(1)} %slice.3), channel_id=1, source_target_pairs={{0,1},{1,2},{2,3},{3,4},{4,5},{5,6},{6,7},{7,8},{8,9},{9,10},{10,1... | collective-permute-start | bytes 98312 | tf_op jit(solution)/shard_map/ppermute | solution.py:408
  6.6 9.1 %collective-permute-start.2 = (bf16[1024,128]{1,0:T(8,128)(2,1)}, bf16[1024,128]{1,0:T(8,128)(2,1)S(1)}, u32[]{:S(2)}, u32[]{:S(2)}) collective-permute-start(bf16[1024,128]{1,0:T(8,128)(2,1)} %refs_6_), channel_id=1, source_target_pairs={{0,8},{4,12},{8,0},{12,4},{16,24},{20,28},{24,16},{28,20},{1,9},{5... | collective-permute-start | bytes 786440 | tf_op jit(solution)/shard_map/ppermute | solution.py:412
  8.1 8.5 %collective-permute-start.3 = (bf16[1024,128]{1,0:T(8,128)(2,1)}, bf16[1024,128]{1,0:T(8,128)(2,1)}, u32[]{:S(2)}, u32[]{:S(2)}) collective-permute-start(bf16[1024,128]{1,0:T(8,128)(2,1)} %refs_6_), channel_id=1, source_target_pairs={{0,16},{4,20},{8,24},{12,28},{16,0},{20,4},{24,8},{28,12},{1,17},{... | collective-permute-start | bytes 786440 | tf_op jit(solution)/shard_map/ppermute | solution.py:412
  9.6 0.6 copy-start.9
  16.6 6.8 %collective-permute-start.4 = (bf16[72,128]{1,0:T(8,128)(2,1)}, bf16[72,128]{1,0:T(8,128)(2,1)S(1)}, u32[]{:S(2)}, u32[]{:S(2)}) collective-permute-start(bf16[72,128]{1,0:T(8,128)(2,1)} %get-tuple-element.38), channel_id=1, source_target_pairs={{0,8},{4,12},{8,0},{12,4},{16,24},{20,28},{24,16},{28,20},{1,9},{5... | collective-permute-start | bytes 55304 | tf_op jit(solution)/shard_map/ppermute | solution.py:412
  18.3 6.1 %collective-permute-start.5 = (bf16[72,128]{1,0:T(8,128)(2,1)}, bf16[72,128]{1,0:T(8,128)(2,1)S(1)}, u32[]{:S(2)}, u32[]{:S(2)}) collective-permute-start(bf16[72,128]{1,0:T(8,128)(2,1)} %get-tuple-element.39), channel_id=1, source_target_pairs={{0,16},{4,20},{8,24},{12,28},{16,0},{20,4},{24,8},{28,12},{1,17},{... | collective-permute-start | bytes 55304 | tf_op jit(solution)/shard_map/ppermute | solution.py:412
  19.9 5.2 %collective-permute-start.6 = (bf16[72,128]{1,0:T(8,128)(2,1)}, bf16[72,128]{1,0:T(8,128)(2,1)S(1)}, u32[]{:S(2)}, u32[]{:S(2)}) collective-permute-start(bf16[72,128]{1,0:T(8,128)(2,1)} %get-tuple-element.40), channel_id=1, source_target_pairs={{0,24},{4,28},{8,16},{12,20},{16,8},{20,12},{24,0},{28,4},{1,25},{... | collective-permute-start | bytes 55304 | tf_op jit(solution)/shard_map/ppermute | solution.py:412
  20.8 20.4 %copy-start = (bf16[128,768]{1,0:T(8,128)(2,1)S(1)}, bf16[128,768]{1,0:T(8,128)(2,1)}, u32[]{:S(2)}) copy-start(bf16[128,768]{1,0:T(8,128)(2,1)} %get-tuple-element.51.refs_8_) | copy-start | bytes 589828
  20.8 20.4 %copy-start.1 = (s32[8]{0:T(128)S(1)}, s32[8]{0:T(128)}, u32[]{:S(2)}) copy-start(s32[8]{0:T(128)} %slots_ref.7) | copy-start | bytes 100
  20.8 20.4 %copy-start.2 = (s32[8]{0:T(128)S(1)}, s32[8]{0:T(128)}, u32[]{:S(2)}) copy-start(s32[8]{0:T(128)} %starts_ref.5) | copy-start | bytes 100
  20.8 20.4 %copy-start.3 = (s32[8]{0:T(128)S(1)}, s32[8]{0:T(128)}, u32[]{:S(2)}) copy-start(s32[8]{0:T(128)} %lengths_ref.5) | copy-start | bytes 100
  20.9 11.7 %collective-permute-start.16 = (bf16[128,768]{1,0:T(8,128)(2,1)}, bf16[128,768]{1,0:T(8,128)(2,1)S(1)}, u32[]{:S(2)}, u32[]{:S(2)}) collective-permute-start(bf16[128,768]{1,0:T(8,128)(2,1)} %get-tuple-element.51.refs_8_), channel_id=1, source_target_pairs={{0,24},{4,28},{8,16},{12,20},{16,8},{20,12},{24,0},{28,4},{1,25},{... | collective-permute-start | bytes 589832 | tf_op jit(solution)/shard_map/ppermute | solution.py:412
  22.9 10.0 %collective-permute-start.15 = (bf16[128,768]{1,0:T(8,128)(2,1)}, bf16[128,768]{1,0:T(8,128)(2,1)S(1)}, u32[]{:S(2)}, u32[]{:S(2)}) collective-permute-start(bf16[128,768]{1,0:T(8,128)(2,1)} %get-tuple-element.51.refs_8_), channel_id=1, source_target_pairs={{0,16},{4,20},{8,24},{12,28},{16,0},{20,4},{24,8},{28,12},{1,17},{... | collective-permute-start | bytes 589832 | tf_op jit(solution)/shard_map/ppermute | solution.py:412
  23.4 10.8 %collective-permute-start.14 = (bf16[128,768]{1,0:T(8,128)(2,1)}, bf16[128,768]{1,0:T(8,128)(2,1)S(1)}, u32[]{:S(2)}, u32[]{:S(2)}) collective-permute-start(bf16[128,768]{1,0:T(8,128)(2,1)} %get-tuple-element.51.refs_8_), channel_id=1, source_target_pairs={{0,8},{4,12},{8,0},{12,4},{16,24},{20,28},{24,16},{28,20},{1,9},{5... | collective-permute-start | bytes 589832 | tf_op jit(solution)/shard_map/ppermute | solution.py:412
  25.2 0.7 %copy-start.8 = (bf16[72,128]{1,0:T(8,128)(2,1)S(1)}, bf16[72,128]{1,0:T(8,128)(2,1)}, u32[]{:S(2)}) copy-start(bf16[72,128]{1,0:T(8,128)(2,1)} %get-tuple-element.37.refs_0_) | copy-start | bytes 55300
  30.9 13.2 %copy-start.6 = (bf16[1024,128]{1,0:T(8,128)(2,1)S(1)}, bf16[1024,128]{1,0:T(8,128)(2,1)}, u32[]{:S(2)}) copy-start(bf16[1024,128]{1,0:T(8,128)(2,1)} %refs_6_) | copy-start | bytes 786436
  31.0 3.7 %collective-permute-start.7 = (bf16[32,1024]{1,0:T(8,128)(2,1)S(1)}, bf16[32,1024]{1,0:T(8,128)(2,1)S(1)}, u32[]{:S(2)}, u32[]{:S(2)}) collective-permute-start(bf16[32,1024]{1,0:T(8,128)(2,1)S(1)} %get-tuple-element.44), channel_id=1, source_target_pairs={{0,4},{4,0},{8,12},{12,8},{16,20},{20,16},{24,28},{28,24},{1,5},{5... | collective-permute-start | bytes 196616 | tf_op jit(solution)/shard_map/ppermute | solution.py:419
  31.0 4.9 %collective-permute-start.8 = (bf16[32,1024]{1,0:T(8,128)(2,1)S(1)}, bf16[32,1024]{1,0:T(8,128)(2,1)S(1)}, u32[]{:S(2)}, u32[]{:S(2)}) collective-permute-start(bf16[32,1024]{1,0:T(8,128)(2,1)S(1)} %get-tuple-element.45), channel_id=1, source_target_pairs={{0,8},{4,12},{8,0},{12,4},{16,24},{20,28},{24,16},{28,20},{1,9},{5... | collective-permute-start | bytes 196616 | tf_op jit(solution)/shard_map/ppermute | solution.py:419
  32.6 4.7 %collective-permute-start.9 = (bf16[32,1024]{1,0:T(8,128)(2,1)S(1)}, bf16[32,1024]{1,0:T(8,128)(2,1)S(1)}, u32[]{:S(2)}, u32[]{:S(2)}) collective-permute-start(bf16[32,1024]{1,0:T(8,128)(2,1)S(1)} %get-tuple-element.46), channel_id=1, source_target_pairs={{0,12},{4,8},{8,4},{12,0},{16,28},{20,24},{24,20},{28,16},{1,13},{... | collective-permute-start | bytes 196616 | tf_op jit(solution)/shard_map/ppermute | solution.py:419
  32.9 4.4 %collective-permute-start.10 = (bf16[32,1024]{1,0:T(8,128)(2,1)S(1)}, bf16[32,1024]{1,0:T(8,128)(2,1)S(1)}, u32[]{:S(2)}, u32[]{:S(2)}) collective-permute-start(bf16[32,1024]{1,0:T(8,128)(2,1)S(1)} %get-tuple-element.47), channel_id=1, source_target_pairs={{0,16},{4,20},{8,24},{12,28},{16,0},{20,4},{24,8},{28,12},{1,17},{... | collective-permute-start | bytes 196616 | tf_op jit(solution)/shard_map/ppermute | solution.py:419
  34.2 4.2 %collective-permute-start.11 = (bf16[32,1024]{1,0:T(8,128)(2,1)S(1)}, bf16[32,1024]{1,0:T(8,128)(2,1)S(1)}, u32[]{:S(2)}, u32[]{:S(2)}) collective-permute-start(bf16[32,1024]{1,0:T(8,128)(2,1)S(1)} %get-tuple-element.48), channel_id=1, source_target_pairs={{0,20},{4,16},{8,28},{12,24},{16,4},{20,0},{24,12},{28,8},{1,21},{... | collective-permute-start | bytes 196616 | tf_op jit(solution)/shard_map/ppermute | solution.py:419
  34.6 5.7 %collective-permute-start.12 = (bf16[32,1024]{1,0:T(8,128)(2,1)S(1)}, bf16[32,1024]{1,0:T(8,128)(2,1)S(1)}, u32[]{:S(2)}, u32[]{:S(2)}) collective-permute-start(bf16[32,1024]{1,0:T(8,128)(2,1)S(1)} %get-tuple-element.49), channel_id=1, source_target_pairs={{0,24},{4,28},{8,16},{12,20},{16,8},{20,12},{24,0},{28,4},{1,25},{... | collective-permute-start | bytes 196616 | tf_op jit(solution)/shard_map/ppermute | solution.py:419
  35.9 5.3 %collective-permute-start.13 = (bf16[32,1024]{1,0:T(8,128)(2,1)S(1)}, bf16[32,1024]{1,0:T(8,128)(2,1)S(1)}, u32[]{:S(2)}, u32[]{:S(2)}) collective-permute-start(bf16[32,1024]{1,0:T(8,128)(2,1)S(1)} %get-tuple-element.50), channel_id=1, source_target_pairs={{0,28},{4,24},{8,20},{12,16},{16,12},{20,8},{24,4},{28,0},{1,29},{... | collective-permute-start | bytes 196616 | tf_op jit(solution)/shard_map/ppermute | solution.py:419
  44.0 15.1 %collective-permute-start.20 = (bf16[4,128,768]{2,1,0:T(8,128)(2,1)S(1)}, bf16[4,128,768]{2,1,0:T(8,128)(2,1)S(1)}, u32[]{:S(2)}, u32[]{:S(2)}) collective-permute-start(bf16[4,128,768]{2,1,0:T(8,128)(2,1)S(1)} %get-tuple-element.55.refs_4_), channel_id=1, source_target_pairs={{0,4},{4,0},{8,12},{12,8},{16,20},{20,16},{24,28},{28,24},{1,5},{5... | collective-permute-start | bytes 2359304 | tf_op jit(solution)/shard_map/ppermute | solution.py:416
  44.1 15.0 %collective-permute-start.21 = (bf16[1024,128]{1,0:T(8,128)(2,1)S(1)}, bf16[1024,128]{1,0:T(8,128)(2,1)S(1)}, u32[]{:S(2)}, u32[]{:S(2)}) collective-permute-start(bf16[1024,128]{1,0:T(8,128)(2,1)S(1)} %copy-done.6), channel_id=1, source_target_pairs={{0,24},{4,28},{8,16},{12,20},{16,8},{20,12},{24,0},{28,4},{1,25},{... | collective-permute-start | bytes 786440 | tf_op jit(solution)/shard_map/ppermute | solution.py:412
  45.7 8.2 %collective-permute-start.19 = (bf16[64,1024]{1,0:T(8,128)(2,1)S(1)}, bf16[64,1024]{1,0:T(8,128)(2,1)S(1)}, u32[]{:S(2)}, u32[]{:S(2)}) collective-permute-start(bf16[64,1024]{1,0:T(8,128)(2,1)S(1)} %get-tuple-element.54.refs_0_), channel_id=1, source_target_pairs={{0,3},{1,2},{2,1},{3,0},{4,7},{5,6},{6,5},{7,4},{8,11},{9,10},{10,... | collective-permute-start | bytes 393224 | tf_op jit(solution)/shard_map/ppermute | solution.py:422
  47.2 11.9 %collective-permute-start.18 = (bf16[64,1024]{1,0:T(8,128)(2,1)S(1)}, bf16[64,1024]{1,0:T(8,128)(2,1)S(1)}, u32[]{:S(2)}, u32[]{:S(2)}) collective-permute-start(bf16[64,1024]{1,0:T(8,128)(2,1)S(1)} %get-tuple-element.54.refs_0_), channel_id=1, source_target_pairs={{0,2},{1,3},{2,0},{3,1},{4,6},{5,7},{6,4},{7,5},{8,10},{9,11},{10,... | collective-permute-start | bytes 393224 | tf_op jit(solution)/shard_map/ppermute | solution.py:422
  47.2 11.9 %collective-permute-start.17 = (bf16[64,1024]{1,0:T(8,128)(2,1)S(1)}, bf16[64,1024]{1,0:T(8,128)(2,1)S(1)}, u32[]{:S(2)}, u32[]{:S(2)}) collective-permute-start(bf16[64,1024]{1,0:T(8,128)(2,1)S(1)} %get-tuple-element.54.refs_0_), channel_id=1, source_target_pairs={{0,1},{1,0},{2,3},{3,2},{4,5},{5,4},{6,7},{7,6},{8,9},{9,8},{10,11... | collective-permute-start | bytes 393224 | tf_op jit(solution)/shard_map/ppermute | solution.py:422
  61.0 8.9 %collective-permute-start.25 = (bf16[4,1024,128]{2,1,0:T(8,128)(2,1)S(1)}, bf16[4,1024,128]{2,1,0:T(8,128)(2,1)S(1)}, u32[]{:S(2)}, u32[]{:S(2)}) collective-permute-start(bf16[4,1024,128]{2,1,0:T(8,128)(2,1)S(1)} %get-tuple-element.63.refs_4_), channel_id=1, source_target_pairs={{0,4},{4,0},{8,12},{12,8},{16,20},{20,16},{24,28},{28,24},{1,5},{5... | collective-permute-start | bytes 3145736 | tf_op jit(solution)/shard_map/ppermute | solution.py:416
  61.1 4.5 %collective-permute-start.22 = (bf16[64,256]{1,0:T(8,128)(2,1)S(1)}, bf16[64,256]{1,0:T(8,128)(2,1)S(1)}, u32[]{:S(2)}, u32[]{:S(2)}) collective-permute-start(bf16[64,256]{1,0:T(8,128)(2,1)S(1)} %get-tuple-element.60), channel_id=1, source_target_pairs={{0,1},{1,0},{2,3},{3,2},{4,5},{5,4},{6,7},{7,6},{8,9},{9,8},{10,11... | collective-permute-start | bytes 98312 | tf_op jit(solution)/shard_map/ppermute | solution.py:422
  61.2 4.9 %collective-permute-start.23 = (bf16[64,256]{1,0:T(8,128)(2,1)S(1)}, bf16[64,256]{1,0:T(8,128)(2,1)S(1)}, u32[]{:S(2)}, u32[]{:S(2)}) collective-permute-start(bf16[64,256]{1,0:T(8,128)(2,1)S(1)} %get-tuple-element.61), channel_id=1, source_target_pairs={{0,2},{1,3},{2,0},{3,1},{4,6},{5,7},{6,4},{7,5},{8,10},{9,11},{10,... | collective-permute-start | bytes 98312 | tf_op jit(solution)/shard_map/ppermute | solution.py:422
  64.2 5.7 %collective-permute-start.24 = (bf16[64,256]{1,0:T(8,128)(2,1)S(1)}, bf16[64,256]{1,0:T(8,128)(2,1)S(1)}, u32[]{:S(2)}, u32[]{:S(2)}) collective-permute-start(bf16[64,256]{1,0:T(8,128)(2,1)S(1)} %get-tuple-element.62), channel_id=1, source_target_pairs={{0,3},{1,2},{2,1},{3,0},{4,7},{5,6},{6,5},{7,4},{8,11},{9,10},{10,... | collective-permute-start | bytes 98312 | tf_op jit(solution)/shard_map/ppermute | solution.py:422

commit v4 on v3

--- a/solution.py
+++ b/solution.py
@@ -228,7 +228,9 @@
     mel_refs, refs = refs[:parts], refs[parts:]
     proj_refs, refs = refs[:copies], refs[copies:]
     outs_refs, refs = refs[:windows], refs[windows:]
-    mel, banded_ref, even, odd, second, conv2, proj, partial, sems = refs
+    mel, own, banded_ref, even, odd, second, conv2, proj, partial, sems = refs
+    load_own = pltpu.make_async_copy(mel_refs[0], own, sems.at[1 + copies])
+    load_own.start()
     load_conv2 = pltpu.make_async_copy(conv2_ref, conv2, sems.at[0])
     load_conv2.start()
     loads = []
@@ -239,7 +241,9 @@
     banded_weights(width, conv1_ref, banded_ref)
     streams = mel_refs[0].shape[0] // JS
     n = parts * streams
-    for step in range(parts):
+    load_own.wait()
+    mel[part] = own[...].astype(F32)
+    for step in range(1, parts):
         mel[part ^ step] = mel_refs[step][...].astype(F32)
     evens = jnp.concatenate(
         [mel[p, j * streams : (j + 1) * streams, :] for j in range(JS) for p in range(parts)], axis=0
@@ -282,7 +286,7 @@
     return begin, begin + span
 
 
-def norm_kernel(parts, group, slots_ref, starts_ref, lengths_ref, *refs):
+def norm_kernel(parts, *refs):
     _, copy_index = place(parts)
     windows = lax.axis_size("dp")
     copies = windows // parts
@@ -291,7 +295,6 @@
     rows_out, normed_out, stack_out, encoded, sems = refs
     moves = stacked(parts, piece_refs, stack_out, sems, 0)
     start_all(moves)
-    begin, end = bounds(lax.axis_index("dp"), slots_ref, starts_ref, lengths_ref)
     rows = W * parts
     for copy in range(copies):
         total = part_refs[copy][...].astype(F32)
@@ -300,17 +303,25 @@
         at = pl.multiple_of((copy_index ^ copy) * rows, rows)
         encoded[pl.ds(at, rows), :] = total.astype(BF16)
     values = jnp.dot(frame_order(parts, copies), encoded[...], preferred_element_type=F32)
+    rows_out[...] = values.astype(BF16)
     mean = jnp.mean(values, axis=-1, keepdims=True)
     centered = values - mean
     variance = jnp.mean(centered * centered, axis=-1, keepdims=True)
     normed_out[...] = (centered * lax.rsqrt(variance + EPS_NORM)).astype(BF16)
+    wait_all(moves)
+
+
+def mask_kernel(windows, group, slots_ref, starts_ref, lengths_ref, rows_ref, rows_out, keys_out, valid_out):
+    begin, end = bounds(lax.axis_index("dp"), slots_ref, starts_ref, lengths_ref)
     sample = samples(iota(windows * W, 1, 0), windows, group) + lax.axis_index("seq") * (W * SPAN)
     valid = (sample >= begin) & (sample < end)
-    rows_out[...] = jnp.where(valid, values, 0.0).astype(BF16)
-    wait_all(moves)
-
-
-def attention_kernel(parts, windows, group, slots_ref, starts_ref, lengths_ref, *refs):
+    rows_out[...] = jnp.where(valid, rows_ref[...].astype(F32), 0.0).astype(BF16)
+    valid_out[...] = valid.astype(F32)
+    keys = samples(iota(group, windows * W, 1), windows, group) + iota(group, windows * W, 0) * (W * SPAN)
+    keys_out[...] = ((keys >= begin) & (keys < end)).astype(F32)
+
+
+def attention_kernel(parts, windows, group, keys_ref, *refs):
     _, copy_index = place(parts)
     plane = lax.axis_index("seq")
     copies = windows // parts
@@ -320,12 +331,8 @@
     outs_refs, (stack_out, pieces, sems) = refs[:group], refs[group:]
     moves = stacked(parts, weight_refs, stack_out, sems, 0)
     start_all(moves)
-    begin, end = bounds(lax.axis_index("dp"), slots_ref, starts_ref, lengths_ref)
-    masks = []
-    for step in range(group):
-        sample = samples(iota(1, windows * W, 1), windows, group) + (plane ^ step) * (W * SPAN)
-        masks.append(((sample >= begin) & (sample < end)).astype(F32))
-    valid = jnp.concatenate(masks, axis=1) > 0.5
+    keys = [keys_ref[pl.ds(plane ^ step, 1), :] for step in range(group)]
+    valid = jnp.concatenate(keys, axis=1) > 0.5
     local = normed_refs[0].shape[0]
     depth = pieces.shape[2]
     for step in range(group):
@@ -359,21 +366,18 @@
     wait_all(moves)
 
 
-def output_kernel(parts, windows, group, slots_ref, starts_ref, lengths_ref, *refs):
+def output_kernel(parts, windows, group, valid_ref, *refs):
     context_refs, refs = refs[:group], refs[group:]
     stack_refs, refs = refs[: windows // parts], refs[windows // parts :]
     out_ref, context, pieces = refs
     _, copy_index = place(parts)
     copies = windows // parts
     plane = lax.axis_index("seq")
-    begin, end = bounds(lax.axis_index("dp"), slots_ref, starts_ref, lengths_ref)
     head_width = context_refs[0].shape[1]
     for step in range(group):
         at = pl.multiple_of((plane ^ step) * head_width, LANES)
         context[:, pl.ds(at, head_width)] = context_refs[step][...]
     ordered = context[...]
-    sample = samples(iota(windows * W, 1, 0), windows, group) + plane * (W * SPAN)
-    valid = (sample >= begin) & (sample < end)
     for step in range(copies):
         slot = copy_index ^ step
         for piece in range(parts):
@@ -381,7 +385,7 @@
                 ordered, stack_refs[step][piece], preferred_element_type=F32
             )
     result = jnp.concatenate([pieces[d] for d in range(windows)], axis=1)
-    out_ref[...] = jnp.where(valid, result, 0.0).astype(BF16)
+    out_ref[...] = jnp.where(valid_ref[...] > 0.5, result, 0.0).astype(BF16)
 
 
 def on_device(
@@ -449,10 +453,11 @@
     partials = pl.pallas_call(
         functools.partial(conv_kernel, parts, width),
         out_shape=tuple([jax.ShapeDtypeStruct((W * parts, features), BF16)] * windows),
-        in_specs=[vmem()] + [anywhere()] + [vmem()] * parts + [anywhere()] * copies,
+        in_specs=[vmem()] + [anywhere()] * 2 + [vmem()] * (parts - 1) + [anywhere()] * copies,
         out_specs=tuple([vmem()] * windows),
         scratch_shapes=[
             pltpu.VMEM((parts, rows, LANES), F32),
+            pltpu.VMEM((rows, LANES), BF16),
             pltpu.VMEM((LANES, outs * channels), BF16),
             pltpu.VMEM((JS * n, outs * channels), BF16),
             pltpu.VMEM((W * n, outs * channels), BF16),
@@ -460,7 +465,7 @@
             pltpu.VMEM(conv2_weight.shape, BF16),
             pltpu.VMEM((copies,) + proj_weight.shape, BF16),
             pltpu.VMEM((features // LANES, W * n, LANES), F32),
-            pltpu.SemaphoreType.DMA((1 + copies,)),
+            pltpu.SemaphoreType.DMA((2 + copies,)),
         ],
         compiler_params=params(min(40 + 4 * scale, 56)),
         cost_estimate=cost(2e9, 4e6),
@@ -468,17 +473,30 @@
     )(conv1_weight, conv2_weight, *mel_all, *proj_all)
     partials = [partials[0]] + [to_window(partials[step], step) for step in range(1, windows)]
 
-    regrouped, normed, stack = pl.pallas_call(
-        functools.partial(norm_kernel, parts, group),
+    ordered, normed, stack = pl.pallas_call(
+        functools.partial(norm_kernel, parts),
         out_shape=(block, block, jax.ShapeDtypeStruct((parts,) + mix_piece.shape, BF16)),
-        in_specs=[smem()] * 3 + [vmem()] * windows + [anywhere()] * parts,
+        in_specs=[vmem()] * windows + [anywhere()] * parts,
         out_specs=(vmem(), vmem(), vmem()),
         scratch_shapes=[pltpu.VMEM((local, features), BF16), pltpu.SemaphoreType.DMA((parts,))],
         compiler_params=params(min(12 * scale, 32)),
         cost_estimate=cost(1e8, 1e6),
         name="layer_norm",
-    )(slots, starts, lengths, *partials, *mix_all)
+    )(*partials, *mix_all)
     mix_stacks = [stack] + [to_copy(stack, step) for step in range(1, copies)]
+    regrouped, keys, valid = pl.pallas_call(
+        functools.partial(mask_kernel, windows, group),
+        out_shape=(
+            block,
+            jax.ShapeDtypeStruct((group, local), F32),
+            jax.ShapeDtypeStruct((local, 1), F32),
+        ),
+        in_specs=[smem()] * 3 + [vmem()],
+        out_specs=(vmem(), vmem(), vmem()),
+        compiler_params=params(min(8 * scale, 32)),
+        cost_estimate=cost(1e8, 1e6),
+        name="mask",
+    )(slots, starts, lengths, ordered)
     normed, out_here = lax.optimization_barrier((normed, out_weight))
     normed = [normed] + [to_plane(normed, step) for step in range(1, group)]
     out_all = [out_here] + near + [to_part(out_here, parts - 1)]
@@ -489,7 +507,7 @@
             [jax.ShapeDtypeStruct((local, head_width), BF16)] * group
             + [jax.ShapeDtypeStruct((parts,) + out_weight.shape, BF16)]
         ),
-        in_specs=[smem()] * 3 + [vmem()] * (group + copies) + [anywhere()] * parts,
+        in_specs=[vmem()] * (1 + group + copies) + [anywhere()] * parts,
         out_specs=tuple([vmem()] * (group + 1)),
         scratch_shapes=[
             pltpu.VMEM((windows, group * local, qkv_weight.shape[0]), BF16),
@@ -498,14 +516,14 @@
         compiler_params=params(min(16 * scale, 48)),
         cost_estimate=cost(1e9, 2e6),
         name="attention",
-    )(slots, starts, lengths, *normed, *mix_stacks, *out_all)
+    )(keys, *normed, *mix_stacks, *out_all)
     context = [context[0]] + [to_plane(context[step], step) for step in range(1, group)]
     out_stacks = [stack] + [to_copy(stack, step) for step in range(1, copies)]
 
     attended = pl.pallas_call(
         functools.partial(output_kernel, parts, windows, group),
         out_shape=block,
-        in_specs=[smem()] * 3 + [vmem()] * (group + copies),
+        in_specs=[vmem()] * (1 + group + copies),
         out_specs=vmem(),
         scratch_shapes=[
             pltpu.VMEM((local, features), BF16),
@@ -514,7 +532,7 @@
         compiler_params=params(min(12 * scale, 32)),
         cost_estimate=cost(1e8, 3e6),
         name="output",
-    )(slots, starts, lengths, *context, *out_stacks)
+    )(valid, *context, *out_stacks)
     shape = (1, windows, 1, W, features)
     return (regrouped.reshape(shape), attended.reshape(shape))
 

time: 72 us -> 69.8 us (0.969)
  waiting for transfers between devices: 19.3 us -> 18.1 us
  Pallas kernels: 16.4 us -> 15.5 us
    ppermute x6, waiting for transfers between devices: 13.4 us -> 12.1 us  [to_plane(): return lax.ppermute(block, 'seq', [(i, i ^ step) for i in range(group)])]
    pallas_call x1 -> x2, Pallas kernels: 2.72 us -> 2.72 us  [the longest x1 1.46 us: on_device(): pl.pallas_call(functools.partial(norm_kernel, parts), out_shape=(block, b...]
  transfers between devices with their start and end apart: 26 -> 26, of which waited for: 10 -> 11; matrix products, arithmetic and copies ran while one was open for 1% -> 1% of each run, Pallas kernels for 14% -> 17%
where the time goes in v4:
time: 69.8 us; the launch traced here: 69.5 us
  starting transfers between devices  33 us (47%)
  waiting for transfers between devices  18.1 us (26%)
  Pallas kernels  15.5 us (22%)
  local copies, waits for them, and re-layouts  2.13 us (3%)
  between operations  0.77 us (1%)
    ppermute x9, starting transfers between devices, to_part(): return lax.ppermute(block, 'dp', pairs)  12.4 us
    ppermute x6, waiting for transfers between devices, to_plane(): return lax.ppermute(block, 'seq', [(i, i ^ step) for i in range(group)])  12.1 us
    ppermute x6, starting transfers between devices, to_plane(): return lax.ppermute(block, 'seq', [(i, i ^ step) for i in range(group)])  8.83 us
    ppermute x7, starting transfers between devices, to_window(): return lax.ppermute(block, 'dp', [(i, i ^ step) for i in range(windows)])  6.33 us
    pallas_call x1, Pallas kernels, on_device(): pl.pallas_call(functools.partial(conv_kernel, parts, width), out_shape=tu...  5.23 us
    pallas_call x1, Pallas kernels, on_device(): pl.pallas_call(functools.partial(mel_kernel, parts, group), out_shape=tup...  5.03 us
    ppermute x1, starting transfers between devices, on_device(): rim = lax.ppermute(audio[:, audio.shape[1] - RIM:], ('dp', 'seq'), route)  4.63 us
    ppermute x7, waiting for transfers between devices, to_window(): return lax.ppermute(block, 'dp', [(i, i ^ step) for i in range(windows)])  3.94 us
  transfers between devices with their start and end apart: 26, of which 11 were waited for; matrix products, arithmetic and copies ran while one was open for 1% of the time, Pallas kernels for 17%

profile of v4, /device:TPU:0, one launch (start us, length us, event | category | flops | bytes accessed | tf_op | source)
XLA Modules:
  0.0 69.5 jit_solution(5791261116974035238)
XLA Ops:
  0.6 0.5 collective-permute-start.1
  1.1 0.8 %slice.3 = f32[8,1024]{1,0:T(8,128)S(1)} slice(f32[8,5120]{1,0:T(8,128)} %audio_ref.1), slice={[0:8], [4096:5120]} | slice | bytes 65536 | tf_op jit(solution)/shard_map/slice | solution.py:412
  1.9 4.6 %collective-permute-start = (f32[8,1024]{1,0:T(8,128)S(1)}, f32[8,1024]{1,0:T(8,128)S(1)}, u32[]{:S(2)}, u32[]{:S(2)}) collective-permute-start(f32[8,1024]{1,0:T(8,128)S(1)} %slice.3), channel_id=1, source_target_pairs={{0,1},{1,2},{2,3},{3,4},{4,5},{5,6},{6,7},{7,8},{8,9},{9,10},{10,1... | collective-permute-start | bytes 98312 | tf_op jit(solution)/shard_map/ppermute | solution.py:412
  6.6 1.6 %collective-permute-start.2 = (bf16[1024,128]{1,0:T(8,128)(2,1)}, bf16[1024,128]{1,0:T(8,128)(2,1)S(1)}, u32[]{:S(2)}, u32[]{:S(2)}) collective-permute-start(bf16[1024,128]{1,0:T(8,128)(2,1)} %refs_6_), channel_id=1, source_target_pairs={{0,8},{4,12},{8,0},{12,4},{16,24},{20,28},{24,16},{28,20},{1,9},{5... | collective-permute-start | bytes 786440 | tf_op jit(solution)/shard_map/ppermute | solution.py:416
  8.1 1.5 %collective-permute-start.3 = (bf16[1024,128]{1,0:T(8,128)(2,1)}, bf16[1024,128]{1,0:T(8,128)(2,1)}, u32[]{:S(2)}, u32[]{:S(2)}) collective-permute-start(bf16[1024,128]{1,0:T(8,128)(2,1)} %refs_6_), channel_id=1, source_target_pairs={{0,16},{4,20},{8,24},{12,28},{16,0},{20,4},{24,8},{28,12},{1,17},{... | collective-permute-start | bytes 786440 | tf_op jit(solution)/shard_map/ppermute | solution.py:416
  9.6 0.6 copy-done.9
  10.2 5.0 %log_mel.1 = (bf16[72,128]{1,0:T(8,128)(2,1)}, bf16[72,128]{1,0:T(8,128)(2,1)}, bf16[72,128]{1,0:T(8,128)(2,1)}, bf16[72,128]{1,0:T(8,128)(2,1)}, bf16[128,768]{1,0:T(8,128)(2,1)}) custom-call(s32[8]{0:T(128)} %slots_ref.3, f32[8,1024]{1,0:T(8,128)} %copy-done.9, f32[8,5120]{1,0:T(8,128)} %audio_ref.1, f32[512,640]{1,0:T(8,128)} %constant.2.clone.table_ref, ...), custom_call_target="tpu_custom_call" | custom-call | flops 10000000000 | bytes 2000000 | tf_op jit(solution)/shard_map/log_mel/pallas_call | solution.py:432
  15.3 0.3 collective-permute-done.2.refs_7_
  15.6 1.0 %collective-permute-done.3.refs_8_ = bf16[1024,128]{1,0:T(8,128)(2,1)} collective-permute-done((bf16[1024,128]{1,0:T(8,128)(2,1)}, bf16[1024,128]{1,0:T(8,128)(2,1)}, u32[]{:S(2)}, u32[]{:S(2)}) %collective-permute-start.3) | collective-permute-done | bytes 262176 | tf_op jit(solution)/shard_map/ppermute | solution.py:416
  16.6 1.8 %collective-permute-start.4 = (bf16[72,128]{1,0:T(8,128)(2,1)}, bf16[72,128]{1,0:T(8,128)(2,1)S(1)}, u32[]{:S(2)}, u32[]{:S(2)}) collective-permute-start(bf16[72,128]{1,0:T(8,128)(2,1)} %get-tuple-element.41), channel_id=1, source_target_pairs={{0,8},{4,12},{8,0},{12,4},{16,24},{20,28},{24,16},{28,20},{1,9},{5... | collective-permute-start | bytes 55304 | tf_op jit(solution)/shard_map/ppermute | solution.py:416
  18.3 1.6 %collective-permute-start.5 = (bf16[72,128]{1,0:T(8,128)(2,1)}, bf16[72,128]{1,0:T(8,128)(2,1)S(1)}, u32[]{:S(2)}, u32[]{:S(2)}) collective-permute-start(bf16[72,128]{1,0:T(8,128)(2,1)} %get-tuple-element.42), channel_id=1, source_target_pairs={{0,16},{4,20},{8,24},{12,28},{16,0},{20,4},{24,8},{28,12},{1,17},{... | collective-permute-start | bytes 55304 | tf_op jit(solution)/shard_map/ppermute | solution.py:416
  20.0 0.9 %collective-permute-start.6 = (bf16[72,128]{1,0:T(8,128)(2,1)}, bf16[72,128]{1,0:T(8,128)(2,1)S(1)}, u32[]{:S(2)}, u32[]{:S(2)}) collective-permute-start(bf16[72,128]{1,0:T(8,128)(2,1)} %get-tuple-element.43), channel_id=1, source_target_pairs={{0,24},{4,28},{8,16},{12,20},{16,8},{20,12},{24,0},{28,4},{1,25},{... | collective-permute-start | bytes 55304 | tf_op jit(solution)/shard_map/ppermute | solution.py:416
  20.9 2.0 %collective-permute-start.16 = (bf16[128,768]{1,0:T(8,128)(2,1)}, bf16[128,768]{1,0:T(8,128)(2,1)S(1)}, u32[]{:S(2)}, u32[]{:S(2)}) collective-permute-start(bf16[128,768]{1,0:T(8,128)(2,1)} %get-tuple-element.54.refs_8_), channel_id=1, source_target_pairs={{0,24},{4,28},{8,16},{12,20},{16,8},{20,12},{24,0},{28,4},{1,25},{... | collective-permute-start | bytes 589832 | tf_op jit(solution)/shard_map/ppermute | solution.py:416
  22.9 0.4 collective-permute-start.15
  23.3 1.0 %collective-permute-start.14 = (bf16[128,768]{1,0:T(8,128)(2,1)}, bf16[128,768]{1,0:T(8,128)(2,1)S(1)}, u32[]{:S(2)}, u32[]{:S(2)}) collective-permute-start(bf16[128,768]{1,0:T(8,128)(2,1)} %get-tuple-element.54.refs_8_), channel_id=1, source_target_pairs={{0,8},{4,12},{8,0},{12,4},{16,24},{20,28},{24,16},{28,20},{1,9},{5... | collective-permute-start | bytes 589832 | tf_op jit(solution)/shard_map/ppermute | solution.py:416
  24.4 0.8 %collective-permute-done.6.refs_3_ = bf16[72,128]{1,0:T(8,128)(2,1)S(1)} collective-permute-done((bf16[72,128]{1,0:T(8,128)(2,1)}, bf16[72,128]{1,0:T(8,128)(2,1)S(1)}, u32[]{:S(2)}, u32[]{:S(2)}) %collective-permute-start.6) | collective-permute-done | bytes 18464 | tf_op jit(solution)/shard_map/ppermute | solution.py:416
  25.2 0.0 copy-start.8
  25.2 0.7 %copy-done.8 = bf16[72,128]{1,0:T(8,128)(2,1)S(1)} copy-done((bf16[72,128]{1,0:T(8,128)(2,1)S(1)}, bf16[72,128]{1,0:T(8,128)(2,1)}, u32[]{:S(2)}) %copy-start.8) | copy-done | bytes 18456
  25.9 5.2 %conv.1 = (bf16[32,1024]{1,0:T(8,128)(2,1)S(1)}, bf16[32,1024]{1,0:T(8,128)(2,1)S(1)}, bf16[32,1024]{1,0:T(8,128)(2,1)S(1)}, bf16[32,1024]{1,0:T(8,128)(2,1)S(1)...) custom-call(bf16[9,256]{1,0:T(8,128)(2,1)S(1)} %copy-done.4, ...), custom_call_target="tpu_custom_call" | custom-call | flops 2000000000 | bytes 4000000 | tf_op jit(solution)/shard_map/conv/pallas_call | solution.py:453
  31.2 0.0 copy-start.6
  31.2 0.1 collective-permute-start.7
  31.3 1.5 %collective-permute-start.8 = (bf16[32,1024]{1,0:T(8,128)(2,1)S(1)}, bf16[32,1024]{1,0:T(8,128)(2,1)S(1)}, u32[]{:S(2)}, u32[]{:S(2)}) collective-permute-start(bf16[32,1024]{1,0:T(8,128)(2,1)S(1)} %get-tuple-element.48), channel_id=1, source_target_pairs={{0,8},{4,12},{8,0},{12,4},{16,24},{20,28},{24,16},{28,20},{1,9},{5... | collective-permute-start | bytes 196616 | tf_op jit(solution)/shard_map/ppermute | solution.py:423
  32.8 0.3 collective-permute-start.9
  33.1 1.2 %collective-permute-start.10 = (bf16[32,1024]{1,0:T(8,128)(2,1)S(1)}, bf16[32,1024]{1,0:T(8,128)(2,1)S(1)}, u32[]{:S(2)}, u32[]{:S(2)}) collective-permute-start(bf16[32,1024]{1,0:T(8,128)(2,1)S(1)} %get-tuple-element.50), channel_id=1, source_target_pairs={{0,16},{4,20},{8,24},{12,28},{16,0},{20,4},{24,8},{28,12},{1,17},{... | collective-permute-start | bytes 196616 | tf_op jit(solution)/shard_map/ppermute | solution.py:423
  34.4 0.5 collective-permute-start.11
  34.9 1.3 %collective-permute-start.12 = (bf16[32,1024]{1,0:T(8,128)(2,1)S(1)}, bf16[32,1024]{1,0:T(8,128)(2,1)S(1)}, u32[]{:S(2)}, u32[]{:S(2)}) collective-permute-start(bf16[32,1024]{1,0:T(8,128)(2,1)S(1)} %get-tuple-element.52), channel_id=1, source_target_pairs={{0,24},{4,28},{8,16},{12,20},{16,8},{20,12},{24,0},{28,4},{1,25},{... | collective-permute-start | bytes 196616 | tf_op jit(solution)/shard_map/ppermute | solution.py:423
  36.2 1.4 %collective-permute-start.13 = (bf16[32,1024]{1,0:T(8,128)(2,1)S(1)}, bf16[32,1024]{1,0:T(8,128)(2,1)S(1)}, u32[]{:S(2)}, u32[]{:S(2)}) collective-permute-start(bf16[32,1024]{1,0:T(8,128)(2,1)S(1)} %get-tuple-element.53), channel_id=1, source_target_pairs={{0,28},{4,24},{8,20},{12,16},{16,12},{20,8},{24,4},{28,0},{1,29},{... | collective-permute-start | bytes 196616 | tf_op jit(solution)/shard_map/ppermute | solution.py:423
  37.6 0.1 collective-permute-done.10.refs_4_
  37.7 1.0 %collective-permute-done.11.refs_5_ = bf16[32,1024]{1,0:T(8,128)(2,1)S(1)} collective-permute-done((bf16[32,1024]{1,0:T(8,128)(2,1)S(1)}, bf16[32,1024]{1,0:T(8,128)(2,1)S(1)}, u32[]{:S(2)}, u32[]{:S(2)}) %collective-permute-start.11) | collective-permute-done | bytes 65568 | tf_op jit(solution)/shard_map/ppermute | solution.py:423
  38.7 1.8 %collective-permute-done.12.refs_6_ = bf16[32,1024]{1,0:T(8,128)(2,1)S(1)} collective-permute-done((bf16[32,1024]{1,0:T(8,128)(2,1)S(1)}, bf16[32,1024]{1,0:T(8,128)(2,1)S(1)}, u32[]{:S(2)}, u32[]{:S(2)}) %collective-permute-start.12) | collective-permute-done | bytes 65568 | tf_op jit(solution)/shard_map/ppermute | solution.py:423
  40.5 1.0 %collective-permute-done.13.refs_7_ = bf16[32,1024]{1,0:T(8,128)(2,1)S(1)} collective-permute-done((bf16[32,1024]{1,0:T(8,128)(2,1)S(1)}, bf16[32,1024]{1,0:T(8,128)(2,1)S(1)}, u32[]{:S(2)}, u32[]{:S(2)}) %collective-permute-start.13) | collective-permute-done | bytes 65568 | tf_op jit(solution)/shard_map/ppermute | solution.py:423
  41.5 1.5 %layer_norm.1 = (bf16[64,1024]{1,0:T(8,128)(2,1)S(1)}, bf16[64,1024]{1,0:T(8,128)(2,1)S(1)}, bf16[4,128,768]{2,1,0:T(8,128)(2,1)S(1)}) custom-call(bf16[32,1024]{1,0:T(8,128)(2,1)S(1)} %get-tuple-element.46.refs_0_, bf16[32,1024]{1,0:T(8,128)(2,1)S(1)} %collective-permute-done.7.refs_1_, bf16[32,1024]{1,0:T(8,128)(2,1)S(1)} %collective-permute-done.8.refs_2_, ...), custom_call_target="tpu_custom_call" | custom-call | flops 100000000 | bytes 1000000 | tf_op jit(solution)/shard_map/layer_norm/pallas_call | solution.py:476
  43.0 0.2 collective-permute-start.20
  43.1 1.6 %collective-permute-start.21 = (bf16[1024,128]{1,0:T(8,128)(2,1)S(1)}, bf16[1024,128]{1,0:T(8,128)(2,1)S(1)}, u32[]{:S(2)}, u32[]{:S(2)}) collective-permute-start(bf16[1024,128]{1,0:T(8,128)(2,1)S(1)} %copy-done.3), channel_id=1, source_target_pairs={{0,24},{4,28},{8,16},{12,20},{16,8},{20,12},{24,0},{28,4},{1,25},{... | collective-permute-start | bytes 786440 | tf_op jit(solution)/shard_map/ppermute | solution.py:416
  44.7 1.4 %collective-permute-start.19 = (bf16[64,1024]{1,0:T(8,128)(2,1)S(1)}, bf16[64,1024]{1,0:T(8,128)(2,1)S(1)}, u32[]{:S(2)}, u32[]{:S(2)}) collective-permute-start(bf16[64,1024]{1,0:T(8,128)(2,1)S(1)} %get-tuple-element.60.refs_0_), channel_id=1, source_target_pairs={{0,3},{1,2},{2,1},{3,0},{4,7},{5,6},{6,5},{7,4},{8,11},{9,10},{10,... | collective-permute-start | bytes 393224 | tf_op jit(solution)/shard_map/ppermute | solution.py:426
  46.1 0.1 collective-permute-start.18
  46.2 2.9 %collective-permute-start.17 = (bf16[64,1024]{1,0:T(8,128)(2,1)S(1)}, bf16[64,1024]{1,0:T(8,128)(2,1)S(1)}, u32[]{:S(2)}, u32[]{:S(2)}) collective-permute-start(bf16[64,1024]{1,0:T(8,128)(2,1)S(1)} %get-tuple-element.60.refs_0_), channel_id=1, source_target_pairs={{0,1},{1,0},{2,3},{3,2},{4,5},{5,4},{6,7},{7,6},{8,9},{9,8},{10,11... | collective-permute-start | bytes 393224 | tf_op jit(solution)/shard_map/ppermute | solution.py:426
  49.1 1.3 %mask.1 = (bf16[64,1024]{1,0:T(8,128)(2,1)}, f32[4,64]{1,0:T(4,128)S(1)}, f32[64,1]{1,0:T(8,128)S(1)}) custom-call(s32[8]{0:T(128)S(1)} %copy-done.5, s32[8]{0:T(128)S(1)} %copy-done.6, s32[8]{0:T(128)S(1)} %copy-done.7, bf16[64,1024]{1,0:T(8,128)(2,1)S(1)} %get-tuple-element.55.rows_ref), custom_call_target="tpu_custom_call" | custom-call | flops 100000000 | bytes 1000000 | tf_op jit(solution)/shard_map/mask/pallas_call | solution.py:487
  50.4 2.6 %collective-permute-done.19.refs_3_ = bf16[64,1024]{1,0:T(8,128)(2,1)S(1)} collective-permute-done((bf16[64,1024]{1,0:T(8,128)(2,1)S(1)}, bf16[64,1024]{1,0:T(8,128)(2,1)S(1)}, u32[]{:S(2)}, u32[]{:S(2)}) %collective-permute-start.19) | collective-permute-done | bytes 131104 | tf_op jit(solution)/shard_map/ppermute | solution.py:426
  52.9 5.1 %collective-permute-done.18.refs_2_ = bf16[64,1024]{1,0:T(8,128)(2,1)S(1)} collective-permute-done((bf16[64,1024]{1,0:T(8,128)(2,1)S(1)}, bf16[64,1024]{1,0:T(8,128)(2,1)S(1)}, u32[]{:S(2)}, u32[]{:S(2)}) %collective-permute-start.18) | collective-permute-done | bytes 131104 | tf_op jit(solution)/shard_map/ppermute | solution.py:426
  58.1 1.4 %attention.1 = (bf16[64,256]{1,0:T(8,128)(2,1)S(1)}, bf16[64,256]{1,0:T(8,128)(2,1)S(1)}, bf16[64,256]{1,0:T(8,128)(2,1)S(1)}, bf16[64,256]{1,0:T(8,128)(2,1)S(1)}, bf16[4,1024,128]{2,1,0:T(8,128)(2,1)S(1)}) custom-call(f32[4,64]{1,0:T(4,128)S(1)} %get-tuple-element.58.keys_ref, bf16[64,1024]{1,0:T(8,128)(2,1)S(1)} %get-tuple-element.60.refs_0_, ...), custom_call_target="tpu_custom_call" | custom-call | flops 1000000000 | bytes 2000000 | tf_op jit(solution)/shard_map/attention/pallas_call | solution.py:504
  59.4 0.1 collective-permute-start.25
  59.5 0.1 collective-permute-start.22
  59.6 3.0 %collective-permute-start.23 = (bf16[64,256]{1,0:T(8,128)(2,1)S(1)}, bf16[64,256]{1,0:T(8,128)(2,1)S(1)}, u32[]{:S(2)}, u32[]{:S(2)}) collective-permute-start(bf16[64,256]{1,0:T(8,128)(2,1)S(1)} %get-tuple-element.67), channel_id=1, source_target_pairs={{0,2},{1,3},{2,0},{3,1},{4,6},{5,7},{6,4},{7,5},{8,10},{9,11},{10,... | collective-permute-start | bytes 98312 | tf_op jit(solution)/shard_map/ppermute | solution.py:426
  62.6 1.3 %collective-permute-start.24 = (bf16[64,256]{1,0:T(8,128)(2,1)S(1)}, bf16[64,256]{1,0:T(8,128)(2,1)S(1)}, u32[]{:S(2)}, u32[]{:S(2)}) collective-permute-start(bf16[64,256]{1,0:T(8,128)(2,1)S(1)} %get-tuple-element.68), channel_id=1, source_target_pairs={{0,3},{1,2},{2,1},{3,0},{4,7},{5,6},{6,5},{7,4},{8,11},{9,10},{10,... | collective-permute-start | bytes 98312 | tf_op jit(solution)/shard_map/ppermute | solution.py:426
  64.0 0.5 collective-permute-done.23.refs_2_
  64.5 3.8 %collective-permute-done.24.refs_3_ = bf16[64,256]{1,0:T(8,128)(2,1)S(1)} collective-permute-done((bf16[64,256]{1,0:T(8,128)(2,1)S(1)}, bf16[64,256]{1,0:T(8,128)(2,1)S(1)}, u32[]{:S(2)}, u32[]{:S(2)}) %collective-permute-start.24) | collective-permute-done | bytes 32800 | tf_op jit(solution)/shard_map/ppermute | solution.py:426
  68.4 1.1 %output.1 = bf16[64,1024]{1,0:T(8,128)(2,1)} custom-call(f32[64,1]{1,0:T(8,128)S(1)} %get-tuple-element.57.valid_ref, bf16[64,256]{1,0:T(8,128)(2,1)S(1)} %get-tuple-element.65.refs_0_, bf16[64,256]{1,0:T(8,128)(2,1)S(1)} %collective-permute-done.22.refs_1_, bf16[64,256]{1,0:T(8,128)(2,1)S(1)} %collective-permute-done.23.refs_2_, ...), custom_call_target="tpu_custom_call" | custom-call | flops 100000000 | bytes 3000000 | tf_op jit(solution)/shard_map/output/pallas_call | solution.py:523
  (31 shorter events, 0.1 us)
Async XLA Ops:
  0.6 15.9 %collective-permute-start.1 = (bf16[640,1024]{1,0:T(8,128)(2,1)}, bf16[640,1024]{1,0:T(8,128)(2,1)S(1)}, u32[]{:S(2)}, u32[]{:S(2)}) collective-permute-start(bf16[640,1024]{1,0:T(8,128)(2,1)} %refs_4_), channel_id=1, source_target_pairs={{0,4},{4,0},{8,12},{12,8},{16,20},{20,16},{24,28},{28,24},{1,5},{5... | collective-permute-start | bytes 3932168 | tf_op jit(solution)/shard_map/ppermute | solution.py:420
  1.9 23.3 %copy-start.1 = (bf16[640,1024]{1,0:T(8,128)(2,1)S(1)}, bf16[640,1024]{1,0:T(8,128)(2,1)}, u32[]{:S(2)}) copy-start(bf16[640,1024]{1,0:T(8,128)(2,1)} %refs_4_) | copy-start | bytes 3932164
  1.9 23.3 %copy-start.2 = (bf16[2304,256]{1,0:T(8,128)(2,1)S(1)}, bf16[2304,256]{1,0:T(8,128)(2,1)}, u32[]{:S(2)}) copy-start(bf16[2304,256]{1,0:T(8,128)(2,1)} %conv2_ref.1) | copy-start | bytes 3538948
  1.9 23.3 %copy-start.4 = (bf16[9,256]{1,0:T(8,128)(2,1)S(1)}, bf16[9,256]{1,0:T(8,128)(2,1)}, u32[]{:S(2)}) copy-start(bf16[9,256]{1,0:T(8,128)(2,1)} %conv1_ref.1) | copy-start | bytes 13828
  1.9 7.7 %collective-permute-start = (f32[8,1024]{1,0:T(8,128)S(1)}, f32[8,1024]{1,0:T(8,128)S(1)}, u32[]{:S(2)}, u32[]{:S(2)}) collective-permute-start(f32[8,1024]{1,0:T(8,128)S(1)} %slice.3), channel_id=1, source_target_pairs={{0,1},{1,2},{2,3},{3,4},{4,5},{5,6},{6,7},{7,8},{8,9},{9,10},{10,1... | collective-permute-start | bytes 98312 | tf_op jit(solution)/shard_map/ppermute | solution.py:412
  6.6 9.1 %collective-permute-start.2 = (bf16[1024,128]{1,0:T(8,128)(2,1)}, bf16[1024,128]{1,0:T(8,128)(2,1)S(1)}, u32[]{:S(2)}, u32[]{:S(2)}) collective-permute-start(bf16[1024,128]{1,0:T(8,128)(2,1)} %refs_6_), channel_id=1, source_target_pairs={{0,8},{4,12},{8,0},{12,4},{16,24},{20,28},{24,16},{28,20},{1,9},{5... | collective-permute-start | bytes 786440 | tf_op jit(solution)/shard_map/ppermute | solution.py:416
  8.1 8.5 %collective-permute-start.3 = (bf16[1024,128]{1,0:T(8,128)(2,1)}, bf16[1024,128]{1,0:T(8,128)(2,1)}, u32[]{:S(2)}, u32[]{:S(2)}) collective-permute-start(bf16[1024,128]{1,0:T(8,128)(2,1)} %refs_6_), channel_id=1, source_target_pairs={{0,16},{4,20},{8,24},{12,28},{16,0},{20,4},{24,8},{28,12},{1,17},{... | collective-permute-start | bytes 786440 | tf_op jit(solution)/shard_map/ppermute | solution.py:416
  9.6 0.6 copy-start.9
  16.6 6.7 %collective-permute-start.4 = (bf16[72,128]{1,0:T(8,128)(2,1)}, bf16[72,128]{1,0:T(8,128)(2,1)S(1)}, u32[]{:S(2)}, u32[]{:S(2)}) collective-permute-start(bf16[72,128]{1,0:T(8,128)(2,1)} %get-tuple-element.41), channel_id=1, source_target_pairs={{0,8},{4,12},{8,0},{12,4},{16,24},{20,28},{24,16},{28,20},{1,9},{5... | collective-permute-start | bytes 55304 | tf_op jit(solution)/shard_map/ppermute | solution.py:416
  18.3 6.0 %collective-permute-start.5 = (bf16[72,128]{1,0:T(8,128)(2,1)}, bf16[72,128]{1,0:T(8,128)(2,1)S(1)}, u32[]{:S(2)}, u32[]{:S(2)}) collective-permute-start(bf16[72,128]{1,0:T(8,128)(2,1)} %get-tuple-element.42), channel_id=1, source_target_pairs={{0,16},{4,20},{8,24},{12,28},{16,0},{20,4},{24,8},{28,12},{1,17},{... | collective-permute-start | bytes 55304 | tf_op jit(solution)/shard_map/ppermute | solution.py:416
  20.0 5.2 %collective-permute-start.6 = (bf16[72,128]{1,0:T(8,128)(2,1)}, bf16[72,128]{1,0:T(8,128)(2,1)S(1)}, u32[]{:S(2)}, u32[]{:S(2)}) collective-permute-start(bf16[72,128]{1,0:T(8,128)(2,1)} %get-tuple-element.43), channel_id=1, source_target_pairs={{0,24},{4,28},{8,16},{12,20},{16,8},{20,12},{24,0},{28,4},{1,25},{... | collective-permute-start | bytes 55304 | tf_op jit(solution)/shard_map/ppermute | solution.py:416
  20.9 20.6 %copy-start = (bf16[128,768]{1,0:T(8,128)(2,1)S(1)}, bf16[128,768]{1,0:T(8,128)(2,1)}, u32[]{:S(2)}) copy-start(bf16[128,768]{1,0:T(8,128)(2,1)} %get-tuple-element.54.refs_8_) | copy-start | bytes 589828
  20.9 12.0 %collective-permute-start.16 = (bf16[128,768]{1,0:T(8,128)(2,1)}, bf16[128,768]{1,0:T(8,128)(2,1)S(1)}, u32[]{:S(2)}, u32[]{:S(2)}) collective-permute-start(bf16[128,768]{1,0:T(8,128)(2,1)} %get-tuple-element.54.refs_8_), channel_id=1, source_target_pairs={{0,24},{4,28},{8,16},{12,20},{16,8},{20,12},{24,0},{28,4},{1,25},{... | collective-permute-start | bytes 589832 | tf_op jit(solution)/shard_map/ppermute | solution.py:416
  22.9 10.3 %collective-permute-start.15 = (bf16[128,768]{1,0:T(8,128)(2,1)}, bf16[128,768]{1,0:T(8,128)(2,1)S(1)}, u32[]{:S(2)}, u32[]{:S(2)}) collective-permute-start(bf16[128,768]{1,0:T(8,128)(2,1)} %get-tuple-element.54.refs_8_), channel_id=1, source_target_pairs={{0,16},{4,20},{8,24},{12,28},{16,0},{20,4},{24,8},{28,12},{1,17},{... | collective-permute-start | bytes 589832 | tf_op jit(solution)/shard_map/ppermute | solution.py:416
  23.3 11.1 %collective-permute-start.14 = (bf16[128,768]{1,0:T(8,128)(2,1)}, bf16[128,768]{1,0:T(8,128)(2,1)S(1)}, u32[]{:S(2)}, u32[]{:S(2)}) collective-permute-start(bf16[128,768]{1,0:T(8,128)(2,1)} %get-tuple-element.54.refs_8_), channel_id=1, source_target_pairs={{0,8},{4,12},{8,0},{12,4},{16,24},{20,28},{24,16},{28,20},{1,9},{5... | collective-permute-start | bytes 589832 | tf_op jit(solution)/shard_map/ppermute | solution.py:416
  25.2 0.7 %copy-start.8 = (bf16[72,128]{1,0:T(8,128)(2,1)S(1)}, bf16[72,128]{1,0:T(8,128)(2,1)}, u32[]{:S(2)}) copy-start(bf16[72,128]{1,0:T(8,128)(2,1)} %get-tuple-element.40.refs_0_) | copy-start | bytes 55300
  31.2 12.0 %copy-start.3 = (bf16[1024,128]{1,0:T(8,128)(2,1)S(1)}, bf16[1024,128]{1,0:T(8,128)(2,1)}, u32[]{:S(2)}) copy-start(bf16[1024,128]{1,0:T(8,128)(2,1)} %refs_6_) | copy-start | bytes 786436
  31.2 17.9 %copy-start.5 = (s32[8]{0:T(128)S(1)}, s32[8]{0:T(128)}, u32[]{:S(2)}) copy-start(s32[8]{0:T(128)} %slots_ref.3) | copy-start | bytes 100
  31.2 17.9 %copy-start.6 = (s32[8]{0:T(128)S(1)}, s32[8]{0:T(128)}, u32[]{:S(2)}) copy-start(s32[8]{0:T(128)} %starts_ref.1) | copy-start | bytes 100
  31.2 17.9 %copy-start.7 = (s32[8]{0:T(128)S(1)}, s32[8]{0:T(128)}, u32[]{:S(2)}) copy-start(s32[8]{0:T(128)} %lengths_ref.1) | copy-start | bytes 100
  31.2 3.7 %collective-permute-start.7 = (bf16[32,1024]{1,0:T(8,128)(2,1)S(1)}, bf16[32,1024]{1,0:T(8,128)(2,1)S(1)}, u32[]{:S(2)}, u32[]{:S(2)}) collective-permute-start(bf16[32,1024]{1,0:T(8,128)(2,1)S(1)} %get-tuple-element.47), channel_id=1, source_target_pairs={{0,4},{4,0},{8,12},{12,8},{16,20},{20,16},{24,28},{28,24},{1,5},{5... | collective-permute-start | bytes 196616 | tf_op jit(solution)/shard_map/ppermute | solution.py:423
  31.3 4.9 %collective-permute-start.8 = (bf16[32,1024]{1,0:T(8,128)(2,1)S(1)}, bf16[32,1024]{1,0:T(8,128)(2,1)S(1)}, u32[]{:S(2)}, u32[]{:S(2)}) collective-permute-start(bf16[32,1024]{1,0:T(8,128)(2,1)S(1)} %get-tuple-element.48), channel_id=1, source_target_pairs={{0,8},{4,12},{8,0},{12,4},{16,24},{20,28},{24,16},{28,20},{1,9},{5... | collective-permute-start | bytes 196616 | tf_op jit(solution)/shard_map/ppermute | solution.py:423
  32.8 4.7 %collective-permute-start.9 = (bf16[32,1024]{1,0:T(8,128)(2,1)S(1)}, bf16[32,1024]{1,0:T(8,128)(2,1)S(1)}, u32[]{:S(2)}, u32[]{:S(2)}) collective-permute-start(bf16[32,1024]{1,0:T(8,128)(2,1)S(1)} %get-tuple-element.49), channel_id=1, source_target_pairs={{0,12},{4,8},{8,4},{12,0},{16,28},{20,24},{24,20},{28,16},{1,13},{... | collective-permute-start | bytes 196616 | tf_op jit(solution)/shard_map/ppermute | solution.py:423
  33.1 4.5 %collective-permute-start.10 = (bf16[32,1024]{1,0:T(8,128)(2,1)S(1)}, bf16[32,1024]{1,0:T(8,128)(2,1)S(1)}, u32[]{:S(2)}, u32[]{:S(2)}) collective-permute-start(bf16[32,1024]{1,0:T(8,128)(2,1)S(1)} %get-tuple-element.50), channel_id=1, source_target_pairs={{0,16},{4,20},{8,24},{12,28},{16,0},{20,4},{24,8},{28,12},{1,17},{... | collective-permute-start | bytes 196616 | tf_op jit(solution)/shard_map/ppermute | solution.py:423
  34.4 4.3 %collective-permute-start.11 = (bf16[32,1024]{1,0:T(8,128)(2,1)S(1)}, bf16[32,1024]{1,0:T(8,128)(2,1)S(1)}, u32[]{:S(2)}, u32[]{:S(2)}) collective-permute-start(bf16[32,1024]{1,0:T(8,128)(2,1)S(1)} %get-tuple-element.51), channel_id=1, source_target_pairs={{0,20},{4,16},{8,28},{12,24},{16,4},{20,0},{24,12},{28,8},{1,21},{... | collective-permute-start | bytes 196616 | tf_op jit(solution)/shard_map/ppermute | solution.py:423
  34.9 5.6 %collective-permute-start.12 = (bf16[32,1024]{1,0:T(8,128)(2,1)S(1)}, bf16[32,1024]{1,0:T(8,128)(2,1)S(1)}, u32[]{:S(2)}, u32[]{:S(2)}) collective-permute-start(bf16[32,1024]{1,0:T(8,128)(2,1)S(1)} %get-tuple-element.52), channel_id=1, source_target_pairs={{0,24},{4,28},{8,16},{12,20},{16,8},{20,12},{24,0},{28,4},{1,25},{... | collective-permute-start | bytes 196616 | tf_op jit(solution)/shard_map/ppermute | solution.py:423
  36.2 5.3 %collective-permute-start.13 = (bf16[32,1024]{1,0:T(8,128)(2,1)S(1)}, bf16[32,1024]{1,0:T(8,128)(2,1)S(1)}, u32[]{:S(2)}, u32[]{:S(2)}) collective-permute-start(bf16[32,1024]{1,0:T(8,128)(2,1)S(1)} %get-tuple-element.53), channel_id=1, source_target_pairs={{0,28},{4,24},{8,20},{12,16},{16,12},{20,8},{24,4},{28,0},{1,29},{... | collective-permute-start | bytes 196616 | tf_op jit(solution)/shard_map/ppermute | solution.py:423
  43.0 15.1 %collective-permute-start.20 = (bf16[4,128,768]{2,1,0:T(8,128)(2,1)S(1)}, bf16[4,128,768]{2,1,0:T(8,128)(2,1)S(1)}, u32[]{:S(2)}, u32[]{:S(2)}) collective-permute-start(bf16[4,128,768]{2,1,0:T(8,128)(2,1)S(1)} %get-tuple-element.61.refs_4_), channel_id=1, source_target_pairs={{0,4},{4,0},{8,12},{12,8},{16,20},{20,16},{24,28},{28,24},{1,5},{5... | collective-permute-start | bytes 2359304 | tf_op jit(solution)/shard_map/ppermute | solution.py:420
  43.1 14.9 %collective-permute-start.21 = (bf16[1024,128]{1,0:T(8,128)(2,1)S(1)}, bf16[1024,128]{1,0:T(8,128)(2,1)S(1)}, u32[]{:S(2)}, u32[]{:S(2)}) collective-permute-start(bf16[1024,128]{1,0:T(8,128)(2,1)S(1)} %copy-done.3), channel_id=1, source_target_pairs={{0,24},{4,28},{8,16},{12,20},{16,8},{20,12},{24,0},{28,4},{1,25},{... | collective-permute-start | bytes 786440 | tf_op jit(solution)/shard_map/ppermute | solution.py:416
  44.7 8.2 %collective-permute-start.19 = (bf16[64,1024]{1,0:T(8,128)(2,1)S(1)}, bf16[64,1024]{1,0:T(8,128)(2,1)S(1)}, u32[]{:S(2)}, u32[]{:S(2)}) collective-permute-start(bf16[64,1024]{1,0:T(8,128)(2,1)S(1)} %get-tuple-element.60.refs_0_), channel_id=1, source_target_pairs={{0,3},{1,2},{2,1},{3,0},{4,7},{5,6},{6,5},{7,4},{8,11},{9,10},{10,... | collective-permute-start | bytes 393224 | tf_op jit(solution)/shard_map/ppermute | solution.py:426
  46.1 12.0 %collective-permute-start.18 = (bf16[64,1024]{1,0:T(8,128)(2,1)S(1)}, bf16[64,1024]{1,0:T(8,128)(2,1)S(1)}, u32[]{:S(2)}, u32[]{:S(2)}) collective-permute-start(bf16[64,1024]{1,0:T(8,128)(2,1)S(1)} %get-tuple-element.60.refs_0_), channel_id=1, source_target_pairs={{0,2},{1,3},{2,0},{3,1},{4,6},{5,7},{6,4},{7,5},{8,10},{9,11},{10,... | collective-permute-start | bytes 393224 | tf_op jit(solution)/shard_map/ppermute | solution.py:426
  46.2 11.9 %collective-permute-start.17 = (bf16[64,1024]{1,0:T(8,128)(2,1)S(1)}, bf16[64,1024]{1,0:T(8,128)(2,1)S(1)}, u32[]{:S(2)}, u32[]{:S(2)}) collective-permute-start(bf16[64,1024]{1,0:T(8,128)(2,1)S(1)} %get-tuple-element.60.refs_0_), channel_id=1, source_target_pairs={{0,1},{1,0},{2,3},{3,2},{4,5},{5,4},{6,7},{7,6},{8,9},{9,8},{10,11... | collective-permute-start | bytes 393224 | tf_op jit(solution)/shard_map/ppermute | solution.py:426
  59.4 8.9 %collective-permute-start.25 = (bf16[4,1024,128]{2,1,0:T(8,128)(2,1)S(1)}, bf16[4,1024,128]{2,1,0:T(8,128)(2,1)S(1)}, u32[]{:S(2)}, u32[]{:S(2)}) collective-permute-start(bf16[4,1024,128]{2,1,0:T(8,128)(2,1)S(1)} %get-tuple-element.69.refs_4_), channel_id=1, source_target_pairs={{0,4},{4,0},{8,12},{12,8},{16,20},{20,16},{24,28},{28,24},{1,5},{5... | collective-permute-start | bytes 3145736 | tf_op jit(solution)/shard_map/ppermute | solution.py:420
  59.5 4.5 %collective-permute-start.22 = (bf16[64,256]{1,0:T(8,128)(2,1)S(1)}, bf16[64,256]{1,0:T(8,128)(2,1)S(1)}, u32[]{:S(2)}, u32[]{:S(2)}) collective-permute-start(bf16[64,256]{1,0:T(8,128)(2,1)S(1)} %get-tuple-element.66), channel_id=1, source_target_pairs={{0,1},{1,0},{2,3},{3,2},{4,5},{5,4},{6,7},{7,6},{8,9},{9,8},{10,11... | collective-permute-start | bytes 98312 | tf_op jit(solution)/shard_map/ppermute | solution.py:426
  59.6 4.9 %collective-permute-start.23 = (bf16[64,256]{1,0:T(8,128)(2,1)S(1)}, bf16[64,256]{1,0:T(8,128)(2,1)S(1)}, u32[]{:S(2)}, u32[]{:S(2)}) collective-permute-start(bf16[64,256]{1,0:T(8,128)(2,1)S(1)} %get-tuple-element.67), channel_id=1, source_target_pairs={{0,2},{1,3},{2,0},{3,1},{4,6},{5,7},{6,4},{7,5},{8,10},{9,11},{10,... | collective-permute-start | bytes 98312 | tf_op jit(solution)/shard_map/ppermute | solution.py:426
  62.6 5.7 %collective-permute-start.24 = (bf16[64,256]{1,0:T(8,128)(2,1)S(1)}, bf16[64,256]{1,0:T(8,128)(2,1)S(1)}, u32[]{:S(2)}, u32[]{:S(2)}) collective-permute-start(bf16[64,256]{1,0:T(8,128)(2,1)S(1)} %get-tuple-element.68), channel_id=1, source_target_pairs={{0,3},{1,2},{2,1},{3,0},{4,7},{5,6},{6,5},{7,4},{8,11},{9,10},{10,... | collective-permute-start | bytes 98312 | tf_op jit(solution)/shard_map/ppermute | solution.py:426

commit v5 on v4

--- a/solution.py
+++ b/solution.py
@@ -147,8 +147,10 @@
         ).astype(BF16)
 
 
-def mel_kernel(parts, group, slots_ref, rim_ref, audio_ref, table_ref, qkv_ref, *refs):
-    outs_refs, (mix_out, ext, table, blocks, sems) = refs[:parts], refs[parts:]
+def mel_kernel(parts, group, slots_here, rim_ref, audio_ref, table_ref, qkv_ref, *refs):
+    outs_refs, (mix_out, ext, table, blocks, slots_ref, sems) = refs[:parts], refs[parts:]
+    load_slots = pltpu.make_async_copy(slots_here, slots_ref, sems.at[5])
+    load_slots.start()
     load_audio = pltpu.make_async_copy(audio_ref, ext.at[:, pl.ds(RIM, audio_ref.shape[1])], sems.at[3])
     load_table = pltpu.make_async_copy(table_ref, table, sems.at[4])
     load_audio.start()
@@ -158,12 +160,6 @@
     streams = audio_ref.shape[0]
     rows = JS * streams
     ext[:, :RIM] = rim_ref[...]
-    column = iota(1, rows, 1)
-    early = quotient(column, streams, JS)
-    target = jnp.zeros((1, rows), jnp.int32)
-    for u in range(streams):
-        target = jnp.where(column - early * streams == u, early * streams + slots_ref[u], target)
-    routing = (target == iota(rows, rows, 0)).astype(F32).astype(BF16)
     load_audio.wait()
     phases = []
     for phase in range(4):
@@ -187,6 +183,13 @@
     mel_power = jnp.dot(
         power, table[:half, N_FFT:], precision=lax.Precision.HIGHEST, preferred_element_type=F32
     )
+    load_slots.wait()
+    column = iota(1, rows, 1)
+    early = quotient(column, streams, JS)
+    target = jnp.zeros((1, rows), jnp.int32)
+    for u in range(streams):
+        target = jnp.where(column - early * streams == u, early * streams + slots_ref[u], target)
+    routing = (target == iota(rows, rows, 0)).astype(F32).astype(BF16)
     log_mel = jnp.log(mel_power + EPS_LOG)
     share = BANDS // parts
     width = 4 * share + 4
@@ -290,7 +293,7 @@
     _, copy_index = place(parts)
     windows = lax.axis_size("dp")
     copies = windows // parts
-    part_refs, refs = refs[:windows], refs[windows:]
+    part_refs, refs = refs[:windows][::-1], refs[windows:]
     piece_refs, refs = refs[:parts], refs[parts:]
     rows_out, normed_out, stack_out, encoded, sems = refs
     moves = stacked(parts, piece_refs, stack_out, sems, 0)
@@ -432,13 +435,14 @@
     *mel_all, mix = pl.pallas_call(
         functools.partial(mel_kernel, parts, group),
         out_shape=tuple([jax.ShapeDtypeStruct((rows, LANES), BF16)] * parts + [mix_piece]),
-        in_specs=[smem(), vmem()] + [anywhere()] * 3,
+        in_specs=[anywhere(), vmem()] + [anywhere()] * 3,
         out_specs=tuple([vmem()] * (parts + 1)),
         scratch_shapes=[
             pltpu.VMEM((streams, RIM + audio.shape[1]), F32),
             pltpu.VMEM(table.shape, F32),
             pltpu.VMEM((parts, rows, LANES), BF16),
-            pltpu.SemaphoreType.DMA((5,)),
+            pltpu.SMEM((streams,), jnp.int32),
+            pltpu.SemaphoreType.DMA((6,)),
         ],
         compiler_params=params(60),
         cost_estimate=cost(1e10, 2e6),
@@ -471,7 +475,7 @@
         cost_estimate=cost(2e9, 4e6),
         name="conv",
     )(conv1_weight, conv2_weight, *mel_all, *proj_all)
-    partials = [partials[0]] + [to_window(partials[step], step) for step in range(1, windows)]
+    partials = [to_window(partials[step], step) for step in reversed(range(1, windows))] + [partials[0]]
 
     ordered, normed, stack = pl.pallas_call(
         functools.partial(norm_kernel, parts),
@@ -498,7 +502,10 @@
         name="mask",
     )(slots, starts, lengths, ordered)
     normed, out_here = lax.optimization_barrier((normed, out_weight))
-    normed = [normed] + [to_plane(normed, step) for step in range(1, group)]
+    normed = [normed]
+    for step in range(1, group):
+        high = 1 << (step.bit_length() - 1)
+        normed.append(to_plane(normed[high] if step > high else normed[0], step - high if step > high else high))
     out_all = [out_here] + near + [to_part(out_here, parts - 1)]
 
     *context, stack = pl.pallas_call(

time: 69.8 us -> 67.9 us (0.973)
  starting transfers between devices: 33 us -> 29.6 us
  waiting for transfers between devices: 18.1 us -> 19.5 us
    ppermute x6, starting transfers between devices: 8.83 us -> 5.67 us  [to_plane(): return lax.ppermute(block, 'seq', [(i, i ^ step) for i in range(group)])]
    ppermute x6, waiting for transfers between devices: 12.1 us -> 13.2 us  [to_plane(): return lax.ppermute(block, 'seq', [(i, i ^ step) for i in range(group)])]
  transfers between devices with their start and end apart: 26 -> 26, of which waited for: 11 -> 12; matrix products, arithmetic and copies ran while one was open for 1% -> 1% of each run, Pallas kernels for 17% -> 17%
where the time goes in v5:
time: 67.9 us; the launch traced here: 67.5 us
  starting transfers between devices  29.6 us (44%)
  waiting for transfers between devices  19.5 us (29%)
  Pallas kernels  15.6 us (23%)
  local copies, waits for them, and re-layouts  2.13 us (3%)
  between operations  0.77 us (1%)
    ppermute x6, waiting for transfers between devices, to_plane(): return lax.ppermute(block, 'seq', [(i, i ^ step) for i in range(group)])  13.2 us
    ppermute x9, starting transfers between devices, to_part(): return lax.ppermute(block, 'dp', pairs)  12.5 us
    ppermute x7, starting transfers between devices, to_window(): return lax.ppermute(block, 'dp', [(i, i ^ step) for i in range(windows)])  6.04 us
    ppermute x6, starting transfers between devices, to_plane(): return lax.ppermute(block, 'seq', [(i, i ^ step) for i in range(group)])  5.67 us
    pallas_call x1, Pallas kernels, on_device(): pl.pallas_call(functools.partial(conv_kernel, parts, width), out_shape=tu...  5.24 us
    pallas_call x1, Pallas kernels, on_device(): pl.pallas_call(functools.partial(mel_kernel, parts, group), out_shape=tup...  5.15 us
    ppermute x1, starting transfers between devices, on_device(): rim = lax.ppermute(audio[:, audio.shape[1] - RIM:], ('dp', 'seq'), route)  4.63 us
    ppermute x7, waiting for transfers between devices, to_window(): return lax.ppermute(block, 'dp', [(i, i ^ step) for i in range(windows)])  4.21 us
  transfers between devices with their start and end apart: 26, of which 12 were waited for; matrix products, arithmetic and copies ran while one was open for 1% of the time, Pallas kernels for 17%

profile of v5, /device:TPU:0, one launch (start us, length us, event | category | flops | bytes accessed | tf_op | source)
XLA Modules:
  0.0 67.5 jit_solution(1330012374949219057)
XLA Ops:
  0.6 0.5 collective-permute-start.1
  1.1 0.8 %slice.3 = f32[8,1024]{1,0:T(8,128)S(1)} slice(f32[8,5120]{1,0:T(8,128)} %audio_ref.1), slice={[0:8], [4096:5120]} | slice | bytes 65536 | tf_op jit(solution)/shard_map/slice | solution.py:415
  1.9 4.6 %collective-permute-start = (f32[8,1024]{1,0:T(8,128)S(1)}, f32[8,1024]{1,0:T(8,128)S(1)}, u32[]{:S(2)}, u32[]{:S(2)}) collective-permute-start(f32[8,1024]{1,0:T(8,128)S(1)} %slice.3), channel_id=1, source_target_pairs={{0,1},{1,2},{2,3},{3,4},{4,5},{5,6},{6,7},{7,8},{8,9},{9,10},{10,1... | collective-permute-start | bytes 98312 | tf_op jit(solution)/shard_map/ppermute | solution.py:415
  6.6 1.6 %collective-permute-start.2 = (bf16[1024,128]{1,0:T(8,128)(2,1)}, bf16[1024,128]{1,0:T(8,128)(2,1)S(1)}, u32[]{:S(2)}, u32[]{:S(2)}) collective-permute-start(bf16[1024,128]{1,0:T(8,128)(2,1)} %refs_6_), channel_id=1, source_target_pairs={{0,8},{4,12},{8,0},{12,4},{16,24},{20,28},{24,16},{28,20},{1,9},{5... | collective-permute-start | bytes 786440 | tf_op jit(solution)/shard_map/ppermute | solution.py:419
  8.1 1.5 %collective-permute-start.3 = (bf16[1024,128]{1,0:T(8,128)(2,1)}, bf16[1024,128]{1,0:T(8,128)(2,1)}, u32[]{:S(2)}, u32[]{:S(2)}) collective-permute-start(bf16[1024,128]{1,0:T(8,128)(2,1)} %refs_6_), channel_id=1, source_target_pairs={{0,16},{4,20},{8,24},{12,28},{16,0},{20,4},{24,8},{28,12},{1,17},{... | collective-permute-start | bytes 786440 | tf_op jit(solution)/shard_map/ppermute | solution.py:419
  9.6 0.6 copy-done.9
  10.2 5.1 %log_mel.1 = (bf16[72,128]{1,0:T(8,128)(2,1)}, bf16[72,128]{1,0:T(8,128)(2,1)}, bf16[72,128]{1,0:T(8,128)(2,1)}, bf16[72,128]{1,0:T(8,128)(2,1)}, bf16[128,768]{1,0:T(8,128)(2,1)}) custom-call(s32[8]{0:T(128)} %slots_ref.1, f32[8,1024]{1,0:T(8,128)} %copy-done.9, f32[8,5120]{1,0:T(8,128)} %audio_ref.1, f32[512,640]{1,0:T(8,128)} %constant.2.clone.table_ref, ...), custom_call_target="tpu_custom_call" | custom-call | flops 10000000000 | bytes 2000000 | tf_op jit(solution)/shard_map/log_mel/pallas_call | solution.py:435
  15.4 0.2 collective-permute-done.2.refs_7_
  15.6 1.0 %collective-permute-done.3.refs_8_ = bf16[1024,128]{1,0:T(8,128)(2,1)} collective-permute-done((bf16[1024,128]{1,0:T(8,128)(2,1)}, bf16[1024,128]{1,0:T(8,128)(2,1)}, u32[]{:S(2)}, u32[]{:S(2)}) %collective-permute-start.3) | collective-permute-done | bytes 262176 | tf_op jit(solution)/shard_map/ppermute | solution.py:419
  16.6 1.9 %collective-permute-start.4 = (bf16[72,128]{1,0:T(8,128)(2,1)}, bf16[72,128]{1,0:T(8,128)(2,1)S(1)}, u32[]{:S(2)}, u32[]{:S(2)}) collective-permute-start(bf16[72,128]{1,0:T(8,128)(2,1)} %get-tuple-element.41), channel_id=1, source_target_pairs={{0,8},{4,12},{8,0},{12,4},{16,24},{20,28},{24,16},{28,20},{1,9},{5... | collective-permute-start | bytes 55304 | tf_op jit(solution)/shard_map/ppermute | solution.py:419
  18.5 1.6 %collective-permute-start.5 = (bf16[72,128]{1,0:T(8,128)(2,1)}, bf16[72,128]{1,0:T(8,128)(2,1)S(1)}, u32[]{:S(2)}, u32[]{:S(2)}) collective-permute-start(bf16[72,128]{1,0:T(8,128)(2,1)} %get-tuple-element.42), channel_id=1, source_target_pairs={{0,16},{4,20},{8,24},{12,28},{16,0},{20,4},{24,8},{28,12},{1,17},{... | collective-permute-start | bytes 55304 | tf_op jit(solution)/shard_map/ppermute | solution.py:419
  20.1 0.9 %collective-permute-start.6 = (bf16[72,128]{1,0:T(8,128)(2,1)}, bf16[72,128]{1,0:T(8,128)(2,1)S(1)}, u32[]{:S(2)}, u32[]{:S(2)}) collective-permute-start(bf16[72,128]{1,0:T(8,128)(2,1)} %get-tuple-element.43), channel_id=1, source_target_pairs={{0,24},{4,28},{8,16},{12,20},{16,8},{20,12},{24,0},{28,4},{1,25},{... | collective-permute-start | bytes 55304 | tf_op jit(solution)/shard_map/ppermute | solution.py:419
  21.0 2.0 %collective-permute-start.16 = (bf16[128,768]{1,0:T(8,128)(2,1)}, bf16[128,768]{1,0:T(8,128)(2,1)S(1)}, u32[]{:S(2)}, u32[]{:S(2)}) collective-permute-start(bf16[128,768]{1,0:T(8,128)(2,1)} %get-tuple-element.54.refs_8_), channel_id=1, source_target_pairs={{0,24},{4,28},{8,16},{12,20},{16,8},{20,12},{24,0},{28,4},{1,25},{... | collective-permute-start | bytes 589832 | tf_op jit(solution)/shard_map/ppermute | solution.py:419
  23.0 0.4 collective-permute-start.15
  23.4 1.0 %collective-permute-start.14 = (bf16[128,768]{1,0:T(8,128)(2,1)}, bf16[128,768]{1,0:T(8,128)(2,1)S(1)}, u32[]{:S(2)}, u32[]{:S(2)}) collective-permute-start(bf16[128,768]{1,0:T(8,128)(2,1)} %get-tuple-element.54.refs_8_), channel_id=1, source_target_pairs={{0,8},{4,12},{8,0},{12,4},{16,24},{20,28},{24,16},{28,20},{1,9},{5... | collective-permute-start | bytes 589832 | tf_op jit(solution)/shard_map/ppermute | solution.py:419
  24.5 0.8 %collective-permute-done.6.refs_3_ = bf16[72,128]{1,0:T(8,128)(2,1)S(1)} collective-permute-done((bf16[72,128]{1,0:T(8,128)(2,1)}, bf16[72,128]{1,0:T(8,128)(2,1)S(1)}, u32[]{:S(2)}, u32[]{:S(2)}) %collective-permute-start.6) | collective-permute-done | bytes 18464 | tf_op jit(solution)/shard_map/ppermute | solution.py:419
  25.3 0.0 copy-start.8
  25.3 0.7 %copy-done.8 = bf16[72,128]{1,0:T(8,128)(2,1)S(1)} copy-done((bf16[72,128]{1,0:T(8,128)(2,1)S(1)}, bf16[72,128]{1,0:T(8,128)(2,1)}, u32[]{:S(2)}) %copy-start.8) | copy-done | bytes 18456
  26.0 5.2 %conv.1 = (bf16[32,1024]{1,0:T(8,128)(2,1)S(1)}, bf16[32,1024]{1,0:T(8,128)(2,1)S(1)}, bf16[32,1024]{1,0:T(8,128)(2,1)S(1)}, bf16[32,1024]{1,0:T(8,128)(2,1)S(1)...) custom-call(bf16[9,256]{1,0:T(8,128)(2,1)S(1)} %copy-done.4, ...), custom_call_target="tpu_custom_call" | custom-call | flops 2000000000 | bytes 4000000 | tf_op jit(solution)/shard_map/conv/pallas_call | solution.py:457
  31.3 0.0 copy-start.6
  31.3 0.0 copy-start.7
  31.3 0.1 collective-permute-start.7
  31.4 1.3 %collective-permute-start.8 = (bf16[32,1024]{1,0:T(8,128)(2,1)S(1)}, bf16[32,1024]{1,0:T(8,128)(2,1)S(1)}, u32[]{:S(2)}, u32[]{:S(2)}) collective-permute-start(bf16[32,1024]{1,0:T(8,128)(2,1)S(1)} %get-tuple-element.47), channel_id=1, source_target_pairs={{0,24},{4,28},{8,16},{12,20},{16,8},{20,12},{24,0},{28,4},{1,25},{... | collective-permute-start | bytes 196616 | tf_op jit(solution)/shard_map/ppermute | solution.py:426
  32.7 2.3 %collective-permute-start.9 = (bf16[32,1024]{1,0:T(8,128)(2,1)S(1)}, bf16[32,1024]{1,0:T(8,128)(2,1)S(1)}, u32[]{:S(2)}, u32[]{:S(2)}) collective-permute-start(bf16[32,1024]{1,0:T(8,128)(2,1)S(1)} %get-tuple-element.48), channel_id=1, source_target_pairs={{0,20},{4,16},{8,28},{12,24},{16,4},{20,0},{24,12},{28,8},{1,21},{... | collective-permute-start | bytes 196616 | tf_op jit(solution)/shard_map/ppermute | solution.py:426
  35.0 0.8 %collective-permute-start.10 = (bf16[32,1024]{1,0:T(8,128)(2,1)S(1)}, bf16[32,1024]{1,0:T(8,128)(2,1)S(1)}, u32[]{:S(2)}, u32[]{:S(2)}) collective-permute-start(bf16[32,1024]{1,0:T(8,128)(2,1)S(1)} %get-tuple-element.49), channel_id=1, source_target_pairs={{0,16},{4,20},{8,24},{12,28},{16,0},{20,4},{24,8},{28,12},{1,17},{... | collective-permute-start | bytes 196616 | tf_op jit(solution)/shard_map/ppermute | solution.py:426
  35.8 0.3 collective-permute-done.7.refs_0_
  36.1 1.5 %collective-permute-start.12 = (bf16[32,1024]{1,0:T(8,128)(2,1)S(1)}, bf16[32,1024]{1,0:T(8,128)(2,1)S(1)}, u32[]{:S(2)}, u32[]{:S(2)}) collective-permute-start(bf16[32,1024]{1,0:T(8,128)(2,1)S(1)} %get-tuple-element.51), channel_id=1, source_target_pairs={{0,8},{4,12},{8,0},{12,4},{16,24},{20,28},{24,16},{28,20},{1,9},{5... | collective-permute-start | bytes 196616 | tf_op jit(solution)/shard_map/ppermute | solution.py:426
  37.6 0.1 collective-permute-start.13
  37.7 1.0 %collective-permute-done.9.refs_2_ = bf16[32,1024]{1,0:T(8,128)(2,1)S(1)} collective-permute-done((bf16[32,1024]{1,0:T(8,128)(2,1)S(1)}, bf16[32,1024]{1,0:T(8,128)(2,1)S(1)}, u32[]{:S(2)}, u32[]{:S(2)}) %collective-permute-start.9) | collective-permute-done | bytes 65568 | tf_op jit(solution)/shard_map/ppermute | solution.py:426
  38.7 1.5 %collective-permute-done.10.refs_3_ = bf16[32,1024]{1,0:T(8,128)(2,1)S(1)} collective-permute-done((bf16[32,1024]{1,0:T(8,128)(2,1)S(1)}, bf16[32,1024]{1,0:T(8,128)(2,1)S(1)}, u32[]{:S(2)}, u32[]{:S(2)}) %collective-permute-start.10) | collective-permute-done | bytes 65568 | tf_op jit(solution)/shard_map/ppermute | solution.py:426
  40.2 1.4 %collective-permute-done.12.refs_5_ = bf16[32,1024]{1,0:T(8,128)(2,1)S(1)} collective-permute-done((bf16[32,1024]{1,0:T(8,128)(2,1)S(1)}, bf16[32,1024]{1,0:T(8,128)(2,1)S(1)}, u32[]{:S(2)}, u32[]{:S(2)}) %collective-permute-start.12) | collective-permute-done | bytes 65568 | tf_op jit(solution)/shard_map/ppermute | solution.py:426
  41.6 1.5 %layer_norm.1 = (bf16[64,1024]{1,0:T(8,128)(2,1)S(1)}, bf16[64,1024]{1,0:T(8,128)(2,1)S(1)}, bf16[4,128,768]{2,1,0:T(8,128)(2,1)S(1)}) custom-call(bf16[32,1024]{1,0:T(8,128)(2,1)S(1)} %collective-permute-done.7.refs_0_, bf16[32,1024]{1,0:T(8,128)(2,1)S(1)} %collective-permute-done.8.refs_1_, bf16[32,1024]{1,0:T(8,128)(2,1)S(1)} %collective-permute-done.9.refs_2_, ...), custom_call_target="tpu_custom_call" | custom-call | flops 100000000 | bytes 1000000 | tf_op jit(solution)/shard_map/layer_norm/pallas_call | solution.py:480
  43.1 0.2 collective-permute-start.20
  43.2 0.8 %collective-permute-start.18 = (bf16[64,1024]{1,0:T(8,128)(2,1)S(1)}, bf16[64,1024]{1,0:T(8,128)(2,1)S(1)}, u32[]{:S(2)}, u32[]{:S(2)}) collective-permute-start(bf16[64,1024]{1,0:T(8,128)(2,1)S(1)} %get-tuple-element.60.refs_0_), channel_id=1, source_target_pairs={{0,2},{1,3},{2,0},{3,1},{4,6},{5,7},{6,4},{7,5},{8,10},{9,11},{10,... | collective-permute-start | bytes 393224 | tf_op jit(solution)/shard_map/ppermute | solution.py:429
  44.1 1.5 %collective-permute-start.21 = (bf16[1024,128]{1,0:T(8,128)(2,1)S(1)}, bf16[1024,128]{1,0:T(8,128)(2,1)S(1)}, u32[]{:S(2)}, u32[]{:S(2)}) collective-permute-start(bf16[1024,128]{1,0:T(8,128)(2,1)S(1)} %copy-done.3), channel_id=1, source_target_pairs={{0,24},{4,28},{8,16},{12,20},{16,8},{20,12},{24,0},{28,4},{1,25},{... | collective-permute-start | bytes 786440 | tf_op jit(solution)/shard_map/ppermute | solution.py:419
  45.6 0.4 collective-permute-start.17
  46.0 6.1 %collective-permute-done.18.refs_2_ = bf16[64,1024]{1,0:T(8,128)(2,1)S(1)} collective-permute-done((bf16[64,1024]{1,0:T(8,128)(2,1)S(1)}, bf16[64,1024]{1,0:T(8,128)(2,1)S(1)}, u32[]{:S(2)}, u32[]{:S(2)}) %collective-permute-start.18) | collective-permute-done | bytes 131104 | tf_op jit(solution)/shard_map/ppermute | solution.py:429
  52.1 1.3 %mask.1 = (bf16[64,1024]{1,0:T(8,128)(2,1)}, f32[4,64]{1,0:T(4,128)S(1)}, f32[64,1]{1,0:T(8,128)S(1)}) custom-call(s32[8]{0:T(128)S(1)} %copy-done.5, s32[8]{0:T(128)S(1)} %copy-done.6, s32[8]{0:T(128)S(1)} %copy-done.7, bf16[64,1024]{1,0:T(8,128)(2,1)S(1)} %get-tuple-element.55.rows_ref), custom_call_target="tpu_custom_call" | custom-call | flops 100000000 | bytes 1000000 | tf_op jit(solution)/shard_map/mask/pallas_call | solution.py:491
  53.4 0.1 collective-permute-done.17.refs_1_
  53.5 4.0 %collective-permute-done.19.refs_3_ = bf16[64,1024]{1,0:T(8,128)(2,1)S(1)} collective-permute-done((bf16[64,1024]{1,0:T(8,128)(2,1)S(1)}, bf16[64,1024]{1,0:T(8,128)(2,1)S(1)}, u32[]{:S(2)}, u32[]{:S(2)}) %collective-permute-start.19) | collective-permute-done | bytes 131104 | tf_op jit(solution)/shard_map/ppermute | solution.py:429
  57.5 1.4 %attention.1 = (bf16[64,256]{1,0:T(8,128)(2,1)S(1)}, bf16[64,256]{1,0:T(8,128)(2,1)S(1)}, bf16[64,256]{1,0:T(8,128)(2,1)S(1)}, bf16[64,256]{1,0:T(8,128)(2,1)S(1)}, bf16[4,1024,128]{2,1,0:T(8,128)(2,1)S(1)}) custom-call(f32[4,64]{1,0:T(4,128)S(1)} %get-tuple-element.58.keys_ref, bf16[64,1024]{1,0:T(8,128)(2,1)S(1)} %get-tuple-element.60.refs_0_, ...), custom_call_target="tpu_custom_call" | custom-call | flops 1000000000 | bytes 2000000 | tf_op jit(solution)/shard_map/attention/pallas_call | solution.py:511
  58.9 0.1 collective-permute-start.25
  59.0 0.3 collective-permute-start.22
  59.3 1.4 %collective-permute-start.23 = (bf16[64,256]{1,0:T(8,128)(2,1)S(1)}, bf16[64,256]{1,0:T(8,128)(2,1)S(1)}, u32[]{:S(2)}, u32[]{:S(2)}) collective-permute-start(bf16[64,256]{1,0:T(8,128)(2,1)S(1)} %get-tuple-element.67), channel_id=1, source_target_pairs={{0,2},{1,3},{2,0},{3,1},{4,6},{5,7},{6,4},{7,5},{8,10},{9,11},{10,... | collective-permute-start | bytes 98312 | tf_op jit(solution)/shard_map/ppermute | solution.py:429
  60.7 2.7 %collective-permute-start.24 = (bf16[64,256]{1,0:T(8,128)(2,1)S(1)}, bf16[64,256]{1,0:T(8,128)(2,1)S(1)}, u32[]{:S(2)}, u32[]{:S(2)}) collective-permute-start(bf16[64,256]{1,0:T(8,128)(2,1)S(1)} %get-tuple-element.68), channel_id=1, source_target_pairs={{0,3},{1,2},{2,1},{3,0},{4,7},{5,6},{6,5},{7,4},{8,11},{9,10},{10,... | collective-permute-start | bytes 98312 | tf_op jit(solution)/shard_map/ppermute | solution.py:429
  63.4 0.7 %collective-permute-done.23.refs_2_ = bf16[64,256]{1,0:T(8,128)(2,1)S(1)} collective-permute-done((bf16[64,256]{1,0:T(8,128)(2,1)S(1)}, bf16[64,256]{1,0:T(8,128)(2,1)S(1)}, u32[]{:S(2)}, u32[]{:S(2)}) %collective-permute-start.23) | collective-permute-done | bytes 32800 | tf_op jit(solution)/shard_map/ppermute | solution.py:429
  64.1 2.3 %collective-permute-done.24.refs_3_ = bf16[64,256]{1,0:T(8,128)(2,1)S(1)} collective-permute-done((bf16[64,256]{1,0:T(8,128)(2,1)S(1)}, bf16[64,256]{1,0:T(8,128)(2,1)S(1)}, u32[]{:S(2)}, u32[]{:S(2)}) %collective-permute-start.24) | collective-permute-done | bytes 32800 | tf_op jit(solution)/shard_map/ppermute | solution.py:429
  66.4 1.1 %output.1 = bf16[64,1024]{1,0:T(8,128)(2,1)} custom-call(f32[64,1]{1,0:T(8,128)S(1)} %get-tuple-element.57.valid_ref, bf16[64,256]{1,0:T(8,128)(2,1)S(1)} %get-tuple-element.65.refs_0_, bf16[64,256]{1,0:T(8,128)(2,1)S(1)} %collective-permute-done.22.refs_1_, bf16[64,256]{1,0:T(8,128)(2,1)S(1)} %collective-permute-done.23.refs_2_, ...), custom_call_target="tpu_custom_call" | custom-call | flops 100000000 | bytes 3000000 | tf_op jit(solution)/shard_map/output/pallas_call | solution.py:530
  (31 shorter events, 0.1 us)
Async XLA Ops:
  0.6 15.9 %collective-permute-start.1 = (bf16[640,1024]{1,0:T(8,128)(2,1)}, bf16[640,1024]{1,0:T(8,128)(2,1)S(1)}, u32[]{:S(2)}, u32[]{:S(2)}) collective-permute-start(bf16[640,1024]{1,0:T(8,128)(2,1)} %refs_4_), channel_id=1, source_target_pairs={{0,4},{4,0},{8,12},{12,8},{16,20},{20,16},{24,28},{28,24},{1,5},{5... | collective-permute-start | bytes 3932168 | tf_op jit(solution)/shard_map/ppermute | solution.py:423
  1.9 23.4 %copy-start.1 = (bf16[640,1024]{1,0:T(8,128)(2,1)S(1)}, bf16[640,1024]{1,0:T(8,128)(2,1)}, u32[]{:S(2)}) copy-start(bf16[640,1024]{1,0:T(8,128)(2,1)} %refs_4_) | copy-start | bytes 3932164
  1.9 23.4 %copy-start.2 = (bf16[2304,256]{1,0:T(8,128)(2,1)S(1)}, bf16[2304,256]{1,0:T(8,128)(2,1)}, u32[]{:S(2)}) copy-start(bf16[2304,256]{1,0:T(8,128)(2,1)} %conv2_ref.1) | copy-start | bytes 3538948
  1.9 23.4 %copy-start.4 = (bf16[9,256]{1,0:T(8,128)(2,1)S(1)}, bf16[9,256]{1,0:T(8,128)(2,1)}, u32[]{:S(2)}) copy-start(bf16[9,256]{1,0:T(8,128)(2,1)} %conv1_ref.1) | copy-start | bytes 13828
  1.9 7.7 %collective-permute-start = (f32[8,1024]{1,0:T(8,128)S(1)}, f32[8,1024]{1,0:T(8,128)S(1)}, u32[]{:S(2)}, u32[]{:S(2)}) collective-permute-start(f32[8,1024]{1,0:T(8,128)S(1)} %slice.3), channel_id=1, source_target_pairs={{0,1},{1,2},{2,3},{3,4},{4,5},{5,6},{6,7},{7,8},{8,9},{9,10},{10,1... | collective-permute-start | bytes 98312 | tf_op jit(solution)/shard_map/ppermute | solution.py:415
  6.6 9.1 %collective-permute-start.2 = (bf16[1024,128]{1,0:T(8,128)(2,1)}, bf16[1024,128]{1,0:T(8,128)(2,1)S(1)}, u32[]{:S(2)}, u32[]{:S(2)}) collective-permute-start(bf16[1024,128]{1,0:T(8,128)(2,1)} %refs_6_), channel_id=1, source_target_pairs={{0,8},{4,12},{8,0},{12,4},{16,24},{20,28},{24,16},{28,20},{1,9},{5... | collective-permute-start | bytes 786440 | tf_op jit(solution)/shard_map/ppermute | solution.py:419
  8.1 8.5 %collective-permute-start.3 = (bf16[1024,128]{1,0:T(8,128)(2,1)}, bf16[1024,128]{1,0:T(8,128)(2,1)}, u32[]{:S(2)}, u32[]{:S(2)}) collective-permute-start(bf16[1024,128]{1,0:T(8,128)(2,1)} %refs_6_), channel_id=1, source_target_pairs={{0,16},{4,20},{8,24},{12,28},{16,0},{20,4},{24,8},{28,12},{1,17},{... | collective-permute-start | bytes 786440 | tf_op jit(solution)/shard_map/ppermute | solution.py:419
  9.6 0.6 copy-start.9
  16.6 6.8 %collective-permute-start.4 = (bf16[72,128]{1,0:T(8,128)(2,1)}, bf16[72,128]{1,0:T(8,128)(2,1)S(1)}, u32[]{:S(2)}, u32[]{:S(2)}) collective-permute-start(bf16[72,128]{1,0:T(8,128)(2,1)} %get-tuple-element.41), channel_id=1, source_target_pairs={{0,8},{4,12},{8,0},{12,4},{16,24},{20,28},{24,16},{28,20},{1,9},{5... | collective-permute-start | bytes 55304 | tf_op jit(solution)/shard_map/ppermute | solution.py:419
  18.5 6.0 %collective-permute-start.5 = (bf16[72,128]{1,0:T(8,128)(2,1)}, bf16[72,128]{1,0:T(8,128)(2,1)S(1)}, u32[]{:S(2)}, u32[]{:S(2)}) collective-permute-start(bf16[72,128]{1,0:T(8,128)(2,1)} %get-tuple-element.42), channel_id=1, source_target_pairs={{0,16},{4,20},{8,24},{12,28},{16,0},{20,4},{24,8},{28,12},{1,17},{... | collective-permute-start | bytes 55304 | tf_op jit(solution)/shard_map/ppermute | solution.py:419
  20.1 5.2 %collective-permute-start.6 = (bf16[72,128]{1,0:T(8,128)(2,1)}, bf16[72,128]{1,0:T(8,128)(2,1)S(1)}, u32[]{:S(2)}, u32[]{:S(2)}) collective-permute-start(bf16[72,128]{1,0:T(8,128)(2,1)} %get-tuple-element.43), channel_id=1, source_target_pairs={{0,24},{4,28},{8,16},{12,20},{16,8},{20,12},{24,0},{28,4},{1,25},{... | collective-permute-start | bytes 55304 | tf_op jit(solution)/shard_map/ppermute | solution.py:419
  21.0 20.6 %copy-start = (bf16[128,768]{1,0:T(8,128)(2,1)S(1)}, bf16[128,768]{1,0:T(8,128)(2,1)}, u32[]{:S(2)}) copy-start(bf16[128,768]{1,0:T(8,128)(2,1)} %get-tuple-element.54.refs_8_) | copy-start | bytes 589828
  21.0 11.7 %collective-permute-start.16 = (bf16[128,768]{1,0:T(8,128)(2,1)}, bf16[128,768]{1,0:T(8,128)(2,1)S(1)}, u32[]{:S(2)}, u32[]{:S(2)}) collective-permute-start(bf16[128,768]{1,0:T(8,128)(2,1)} %get-tuple-element.54.refs_8_), channel_id=1, source_target_pairs={{0,24},{4,28},{8,16},{12,20},{16,8},{20,12},{24,0},{28,4},{1,25},{... | collective-permute-start | bytes 589832 | tf_op jit(solution)/shard_map/ppermute | solution.py:419
  23.0 12.0 %collective-permute-start.15 = (bf16[128,768]{1,0:T(8,128)(2,1)}, bf16[128,768]{1,0:T(8,128)(2,1)S(1)}, u32[]{:S(2)}, u32[]{:S(2)}) collective-permute-start(bf16[128,768]{1,0:T(8,128)(2,1)} %get-tuple-element.54.refs_8_), channel_id=1, source_target_pairs={{0,16},{4,20},{8,24},{12,28},{16,0},{20,4},{24,8},{28,12},{1,17},{... | collective-permute-start | bytes 589832 | tf_op jit(solution)/shard_map/ppermute | solution.py:419
  23.4 12.4 %collective-permute-start.14 = (bf16[128,768]{1,0:T(8,128)(2,1)}, bf16[128,768]{1,0:T(8,128)(2,1)S(1)}, u32[]{:S(2)}, u32[]{:S(2)}) collective-permute-start(bf16[128,768]{1,0:T(8,128)(2,1)} %get-tuple-element.54.refs_8_), channel_id=1, source_target_pairs={{0,8},{4,12},{8,0},{12,4},{16,24},{20,28},{24,16},{28,20},{1,9},{5... | collective-permute-start | bytes 589832 | tf_op jit(solution)/shard_map/ppermute | solution.py:419
  25.3 0.7 %copy-start.8 = (bf16[72,128]{1,0:T(8,128)(2,1)S(1)}, bf16[72,128]{1,0:T(8,128)(2,1)}, u32[]{:S(2)}) copy-start(bf16[72,128]{1,0:T(8,128)(2,1)} %get-tuple-element.40.refs_0_) | copy-start | bytes 55300
  31.3 12.8 %copy-start.3 = (bf16[1024,128]{1,0:T(8,128)(2,1)S(1)}, bf16[1024,128]{1,0:T(8,128)(2,1)}, u32[]{:S(2)}) copy-start(bf16[1024,128]{1,0:T(8,128)(2,1)} %refs_6_) | copy-start | bytes 786436
  31.3 20.8 %copy-start.5 = (s32[8]{0:T(128)S(1)}, s32[8]{0:T(128)}, u32[]{:S(2)}) copy-start(s32[8]{0:T(128)} %slots_ref.1) | copy-start | bytes 100
  31.3 20.8 %copy-start.6 = (s32[8]{0:T(128)S(1)}, s32[8]{0:T(128)}, u32[]{:S(2)}) copy-start(s32[8]{0:T(128)} %starts_ref.1) | copy-start | bytes 100
  31.3 20.8 %copy-start.7 = (s32[8]{0:T(128)S(1)}, s32[8]{0:T(128)}, u32[]{:S(2)}) copy-start(s32[8]{0:T(128)} %lengths_ref.1) | copy-start | bytes 100
  31.3 4.7 %collective-permute-start.7 = (bf16[32,1024]{1,0:T(8,128)(2,1)S(1)}, bf16[32,1024]{1,0:T(8,128)(2,1)S(1)}, u32[]{:S(2)}, u32[]{:S(2)}) collective-permute-start(bf16[32,1024]{1,0:T(8,128)(2,1)S(1)} %get-tuple-element.46), channel_id=1, source_target_pairs={{0,28},{4,24},{8,20},{12,16},{16,12},{20,8},{24,4},{28,0},{1,29},{... | collective-permute-start | bytes 196616 | tf_op jit(solution)/shard_map/ppermute | solution.py:426
  31.4 6.2 %collective-permute-start.8 = (bf16[32,1024]{1,0:T(8,128)(2,1)S(1)}, bf16[32,1024]{1,0:T(8,128)(2,1)S(1)}, u32[]{:S(2)}, u32[]{:S(2)}) collective-permute-start(bf16[32,1024]{1,0:T(8,128)(2,1)S(1)} %get-tuple-element.47), channel_id=1, source_target_pairs={{0,24},{4,28},{8,16},{12,20},{16,8},{20,12},{24,0},{28,4},{1,25},{... | collective-permute-start | bytes 196616 | tf_op jit(solution)/shard_map/ppermute | solution.py:426
  32.7 6.0 %collective-permute-start.9 = (bf16[32,1024]{1,0:T(8,128)(2,1)S(1)}, bf16[32,1024]{1,0:T(8,128)(2,1)S(1)}, u32[]{:S(2)}, u32[]{:S(2)}) collective-permute-start(bf16[32,1024]{1,0:T(8,128)(2,1)S(1)} %get-tuple-element.48), channel_id=1, source_target_pairs={{0,20},{4,16},{8,28},{12,24},{16,4},{20,0},{24,12},{28,8},{1,21},{... | collective-permute-start | bytes 196616 | tf_op jit(solution)/shard_map/ppermute | solution.py:426
  35.0 5.2 %collective-permute-start.10 = (bf16[32,1024]{1,0:T(8,128)(2,1)S(1)}, bf16[32,1024]{1,0:T(8,128)(2,1)S(1)}, u32[]{:S(2)}, u32[]{:S(2)}) collective-permute-start(bf16[32,1024]{1,0:T(8,128)(2,1)S(1)} %get-tuple-element.49), channel_id=1, source_target_pairs={{0,16},{4,20},{8,24},{12,28},{16,0},{20,4},{24,8},{28,12},{1,17},{... | collective-permute-start | bytes 196616 | tf_op jit(solution)/shard_map/ppermute | solution.py:426
  35.8 4.4 %collective-permute-start.11 = (bf16[32,1024]{1,0:T(8,128)(2,1)S(1)}, bf16[32,1024]{1,0:T(8,128)(2,1)S(1)}, u32[]{:S(2)}, u32[]{:S(2)}) collective-permute-start(bf16[32,1024]{1,0:T(8,128)(2,1)S(1)} %get-tuple-element.50), channel_id=1, source_target_pairs={{0,12},{4,8},{8,4},{12,0},{16,28},{20,24},{24,20},{28,16},{1,13},{... | collective-permute-start | bytes 196616 | tf_op jit(solution)/shard_map/ppermute | solution.py:426
  36.1 5.5 %collective-permute-start.12 = (bf16[32,1024]{1,0:T(8,128)(2,1)S(1)}, bf16[32,1024]{1,0:T(8,128)(2,1)S(1)}, u32[]{:S(2)}, u32[]{:S(2)}) collective-permute-start(bf16[32,1024]{1,0:T(8,128)(2,1)S(1)} %get-tuple-element.51), channel_id=1, source_target_pairs={{0,8},{4,12},{8,0},{12,4},{16,24},{20,28},{24,16},{28,20},{1,9},{5... | collective-permute-start | bytes 196616 | tf_op jit(solution)/shard_map/ppermute | solution.py:426
  37.6 4.0 %collective-permute-start.13 = (bf16[32,1024]{1,0:T(8,128)(2,1)S(1)}, bf16[32,1024]{1,0:T(8,128)(2,1)S(1)}, u32[]{:S(2)}, u32[]{:S(2)}) collective-permute-start(bf16[32,1024]{1,0:T(8,128)(2,1)S(1)} %get-tuple-element.52), channel_id=1, source_target_pairs={{0,4},{4,0},{8,12},{12,8},{16,20},{20,16},{24,28},{28,24},{1,5},{5... | collective-permute-start | bytes 196616 | tf_op jit(solution)/shard_map/ppermute | solution.py:426
  43.1 14.4 %collective-permute-start.20 = (bf16[4,128,768]{2,1,0:T(8,128)(2,1)S(1)}, bf16[4,128,768]{2,1,0:T(8,128)(2,1)S(1)}, u32[]{:S(2)}, u32[]{:S(2)}) collective-permute-start(bf16[4,128,768]{2,1,0:T(8,128)(2,1)S(1)} %get-tuple-element.61.refs_4_), channel_id=1, source_target_pairs={{0,4},{4,0},{8,12},{12,8},{16,20},{20,16},{24,28},{28,24},{1,5},{5... | collective-permute-start | bytes 2359304 | tf_op jit(solution)/shard_map/ppermute | solution.py:423
  43.2 8.9 %collective-permute-start.18 = (bf16[64,1024]{1,0:T(8,128)(2,1)S(1)}, bf16[64,1024]{1,0:T(8,128)(2,1)S(1)}, u32[]{:S(2)}, u32[]{:S(2)}) collective-permute-start(bf16[64,1024]{1,0:T(8,128)(2,1)S(1)} %get-tuple-element.60.refs_0_), channel_id=1, source_target_pairs={{0,2},{1,3},{2,0},{3,1},{4,6},{5,7},{6,4},{7,5},{8,10},{9,11},{10,... | collective-permute-start | bytes 393224 | tf_op jit(solution)/shard_map/ppermute | solution.py:429
  44.1 13.5 %collective-permute-start.21 = (bf16[1024,128]{1,0:T(8,128)(2,1)S(1)}, bf16[1024,128]{1,0:T(8,128)(2,1)S(1)}, u32[]{:S(2)}, u32[]{:S(2)}) collective-permute-start(bf16[1024,128]{1,0:T(8,128)(2,1)S(1)} %copy-done.3), channel_id=1, source_target_pairs={{0,24},{4,28},{8,16},{12,20},{16,8},{20,12},{24,0},{28,4},{1,25},{... | collective-permute-start | bytes 786440 | tf_op jit(solution)/shard_map/ppermute | solution.py:419
  45.6 7.9 %collective-permute-start.17 = (bf16[64,1024]{1,0:T(8,128)(2,1)S(1)}, bf16[64,1024]{1,0:T(8,128)(2,1)S(1)}, u32[]{:S(2)}, u32[]{:S(2)}) collective-permute-start(bf16[64,1024]{1,0:T(8,128)(2,1)S(1)} %get-tuple-element.60.refs_0_), channel_id=1, source_target_pairs={{0,1},{1,0},{2,3},{3,2},{4,5},{5,4},{6,7},{7,6},{8,9},{9,8},{10,11... | collective-permute-start | bytes 393224 | tf_op jit(solution)/shard_map/ppermute | solution.py:429
  52.1 5.4 %collective-permute-start.19 = (bf16[64,1024]{1,0:T(8,128)(2,1)S(1)}, bf16[64,1024]{1,0:T(8,128)(2,1)S(1)}, u32[]{:S(2)}, u32[]{:S(2)}) collective-permute-start(bf16[64,1024]{1,0:T(8,128)(2,1)S(1)} %collective-permute-done.18.refs_2_), channel_id=1, source_target_pairs={{0,1},{1,0},{2,3},{3,2},{4,5},{5,4},{6,7},{7,6},{8,9},{9,8},{10,11... | collective-permute-start | bytes 393224 | tf_op jit(solution)/shard_map/ppermute | solution.py:429
  58.9 7.5 %collective-permute-start.25 = (bf16[4,1024,128]{2,1,0:T(8,128)(2,1)S(1)}, bf16[4,1024,128]{2,1,0:T(8,128)(2,1)S(1)}, u32[]{:S(2)}, u32[]{:S(2)}) collective-permute-start(bf16[4,1024,128]{2,1,0:T(8,128)(2,1)S(1)} %get-tuple-element.69.refs_4_), channel_id=1, source_target_pairs={{0,4},{4,0},{8,12},{12,8},{16,20},{20,16},{24,28},{28,24},{1,5},{5... | collective-permute-start | bytes 3145736 | tf_op jit(solution)/shard_map/ppermute | solution.py:423
  59.0 4.5 %collective-permute-start.22 = (bf16[64,256]{1,0:T(8,128)(2,1)S(1)}, bf16[64,256]{1,0:T(8,128)(2,1)S(1)}, u32[]{:S(2)}, u32[]{:S(2)}) collective-permute-start(bf16[64,256]{1,0:T(8,128)(2,1)S(1)} %get-tuple-element.66), channel_id=1, source_target_pairs={{0,1},{1,0},{2,3},{3,2},{4,5},{5,4},{6,7},{7,6},{8,9},{9,8},{10,11... | collective-permute-start | bytes 98312 | tf_op jit(solution)/shard_map/ppermute | solution.py:429
  59.3 4.8 %collective-permute-start.23 = (bf16[64,256]{1,0:T(8,128)(2,1)S(1)}, bf16[64,256]{1,0:T(8,128)(2,1)S(1)}, u32[]{:S(2)}, u32[]{:S(2)}) collective-permute-start(bf16[64,256]{1,0:T(8,128)(2,1)S(1)} %get-tuple-element.67), channel_id=1, source_target_pairs={{0,2},{1,3},{2,0},{3,1},{4,6},{5,7},{6,4},{7,5},{8,10},{9,11},{10,... | collective-permute-start | bytes 98312 | tf_op jit(solution)/shard_map/ppermute | solution.py:429
  60.7 5.7 %collective-permute-start.24 = (bf16[64,256]{1,0:T(8,128)(2,1)S(1)}, bf16[64,256]{1,0:T(8,128)(2,1)S(1)}, u32[]{:S(2)}, u32[]{:S(2)}) collective-permute-start(bf16[64,256]{1,0:T(8,128)(2,1)S(1)} %get-tuple-element.68), channel_id=1, source_target_pairs={{0,3},{1,2},{2,1},{3,0},{4,7},{5,6},{6,5},{7,4},{8,11},{9,10},{10,... | collective-permute-start | bytes 98312 | tf_op jit(solution)/shard_map/ppermute | solution.py:429

commit v6 on v5

--- a/solution.py
+++ b/solution.py
@@ -295,7 +295,7 @@
     copies = windows // parts
     part_refs, refs = refs[:windows][::-1], refs[windows:]
     piece_refs, refs = refs[:parts], refs[parts:]
-    rows_out, normed_out, stack_out, encoded, sems = refs
+    rows_out, normed_out, first_out, second_out, stack_out, encoded, sems = refs
     moves = stacked(parts, piece_refs, stack_out, sems, 0)
     start_all(moves)
     rows = W * parts
@@ -310,7 +310,10 @@
     mean = jnp.mean(values, axis=-1, keepdims=True)
     centered = values - mean
     variance = jnp.mean(centered * centered, axis=-1, keepdims=True)
-    normed_out[...] = (centered * lax.rsqrt(variance + EPS_NORM)).astype(BF16)
+    normed = (centered * lax.rsqrt(variance + EPS_NORM)).astype(BF16)
+    normed_out[...] = normed
+    first_out[...] = normed[: normed.shape[0] // 2]
+    second_out[...] = normed[normed.shape[0] // 2 :]
     wait_all(moves)
 
 
@@ -328,7 +331,7 @@
     _, copy_index = place(parts)
     plane = lax.axis_index("seq")
     copies = windows // parts
-    normed_refs, refs = refs[:group], refs[group:]
+    normed_refs, refs = refs[: 2 * group - 2], refs[2 * group - 2 :]
     stack_refs, refs = refs[:copies], refs[copies:]
     weight_refs, refs = refs[:parts], refs[parts:]
     outs_refs, (stack_out, pieces, sems) = refs[:group], refs[group:]
@@ -338,11 +341,11 @@
     valid = jnp.concatenate(keys, axis=1) > 0.5
     local = normed_refs[0].shape[0]
     depth = pieces.shape[2]
-    for step in range(group):
+    at = 0
+    for ref in normed_refs:
         for piece in range(windows):
-            pieces[piece, step * local : (step + 1) * local, :] = normed_refs[step][
-                :, piece * depth : (piece + 1) * depth
-            ]
+            pieces[piece, at : at + ref.shape[0], :] = ref[:, piece * depth : (piece + 1) * depth]
+        at += ref.shape[0]
     mixed = 0.0
     for step in range(copies):
         slot = copy_index ^ step
@@ -370,7 +373,7 @@
 
 
 def output_kernel(parts, windows, group, valid_ref, *refs):
-    context_refs, refs = refs[:group], refs[group:]
+    context_refs, refs = refs[:group][::-1], refs[group:]
     stack_refs, refs = refs[: windows // parts], refs[windows // parts :]
     out_ref, context, pieces = refs
     _, copy_index = place(parts)
@@ -449,8 +452,9 @@
         name="log_mel",
     )(slots, rim, audio, table, qkv_weight)
     near = [to_part(out_weight, step) for step in range(1, parts - 1)]
-    mel_all, proj_all, near = lax.optimization_barrier((mel_all, proj_all, near))
+    mel_all, proj_all = lax.optimization_barrier((mel_all, proj_all))
     mel_all = [mel_all[0]] + [to_part(mel_all[step], step) for step in range(1, parts)]
+    mel_all, near = lax.optimization_barrier((mel_all, near))
     mix_all = [mix] + [to_part(mix, step) for step in range(1, parts)]
 
     block = jax.ShapeDtypeStruct((local, features), BF16)
@@ -477,11 +481,12 @@
     )(conv1_weight, conv2_weight, *mel_all, *proj_all)
     partials = [to_window(partials[step], step) for step in reversed(range(1, windows))] + [partials[0]]
 
-    ordered, normed, stack = pl.pallas_call(
+    half = jax.ShapeDtypeStruct((local // 2, features), BF16)
+    ordered, normed, *halves, stack = pl.pallas_call(
         functools.partial(norm_kernel, parts),
-        out_shape=(block, block, jax.ShapeDtypeStruct((parts,) + mix_piece.shape, BF16)),
+        out_shape=(block, block, half, half, jax.ShapeDtypeStruct((parts,) + mix_piece.shape, BF16)),
         in_specs=[vmem()] * windows + [anywhere()] * parts,
-        out_specs=(vmem(), vmem(), vmem()),
+        out_specs=tuple([vmem()] * 5),
         scratch_shapes=[pltpu.VMEM((local, features), BF16), pltpu.SemaphoreType.DMA((parts,))],
         compiler_params=params(min(12 * scale, 32)),
         cost_estimate=cost(1e8, 1e6),
@@ -502,10 +507,12 @@
         name="mask",
     )(slots, starts, lengths, ordered)
     normed, out_here = lax.optimization_barrier((normed, out_weight))
-    normed = [normed]
-    for step in range(1, group):
+    by_plane = {0: [normed], 1: [to_plane(normed, 1)]}
+    for step in range(2, group):
         high = 1 << (step.bit_length() - 1)
-        normed.append(to_plane(normed[high] if step > high else normed[0], step - high if step > high else high))
+        source = halves if step == high else by_plane[high]
+        by_plane[step] = [to_plane(piece, high if step == high else step - high) for piece in source]
+    normed = [piece for step in range(group) for piece in by_plane[step]]
     out_all = [out_here] + near + [to_part(out_here, parts - 1)]
 
     *context, stack = pl.pallas_call(
@@ -514,7 +521,7 @@
             [jax.ShapeDtypeStruct((local, head_width), BF16)] * group
             + [jax.ShapeDtypeStruct((parts,) + out_weight.shape, BF16)]
         ),
-        in_specs=[vmem()] * (1 + group + copies) + [anywhere()] * parts,
+        in_specs=[vmem()] * (1 + len(normed) + copies) + [anywhere()] * parts,
         out_specs=tuple([vmem()] * (group + 1)),
         scratch_shapes=[
             pltpu.VMEM((windows, group * local, qkv_weight.shape[0]), BF16),
@@ -524,7 +531,7 @@
         cost_estimate=cost(1e9, 2e6),
         name="attention",
     )(keys, *normed, *mix_stacks, *out_all)
-    context = [context[0]] + [to_plane(context[step], step) for step in range(1, group)]
+    context = [to_plane(context[step], step) for step in reversed(range(1, group))] + [context[0]]
     out_stacks = [stack] + [to_copy(stack, step) for step in range(1, copies)]
 
     attended = pl.pallas_call(

time: 67.9 us -> 67.6 us (level)
  waiting for transfers between devices: 19.5 us -> 12.9 us
  starting transfers between devices: 29.6 us -> 35.9 us
    ppermute x6 -> x8, starting transfers between devices: 5.67 us -> 11.1 us  [to_plane(): return lax.ppermute(block, 'seq', [(i, i ^ step) for i in range(group)])]
    ppermute x6 -> x8, waiting for transfers between devices: 13.2 us -> 7.95 us  [to_plane(): return lax.ppermute(block, 'seq', [(i, i ^ step) for i in range(group)])]
    ppermute x9, waiting for transfers between devices: 2 us -> 0.77 us  [to_part(): return lax.ppermute(block, 'dp', pairs)]
    ppermute x9, starting transfers between devices: 12.5 us -> 13.4 us  [to_part(): return lax.ppermute(block, 'dp', pairs)]
  transfers between devices with their start and end apart: 26 -> 28, of which waited for: 12 -> 11; matrix products, arithmetic and copies ran while one was open for 1% -> 1% of each run, Pallas kernels for 17% -> 17%
where the time goes in v6:
time: 67.6 us; the launch traced here: 67.3 us
  starting transfers between devices  35.9 us (53%)
  Pallas kernels  15.6 us (23%)
  waiting for transfers between devices  12.9 us (19%)
  local copies, waits for them, and re-layouts  2.13 us (3%)
  between operations  0.77 us (1%)
    ppermute x9, starting transfers between devices, to_part(): return lax.ppermute(block, 'dp', pairs)  13.4 us
    ppermute x8, starting transfers between devices, to_plane(): return lax.ppermute(block, 'seq', [(i, i ^ step) for i in range(group)])  11.1 us
    ppermute x8, waiting for transfers between devices, to_plane(): return lax.ppermute(block, 'seq', [(i, i ^ step) for i in range(group)])  7.95 us
    ppermute x7, starting transfers between devices, to_window(): return lax.ppermute(block, 'dp', [(i, i ^ step) for i in range(windows)])  6.04 us
    pallas_call x1, Pallas kernels, on_device(): pl.pallas_call(functools.partial(conv_kernel, parts, width), out_shape=tu...  5.24 us
    pallas_call x1, Pallas kernels, on_device(): pl.pallas_call(functools.partial(mel_kernel, parts, group), out_shape=tup...  5.14 us
    ppermute x1, starting transfers between devices, on_device(): rim = lax.ppermute(audio[:, audio.shape[1] - RIM:], ('dp', 'seq'), route)  4.63 us
    ppermute x7, waiting for transfers between devices, to_window(): return lax.ppermute(block, 'dp', [(i, i ^ step) for i in range(windows)])  4.21 us
  transfers between devices with their start and end apart: 28, of which 11 were waited for; matrix products, arithmetic and copies ran while one was open for 1% of the time, Pallas kernels for 17%

profile of v6, /device:TPU:0, one launch (start us, length us, event | category | flops | bytes accessed | tf_op | source)
XLA Modules:
  0.0 67.3 jit_solution(17246796097908103511)
XLA Ops:
  0.6 0.5 collective-permute-start.1
  1.1 0.8 %slice.3 = f32[8,1024]{1,0:T(8,128)S(1)} slice(f32[8,5120]{1,0:T(8,128)} %audio_ref.1), slice={[0:8], [4096:5120]} | slice | bytes 65536 | tf_op jit(solution)/shard_map/slice | solution.py:418
  1.9 4.6 %collective-permute-start = (f32[8,1024]{1,0:T(8,128)S(1)}, f32[8,1024]{1,0:T(8,128)S(1)}, u32[]{:S(2)}, u32[]{:S(2)}) collective-permute-start(f32[8,1024]{1,0:T(8,128)S(1)} %slice.3), channel_id=1, source_target_pairs={{0,1},{1,2},{2,3},{3,4},{4,5},{5,6},{6,7},{7,8},{8,9},{9,10},{10,1... | collective-permute-start | bytes 98312 | tf_op jit(solution)/shard_map/ppermute | solution.py:418
  6.6 1.6 %collective-permute-start.5 = (bf16[1024,128]{1,0:T(8,128)(2,1)}, bf16[1024,128]{1,0:T(8,128)(2,1)S(1)}, u32[]{:S(2)}, u32[]{:S(2)}) collective-permute-start(bf16[1024,128]{1,0:T(8,128)(2,1)} %refs_8_), channel_id=1, source_target_pairs={{0,8},{4,12},{8,0},{12,4},{16,24},{20,28},{24,16},{28,20},{1,9},{5... | collective-permute-start | bytes 786440 | tf_op jit(solution)/shard_map/ppermute | solution.py:422
  8.1 1.5 %collective-permute-start.6 = (bf16[1024,128]{1,0:T(8,128)(2,1)}, bf16[1024,128]{1,0:T(8,128)(2,1)}, u32[]{:S(2)}, u32[]{:S(2)}) collective-permute-start(bf16[1024,128]{1,0:T(8,128)(2,1)} %refs_8_), channel_id=1, source_target_pairs={{0,16},{4,20},{8,24},{12,28},{16,0},{20,4},{24,8},{28,12},{1,17},{... | collective-permute-start | bytes 786440 | tf_op jit(solution)/shard_map/ppermute | solution.py:422
  9.6 0.6 copy-done.9
  10.2 5.1 %log_mel.1 = (bf16[72,128]{1,0:T(8,128)(2,1)}, bf16[72,128]{1,0:T(8,128)(2,1)}, bf16[72,128]{1,0:T(8,128)(2,1)}, bf16[72,128]{1,0:T(8,128)(2,1)}, bf16[128,768]{1,0:T(8,128)(2,1)}) custom-call(s32[8]{0:T(128)} %slots_ref.1, f32[8,1024]{1,0:T(8,128)} %copy-done.9, f32[8,5120]{1,0:T(8,128)} %audio_ref.1, f32[512,640]{1,0:T(8,128)} %constant.2.clone.table_ref, ...), custom_call_target="tpu_custom_call" | custom-call | flops 10000000000 | bytes 2000000 | tf_op jit(solution)/shard_map/log_mel/pallas_call | solution.py:438
  15.4 3.0 %collective-permute-start.2 = (bf16[72,128]{1,0:T(8,128)(2,1)}, bf16[72,128]{1,0:T(8,128)(2,1)S(1)}, u32[]{:S(2)}, u32[]{:S(2)}) collective-permute-start(bf16[72,128]{1,0:T(8,128)(2,1)} %get-tuple-element.47), channel_id=1, source_target_pairs={{0,8},{4,12},{8,0},{12,4},{16,24},{20,28},{24,16},{28,20},{1,9},{5... | collective-permute-start | bytes 55304 | tf_op jit(solution)/shard_map/ppermute | solution.py:422
  18.4 1.6 %collective-permute-start.3 = (bf16[72,128]{1,0:T(8,128)(2,1)}, bf16[72,128]{1,0:T(8,128)(2,1)S(1)}, u32[]{:S(2)}, u32[]{:S(2)}) collective-permute-start(bf16[72,128]{1,0:T(8,128)(2,1)} %get-tuple-element.48), channel_id=1, source_target_pairs={{0,16},{4,20},{8,24},{12,28},{16,0},{20,4},{24,8},{28,12},{1,17},{... | collective-permute-start | bytes 55304 | tf_op jit(solution)/shard_map/ppermute | solution.py:422
  20.1 0.9 %collective-permute-start.4 = (bf16[72,128]{1,0:T(8,128)(2,1)}, bf16[72,128]{1,0:T(8,128)(2,1)S(1)}, u32[]{:S(2)}, u32[]{:S(2)}) collective-permute-start(bf16[72,128]{1,0:T(8,128)(2,1)} %get-tuple-element.49), channel_id=1, source_target_pairs={{0,24},{4,28},{8,16},{12,20},{16,8},{20,12},{24,0},{28,4},{1,25},{... | collective-permute-start | bytes 55304 | tf_op jit(solution)/shard_map/ppermute | solution.py:422
  21.0 2.0 %collective-permute-start.16 = (bf16[128,768]{1,0:T(8,128)(2,1)}, bf16[128,768]{1,0:T(8,128)(2,1)S(1)}, u32[]{:S(2)}, u32[]{:S(2)}) collective-permute-start(bf16[128,768]{1,0:T(8,128)(2,1)} %get-tuple-element.64.refs_8_), channel_id=1, source_target_pairs={{0,24},{4,28},{8,16},{12,20},{16,8},{20,12},{24,0},{28,4},{1,25},{... | collective-permute-start | bytes 589832 | tf_op jit(solution)/shard_map/ppermute | solution.py:422
  23.0 0.4 collective-permute-start.15
  23.4 1.1 %collective-permute-start.14 = (bf16[128,768]{1,0:T(8,128)(2,1)}, bf16[128,768]{1,0:T(8,128)(2,1)S(1)}, u32[]{:S(2)}, u32[]{:S(2)}) collective-permute-start(bf16[128,768]{1,0:T(8,128)(2,1)} %get-tuple-element.64.refs_8_), channel_id=1, source_target_pairs={{0,8},{4,12},{8,0},{12,4},{16,24},{20,28},{24,16},{28,20},{1,9},{5... | collective-permute-start | bytes 589832 | tf_op jit(solution)/shard_map/ppermute | solution.py:422
  24.5 0.7 %collective-permute-done.4.refs_3_ = bf16[72,128]{1,0:T(8,128)(2,1)S(1)} collective-permute-done((bf16[72,128]{1,0:T(8,128)(2,1)}, bf16[72,128]{1,0:T(8,128)(2,1)S(1)}, u32[]{:S(2)}, u32[]{:S(2)}) %collective-permute-start.4) | collective-permute-done | bytes 18464 | tf_op jit(solution)/shard_map/ppermute | solution.py:422
  25.3 0.0 copy-start.8
  25.3 0.7 %copy-done.8 = bf16[72,128]{1,0:T(8,128)(2,1)S(1)} copy-done((bf16[72,128]{1,0:T(8,128)(2,1)S(1)}, bf16[72,128]{1,0:T(8,128)(2,1)}, u32[]{:S(2)}) %copy-start.8) | copy-done | bytes 18456
  26.0 5.2 %conv.1 = (bf16[32,1024]{1,0:T(8,128)(2,1)S(1)}, bf16[32,1024]{1,0:T(8,128)(2,1)S(1)}, bf16[32,1024]{1,0:T(8,128)(2,1)S(1)}, bf16[32,1024]{1,0:T(8,128)(2,1)S(1)...) custom-call(bf16[9,256]{1,0:T(8,128)(2,1)S(1)} %copy-done.4, ...), custom_call_target="tpu_custom_call" | custom-call | flops 2000000000 | bytes 4000000 | tf_op jit(solution)/shard_map/conv/pallas_call | solution.py:461
  31.3 0.0 copy-start.6
  31.3 0.0 copy-start.7
  31.3 0.1 collective-permute-start.7
  31.4 1.3 %collective-permute-start.8 = (bf16[32,1024]{1,0:T(8,128)(2,1)S(1)}, bf16[32,1024]{1,0:T(8,128)(2,1)S(1)}, u32[]{:S(2)}, u32[]{:S(2)}) collective-permute-start(bf16[32,1024]{1,0:T(8,128)(2,1)S(1)} %get-tuple-element.57), channel_id=1, source_target_pairs={{0,24},{4,28},{8,16},{12,20},{16,8},{20,12},{24,0},{28,4},{1,25},{... | collective-permute-start | bytes 196616 | tf_op jit(solution)/shard_map/ppermute | solution.py:429
  32.7 2.3 %collective-permute-start.9 = (bf16[32,1024]{1,0:T(8,128)(2,1)S(1)}, bf16[32,1024]{1,0:T(8,128)(2,1)S(1)}, u32[]{:S(2)}, u32[]{:S(2)}) collective-permute-start(bf16[32,1024]{1,0:T(8,128)(2,1)S(1)} %get-tuple-element.58), channel_id=1, source_target_pairs={{0,20},{4,16},{8,28},{12,24},{16,4},{20,0},{24,12},{28,8},{1,21},{... | collective-permute-start | bytes 196616 | tf_op jit(solution)/shard_map/ppermute | solution.py:429
  35.0 0.8 %collective-permute-start.10 = (bf16[32,1024]{1,0:T(8,128)(2,1)S(1)}, bf16[32,1024]{1,0:T(8,128)(2,1)S(1)}, u32[]{:S(2)}, u32[]{:S(2)}) collective-permute-start(bf16[32,1024]{1,0:T(8,128)(2,1)S(1)} %get-tuple-element.59), channel_id=1, source_target_pairs={{0,16},{4,20},{8,24},{12,28},{16,0},{20,4},{24,8},{28,12},{1,17},{... | collective-permute-start | bytes 196616 | tf_op jit(solution)/shard_map/ppermute | solution.py:429
  35.8 0.3 collective-permute-done.7.refs_0_
  36.0 1.5 %collective-permute-start.12 = (bf16[32,1024]{1,0:T(8,128)(2,1)S(1)}, bf16[32,1024]{1,0:T(8,128)(2,1)S(1)}, u32[]{:S(2)}, u32[]{:S(2)}) collective-permute-start(bf16[32,1024]{1,0:T(8,128)(2,1)S(1)} %get-tuple-element.61), channel_id=1, source_target_pairs={{0,8},{4,12},{8,0},{12,4},{16,24},{20,28},{24,16},{28,20},{1,9},{5... | collective-permute-start | bytes 196616 | tf_op jit(solution)/shard_map/ppermute | solution.py:429
  37.6 0.1 collective-permute-start.13
  37.6 1.0 %collective-permute-done.9.refs_2_ = bf16[32,1024]{1,0:T(8,128)(2,1)S(1)} collective-permute-done((bf16[32,1024]{1,0:T(8,128)(2,1)S(1)}, bf16[32,1024]{1,0:T(8,128)(2,1)S(1)}, u32[]{:S(2)}, u32[]{:S(2)}) %collective-permute-start.9) | collective-permute-done | bytes 65568 | tf_op jit(solution)/shard_map/ppermute | solution.py:429
  38.7 1.5 %collective-permute-done.10.refs_3_ = bf16[32,1024]{1,0:T(8,128)(2,1)S(1)} collective-permute-done((bf16[32,1024]{1,0:T(8,128)(2,1)S(1)}, bf16[32,1024]{1,0:T(8,128)(2,1)S(1)}, u32[]{:S(2)}, u32[]{:S(2)}) %collective-permute-start.10) | collective-permute-done | bytes 65568 | tf_op jit(solution)/shard_map/ppermute | solution.py:429
  40.2 1.4 %collective-permute-done.12.refs_5_ = bf16[32,1024]{1,0:T(8,128)(2,1)S(1)} collective-permute-done((bf16[32,1024]{1,0:T(8,128)(2,1)S(1)}, bf16[32,1024]{1,0:T(8,128)(2,1)S(1)}, u32[]{:S(2)}, u32[]{:S(2)}) %collective-permute-start.12) | collective-permute-done | bytes 65568 | tf_op jit(solution)/shard_map/ppermute | solution.py:429
  41.6 1.5 %layer_norm.1 = (bf16[64,1024]{1,0:T(8,128)(2,1)S(1)}, bf16[64,1024]{1,0:T(8,128)(2,1)S(1)}, bf16[32,1024]{1,0:T(8,128)(2,1)S(1)}, bf16[32,1024]{1,0:T(8,128)(2,1)S(1)}, bf16[4,128,768]{2,1,0:T(8,128)(2,1)S(1)}) custom-call(bf16[32,1024]{1,0:T(8,128)(2,1)S(1)} %collective-permute-done.7.refs_0_, bf16[32,1024]{1,0:T(8,128)(2,1)S(1)} %collective-permute-done.8.refs_1_, ...), custom_call_target="tpu_custom_call" | custom-call | flops 100000000 | bytes 1000000 | tf_op jit(solution)/shard_map/layer_norm/pallas_call | solution.py:485
  43.0 0.2 collective-permute-start.22
  43.2 1.2 %collective-permute-start.23 = (bf16[1024,128]{1,0:T(8,128)(2,1)S(1)}, bf16[1024,128]{1,0:T(8,128)(2,1)S(1)}, u32[]{:S(2)}, u32[]{:S(2)}) collective-permute-start(bf16[1024,128]{1,0:T(8,128)(2,1)S(1)} %copy-done.3), channel_id=1, source_target_pairs={{0,24},{4,28},{8,16},{12,20},{16,8},{20,12},{24,0},{28,4},{1,25},{... | collective-permute-start | bytes 786440 | tf_op jit(solution)/shard_map/ppermute | solution.py:422
  44.4 1.1 %collective-permute-start.17 = (bf16[64,1024]{1,0:T(8,128)(2,1)S(1)}, bf16[64,1024]{1,0:T(8,128)(2,1)S(1)}, u32[]{:S(2)}, u32[]{:S(2)}) collective-permute-start(bf16[64,1024]{1,0:T(8,128)(2,1)S(1)} %get-tuple-element.70.refs_0_), channel_id=1, source_target_pairs={{0,1},{1,0},{2,3},{3,2},{4,5},{5,4},{6,7},{7,6},{8,9},{9,8},{10,11... | collective-permute-start | bytes 393224 | tf_op jit(solution)/shard_map/ppermute | solution.py:432
  45.6 1.8 %collective-permute-start.19 = (bf16[32,1024]{1,0:T(8,128)(2,1)S(1)}, bf16[32,1024]{1,0:T(8,128)(2,1)S(1)}, u32[]{:S(2)}, u32[]{:S(2)}) collective-permute-start(bf16[32,1024]{1,0:T(8,128)(2,1)S(1)} %get-tuple-element.72), channel_id=1, source_target_pairs={{0,2},{1,3},{2,0},{3,1},{4,6},{5,7},{6,4},{7,5},{8,10},{9,11},{10,... | collective-permute-start | bytes 196616 | tf_op jit(solution)/shard_map/ppermute | solution.py:432
  47.4 2.9 %collective-permute-done.18.refs_2_ = bf16[32,1024]{1,0:T(8,128)(2,1)S(1)} collective-permute-done((bf16[32,1024]{1,0:T(8,128)(2,1)S(1)}, bf16[32,1024]{1,0:T(8,128)(2,1)S(1)}, u32[]{:S(2)}, u32[]{:S(2)}) %collective-permute-start.18) | collective-permute-done | bytes 65568 | tf_op jit(solution)/shard_map/ppermute | solution.py:432
  50.3 0.8 %collective-permute-done.19.refs_3_ = bf16[32,1024]{1,0:T(8,128)(2,1)S(1)} collective-permute-done((bf16[32,1024]{1,0:T(8,128)(2,1)S(1)}, bf16[32,1024]{1,0:T(8,128)(2,1)S(1)}, u32[]{:S(2)}, u32[]{:S(2)}) %collective-permute-start.19) | collective-permute-done | bytes 65568 | tf_op jit(solution)/shard_map/ppermute | solution.py:432
  51.1 3.7 %collective-permute-start.21 = (bf16[32,1024]{1,0:T(8,128)(2,1)S(1)}, bf16[32,1024]{1,0:T(8,128)(2,1)S(1)}, u32[]{:S(2)}, u32[]{:S(2)}) collective-permute-start(bf16[32,1024]{1,0:T(8,128)(2,1)S(1)} %collective-permute-done.19.refs_3_), channel_id=1, source_target_pairs={{0,1},{1,0},{2,3},{3,2},{4,5},{5,4},{6,7},{7,6},{8,9},{9,8},{10,11... | collective-permute-start | bytes 196616 | tf_op jit(solution)/shard_map/ppermute | solution.py:432
  54.8 1.3 %mask.1 = (bf16[64,1024]{1,0:T(8,128)(2,1)}, f32[4,64]{1,0:T(4,128)S(1)}, f32[64,1]{1,0:T(8,128)S(1)}) custom-call(s32[8]{0:T(128)S(1)} %copy-done.5, s32[8]{0:T(128)S(1)} %copy-done.6, s32[8]{0:T(128)S(1)} %copy-done.7, bf16[64,1024]{1,0:T(8,128)(2,1)S(1)} %get-tuple-element.65.rows_ref), custom_call_target="tpu_custom_call" | custom-call | flops 100000000 | bytes 1000000 | tf_op jit(solution)/shard_map/mask/pallas_call | solution.py:496
  56.0 1.0 %collective-permute-done.21.refs_5_ = bf16[32,1024]{1,0:T(8,128)(2,1)S(1)} collective-permute-done((bf16[32,1024]{1,0:T(8,128)(2,1)S(1)}, bf16[32,1024]{1,0:T(8,128)(2,1)S(1)}, u32[]{:S(2)}, u32[]{:S(2)}) %collective-permute-start.21) | collective-permute-done | bytes 65568 | tf_op jit(solution)/shard_map/ppermute | solution.py:432
  57.0 1.4 %attention.1 = (bf16[64,256]{1,0:T(8,128)(2,1)S(1)}, bf16[64,256]{1,0:T(8,128)(2,1)S(1)}, bf16[64,256]{1,0:T(8,128)(2,1)S(1)}, bf16[64,256]{1,0:T(8,128)(2,1)S(1)}, bf16[4,1024,128]{2,1,0:T(8,128)(2,1)S(1)}) custom-call(f32[4,64]{1,0:T(4,128)S(1)} %get-tuple-element.68.keys_ref, bf16[64,1024]{1,0:T(8,128)(2,1)S(1)} %get-tuple-element.70.refs_0_, ...), custom_call_target="tpu_custom_call" | custom-call | flops 1000000000 | bytes 2000000 | tf_op jit(solution)/shard_map/attention/pallas_call | solution.py:518
  58.4 0.1 collective-permute-start.27
  58.4 2.5 %collective-permute-start.24 = (bf16[64,256]{1,0:T(8,128)(2,1)S(1)}, bf16[64,256]{1,0:T(8,128)(2,1)S(1)}, u32[]{:S(2)}, u32[]{:S(2)}) collective-permute-start(bf16[64,256]{1,0:T(8,128)(2,1)S(1)} %get-tuple-element.77), channel_id=1, source_target_pairs={{0,3},{1,2},{2,1},{3,0},{4,7},{5,6},{6,5},{7,4},{8,11},{9,10},{10,... | collective-permute-start | bytes 98312 | tf_op jit(solution)/shard_map/ppermute | solution.py:432
  61.0 1.0 %collective-permute-start.25 = (bf16[64,256]{1,0:T(8,128)(2,1)S(1)}, bf16[64,256]{1,0:T(8,128)(2,1)S(1)}, u32[]{:S(2)}, u32[]{:S(2)}) collective-permute-start(bf16[64,256]{1,0:T(8,128)(2,1)S(1)} %get-tuple-element.78), channel_id=1, source_target_pairs={{0,2},{1,3},{2,0},{3,1},{4,6},{5,7},{6,4},{7,5},{8,10},{9,11},{10,... | collective-permute-start | bytes 98312 | tf_op jit(solution)/shard_map/ppermute | solution.py:432
  62.0 0.9 %collective-permute-start.26 = (bf16[64,256]{1,0:T(8,128)(2,1)S(1)}, bf16[64,256]{1,0:T(8,128)(2,1)S(1)}, u32[]{:S(2)}, u32[]{:S(2)}) collective-permute-start(bf16[64,256]{1,0:T(8,128)(2,1)S(1)} %get-tuple-element.79), channel_id=1, source_target_pairs={{0,1},{1,0},{2,3},{3,2},{4,5},{5,4},{6,7},{7,6},{8,9},{9,8},{10,11... | collective-permute-start | bytes 98312 | tf_op jit(solution)/shard_map/ppermute | solution.py:432
  62.9 1.7 %collective-permute-done.24.refs_0_ = bf16[64,256]{1,0:T(8,128)(2,1)S(1)} collective-permute-done((bf16[64,256]{1,0:T(8,128)(2,1)S(1)}, bf16[64,256]{1,0:T(8,128)(2,1)S(1)}, u32[]{:S(2)}, u32[]{:S(2)}) %collective-permute-start.24) | collective-permute-done | bytes 32800 | tf_op jit(solution)/shard_map/ppermute | solution.py:432
  64.6 1.2 %collective-permute-done.25.refs_1_ = bf16[64,256]{1,0:T(8,128)(2,1)S(1)} collective-permute-done((bf16[64,256]{1,0:T(8,128)(2,1)S(1)}, bf16[64,256]{1,0:T(8,128)(2,1)S(1)}, u32[]{:S(2)}, u32[]{:S(2)}) %collective-permute-start.25) | collective-permute-done | bytes 32800 | tf_op jit(solution)/shard_map/ppermute | solution.py:432
  65.8 0.3 collective-permute-done.26.refs_2_
  66.2 1.1 %output.1 = bf16[64,1024]{1,0:T(8,128)(2,1)} custom-call(f32[64,1]{1,0:T(8,128)S(1)} %get-tuple-element.67.valid_ref, bf16[64,256]{1,0:T(8,128)(2,1)S(1)} %collective-permute-done.24.refs_0_, bf16[64,256]{1,0:T(8,128)(2,1)S(1)} %collective-permute-done.25.refs_1_, bf16[64,256]{1,0:T(8,128)(2,1)S(1)} %collective-permute-done.26.refs_2_, ...), custom_call_target="tpu_custom_call" | custom-call | flops 100000000 | bytes 3000000 | tf_op jit(solution)/shard_map/output/pallas_call | solution.py:537
  (35 shorter events, 0.1 us)
Async XLA Ops:
  0.6 14.8 %collective-permute-start.1 = (bf16[640,1024]{1,0:T(8,128)(2,1)}, bf16[640,1024]{1,0:T(8,128)(2,1)S(1)}, u32[]{:S(2)}, u32[]{:S(2)}) collective-permute-start(bf16[640,1024]{1,0:T(8,128)(2,1)} %refs_4_), channel_id=1, source_target_pairs={{0,4},{4,0},{8,12},{12,8},{16,20},{20,16},{24,28},{28,24},{1,5},{5... | collective-permute-start | bytes 3932168 | tf_op jit(solution)/shard_map/ppermute | solution.py:426
  1.9 23.4 %copy-start.1 = (bf16[640,1024]{1,0:T(8,128)(2,1)S(1)}, bf16[640,1024]{1,0:T(8,128)(2,1)}, u32[]{:S(2)}) copy-start(bf16[640,1024]{1,0:T(8,128)(2,1)} %refs_4_) | copy-start | bytes 3932164
  1.9 23.4 %copy-start.2 = (bf16[2304,256]{1,0:T(8,128)(2,1)S(1)}, bf16[2304,256]{1,0:T(8,128)(2,1)}, u32[]{:S(2)}) copy-start(bf16[2304,256]{1,0:T(8,128)(2,1)} %conv2_ref.1) | copy-start | bytes 3538948
  1.9 23.4 %copy-start.4 = (bf16[9,256]{1,0:T(8,128)(2,1)S(1)}, bf16[9,256]{1,0:T(8,128)(2,1)}, u32[]{:S(2)}) copy-start(bf16[9,256]{1,0:T(8,128)(2,1)} %conv1_ref.1) | copy-start | bytes 13828
  1.9 7.7 %collective-permute-start = (f32[8,1024]{1,0:T(8,128)S(1)}, f32[8,1024]{1,0:T(8,128)S(1)}, u32[]{:S(2)}, u32[]{:S(2)}) collective-permute-start(f32[8,1024]{1,0:T(8,128)S(1)} %slice.3), channel_id=1, source_target_pairs={{0,1},{1,2},{2,3},{3,4},{4,5},{5,6},{6,7},{7,8},{8,9},{9,10},{10,1... | collective-permute-start | bytes 98312 | tf_op jit(solution)/shard_map/ppermute | solution.py:418
  6.6 14.4 %collective-permute-start.5 = (bf16[1024,128]{1,0:T(8,128)(2,1)}, bf16[1024,128]{1,0:T(8,128)(2,1)S(1)}, u32[]{:S(2)}, u32[]{:S(2)}) collective-permute-start(bf16[1024,128]{1,0:T(8,128)(2,1)} %refs_8_), channel_id=1, source_target_pairs={{0,8},{4,12},{8,0},{12,4},{16,24},{20,28},{24,16},{28,20},{1,9},{5... | collective-permute-start | bytes 786440 | tf_op jit(solution)/shard_map/ppermute | solution.py:422
  8.1 14.9 %collective-permute-start.6 = (bf16[1024,128]{1,0:T(8,128)(2,1)}, bf16[1024,128]{1,0:T(8,128)(2,1)}, u32[]{:S(2)}, u32[]{:S(2)}) collective-permute-start(bf16[1024,128]{1,0:T(8,128)(2,1)} %refs_8_), channel_id=1, source_target_pairs={{0,16},{4,20},{8,24},{12,28},{16,0},{20,4},{24,8},{28,12},{1,17},{... | collective-permute-start | bytes 786440 | tf_op jit(solution)/shard_map/ppermute | solution.py:422
  9.6 0.6 copy-start.9
  15.4 8.0 %collective-permute-start.2 = (bf16[72,128]{1,0:T(8,128)(2,1)}, bf16[72,128]{1,0:T(8,128)(2,1)S(1)}, u32[]{:S(2)}, u32[]{:S(2)}) collective-permute-start(bf16[72,128]{1,0:T(8,128)(2,1)} %get-tuple-element.47), channel_id=1, source_target_pairs={{0,8},{4,12},{8,0},{12,4},{16,24},{20,28},{24,16},{28,20},{1,9},{5... | collective-permute-start | bytes 55304 | tf_op jit(solution)/shard_map/ppermute | solution.py:422
  18.4 6.1 %collective-permute-start.3 = (bf16[72,128]{1,0:T(8,128)(2,1)}, bf16[72,128]{1,0:T(8,128)(2,1)S(1)}, u32[]{:S(2)}, u32[]{:S(2)}) collective-permute-start(bf16[72,128]{1,0:T(8,128)(2,1)} %get-tuple-element.48), channel_id=1, source_target_pairs={{0,16},{4,20},{8,24},{12,28},{16,0},{20,4},{24,8},{28,12},{1,17},{... | collective-permute-start | bytes 55304 | tf_op jit(solution)/shard_map/ppermute | solution.py:422
  20.1 5.2 %collective-permute-start.4 = (bf16[72,128]{1,0:T(8,128)(2,1)}, bf16[72,128]{1,0:T(8,128)(2,1)S(1)}, u32[]{:S(2)}, u32[]{:S(2)}) collective-permute-start(bf16[72,128]{1,0:T(8,128)(2,1)} %get-tuple-element.49), channel_id=1, source_target_pairs={{0,24},{4,28},{8,16},{12,20},{16,8},{20,12},{24,0},{28,4},{1,25},{... | collective-permute-start | bytes 55304 | tf_op jit(solution)/shard_map/ppermute | solution.py:422
  20.9 20.6 %copy-start = (bf16[128,768]{1,0:T(8,128)(2,1)S(1)}, bf16[128,768]{1,0:T(8,128)(2,1)}, u32[]{:S(2)}) copy-start(bf16[128,768]{1,0:T(8,128)(2,1)} %get-tuple-element.64.refs_8_) | copy-start | bytes 589828
  21.0 11.7 %collective-permute-start.16 = (bf16[128,768]{1,0:T(8,128)(2,1)}, bf16[128,768]{1,0:T(8,128)(2,1)S(1)}, u32[]{:S(2)}, u32[]{:S(2)}) collective-permute-start(bf16[128,768]{1,0:T(8,128)(2,1)} %get-tuple-element.64.refs_8_), channel_id=1, source_target_pairs={{0,24},{4,28},{8,16},{12,20},{16,8},{20,12},{24,0},{28,4},{1,25},{... | collective-permute-start | bytes 589832 | tf_op jit(solution)/shard_map/ppermute | solution.py:422
  23.0 12.0 %collective-permute-start.15 = (bf16[128,768]{1,0:T(8,128)(2,1)}, bf16[128,768]{1,0:T(8,128)(2,1)S(1)}, u32[]{:S(2)}, u32[]{:S(2)}) collective-permute-start(bf16[128,768]{1,0:T(8,128)(2,1)} %get-tuple-element.64.refs_8_), channel_id=1, source_target_pairs={{0,16},{4,20},{8,24},{12,28},{16,0},{20,4},{24,8},{28,12},{1,17},{... | collective-permute-start | bytes 589832 | tf_op jit(solution)/shard_map/ppermute | solution.py:422
  23.4 12.4 %collective-permute-start.14 = (bf16[128,768]{1,0:T(8,128)(2,1)}, bf16[128,768]{1,0:T(8,128)(2,1)S(1)}, u32[]{:S(2)}, u32[]{:S(2)}) collective-permute-start(bf16[128,768]{1,0:T(8,128)(2,1)} %get-tuple-element.64.refs_8_), channel_id=1, source_target_pairs={{0,8},{4,12},{8,0},{12,4},{16,24},{20,28},{24,16},{28,20},{1,9},{5... | collective-permute-start | bytes 589832 | tf_op jit(solution)/shard_map/ppermute | solution.py:422
  25.3 0.7 %copy-start.8 = (bf16[72,128]{1,0:T(8,128)(2,1)S(1)}, bf16[72,128]{1,0:T(8,128)(2,1)}, u32[]{:S(2)}) copy-start(bf16[72,128]{1,0:T(8,128)(2,1)} %get-tuple-element.50.refs_0_) | copy-start | bytes 55300
  31.2 12.0 %copy-start.3 = (bf16[1024,128]{1,0:T(8,128)(2,1)S(1)}, bf16[1024,128]{1,0:T(8,128)(2,1)}, u32[]{:S(2)}) copy-start(bf16[1024,128]{1,0:T(8,128)(2,1)} %refs_8_) | copy-start | bytes 786436
  31.3 23.5 %copy-start.5 = (s32[8]{0:T(128)S(1)}, s32[8]{0:T(128)}, u32[]{:S(2)}) copy-start(s32[8]{0:T(128)} %slots_ref.1) | copy-start | bytes 100
  31.3 23.5 %copy-start.6 = (s32[8]{0:T(128)S(1)}, s32[8]{0:T(128)}, u32[]{:S(2)}) copy-start(s32[8]{0:T(128)} %starts_ref.1) | copy-start | bytes 100
  31.3 23.5 %copy-start.7 = (s32[8]{0:T(128)S(1)}, s32[8]{0:T(128)}, u32[]{:S(2)}) copy-start(s32[8]{0:T(128)} %lengths_ref.1) | copy-start | bytes 100
  31.3 4.7 %collective-permute-start.7 = (bf16[32,1024]{1,0:T(8,128)(2,1)S(1)}, bf16[32,1024]{1,0:T(8,128)(2,1)S(1)}, u32[]{:S(2)}, u32[]{:S(2)}) collective-permute-start(bf16[32,1024]{1,0:T(8,128)(2,1)S(1)} %get-tuple-element.56), channel_id=1, source_target_pairs={{0,28},{4,24},{8,20},{12,16},{16,12},{20,8},{24,4},{28,0},{1,29},{... | collective-permute-start | bytes 196616 | tf_op jit(solution)/shard_map/ppermute | solution.py:429
  31.4 6.2 %collective-permute-start.8 = (bf16[32,1024]{1,0:T(8,128)(2,1)S(1)}, bf16[32,1024]{1,0:T(8,128)(2,1)S(1)}, u32[]{:S(2)}, u32[]{:S(2)}) collective-permute-start(bf16[32,1024]{1,0:T(8,128)(2,1)S(1)} %get-tuple-element.57), channel_id=1, source_target_pairs={{0,24},{4,28},{8,16},{12,20},{16,8},{20,12},{24,0},{28,4},{1,25},{... | collective-permute-start | bytes 196616 | tf_op jit(solution)/shard_map/ppermute | solution.py:429
  32.7 6.0 %collective-permute-start.9 = (bf16[32,1024]{1,0:T(8,128)(2,1)S(1)}, bf16[32,1024]{1,0:T(8,128)(2,1)S(1)}, u32[]{:S(2)}, u32[]{:S(2)}) collective-permute-start(bf16[32,1024]{1,0:T(8,128)(2,1)S(1)} %get-tuple-element.58), channel_id=1, source_target_pairs={{0,20},{4,16},{8,28},{12,24},{16,4},{20,0},{24,12},{28,8},{1,21},{... | collective-permute-start | bytes 196616 | tf_op jit(solution)/shard_map/ppermute | solution.py:429
  35.0 5.2 %collective-permute-start.10 = (bf16[32,1024]{1,0:T(8,128)(2,1)S(1)}, bf16[32,1024]{1,0:T(8,128)(2,1)S(1)}, u32[]{:S(2)}, u32[]{:S(2)}) collective-permute-start(bf16[32,1024]{1,0:T(8,128)(2,1)S(1)} %get-tuple-element.59), channel_id=1, source_target_pairs={{0,16},{4,20},{8,24},{12,28},{16,0},{20,4},{24,8},{28,12},{1,17},{... | collective-permute-start | bytes 196616 | tf_op jit(solution)/shard_map/ppermute | solution.py:429
  35.8 4.4 %collective-permute-start.11 = (bf16[32,1024]{1,0:T(8,128)(2,1)S(1)}, bf16[32,1024]{1,0:T(8,128)(2,1)S(1)}, u32[]{:S(2)}, u32[]{:S(2)}) collective-permute-start(bf16[32,1024]{1,0:T(8,128)(2,1)S(1)} %get-tuple-element.60), channel_id=1, source_target_pairs={{0,12},{4,8},{8,4},{12,0},{16,28},{20,24},{24,20},{28,16},{1,13},{... | collective-permute-start | bytes 196616 | tf_op jit(solution)/shard_map/ppermute | solution.py:429
  36.0 5.5 %collective-permute-start.12 = (bf16[32,1024]{1,0:T(8,128)(2,1)S(1)}, bf16[32,1024]{1,0:T(8,128)(2,1)S(1)}, u32[]{:S(2)}, u32[]{:S(2)}) collective-permute-start(bf16[32,1024]{1,0:T(8,128)(2,1)S(1)} %get-tuple-element.61), channel_id=1, source_target_pairs={{0,8},{4,12},{8,0},{12,4},{16,24},{20,28},{24,16},{28,20},{1,9},{5... | collective-permute-start | bytes 196616 | tf_op jit(solution)/shard_map/ppermute | solution.py:429
  37.6 4.0 %collective-permute-start.13 = (bf16[32,1024]{1,0:T(8,128)(2,1)S(1)}, bf16[32,1024]{1,0:T(8,128)(2,1)S(1)}, u32[]{:S(2)}, u32[]{:S(2)}) collective-permute-start(bf16[32,1024]{1,0:T(8,128)(2,1)S(1)} %get-tuple-element.62), channel_id=1, source_target_pairs={{0,4},{4,0},{8,12},{12,8},{16,20},{20,16},{24,28},{28,24},{1,5},{5... | collective-permute-start | bytes 196616 | tf_op jit(solution)/shard_map/ppermute | solution.py:429
  43.0 14.0 %collective-permute-start.22 = (bf16[4,128,768]{2,1,0:T(8,128)(2,1)S(1)}, bf16[4,128,768]{2,1,0:T(8,128)(2,1)S(1)}, u32[]{:S(2)}, u32[]{:S(2)}) collective-permute-start(bf16[4,128,768]{2,1,0:T(8,128)(2,1)S(1)} %get-tuple-element.73.refs_6_), channel_id=1, source_target_pairs={{0,4},{4,0},{8,12},{12,8},{16,20},{20,16},{24,28},{28,24},{1,5},{5... | collective-permute-start | bytes 2359304 | tf_op jit(solution)/shard_map/ppermute | solution.py:426
  43.2 13.8 %collective-permute-start.23 = (bf16[1024,128]{1,0:T(8,128)(2,1)S(1)}, bf16[1024,128]{1,0:T(8,128)(2,1)S(1)}, u32[]{:S(2)}, u32[]{:S(2)}) collective-permute-start(bf16[1024,128]{1,0:T(8,128)(2,1)S(1)} %copy-done.3), channel_id=1, source_target_pairs={{0,24},{4,28},{8,16},{12,20},{16,8},{20,12},{24,0},{28,4},{1,25},{... | collective-permute-start | bytes 786440 | tf_op jit(solution)/shard_map/ppermute | solution.py:422
  44.4 5.9 %collective-permute-start.18 = (bf16[32,1024]{1,0:T(8,128)(2,1)S(1)}, bf16[32,1024]{1,0:T(8,128)(2,1)S(1)}, u32[]{:S(2)}, u32[]{:S(2)}) collective-permute-start(bf16[32,1024]{1,0:T(8,128)(2,1)S(1)} %get-tuple-element.71), channel_id=1, source_target_pairs={{0,2},{1,3},{2,0},{3,1},{4,6},{5,7},{6,4},{7,5},{8,10},{9,11},{10,... | collective-permute-start | bytes 196616 | tf_op jit(solution)/shard_map/ppermute | solution.py:432
  44.4 11.6 %collective-permute-start.17 = (bf16[64,1024]{1,0:T(8,128)(2,1)S(1)}, bf16[64,1024]{1,0:T(8,128)(2,1)S(1)}, u32[]{:S(2)}, u32[]{:S(2)}) collective-permute-start(bf16[64,1024]{1,0:T(8,128)(2,1)S(1)} %get-tuple-element.70.refs_0_), channel_id=1, source_target_pairs={{0,1},{1,0},{2,3},{3,2},{4,5},{5,4},{6,7},{7,6},{8,9},{9,8},{10,11... | collective-permute-start | bytes 393224 | tf_op jit(solution)/shard_map/ppermute | solution.py:432
  45.6 5.5 %collective-permute-start.19 = (bf16[32,1024]{1,0:T(8,128)(2,1)S(1)}, bf16[32,1024]{1,0:T(8,128)(2,1)S(1)}, u32[]{:S(2)}, u32[]{:S(2)}) collective-permute-start(bf16[32,1024]{1,0:T(8,128)(2,1)S(1)} %get-tuple-element.72), channel_id=1, source_target_pairs={{0,2},{1,3},{2,0},{3,1},{4,6},{5,7},{6,4},{7,5},{8,10},{9,11},{10,... | collective-permute-start | bytes 196616 | tf_op jit(solution)/shard_map/ppermute | solution.py:432
  50.3 5.7 %collective-permute-start.20 = (bf16[32,1024]{1,0:T(8,128)(2,1)S(1)}, bf16[32,1024]{1,0:T(8,128)(2,1)S(1)}, u32[]{:S(2)}, u32[]{:S(2)}) collective-permute-start(bf16[32,1024]{1,0:T(8,128)(2,1)S(1)} %collective-permute-done.18.refs_2_), channel_id=1, source_target_pairs={{0,1},{1,0},{2,3},{3,2},{4,5},{5,4},{6,7},{7,6},{8,9},{9,8},{10,11... | collective-permute-start | bytes 196616 | tf_op jit(solution)/shard_map/ppermute | solution.py:432
  51.1 5.9 %collective-permute-start.21 = (bf16[32,1024]{1,0:T(8,128)(2,1)S(1)}, bf16[32,1024]{1,0:T(8,128)(2,1)S(1)}, u32[]{:S(2)}, u32[]{:S(2)}) collective-permute-start(bf16[32,1024]{1,0:T(8,128)(2,1)S(1)} %collective-permute-done.19.refs_3_), channel_id=1, source_target_pairs={{0,1},{1,0},{2,3},{3,2},{4,5},{5,4},{6,7},{7,6},{8,9},{9,8},{10,11... | collective-permute-start | bytes 196616 | tf_op jit(solution)/shard_map/ppermute | solution.py:432
  58.4 7.8 %collective-permute-start.27 = (bf16[4,1024,128]{2,1,0:T(8,128)(2,1)S(1)}, bf16[4,1024,128]{2,1,0:T(8,128)(2,1)S(1)}, u32[]{:S(2)}, u32[]{:S(2)}) collective-permute-start(bf16[4,1024,128]{2,1,0:T(8,128)(2,1)S(1)} %get-tuple-element.81.refs_4_), channel_id=1, source_target_pairs={{0,4},{4,0},{8,12},{12,8},{16,20},{20,16},{24,28},{28,24},{1,5},{5... | collective-permute-start | bytes 3145736 | tf_op jit(solution)/shard_map/ppermute | solution.py:426
  58.4 6.2 %collective-permute-start.24 = (bf16[64,256]{1,0:T(8,128)(2,1)S(1)}, bf16[64,256]{1,0:T(8,128)(2,1)S(1)}, u32[]{:S(2)}, u32[]{:S(2)}) collective-permute-start(bf16[64,256]{1,0:T(8,128)(2,1)S(1)} %get-tuple-element.77), channel_id=1, source_target_pairs={{0,3},{1,2},{2,1},{3,0},{4,7},{5,6},{6,5},{7,4},{8,11},{9,10},{10,... | collective-permute-start | bytes 98312 | tf_op jit(solution)/shard_map/ppermute | solution.py:432
  61.0 4.9 %collective-permute-start.25 = (bf16[64,256]{1,0:T(8,128)(2,1)S(1)}, bf16[64,256]{1,0:T(8,128)(2,1)S(1)}, u32[]{:S(2)}, u32[]{:S(2)}) collective-permute-start(bf16[64,256]{1,0:T(8,128)(2,1)S(1)} %get-tuple-element.78), channel_id=1, source_target_pairs={{0,2},{1,3},{2,0},{3,1},{4,6},{5,7},{6,4},{7,5},{8,10},{9,11},{10,... | collective-permute-start | bytes 98312 | tf_op jit(solution)/shard_map/ppermute | solution.py:432
  62.0 4.2 %collective-permute-start.26 = (bf16[64,256]{1,0:T(8,128)(2,1)S(1)}, bf16[64,256]{1,0:T(8,128)(2,1)S(1)}, u32[]{:S(2)}, u32[]{:S(2)}) collective-permute-start(bf16[64,256]{1,0:T(8,128)(2,1)S(1)} %get-tuple-element.79), channel_id=1, source_target_pairs={{0,1},{1,0},{2,3},{3,2},{4,5},{5,4},{6,7},{7,6},{8,9},{9,8},{10,11... | collective-permute-start | bytes 98312 | tf_op jit(solution)/shard_map/ppermute | solution.py:432

commit v7 on v6

--- a/solution.py
+++ b/solution.py
@@ -215,12 +215,19 @@
     wait_all(pieces)
 
 
-def stacked(parts, pieces, stack_out, sems, base):
+def packed(parts, mix_refs, out_refs, stack_out, sems):
     part, _ = place(parts)
-    return [
-        pltpu.make_async_copy(pieces[step], stack_out.at[part ^ step], sems.at[base + step])
-        for step in range(parts)
-    ]
+    rows = mix_refs[0].shape[0]
+    blocks = mix_refs[0].shape[1] // LANES
+    copies = []
+    for step in range(parts):
+        for block in range(blocks):
+            source = mix_refs[step].at[:, pl.ds(block * LANES, LANES)]
+            target = stack_out.at[part ^ step, pl.ds(block * rows, rows)]
+            copies.append(pltpu.make_async_copy(source, target, sems.at[len(copies)]))
+        target = stack_out.at[part ^ step, pl.ds(blocks * rows, out_refs[step].shape[0])]
+        copies.append(pltpu.make_async_copy(out_refs[step], target, sems.at[len(copies)]))
+    return copies
 
 
 def conv_kernel(parts, width, conv1_ref, conv2_ref, *refs):
@@ -294,9 +301,10 @@
     windows = lax.axis_size("dp")
     copies = windows // parts
     part_refs, refs = refs[:windows][::-1], refs[windows:]
-    piece_refs, refs = refs[:parts], refs[parts:]
+    mix_refs, refs = refs[:parts], refs[parts:]
+    weight_refs, refs = refs[:parts], refs[parts:]
     rows_out, normed_out, first_out, second_out, stack_out, encoded, sems = refs
-    moves = stacked(parts, piece_refs, stack_out, sems, 0)
+    moves = packed(parts, mix_refs, weight_refs, stack_out, sems)
     start_all(moves)
     rows = W * parts
     for copy in range(copies):
@@ -333,10 +341,8 @@
     copies = windows // parts
     normed_refs, refs = refs[: 2 * group - 2], refs[2 * group - 2 :]
     stack_refs, refs = refs[:copies], refs[copies:]
-    weight_refs, refs = refs[:parts], refs[parts:]
-    outs_refs, (stack_out, pieces, sems) = refs[:group], refs[group:]
-    moves = stacked(parts, weight_refs, stack_out, sems, 0)
-    start_all(moves)
+    outs_refs, (pieces,) = refs[:group], refs[group:]
+    blocks = 3 * outs_refs[0].shape[1] // LANES
     keys = [keys_ref[pl.ds(plane ^ step, 1), :] for step in range(group)]
     valid = jnp.concatenate(keys, axis=1) > 0.5
     local = normed_refs[0].shape[0]
@@ -350,7 +356,13 @@
     for step in range(copies):
         slot = copy_index ^ step
         normed = jnp.concatenate([pieces[piece * copies + slot] for piece in range(parts)], axis=1)
-        weights = stack_refs[step][...].reshape(parts * depth, stack_refs[step].shape[2])
+        columns = [
+            jnp.concatenate(
+                [stack_refs[step][piece, block * depth : (block + 1) * depth, :] for piece in range(parts)], axis=0
+            )
+            for block in range(blocks)
+        ]
+        weights = jnp.concatenate(columns, axis=1)
         mixed += jnp.dot(normed, weights, preferred_element_type=F32)
     mixed = mixed.astype(BF16)
     width = mixed.shape[1] // 3
@@ -369,10 +381,9 @@
         context = (summed / total).astype(BF16)
         for step in range(group):
             outs_refs[step][:, at : at + HEAD_DIM] = context[step * local : (step + 1) * local]
-    wait_all(moves)
-
-
-def output_kernel(parts, windows, group, valid_ref, *refs):
+
+
+def output_kernel(parts, windows, group, base, valid_ref, *refs):
     context_refs, refs = refs[:group][::-1], refs[group:]
     stack_refs, refs = refs[: windows // parts], refs[windows // parts :]
     out_ref, context, pieces = refs
@@ -388,7 +399,7 @@
         slot = copy_index ^ step
         for piece in range(parts):
             pieces[piece * copies + slot] = jnp.dot(
-                ordered, stack_refs[step][piece], preferred_element_type=F32
+                ordered, stack_refs[step][piece, base:, :], preferred_element_type=F32
             )
     result = jnp.concatenate([pieces[d] for d in range(windows)], axis=1)
     out_ref[...] = jnp.where(valid_ref[...] > 0.5, result, 0.0).astype(BF16)
@@ -447,7 +458,7 @@
             pltpu.SMEM((streams,), jnp.int32),
             pltpu.SemaphoreType.DMA((6,)),
         ],
-        compiler_params=params(60),
+        compiler_params=params(58),
         cost_estimate=cost(1e10, 2e6),
         name="log_mel",
     )(slots, rim, audio, table, qkv_weight)
@@ -455,6 +466,9 @@
     mel_all, proj_all = lax.optimization_barrier((mel_all, proj_all))
     mel_all = [mel_all[0]] + [to_part(mel_all[step], step) for step in range(1, parts)]
     mel_all, near = lax.optimization_barrier((mel_all, near))
+    out_rows, *near = [piece.reshape(-1, LANES) for piece in [out_weight] + near]
+    mix, out_here = lax.optimization_barrier((mix, out_rows))
+    out_all = [out_rows] + near + [to_part(out_here, parts - 1)]
     mix_all = [mix] + [to_part(mix, step) for step in range(1, parts)]
 
     block = jax.ShapeDtypeStruct((local, features), BF16)
@@ -482,17 +496,20 @@
     partials = [to_window(partials[step], step) for step in reversed(range(1, windows))] + [partials[0]]
 
     half = jax.ShapeDtypeStruct((local // 2, features), BF16)
+    blocks = 3 * head_width // LANES
+    mix_rows = blocks * qkv_weight.shape[0]
+    pack = jax.ShapeDtypeStruct((parts, mix_rows + out_rows.shape[0], LANES), BF16)
     ordered, normed, *halves, stack = pl.pallas_call(
         functools.partial(norm_kernel, parts),
-        out_shape=(block, block, half, half, jax.ShapeDtypeStruct((parts,) + mix_piece.shape, BF16)),
-        in_specs=[vmem()] * windows + [anywhere()] * parts,
+        out_shape=(block, block, half, half, pack),
+        in_specs=[vmem()] * windows + [anywhere()] * (2 * parts),
         out_specs=tuple([vmem()] * 5),
-        scratch_shapes=[pltpu.VMEM((local, features), BF16), pltpu.SemaphoreType.DMA((parts,))],
+        scratch_shapes=[pltpu.VMEM((local, features), BF16), pltpu.SemaphoreType.DMA((parts * (blocks + 1),))],
         compiler_params=params(min(12 * scale, 32)),
         cost_estimate=cost(1e8, 1e6),
         name="layer_norm",
-    )(*partials, *mix_all)
-    mix_stacks = [stack] + [to_copy(stack, step) for step in range(1, copies)]
+    )(*partials, *mix_all, *out_all)
+    stacks = [stack] + [to_copy(stack, step) for step in range(1, copies)]
     regrouped, keys, valid = pl.pallas_call(
         functools.partial(mask_kernel, windows, group),
         out_shape=(
@@ -506,36 +523,30 @@
         cost_estimate=cost(1e8, 1e6),
         name="mask",
     )(slots, starts, lengths, ordered)
-    normed, out_here = lax.optimization_barrier((normed, out_weight))
     by_plane = {0: [normed], 1: [to_plane(normed, 1)]}
     for step in range(2, group):
         high = 1 << (step.bit_length() - 1)
         source = halves if step == high else by_plane[high]
         by_plane[step] = [to_plane(piece, high if step == high else step - high) for piece in source]
     normed = [piece for step in range(group) for piece in by_plane[step]]
-    out_all = [out_here] + near + [to_part(out_here, parts - 1)]
-
-    *context, stack = pl.pallas_call(
+
+    context = pl.pallas_call(
         functools.partial(attention_kernel, parts, windows, group),
-        out_shape=tuple(
-            [jax.ShapeDtypeStruct((local, head_width), BF16)] * group
-            + [jax.ShapeDtypeStruct((parts,) + out_weight.shape, BF16)]
-        ),
-        in_specs=[vmem()] * (1 + len(normed) + copies) + [anywhere()] * parts,
-        out_specs=tuple([vmem()] * (group + 1)),
-        scratch_shapes=[
-            pltpu.VMEM((windows, group * local, qkv_weight.shape[0]), BF16),
-            pltpu.SemaphoreType.DMA((parts,)),
-        ],
+        out_shape=tuple([jax.ShapeDtypeStruct((local, head_width), BF16)] * group),
+        in_specs=[vmem()] * (1 + len(normed) + copies),
+        out_specs=tuple([vmem()] * group),
+        scratch_shapes=[pltpu.VMEM((windows, group * local, qkv_weight.shape[0]), BF16)],
         compiler_params=params(min(16 * scale, 48)),
         cost_estimate=cost(1e9, 2e6),
         name="attention",
-    )(keys, *normed, *mix_stacks, *out_all)
+    )(keys, *normed, *stacks)
     context = [to_plane(context[step], step) for step in reversed(range(1, group))] + [context[0]]
-    out_stacks = [stack] + [to_copy(stack, step) for step in range(1, copies)]
+    if out_rows.shape != out_weight.shape:
+        stacks = [stack[:, mix_rows:].reshape((parts,) + out_weight.shape) for stack in stacks]
+        mix_rows = 0
 
     attended = pl.pallas_call(
-        functools.partial(output_kernel, parts, windows, group),
+        functools.partial(output_kernel, parts, windows, group, mix_rows),
         out_shape=block,
         in_specs=[vmem()] * (1 + group + copies),
         out_specs=vmem(),
@@ -546,7 +557,7 @@
         compiler_params=params(min(12 * scale, 32)),
         cost_estimate=cost(1e8, 3e6),
         name="output",
-    )(valid, *context, *out_stacks)
+    )(valid, *context, *stacks)
     shape = (1, windows, 1, W, features)
     return (regrouped.reshape(shape), attended.reshape(shape))
 

time: 67.6 us -> 70 us (1.036)
  waiting for transfers between devices: 12.9 us -> 16.4 us
    ppermute x9, waiting for transfers between devices: 0.77 us -> 3.27 us  [to_part(): return lax.ppermute(block, 'dp', pairs)]
    ppermute x8, waiting for transfers between devices: 7.95 us -> 9.24 us  [to_plane(): return lax.ppermute(block, 'seq', [(i, i ^ step) for i in range(group)])]
    ppermute x8, starting transfers between devices: 11.1 us -> 9.86 us  [to_plane(): return lax.ppermute(block, 'seq', [(i, i ^ step) for i in range(group)])]
    ppermute x9, starting transfers between devices: 13.4 us -> 14.2 us  [to_part(): return lax.ppermute(block, 'dp', pairs)]
  transfers between devices with their start and end apart: 28 -> 27, of which waited for: 11 -> 11; matrix products, arithmetic and copies ran while one was open for 1% -> 1% of each run, Pallas kernels for 17% -> 17%
where the time goes in v7:
time: 70 us; the launch traced here: 69.7 us
  starting transfers between devices  35.4 us (51%)
  waiting for transfers between devices  16.4 us (23%)
  Pallas kernels  14.9 us (21%)
  local copies, waits for them, and re-layouts  2.13 us (3%)
  between operations  0.78 us (1%)
    ppermute x9, starting transfers between devices, to_part(): return lax.ppermute(block, 'dp', pairs)  14.2 us
    ppermute x8, starting transfers between devices, to_plane(): return lax.ppermute(block, 'seq', [(i, i ^ step) for i in range(group)])  9.86 us
    ppermute x8, waiting for transfers between devices, to_plane(): return lax.ppermute(block, 'seq', [(i, i ^ step) for i in range(group)])  9.24 us
    ppermute x7, starting transfers between devices, to_window(): return lax.ppermute(block, 'dp', [(i, i ^ step) for i in range(windows)])  5.98 us
    pallas_call x1, Pallas kernels, on_device(): pl.pallas_call(functools.partial(conv_kernel, parts, width), out_shape=tu...  5.23 us
    pallas_call x1, Pallas kernels, on_device(): pl.pallas_call(functools.partial(mel_kernel, parts, group), out_shape=tup...  5.13 us
    ppermute x1, starting transfers between devices, on_device(): rim = lax.ppermute(audio[:, audio.shape[1] - RIM:], ('dp', 'seq'), route)  4.76 us
    ppermute x7, waiting for transfers between devices, to_window(): return lax.ppermute(block, 'dp', [(i, i ^ step) for i in range(windows)])  3.93 us
  transfers between devices with their start and end apart: 27, of which 11 were waited for; matrix products, arithmetic and copies ran while one was open for 1% of the time, Pallas kernels for 17%

profile of v7, /device:TPU:0, one launch (start us, length us, event | category | flops | bytes accessed | tf_op | source)
XLA Modules:
  0.0 69.7 jit_solution(3079591174405542)
XLA Ops:
  0.6 0.5 collective-permute-start.1
  1.1 0.8 %slice.3 = f32[8,1024]{1,0:T(8,128)S(1)} slice(f32[8,5120]{1,0:T(8,128)} %audio_ref.1), slice={[0:8], [4096:5120]} | slice | bytes 65536 | tf_op jit(solution)/shard_map/slice | solution.py:429
  1.9 4.8 %collective-permute-start = (f32[8,1024]{1,0:T(8,128)S(1)}, f32[8,1024]{1,0:T(8,128)S(1)}, u32[]{:S(2)}, u32[]{:S(2)}) collective-permute-start(f32[8,1024]{1,0:T(8,128)S(1)} %slice.3), channel_id=1, source_target_pairs={{0,1},{1,2},{2,3},{3,4},{4,5},{5,6},{6,7},{7,8},{8,9},{9,10},{10,1... | collective-permute-start | bytes 98312 | tf_op jit(solution)/shard_map/ppermute | solution.py:429
  6.7 1.6 %collective-permute-start.6 = (bf16[1024,128]{1,0:T(8,128)(2,1)}, bf16[1024,128]{1,0:T(8,128)(2,1)S(1)}, u32[]{:S(2)}, u32[]{:S(2)}) collective-permute-start(bf16[1024,128]{1,0:T(8,128)(2,1)} %refs_12_.1), channel_id=1, source_target_pairs={{0,16},{4,20},{8,24},{12,28},{16,0},{20,4},{24,8},{28,12},{1,17},{... | collective-permute-start | bytes 786440 | tf_op jit(solution)/shard_map/ppermute | solution.py:433
  8.3 1.5 %collective-permute-start.5 = (bf16[1024,128]{1,0:T(8,128)(2,1)}, bf16[1024,128]{1,0:T(8,128)(2,1)S(1)}, u32[]{:S(2)}, u32[]{:S(2)}) collective-permute-start(bf16[1024,128]{1,0:T(8,128)(2,1)} %refs_12_.1), channel_id=1, source_target_pairs={{0,8},{4,12},{8,0},{12,4},{16,24},{20,28},{24,16},{28,20},{1,9},{5... | collective-permute-start | bytes 786440 | tf_op jit(solution)/shard_map/ppermute | solution.py:433
  9.8 0.6 copy-done.9
  10.4 5.1 %log_mel.1 = (bf16[72,128]{1,0:T(8,128)(2,1)}, bf16[72,128]{1,0:T(8,128)(2,1)}, bf16[72,128]{1,0:T(8,128)(2,1)}, bf16[72,128]{1,0:T(8,128)(2,1)}, bf16[128,768]{1,0:T(8,128)(2,1)}) custom-call(s32[8]{0:T(128)} %slots_ref.1, f32[8,1024]{1,0:T(8,128)} %copy-done.9, f32[8,5120]{1,0:T(8,128)} %audio_ref.1, f32[512,640]{1,0:T(8,128)} %constant.2.clone.table_ref, ...), custom_call_target="tpu_custom_call" | custom-call | flops 10000000000 | bytes 2000000 | tf_op jit(solution)/shard_map/log_mel/pallas_call | solution.py:449
  15.5 2.9 %collective-permute-start.2 = (bf16[72,128]{1,0:T(8,128)(2,1)}, bf16[72,128]{1,0:T(8,128)(2,1)S(1)}, u32[]{:S(2)}, u32[]{:S(2)}) collective-permute-start(bf16[72,128]{1,0:T(8,128)(2,1)} %get-tuple-element.46), channel_id=1, source_target_pairs={{0,8},{4,12},{8,0},{12,4},{16,24},{20,28},{24,16},{28,20},{1,9},{5... | collective-permute-start | bytes 55304 | tf_op jit(solution)/shard_map/ppermute | solution.py:433
  18.5 1.7 %collective-permute-start.3 = (bf16[72,128]{1,0:T(8,128)(2,1)}, bf16[72,128]{1,0:T(8,128)(2,1)S(1)}, u32[]{:S(2)}, u32[]{:S(2)}) collective-permute-start(bf16[72,128]{1,0:T(8,128)(2,1)} %get-tuple-element.47), channel_id=1, source_target_pairs={{0,16},{4,20},{8,24},{12,28},{16,0},{20,4},{24,8},{28,12},{1,17},{... | collective-permute-start | bytes 55304 | tf_op jit(solution)/shard_map/ppermute | solution.py:433
  20.2 0.9 %collective-permute-start.4 = (bf16[72,128]{1,0:T(8,128)(2,1)}, bf16[72,128]{1,0:T(8,128)(2,1)S(1)}, u32[]{:S(2)}, u32[]{:S(2)}) collective-permute-start(bf16[72,128]{1,0:T(8,128)(2,1)} %get-tuple-element.48), channel_id=1, source_target_pairs={{0,24},{4,28},{8,16},{12,20},{16,8},{20,12},{24,0},{28,4},{1,25},{... | collective-permute-start | bytes 55304 | tf_op jit(solution)/shard_map/ppermute | solution.py:433
  21.1 2.1 %collective-permute-start.17 = (bf16[1024,128]{1,0:T(8,128)(2,1)S(1)}, bf16[1024,128]{1,0:T(8,128)(2,1)S(1)}, u32[]{:S(2)}, u32[]{:S(2)}) collective-permute-start(bf16[1024,128]{1,0:T(8,128)(2,1)S(1)} %copy-done), channel_id=1, source_target_pairs={{0,24},{4,28},{8,16},{12,20},{16,8},{20,12},{24,0},{28,4},{1,25},{... | collective-permute-start | bytes 786440 | tf_op jit(solution)/shard_map/ppermute | solution.py:433
  23.2 0.9 %collective-permute-start.16 = (bf16[128,768]{1,0:T(8,128)(2,1)}, bf16[128,768]{1,0:T(8,128)(2,1)S(1)}, u32[]{:S(2)}, u32[]{:S(2)}) collective-permute-start(bf16[128,768]{1,0:T(8,128)(2,1)} %get-tuple-element.64.refs_8_), channel_id=1, source_target_pairs={{0,24},{4,28},{8,16},{12,20},{16,8},{20,12},{24,0},{28,4},{1,25},{... | collective-permute-start | bytes 589832 | tf_op jit(solution)/shard_map/ppermute | solution.py:433
  24.1 2.0 %collective-permute-start.15 = (bf16[128,768]{1,0:T(8,128)(2,1)}, bf16[128,768]{1,0:T(8,128)(2,1)S(1)}, u32[]{:S(2)}, u32[]{:S(2)}) collective-permute-start(bf16[128,768]{1,0:T(8,128)(2,1)} %get-tuple-element.64.refs_8_), channel_id=1, source_target_pairs={{0,16},{4,20},{8,24},{12,28},{16,0},{20,4},{24,8},{28,12},{1,17},{... | collective-permute-start | bytes 589832 | tf_op jit(solution)/shard_map/ppermute | solution.py:433
  26.1 0.6 collective-permute-start.14
  26.7 0.0 copy-start.8
  26.7 0.7 %copy-done.8 = bf16[72,128]{1,0:T(8,128)(2,1)S(1)} copy-done((bf16[72,128]{1,0:T(8,128)(2,1)S(1)}, bf16[72,128]{1,0:T(8,128)(2,1)}, u32[]{:S(2)}) %copy-start.8) | copy-done | bytes 18456
  27.4 5.2 %conv.1 = (bf16[32,1024]{1,0:T(8,128)(2,1)S(1)}, bf16[32,1024]{1,0:T(8,128)(2,1)S(1)}, bf16[32,1024]{1,0:T(8,128)(2,1)S(1)}, bf16[32,1024]{1,0:T(8,128)(2,1)S(1)...) custom-call(bf16[9,256]{1,0:T(8,128)(2,1)S(1)} %copy-done.4, ...), custom_call_target="tpu_custom_call" | custom-call | flops 2000000000 | bytes 4000000 | tf_op jit(solution)/shard_map/conv/pallas_call | solution.py:475
  32.7 0.1 collective-permute-start.7
  32.8 2.6 %collective-permute-done.16.refs_11_ = bf16[128,768]{1,0:T(8,128)(2,1)S(1)} collective-permute-done((bf16[128,768]{1,0:T(8,128)(2,1)}, bf16[128,768]{1,0:T(8,128)(2,1)S(1)}, u32[]{:S(2)}, u32[]{:S(2)}) %collective-permute-start.16) | collective-permute-done | bytes 196640 | tf_op jit(solution)/shard_map/ppermute | solution.py:433
  35.4 2.2 %collective-permute-start.8 = (bf16[32,1024]{1,0:T(8,128)(2,1)S(1)}, bf16[32,1024]{1,0:T(8,128)(2,1)S(1)}, u32[]{:S(2)}, u32[]{:S(2)}) collective-permute-start(bf16[32,1024]{1,0:T(8,128)(2,1)S(1)} %get-tuple-element.56), channel_id=1, source_target_pairs={{0,24},{4,28},{8,16},{12,20},{16,8},{20,12},{24,0},{28,4},{1,25},{... | collective-permute-start | bytes 196616 | tf_op jit(solution)/shard_map/ppermute | solution.py:440
  37.6 0.6 collective-permute-done.15.refs_10_
  38.2 0.8 %collective-permute-start.9 = (bf16[32,1024]{1,0:T(8,128)(2,1)S(1)}, bf16[32,1024]{1,0:T(8,128)(2,1)S(1)}, u32[]{:S(2)}, u32[]{:S(2)}) collective-permute-start(bf16[32,1024]{1,0:T(8,128)(2,1)S(1)} %get-tuple-element.57), channel_id=1, source_target_pairs={{0,20},{4,16},{8,28},{12,24},{16,4},{20,0},{24,12},{28,8},{1,21},{... | collective-permute-start | bytes 196616 | tf_op jit(solution)/shard_map/ppermute | solution.py:440
  39.0 0.8 %collective-permute-start.10 = (bf16[32,1024]{1,0:T(8,128)(2,1)S(1)}, bf16[32,1024]{1,0:T(8,128)(2,1)S(1)}, u32[]{:S(2)}, u32[]{:S(2)}) collective-permute-start(bf16[32,1024]{1,0:T(8,128)(2,1)S(1)} %get-tuple-element.58), channel_id=1, source_target_pairs={{0,16},{4,20},{8,24},{12,28},{16,0},{20,4},{24,8},{28,12},{1,17},{... | collective-permute-start | bytes 196616 | tf_op jit(solution)/shard_map/ppermute | solution.py:440
  39.8 1.8 %collective-permute-start.11 = (bf16[32,1024]{1,0:T(8,128)(2,1)S(1)}, bf16[32,1024]{1,0:T(8,128)(2,1)S(1)}, u32[]{:S(2)}, u32[]{:S(2)}) collective-permute-start(bf16[32,1024]{1,0:T(8,128)(2,1)S(1)} %get-tuple-element.59), channel_id=1, source_target_pairs={{0,12},{4,8},{8,4},{12,0},{16,28},{20,24},{24,20},{28,16},{1,13},{... | collective-permute-start | bytes 196616 | tf_op jit(solution)/shard_map/ppermute | solution.py:440
  41.5 0.3 collective-permute-start.12
  41.8 0.1 collective-permute-start.13
  42.0 0.5 collective-permute-done.9.refs_2_
  42.5 1.5 %collective-permute-done.10.refs_3_ = bf16[32,1024]{1,0:T(8,128)(2,1)S(1)} collective-permute-done((bf16[32,1024]{1,0:T(8,128)(2,1)S(1)}, bf16[32,1024]{1,0:T(8,128)(2,1)S(1)}, u32[]{:S(2)}, u32[]{:S(2)}) %collective-permute-start.10) | collective-permute-done | bytes 65568 | tf_op jit(solution)/shard_map/ppermute | solution.py:440
  44.0 0.0 collective-permute-done.11.refs_4_
  44.0 1.9 %collective-permute-done.12.refs_5_ = bf16[32,1024]{1,0:T(8,128)(2,1)S(1)} collective-permute-done((bf16[32,1024]{1,0:T(8,128)(2,1)S(1)}, bf16[32,1024]{1,0:T(8,128)(2,1)S(1)}, u32[]{:S(2)}, u32[]{:S(2)}) %collective-permute-start.12) | collective-permute-done | bytes 65568 | tf_op jit(solution)/shard_map/ppermute | solution.py:440
  45.9 1.0 %layer_norm.1 = (bf16[64,1024]{1,0:T(8,128)(2,1)S(1)}, bf16[64,1024]{1,0:T(8,128)(2,1)S(1)}, bf16[32,1024]{1,0:T(8,128)(2,1)S(1)}, bf16[32,1024]{1,0:T(8,128)(2,1)S(1)}, bf16[4,1792,128]{2,1,0:T(8,128)(2,1)S(1)}) custom-call(bf16[32,1024]{1,0:T(8,128)(2,1)S(1)} %collective-permute-done.7.refs_0_, bf16[32,1024]{1,0:T(8,128)(2,1)S(1)} %collective-permute-done.8.refs_1_, ...), custom_call_target="tpu_custom_call" | custom-call | flops 100000000 | bytes 1000000 | tf_op jit(solution)/shard_map/layer_norm/pallas_call | solution.py:502
  46.9 0.1 collective-permute-start.23
  46.9 1.2 %collective-permute-start.19 = (bf16[32,1024]{1,0:T(8,128)(2,1)S(1)}, bf16[32,1024]{1,0:T(8,128)(2,1)S(1)}, u32[]{:S(2)}, u32[]{:S(2)}) collective-permute-start(bf16[32,1024]{1,0:T(8,128)(2,1)S(1)} %get-tuple-element.73), channel_id=1, source_target_pairs={{0,2},{1,3},{2,0},{3,1},{4,6},{5,7},{6,4},{7,5},{8,10},{9,11},{10,... | collective-permute-start | bytes 196616 | tf_op jit(solution)/shard_map/ppermute | solution.py:443
  48.1 0.5 collective-permute-start.18
  48.5 1.5 %collective-permute-start.20 = (bf16[32,1024]{1,0:T(8,128)(2,1)S(1)}, bf16[32,1024]{1,0:T(8,128)(2,1)S(1)}, u32[]{:S(2)}, u32[]{:S(2)}) collective-permute-start(bf16[32,1024]{1,0:T(8,128)(2,1)S(1)} %get-tuple-element.74), channel_id=1, source_target_pairs={{0,2},{1,3},{2,0},{3,1},{4,6},{5,7},{6,4},{7,5},{8,10},{9,11},{10,... | collective-permute-start | bytes 196616 | tf_op jit(solution)/shard_map/ppermute | solution.py:443
  50.0 3.4 %collective-permute-done.19.refs_2_ = bf16[32,1024]{1,0:T(8,128)(2,1)S(1)} collective-permute-done((bf16[32,1024]{1,0:T(8,128)(2,1)S(1)}, bf16[32,1024]{1,0:T(8,128)(2,1)S(1)}, u32[]{:S(2)}, u32[]{:S(2)}) %collective-permute-start.19) | collective-permute-done | bytes 65568 | tf_op jit(solution)/shard_map/ppermute | solution.py:443
  53.4 1.9 %collective-permute-done.20.refs_3_ = bf16[32,1024]{1,0:T(8,128)(2,1)S(1)} collective-permute-done((bf16[32,1024]{1,0:T(8,128)(2,1)S(1)}, bf16[32,1024]{1,0:T(8,128)(2,1)S(1)}, u32[]{:S(2)}, u32[]{:S(2)}) %collective-permute-start.20) | collective-permute-done | bytes 65568 | tf_op jit(solution)/shard_map/ppermute | solution.py:443
  55.3 2.3 %collective-permute-start.22 = (bf16[32,1024]{1,0:T(8,128)(2,1)S(1)}, bf16[32,1024]{1,0:T(8,128)(2,1)S(1)}, u32[]{:S(2)}, u32[]{:S(2)}) collective-permute-start(bf16[32,1024]{1,0:T(8,128)(2,1)S(1)} %collective-permute-done.20.refs_3_), channel_id=1, source_target_pairs={{0,1},{1,0},{2,3},{3,2},{4,5},{5,4},{6,7},{7,6},{8,9},{9,8},{10,11... | collective-permute-start | bytes 196616 | tf_op jit(solution)/shard_map/ppermute | solution.py:443
  57.6 1.3 %mask.1 = (bf16[64,1024]{1,0:T(8,128)(2,1)}, f32[4,64]{1,0:T(4,128)S(1)}, f32[64,1]{1,0:T(8,128)S(1)}) custom-call(s32[8]{0:T(128)S(1)} %copy-done.5, s32[8]{0:T(128)S(1)} %copy-done.6, s32[8]{0:T(128)S(1)} %copy-done.7, bf16[64,1024]{1,0:T(8,128)(2,1)S(1)} %get-tuple-element.68.rows_ref), custom_call_target="tpu_custom_call" | custom-call | flops 100000000 | bytes 1000000 | tf_op jit(solution)/shard_map/mask/pallas_call | solution.py:513
  58.9 1.0 %collective-permute-done.22.refs_5_ = bf16[32,1024]{1,0:T(8,128)(2,1)S(1)} collective-permute-done((bf16[32,1024]{1,0:T(8,128)(2,1)S(1)}, bf16[32,1024]{1,0:T(8,128)(2,1)S(1)}, u32[]{:S(2)}, u32[]{:S(2)}) %collective-permute-start.22) | collective-permute-done | bytes 65568 | tf_op jit(solution)/shard_map/ppermute | solution.py:443
  59.8 1.3 %attention.1 = (bf16[64,256]{1,0:T(8,128)(2,1)S(1)}, bf16[64,256]{1,0:T(8,128)(2,1)S(1)}, bf16[64,256]{1,0:T(8,128)(2,1)S(1)}, bf16[64,256]{1,0:T(8,128)(2,1)S(1)}) custom-call(f32[4,64]{1,0:T(4,128)S(1)} %get-tuple-element.71.keys_ref, bf16[64,1024]{1,0:T(8,128)(2,1)S(1)} %get-tuple-element.72.refs_0_, ...), custom_call_target="tpu_custom_call" | custom-call | flops 1000000000 | bytes 2000000 | tf_op jit(solution)/shard_map/attention/pallas_call | solution.py:533
  61.1 2.1 %collective-permute-start.24 = (bf16[64,256]{1,0:T(8,128)(2,1)S(1)}, bf16[64,256]{1,0:T(8,128)(2,1)S(1)}, u32[]{:S(2)}, u32[]{:S(2)}) collective-permute-start(bf16[64,256]{1,0:T(8,128)(2,1)S(1)} %get-tuple-element.76), channel_id=1, source_target_pairs={{0,3},{1,2},{2,1},{3,0},{4,7},{5,6},{6,5},{7,4},{8,11},{9,10},{10,... | collective-permute-start | bytes 98312 | tf_op jit(solution)/shard_map/ppermute | solution.py:443
  63.2 1.5 %collective-permute-start.25 = (bf16[64,256]{1,0:T(8,128)(2,1)S(1)}, bf16[64,256]{1,0:T(8,128)(2,1)S(1)}, u32[]{:S(2)}, u32[]{:S(2)}) collective-permute-start(bf16[64,256]{1,0:T(8,128)(2,1)S(1)} %get-tuple-element.77), channel_id=1, source_target_pairs={{0,2},{1,3},{2,0},{3,1},{4,6},{5,7},{6,4},{7,5},{8,10},{9,11},{10,... | collective-permute-start | bytes 98312 | tf_op jit(solution)/shard_map/ppermute | solution.py:443
  64.7 0.9 %collective-permute-start.26 = (bf16[64,256]{1,0:T(8,128)(2,1)S(1)}, bf16[64,256]{1,0:T(8,128)(2,1)S(1)}, u32[]{:S(2)}, u32[]{:S(2)}) collective-permute-start(bf16[64,256]{1,0:T(8,128)(2,1)S(1)} %get-tuple-element.78), channel_id=1, source_target_pairs={{0,1},{1,0},{2,3},{3,2},{4,5},{5,4},{6,7},{7,6},{8,9},{9,8},{10,11... | collective-permute-start | bytes 98312 | tf_op jit(solution)/shard_map/ppermute | solution.py:443
  65.6 1.3 %collective-permute-done.24.refs_0_ = bf16[64,256]{1,0:T(8,128)(2,1)S(1)} collective-permute-done((bf16[64,256]{1,0:T(8,128)(2,1)S(1)}, bf16[64,256]{1,0:T(8,128)(2,1)S(1)}, u32[]{:S(2)}, u32[]{:S(2)}) %collective-permute-start.24) | collective-permute-done | bytes 32800 | tf_op jit(solution)/shard_map/ppermute | solution.py:443
  66.9 1.1 %collective-permute-done.25.refs_1_ = bf16[64,256]{1,0:T(8,128)(2,1)S(1)} collective-permute-done((bf16[64,256]{1,0:T(8,128)(2,1)S(1)}, bf16[64,256]{1,0:T(8,128)(2,1)S(1)}, u32[]{:S(2)}, u32[]{:S(2)}) %collective-permute-start.25) | collective-permute-done | bytes 32800 | tf_op jit(solution)/shard_map/ppermute | solution.py:443
  68.0 0.6 collective-permute-done.26.refs_2_
  68.6 1.1 %output.1 = bf16[64,1024]{1,0:T(8,128)(2,1)} custom-call(f32[64,1]{1,0:T(8,128)S(1)} %get-tuple-element.70.valid_ref, bf16[64,256]{1,0:T(8,128)(2,1)S(1)} %collective-permute-done.24.refs_0_, bf16[64,256]{1,0:T(8,128)(2,1)S(1)} %collective-permute-done.25.refs_1_, bf16[64,256]{1,0:T(8,128)(2,1)S(1)} %collective-permute-done.26.refs_2_, ...), custom_call_target="tpu_custom_call" | custom-call | flops 100000000 | bytes 3000000 | tf_op jit(solution)/shard_map/output/pallas_call | solution.py:548
  (33 shorter events, 0.1 us)
Async XLA Ops:
  0.6 14.9 %collective-permute-start.1 = (bf16[640,1024]{1,0:T(8,128)(2,1)}, bf16[640,1024]{1,0:T(8,128)(2,1)S(1)}, u32[]{:S(2)}, u32[]{:S(2)}) collective-permute-start(bf16[640,1024]{1,0:T(8,128)(2,1)} %refs_4_), channel_id=1, source_target_pairs={{0,4},{4,0},{8,12},{12,8},{16,20},{20,16},{24,28},{28,24},{1,5},{5... | collective-permute-start | bytes 3932168 | tf_op jit(solution)/shard_map/ppermute | solution.py:437
  1.9 19.2 %copy-start = (bf16[1024,128]{1,0:T(8,128)(2,1)S(1)}, bf16[1024,128]{1,0:T(8,128)(2,1)}, u32[]{:S(2)}) copy-start(bf16[1024,128]{1,0:T(8,128)(2,1)} %refs_12_.1) | copy-start | bytes 786436
  1.9 24.8 %copy-start.2 = (bf16[640,1024]{1,0:T(8,128)(2,1)S(1)}, bf16[640,1024]{1,0:T(8,128)(2,1)}, u32[]{:S(2)}) copy-start(bf16[640,1024]{1,0:T(8,128)(2,1)} %refs_4_) | copy-start | bytes 3932164
  1.9 24.8 %copy-start.3 = (bf16[2304,256]{1,0:T(8,128)(2,1)S(1)}, bf16[2304,256]{1,0:T(8,128)(2,1)}, u32[]{:S(2)}) copy-start(bf16[2304,256]{1,0:T(8,128)(2,1)} %conv2_ref.1) | copy-start | bytes 3538948
  1.9 24.8 %copy-start.4 = (bf16[9,256]{1,0:T(8,128)(2,1)S(1)}, bf16[9,256]{1,0:T(8,128)(2,1)}, u32[]{:S(2)}) copy-start(bf16[9,256]{1,0:T(8,128)(2,1)} %conv1_ref.1) | copy-start | bytes 13828
  1.9 7.8 %collective-permute-start = (f32[8,1024]{1,0:T(8,128)S(1)}, f32[8,1024]{1,0:T(8,128)S(1)}, u32[]{:S(2)}, u32[]{:S(2)}) collective-permute-start(f32[8,1024]{1,0:T(8,128)S(1)} %slice.3), channel_id=1, source_target_pairs={{0,1},{1,2},{2,3},{3,4},{4,5},{5,6},{6,7},{7,8},{8,9},{9,10},{10,1... | collective-permute-start | bytes 98312 | tf_op jit(solution)/shard_map/ppermute | solution.py:429
  6.7 14.4 %collective-permute-start.6 = (bf16[1024,128]{1,0:T(8,128)(2,1)}, bf16[1024,128]{1,0:T(8,128)(2,1)S(1)}, u32[]{:S(2)}, u32[]{:S(2)}) collective-permute-start(bf16[1024,128]{1,0:T(8,128)(2,1)} %refs_12_.1), channel_id=1, source_target_pairs={{0,16},{4,20},{8,24},{12,28},{16,0},{20,4},{24,8},{28,12},{1,17},{... | collective-permute-start | bytes 786440 | tf_op jit(solution)/shard_map/ppermute | solution.py:433
  8.3 14.9 %collective-permute-start.5 = (bf16[1024,128]{1,0:T(8,128)(2,1)}, bf16[1024,128]{1,0:T(8,128)(2,1)S(1)}, u32[]{:S(2)}, u32[]{:S(2)}) collective-permute-start(bf16[1024,128]{1,0:T(8,128)(2,1)} %refs_12_.1), channel_id=1, source_target_pairs={{0,8},{4,12},{8,0},{12,4},{16,24},{20,28},{24,16},{28,20},{1,9},{5... | collective-permute-start | bytes 786440 | tf_op jit(solution)/shard_map/ppermute | solution.py:433
  9.8 0.6 copy-start.9
  15.5 8.5 %collective-permute-start.2 = (bf16[72,128]{1,0:T(8,128)(2,1)}, bf16[72,128]{1,0:T(8,128)(2,1)S(1)}, u32[]{:S(2)}, u32[]{:S(2)}) collective-permute-start(bf16[72,128]{1,0:T(8,128)(2,1)} %get-tuple-element.46), channel_id=1, source_target_pairs={{0,8},{4,12},{8,0},{12,4},{16,24},{20,28},{24,16},{28,20},{1,9},{5... | collective-permute-start | bytes 55304 | tf_op jit(solution)/shard_map/ppermute | solution.py:433
  18.5 7.6 %collective-permute-start.3 = (bf16[72,128]{1,0:T(8,128)(2,1)}, bf16[72,128]{1,0:T(8,128)(2,1)S(1)}, u32[]{:S(2)}, u32[]{:S(2)}) collective-permute-start(bf16[72,128]{1,0:T(8,128)(2,1)} %get-tuple-element.47), channel_id=1, source_target_pairs={{0,16},{4,20},{8,24},{12,28},{16,0},{20,4},{24,8},{28,12},{1,17},{... | collective-permute-start | bytes 55304 | tf_op jit(solution)/shard_map/ppermute | solution.py:433
  20.2 6.5 %collective-permute-start.4 = (bf16[72,128]{1,0:T(8,128)(2,1)}, bf16[72,128]{1,0:T(8,128)(2,1)S(1)}, u32[]{:S(2)}, u32[]{:S(2)}) collective-permute-start(bf16[72,128]{1,0:T(8,128)(2,1)} %get-tuple-element.48), channel_id=1, source_target_pairs={{0,24},{4,28},{8,16},{12,20},{16,8},{20,12},{24,0},{28,4},{1,25},{... | collective-permute-start | bytes 55304 | tf_op jit(solution)/shard_map/ppermute | solution.py:433
  21.1 24.8 %copy-start.1 = (bf16[128,768]{1,0:T(8,128)(2,1)S(1)}, bf16[128,768]{1,0:T(8,128)(2,1)}, u32[]{:S(2)}) copy-start(bf16[128,768]{1,0:T(8,128)(2,1)} %get-tuple-element.64.refs_8_) | copy-start | bytes 589828
  21.1 18.7 %collective-permute-start.17 = (bf16[1024,128]{1,0:T(8,128)(2,1)S(1)}, bf16[1024,128]{1,0:T(8,128)(2,1)S(1)}, u32[]{:S(2)}, u32[]{:S(2)}) collective-permute-start(bf16[1024,128]{1,0:T(8,128)(2,1)S(1)} %copy-done), channel_id=1, source_target_pairs={{0,24},{4,28},{8,16},{12,20},{16,8},{20,12},{24,0},{28,4},{1,25},{... | collective-permute-start | bytes 786440 | tf_op jit(solution)/shard_map/ppermute | solution.py:433
  23.2 12.2 %collective-permute-start.16 = (bf16[128,768]{1,0:T(8,128)(2,1)}, bf16[128,768]{1,0:T(8,128)(2,1)S(1)}, u32[]{:S(2)}, u32[]{:S(2)}) collective-permute-start(bf16[128,768]{1,0:T(8,128)(2,1)} %get-tuple-element.64.refs_8_), channel_id=1, source_target_pairs={{0,24},{4,28},{8,16},{12,20},{16,8},{20,12},{24,0},{28,4},{1,25},{... | collective-permute-start | bytes 589832 | tf_op jit(solution)/shard_map/ppermute | solution.py:433
  24.1 14.1 %collective-permute-start.15 = (bf16[128,768]{1,0:T(8,128)(2,1)}, bf16[128,768]{1,0:T(8,128)(2,1)S(1)}, u32[]{:S(2)}, u32[]{:S(2)}) collective-permute-start(bf16[128,768]{1,0:T(8,128)(2,1)} %get-tuple-element.64.refs_8_), channel_id=1, source_target_pairs={{0,16},{4,20},{8,24},{12,28},{16,0},{20,4},{24,8},{28,12},{1,17},{... | collective-permute-start | bytes 589832 | tf_op jit(solution)/shard_map/ppermute | solution.py:433
  26.1 12.9 %collective-permute-start.14 = (bf16[128,768]{1,0:T(8,128)(2,1)}, bf16[128,768]{1,0:T(8,128)(2,1)S(1)}, u32[]{:S(2)}, u32[]{:S(2)}) collective-permute-start(bf16[128,768]{1,0:T(8,128)(2,1)} %get-tuple-element.64.refs_8_), channel_id=1, source_target_pairs={{0,8},{4,12},{8,0},{12,4},{16,24},{20,28},{24,16},{28,20},{1,9},{5... | collective-permute-start | bytes 589832 | tf_op jit(solution)/shard_map/ppermute | solution.py:433
  26.7 0.7 %copy-start.8 = (bf16[72,128]{1,0:T(8,128)(2,1)S(1)}, bf16[72,128]{1,0:T(8,128)(2,1)}, u32[]{:S(2)}) copy-start(bf16[72,128]{1,0:T(8,128)(2,1)} %get-tuple-element.49.refs_0_) | copy-start | bytes 55300
  32.7 24.9 %copy-start.5 = (s32[8]{0:T(128)S(1)}, s32[8]{0:T(128)}, u32[]{:S(2)}) copy-start(s32[8]{0:T(128)} %slots_ref.1) | copy-start | bytes 100
  32.7 24.9 %copy-start.6 = (s32[8]{0:T(128)S(1)}, s32[8]{0:T(128)}, u32[]{:S(2)}) copy-start(s32[8]{0:T(128)} %starts_ref.1) | copy-start | bytes 100
  32.7 24.9 %copy-start.7 = (s32[8]{0:T(128)S(1)}, s32[8]{0:T(128)}, u32[]{:S(2)}) copy-start(s32[8]{0:T(128)} %lengths_ref.1) | copy-start | bytes 100
  32.7 8.8 %collective-permute-start.7 = (bf16[32,1024]{1,0:T(8,128)(2,1)S(1)}, bf16[32,1024]{1,0:T(8,128)(2,1)S(1)}, u32[]{:S(2)}, u32[]{:S(2)}) collective-permute-start(bf16[32,1024]{1,0:T(8,128)(2,1)S(1)} %get-tuple-element.55), channel_id=1, source_target_pairs={{0,28},{4,24},{8,20},{12,16},{16,12},{20,8},{24,4},{28,0},{1,29},{... | collective-permute-start | bytes 196616 | tf_op jit(solution)/shard_map/ppermute | solution.py:440
  35.4 6.4 %collective-permute-start.8 = (bf16[32,1024]{1,0:T(8,128)(2,1)S(1)}, bf16[32,1024]{1,0:T(8,128)(2,1)S(1)}, u32[]{:S(2)}, u32[]{:S(2)}) collective-permute-start(bf16[32,1024]{1,0:T(8,128)(2,1)S(1)} %get-tuple-element.56), channel_id=1, source_target_pairs={{0,24},{4,28},{8,16},{12,20},{16,8},{20,12},{24,0},{28,4},{1,25},{... | collective-permute-start | bytes 196616 | tf_op jit(solution)/shard_map/ppermute | solution.py:440
  38.2 4.3 %collective-permute-start.9 = (bf16[32,1024]{1,0:T(8,128)(2,1)S(1)}, bf16[32,1024]{1,0:T(8,128)(2,1)S(1)}, u32[]{:S(2)}, u32[]{:S(2)}) collective-permute-start(bf16[32,1024]{1,0:T(8,128)(2,1)S(1)} %get-tuple-element.57), channel_id=1, source_target_pairs={{0,20},{4,16},{8,28},{12,24},{16,4},{20,0},{24,12},{28,8},{1,21},{... | collective-permute-start | bytes 196616 | tf_op jit(solution)/shard_map/ppermute | solution.py:440
  39.0 5.0 %collective-permute-start.10 = (bf16[32,1024]{1,0:T(8,128)(2,1)S(1)}, bf16[32,1024]{1,0:T(8,128)(2,1)S(1)}, u32[]{:S(2)}, u32[]{:S(2)}) collective-permute-start(bf16[32,1024]{1,0:T(8,128)(2,1)S(1)} %get-tuple-element.58), channel_id=1, source_target_pairs={{0,16},{4,20},{8,24},{12,28},{16,0},{20,4},{24,8},{28,12},{1,17},{... | collective-permute-start | bytes 196616 | tf_op jit(solution)/shard_map/ppermute | solution.py:440
  39.8 4.3 %collective-permute-start.11 = (bf16[32,1024]{1,0:T(8,128)(2,1)S(1)}, bf16[32,1024]{1,0:T(8,128)(2,1)S(1)}, u32[]{:S(2)}, u32[]{:S(2)}) collective-permute-start(bf16[32,1024]{1,0:T(8,128)(2,1)S(1)} %get-tuple-element.59), channel_id=1, source_target_pairs={{0,12},{4,8},{8,4},{12,0},{16,28},{20,24},{24,20},{28,16},{1,13},{... | collective-permute-start | bytes 196616 | tf_op jit(solution)/shard_map/ppermute | solution.py:440
  41.5 4.4 %collective-permute-start.12 = (bf16[32,1024]{1,0:T(8,128)(2,1)S(1)}, bf16[32,1024]{1,0:T(8,128)(2,1)S(1)}, u32[]{:S(2)}, u32[]{:S(2)}) collective-permute-start(bf16[32,1024]{1,0:T(8,128)(2,1)S(1)} %get-tuple-element.60), channel_id=1, source_target_pairs={{0,8},{4,12},{8,0},{12,4},{16,24},{20,28},{24,16},{28,20},{1,9},{5... | collective-permute-start | bytes 196616 | tf_op jit(solution)/shard_map/ppermute | solution.py:440
  41.8 4.0 %collective-permute-start.13 = (bf16[32,1024]{1,0:T(8,128)(2,1)S(1)}, bf16[32,1024]{1,0:T(8,128)(2,1)S(1)}, u32[]{:S(2)}, u32[]{:S(2)}) collective-permute-start(bf16[32,1024]{1,0:T(8,128)(2,1)S(1)} %get-tuple-element.61), channel_id=1, source_target_pairs={{0,4},{4,0},{8,12},{12,8},{16,20},{20,16},{24,28},{28,24},{1,5},{5... | collective-permute-start | bytes 196616 | tf_op jit(solution)/shard_map/ppermute | solution.py:440
  46.9 13.0 %collective-permute-start.23 = (bf16[4,1792,128]{2,1,0:T(8,128)(2,1)S(1)}, bf16[4,1792,128]{2,1,0:T(8,128)(2,1)S(1)}, u32[]{:S(2)}, u32[]{:S(2)}) collective-permute-start(bf16[4,1792,128]{2,1,0:T(8,128)(2,1)S(1)} %get-tuple-element.75.refs_6_.refs_4_), channel_id=1, source_target_pairs={{0,4},{4,0},{8,12},{12,8},{16,20},{20,16},{24,28},{28,24},{1,5},{5... | collective-permute-start | bytes 5505032 | tf_op jit(solution)/shard_map/ppermute | solution.py:437
  46.9 6.5 %collective-permute-start.19 = (bf16[32,1024]{1,0:T(8,128)(2,1)S(1)}, bf16[32,1024]{1,0:T(8,128)(2,1)S(1)}, u32[]{:S(2)}, u32[]{:S(2)}) collective-permute-start(bf16[32,1024]{1,0:T(8,128)(2,1)S(1)} %get-tuple-element.73), channel_id=1, source_target_pairs={{0,2},{1,3},{2,0},{3,1},{4,6},{5,7},{6,4},{7,5},{8,10},{9,11},{10,... | collective-permute-start | bytes 196616 | tf_op jit(solution)/shard_map/ppermute | solution.py:443
  48.1 10.8 %collective-permute-start.18 = (bf16[64,1024]{1,0:T(8,128)(2,1)S(1)}, bf16[64,1024]{1,0:T(8,128)(2,1)S(1)}, u32[]{:S(2)}, u32[]{:S(2)}) collective-permute-start(bf16[64,1024]{1,0:T(8,128)(2,1)S(1)} %get-tuple-element.72.refs_0_), channel_id=1, source_target_pairs={{0,1},{1,0},{2,3},{3,2},{4,5},{5,4},{6,7},{7,6},{8,9},{9,8},{10,11... | collective-permute-start | bytes 393224 | tf_op jit(solution)/shard_map/ppermute | solution.py:443
  48.5 6.7 %collective-permute-start.20 = (bf16[32,1024]{1,0:T(8,128)(2,1)S(1)}, bf16[32,1024]{1,0:T(8,128)(2,1)S(1)}, u32[]{:S(2)}, u32[]{:S(2)}) collective-permute-start(bf16[32,1024]{1,0:T(8,128)(2,1)S(1)} %get-tuple-element.74), channel_id=1, source_target_pairs={{0,2},{1,3},{2,0},{3,1},{4,6},{5,7},{6,4},{7,5},{8,10},{9,11},{10,... | collective-permute-start | bytes 196616 | tf_op jit(solution)/shard_map/ppermute | solution.py:443
  53.4 5.5 %collective-permute-start.21 = (bf16[32,1024]{1,0:T(8,128)(2,1)S(1)}, bf16[32,1024]{1,0:T(8,128)(2,1)S(1)}, u32[]{:S(2)}, u32[]{:S(2)}) collective-permute-start(bf16[32,1024]{1,0:T(8,128)(2,1)S(1)} %collective-permute-done.19.refs_2_), channel_id=1, source_target_pairs={{0,1},{1,0},{2,3},{3,2},{4,5},{5,4},{6,7},{7,6},{8,9},{9,8},{10,11... | collective-permute-start | bytes 196616 | tf_op jit(solution)/shard_map/ppermute | solution.py:443
  55.3 4.6 %collective-permute-start.22 = (bf16[32,1024]{1,0:T(8,128)(2,1)S(1)}, bf16[32,1024]{1,0:T(8,128)(2,1)S(1)}, u32[]{:S(2)}, u32[]{:S(2)}) collective-permute-start(bf16[32,1024]{1,0:T(8,128)(2,1)S(1)} %collective-permute-done.20.refs_3_), channel_id=1, source_target_pairs={{0,1},{1,0},{2,3},{3,2},{4,5},{5,4},{6,7},{7,6},{8,9},{9,8},{10,11... | collective-permute-start | bytes 196616 | tf_op jit(solution)/shard_map/ppermute | solution.py:443
  61.1 5.8 %collective-permute-start.24 = (bf16[64,256]{1,0:T(8,128)(2,1)S(1)}, bf16[64,256]{1,0:T(8,128)(2,1)S(1)}, u32[]{:S(2)}, u32[]{:S(2)}) collective-permute-start(bf16[64,256]{1,0:T(8,128)(2,1)S(1)} %get-tuple-element.76), channel_id=1, source_target_pairs={{0,3},{1,2},{2,1},{3,0},{4,7},{5,6},{6,5},{7,4},{8,11},{9,10},{10,... | collective-permute-start | bytes 98312 | tf_op jit(solution)/shard_map/ppermute | solution.py:443
  63.2 4.8 %collective-permute-start.25 = (bf16[64,256]{1,0:T(8,128)(2,1)S(1)}, bf16[64,256]{1,0:T(8,128)(2,1)S(1)}, u32[]{:S(2)}, u32[]{:S(2)}) collective-permute-start(bf16[64,256]{1,0:T(8,128)(2,1)S(1)} %get-tuple-element.77), channel_id=1, source_target_pairs={{0,2},{1,3},{2,0},{3,1},{4,6},{5,7},{6,4},{7,5},{8,10},{9,11},{10,... | collective-permute-start | bytes 98312 | tf_op jit(solution)/shard_map/ppermute | solution.py:443
  64.7 3.9 %collective-permute-start.26 = (bf16[64,256]{1,0:T(8,128)(2,1)S(1)}, bf16[64,256]{1,0:T(8,128)(2,1)S(1)}, u32[]{:S(2)}, u32[]{:S(2)}) collective-permute-start(bf16[64,256]{1,0:T(8,128)(2,1)S(1)} %get-tuple-element.78), channel_id=1, source_target_pairs={{0,1},{1,0},{2,3},{3,2},{4,5},{5,4},{6,7},{7,6},{8,9},{9,8},{10,11... | collective-permute-start | bytes 98312 | tf_op jit(solution)/shard_map/ppermute | solution.py:443

commit v8 on v5

--- a/solution.py
+++ b/solution.py
@@ -46,14 +46,17 @@
 
 
 def spectrum_table(size):
-    sample = np.arange(size)
-    phase = sample[:, None] * np.arange(size // 2)[None, :] % size
-    angle = phase * (2.0 * math.pi / size)
-    window = 0.5 - 0.5 * np.cos(sample * (2.0 * math.pi / size))
-    both = np.concatenate([np.cos(angle), np.sin(angle)], axis=1) * window[:, None]
-    filters = np.zeros((size, LANES))
-    filters[: size // 2, :MELS] = mel_table(size, MELS)[: size // 2]
-    return np.concatenate([both, filters], axis=1).astype(np.float32)
+    half = size // 2
+    sample = np.arange(half)
+    bins = np.concatenate([np.arange(0, half, 2), np.arange(1, half, 2)])
+    angle = sample[:, None] * bins[None, :] % size * (2.0 * math.pi / size)
+    table = np.zeros((half + 8, size + LANES))
+    for odd in range(2):
+        part = angle[:, odd * half // 2 : (odd + 1) * half // 2]
+        table[:half, odd * half : (odd + 1) * half] = np.concatenate([np.cos(part), np.sin(part)], axis=1)
+    table[:half, size : size + MELS] = mel_table(size, MELS)[bins]
+    table[half, :size] = 0.5 - 0.5 * np.cos(np.arange(size) * (2.0 * math.pi / size))
+    return table.astype(np.float32)
 
 
 def vmem():
@@ -174,14 +177,24 @@
         phases.append(block)
     frames = jnp.concatenate(phases, axis=0)
     load_table.wait()
-    spectrum = jnp.dot(
-        frames, table[:, :N_FFT], precision=lax.Precision.HIGHEST, preferred_element_type=F32
-    )
     half = N_FFT // 2
-    real, imag = spectrum[:, :half], spectrum[:, half:]
-    power = real * real + imag * imag
+    frames = frames * table[half : half + 1, :N_FFT]
+    low, high = frames[:, :half], frames[:, half:]
+    powers = []
+    for odd in range(2):
+        spectrum = jnp.dot(
+            low - high if odd else low + high,
+            table[:half, odd * half : (odd + 1) * half],
+            precision=lax.Precision.HIGHEST,
+            preferred_element_type=F32,
+        )
+        real, imag = spectrum[:, : half // 2], spectrum[:, half // 2 :]
+        powers.append(real * real + imag * imag)
     mel_power = jnp.dot(
-        power, table[:half, N_FFT:], precision=lax.Precision.HIGHEST, preferred_element_type=F32
+        jnp.concatenate(powers, axis=1),
+        table[:half, N_FFT:],
+        precision=lax.Precision.HIGHEST,
+        preferred_element_type=F32,
     )
     load_slots.wait()
     column = iota(1, rows, 1)
@@ -264,10 +277,8 @@
     load_conv2.wait()
     for h in range((outs - 1) // 2):
         lanes = slice(2 * h * channels, (2 * h + 3) * channels)
-        depth = 3 * channels
-        total = jnp.dot(even[: W * n, lanes], conv2[:depth], preferred_element_type=F32)
-        total += jnp.dot(odd[:, lanes], conv2[depth : 2 * depth], preferred_element_type=F32)
-        total += jnp.dot(even[n:, lanes], conv2[2 * depth :], preferred_element_type=F32)
+        taps = jnp.concatenate([even[: W * n, lanes], odd[:, lanes], even[n:, lanes]], axis=1)
+        total = jnp.dot(taps, conv2[...], preferred_element_type=F32)
         second[:, h * channels : (h + 1) * channels] = jax.nn.relu(total).astype(BF16)
     wait_all(loads)
     weights = proj[...].reshape(second.shape[1], proj.shape[2])
@@ -449,8 +460,9 @@
         name="log_mel",
     )(slots, rim, audio, table, qkv_weight)
     near = [to_part(out_weight, step) for step in range(1, parts - 1)]
-    mel_all, proj_all, near = lax.optimization_barrier((mel_all, proj_all, near))
+    mel_all, proj_all = lax.optimization_barrier((mel_all, proj_all))
     mel_all = [mel_all[0]] + [to_part(mel_all[step], step) for step in range(1, parts)]
+    mel_all, near = lax.optimization_barrier((mel_all, near))
     mix_all = [mix] + [to_part(mix, step) for step in range(1, parts)]
 
     block = jax.ShapeDtypeStruct((local, features), BF16)

time: 67.9 us -> 66.9 us (0.985)
  waiting for transfers between devices: 19.5 us -> 18.3 us
  starting transfers between devices: 29.6 us -> 30.4 us
  Pallas kernels: 15.6 us -> 14.9 us
    ppermute x9, waiting for transfers between devices: 2 us -> 0.77 us  [to_part(): return lax.ppermute(block, 'dp', pairs)]
    ppermute x9, starting transfers between devices: 12.5 us -> 13.5 us  [to_part(): return lax.ppermute(block, 'dp', pairs)]
  transfers between devices with their start and end apart: 26 -> 26, of which waited for: 12 -> 10; matrix products, arithmetic and copies ran while one was open for 1% -> 1% of each run, Pallas kernels for 17% -> 16%
where the time goes in v8:
time: 66.9 us; the launch traced here: 66.5 us
  starting transfers between devices  30.4 us (45%)
  waiting for transfers between devices  18.3 us (27%)
  Pallas kernels  14.9 us (22%)
  local copies, waits for them, and re-layouts  2.13 us (3%)
  between operations  0.79 us (1%)
    ppermute x9, starting transfers between devices, to_part(): return lax.ppermute(block, 'dp', pairs)  13.5 us
    ppermute x6, waiting for transfers between devices, to_plane(): return lax.ppermute(block, 'seq', [(i, i ^ step) for i in range(group)])  13.3 us
    ppermute x7, starting transfers between devices, to_window(): return lax.ppermute(block, 'dp', [(i, i ^ step) for i in range(windows)])  6.04 us
    ppermute x6, starting transfers between devices, to_plane(): return lax.ppermute(block, 'seq', [(i, i ^ step) for i in range(group)])  5.52 us
    pallas_call x1, Pallas kernels, on_device(): pl.pallas_call(functools.partial(conv_kernel, parts, width), out_shape=tu...  5.23 us
    ppermute x1, starting transfers between devices, on_device(): rim = lax.ppermute(audio[:, audio.shape[1] - RIM:], ('dp', 'seq'), route)  4.63 us
    pallas_call x1, Pallas kernels, on_device(): pl.pallas_call(functools.partial(mel_kernel, parts, group), out_shape=tup...  4.47 us
    ppermute x7, waiting for transfers between devices, to_window(): return lax.ppermute(block, 'dp', [(i, i ^ step) for i in range(windows)])  4.21 us
  transfers between devices with their start and end apart: 26, of which 10 were waited for; matrix products, arithmetic and copies ran while one was open for 1% of the time, Pallas kernels for 16%

profile of v8, /device:TPU:0, one launch (start us, length us, event | category | flops | bytes accessed | tf_op | source)
XLA Modules:
  0.0 66.5 jit_solution(18269149486811650926)
XLA Ops:
  0.6 0.5 collective-permute-start.1
  1.1 0.8 %slice.3 = f32[8,1024]{1,0:T(8,128)S(1)} slice(f32[8,5120]{1,0:T(8,128)} %audio_ref.1), slice={[0:8], [4096:5120]} | slice | bytes 65536 | tf_op jit(solution)/shard_map/slice | solution.py:426
  1.9 4.6 %collective-permute-start = (f32[8,1024]{1,0:T(8,128)S(1)}, f32[8,1024]{1,0:T(8,128)S(1)}, u32[]{:S(2)}, u32[]{:S(2)}) collective-permute-start(f32[8,1024]{1,0:T(8,128)S(1)} %slice.3), channel_id=1, source_target_pairs={{0,1},{1,2},{2,3},{3,4},{4,5},{5,6},{6,7},{7,8},{8,9},{9,10},{10,1... | collective-permute-start | bytes 98312 | tf_op jit(solution)/shard_map/ppermute | solution.py:426
  6.6 1.6 %collective-permute-start.5 = (bf16[1024,128]{1,0:T(8,128)(2,1)}, bf16[1024,128]{1,0:T(8,128)(2,1)S(1)}, u32[]{:S(2)}, u32[]{:S(2)}) collective-permute-start(bf16[1024,128]{1,0:T(8,128)(2,1)} %refs_6_), channel_id=1, source_target_pairs={{0,8},{4,12},{8,0},{12,4},{16,24},{20,28},{24,16},{28,20},{1,9},{5... | collective-permute-start | bytes 786440 | tf_op jit(solution)/shard_map/ppermute | solution.py:430
  8.1 1.5 %collective-permute-start.6 = (bf16[1024,128]{1,0:T(8,128)(2,1)}, bf16[1024,128]{1,0:T(8,128)(2,1)}, u32[]{:S(2)}, u32[]{:S(2)}) collective-permute-start(bf16[1024,128]{1,0:T(8,128)(2,1)} %refs_6_), channel_id=1, source_target_pairs={{0,16},{4,20},{8,24},{12,28},{16,0},{20,4},{24,8},{28,12},{1,17},{... | collective-permute-start | bytes 786440 | tf_op jit(solution)/shard_map/ppermute | solution.py:430
  9.6 0.0 collective-permute-done.rim_ref
  9.6 0.6 copy-done.9
  10.2 4.5 %log_mel.1 = (bf16[72,128]{1,0:T(8,128)(2,1)}, bf16[72,128]{1,0:T(8,128)(2,1)}, bf16[72,128]{1,0:T(8,128)(2,1)}, bf16[72,128]{1,0:T(8,128)(2,1)}, bf16[128,768]{1,0:T(8,128)(2,1)}) custom-call(s32[8]{0:T(128)} %slots_ref.1, f32[8,1024]{1,0:T(8,128)} %copy-done.9, f32[8,5120]{1,0:T(8,128)} %audio_ref.1, f32[264,640]{1,0:T(8,128)} %constant.2.clone.table_ref, ...), custom_call_target="tpu_custom_call" | custom-call | flops 10000000000 | bytes 2000000 | tf_op jit(solution)/shard_map/log_mel/pallas_call | solution.py:446
  14.7 3.0 %collective-permute-start.2 = (bf16[72,128]{1,0:T(8,128)(2,1)}, bf16[72,128]{1,0:T(8,128)(2,1)S(1)}, u32[]{:S(2)}, u32[]{:S(2)}) collective-permute-start(bf16[72,128]{1,0:T(8,128)(2,1)} %get-tuple-element.45), channel_id=1, source_target_pairs={{0,8},{4,12},{8,0},{12,4},{16,24},{20,28},{24,16},{28,20},{1,9},{5... | collective-permute-start | bytes 55304 | tf_op jit(solution)/shard_map/ppermute | solution.py:430
  17.8 1.6 %collective-permute-start.3 = (bf16[72,128]{1,0:T(8,128)(2,1)}, bf16[72,128]{1,0:T(8,128)(2,1)S(1)}, u32[]{:S(2)}, u32[]{:S(2)}) collective-permute-start(bf16[72,128]{1,0:T(8,128)(2,1)} %get-tuple-element.46), channel_id=1, source_target_pairs={{0,16},{4,20},{8,24},{12,28},{16,0},{20,4},{24,8},{28,12},{1,17},{... | collective-permute-start | bytes 55304 | tf_op jit(solution)/shard_map/ppermute | solution.py:430
  19.4 0.9 %collective-permute-start.4 = (bf16[72,128]{1,0:T(8,128)(2,1)}, bf16[72,128]{1,0:T(8,128)(2,1)S(1)}, u32[]{:S(2)}, u32[]{:S(2)}) collective-permute-start(bf16[72,128]{1,0:T(8,128)(2,1)} %get-tuple-element.47), channel_id=1, source_target_pairs={{0,24},{4,28},{8,16},{12,20},{16,8},{20,12},{24,0},{28,4},{1,25},{... | collective-permute-start | bytes 55304 | tf_op jit(solution)/shard_map/ppermute | solution.py:430
  20.3 2.0 %collective-permute-start.16 = (bf16[128,768]{1,0:T(8,128)(2,1)}, bf16[128,768]{1,0:T(8,128)(2,1)S(1)}, u32[]{:S(2)}, u32[]{:S(2)}) collective-permute-start(bf16[128,768]{1,0:T(8,128)(2,1)} %get-tuple-element.62.refs_8_), channel_id=1, source_target_pairs={{0,24},{4,28},{8,16},{12,20},{16,8},{20,12},{24,0},{28,4},{1,25},{... | collective-permute-start | bytes 589832 | tf_op jit(solution)/shard_map/ppermute | solution.py:430
  22.3 0.4 collective-permute-start.15
  22.7 1.1 %collective-permute-start.14 = (bf16[128,768]{1,0:T(8,128)(2,1)}, bf16[128,768]{1,0:T(8,128)(2,1)S(1)}, u32[]{:S(2)}, u32[]{:S(2)}) collective-permute-start(bf16[128,768]{1,0:T(8,128)(2,1)} %get-tuple-element.62.refs_8_), channel_id=1, source_target_pairs={{0,8},{4,12},{8,0},{12,4},{16,24},{20,28},{24,16},{28,20},{1,9},{5... | collective-permute-start | bytes 589832 | tf_op jit(solution)/shard_map/ppermute | solution.py:430
  23.8 0.7 %collective-permute-done.4.refs_3_ = bf16[72,128]{1,0:T(8,128)(2,1)S(1)} collective-permute-done((bf16[72,128]{1,0:T(8,128)(2,1)}, bf16[72,128]{1,0:T(8,128)(2,1)S(1)}, u32[]{:S(2)}, u32[]{:S(2)}) %collective-permute-start.4) | collective-permute-done | bytes 18464 | tf_op jit(solution)/shard_map/ppermute | solution.py:430
  24.6 0.0 copy-start.8
  24.6 0.7 %copy-done.8 = bf16[72,128]{1,0:T(8,128)(2,1)S(1)} copy-done((bf16[72,128]{1,0:T(8,128)(2,1)S(1)}, bf16[72,128]{1,0:T(8,128)(2,1)}, u32[]{:S(2)}) %copy-start.8) | copy-done | bytes 18456
  25.3 5.2 %conv.1 = (bf16[32,1024]{1,0:T(8,128)(2,1)S(1)}, bf16[32,1024]{1,0:T(8,128)(2,1)S(1)}, bf16[32,1024]{1,0:T(8,128)(2,1)S(1)}, bf16[32,1024]{1,0:T(8,128)(2,1)S(1)...) custom-call(bf16[9,256]{1,0:T(8,128)(2,1)S(1)} %copy-done.4, ...), custom_call_target="tpu_custom_call" | custom-call | flops 2000000000 | bytes 4000000 | tf_op jit(solution)/shard_map/conv/pallas_call | solution.py:469
  30.6 0.0 copy-start.3
  30.6 0.0 copy-start.5
  30.6 0.0 copy-start.6
  30.6 0.0 copy-start.7
  30.6 0.1 collective-permute-start.7
  30.7 1.3 %collective-permute-start.8 = (bf16[32,1024]{1,0:T(8,128)(2,1)S(1)}, bf16[32,1024]{1,0:T(8,128)(2,1)S(1)}, u32[]{:S(2)}, u32[]{:S(2)}) collective-permute-start(bf16[32,1024]{1,0:T(8,128)(2,1)S(1)} %get-tuple-element.55), channel_id=1, source_target_pairs={{0,24},{4,28},{8,16},{12,20},{16,8},{20,12},{24,0},{28,4},{1,25},{... | collective-permute-start | bytes 196616 | tf_op jit(solution)/shard_map/ppermute | solution.py:437
  32.0 2.3 %collective-permute-start.9 = (bf16[32,1024]{1,0:T(8,128)(2,1)S(1)}, bf16[32,1024]{1,0:T(8,128)(2,1)S(1)}, u32[]{:S(2)}, u32[]{:S(2)}) collective-permute-start(bf16[32,1024]{1,0:T(8,128)(2,1)S(1)} %get-tuple-element.56), channel_id=1, source_target_pairs={{0,20},{4,16},{8,28},{12,24},{16,4},{20,0},{24,12},{28,8},{1,21},{... | collective-permute-start | bytes 196616 | tf_op jit(solution)/shard_map/ppermute | solution.py:437
  34.3 0.8 %collective-permute-start.10 = (bf16[32,1024]{1,0:T(8,128)(2,1)S(1)}, bf16[32,1024]{1,0:T(8,128)(2,1)S(1)}, u32[]{:S(2)}, u32[]{:S(2)}) collective-permute-start(bf16[32,1024]{1,0:T(8,128)(2,1)S(1)} %get-tuple-element.57), channel_id=1, source_target_pairs={{0,16},{4,20},{8,24},{12,28},{16,0},{20,4},{24,8},{28,12},{1,17},{... | collective-permute-start | bytes 196616 | tf_op jit(solution)/shard_map/ppermute | solution.py:437
  35.1 0.3 collective-permute-done.7.refs_0_
  35.4 1.5 %collective-permute-start.12 = (bf16[32,1024]{1,0:T(8,128)(2,1)S(1)}, bf16[32,1024]{1,0:T(8,128)(2,1)S(1)}, u32[]{:S(2)}, u32[]{:S(2)}) collective-permute-start(bf16[32,1024]{1,0:T(8,128)(2,1)S(1)} %get-tuple-element.59), channel_id=1, source_target_pairs={{0,8},{4,12},{8,0},{12,4},{16,24},{20,28},{24,16},{28,20},{1,9},{5... | collective-permute-start | bytes 196616 | tf_op jit(solution)/shard_map/ppermute | solution.py:437
  36.9 0.1 collective-permute-start.13
  37.0 1.0 %collective-permute-done.9.refs_2_ = bf16[32,1024]{1,0:T(8,128)(2,1)S(1)} collective-permute-done((bf16[32,1024]{1,0:T(8,128)(2,1)S(1)}, bf16[32,1024]{1,0:T(8,128)(2,1)S(1)}, u32[]{:S(2)}, u32[]{:S(2)}) %collective-permute-start.9) | collective-permute-done | bytes 65568 | tf_op jit(solution)/shard_map/ppermute | solution.py:437
  38.0 1.5 %collective-permute-done.10.refs_3_ = bf16[32,1024]{1,0:T(8,128)(2,1)S(1)} collective-permute-done((bf16[32,1024]{1,0:T(8,128)(2,1)S(1)}, bf16[32,1024]{1,0:T(8,128)(2,1)S(1)}, u32[]{:S(2)}, u32[]{:S(2)}) %collective-permute-start.10) | collective-permute-done | bytes 65568 | tf_op jit(solution)/shard_map/ppermute | solution.py:437
  39.5 1.4 %collective-permute-done.12.refs_5_ = bf16[32,1024]{1,0:T(8,128)(2,1)S(1)} collective-permute-done((bf16[32,1024]{1,0:T(8,128)(2,1)S(1)}, bf16[32,1024]{1,0:T(8,128)(2,1)S(1)}, u32[]{:S(2)}, u32[]{:S(2)}) %collective-permute-start.12) | collective-permute-done | bytes 65568 | tf_op jit(solution)/shard_map/ppermute | solution.py:437
  40.9 1.5 %layer_norm.1 = (bf16[64,1024]{1,0:T(8,128)(2,1)S(1)}, bf16[64,1024]{1,0:T(8,128)(2,1)S(1)}, bf16[4,128,768]{2,1,0:T(8,128)(2,1)S(1)}) custom-call(bf16[32,1024]{1,0:T(8,128)(2,1)S(1)} %collective-permute-done.7.refs_0_, bf16[32,1024]{1,0:T(8,128)(2,1)S(1)} %collective-permute-done.8.refs_1_, bf16[32,1024]{1,0:T(8,128)(2,1)S(1)} %collective-permute-done.9.refs_2_, ...), custom_call_target="tpu_custom_call" | custom-call | flops 100000000 | bytes 1000000 | tf_op jit(solution)/shard_map/layer_norm/pallas_call | solution.py:492
  42.4 0.1 collective-permute-start.20
  42.5 1.3 %collective-permute-start.21 = (bf16[1024,128]{1,0:T(8,128)(2,1)S(1)}, bf16[1024,128]{1,0:T(8,128)(2,1)S(1)}, u32[]{:S(2)}, u32[]{:S(2)}) collective-permute-start(bf16[1024,128]{1,0:T(8,128)(2,1)S(1)} %copy-done.3), channel_id=1, source_target_pairs={{0,24},{4,28},{8,16},{12,20},{16,8},{20,12},{24,0},{28,4},{1,25},{... | collective-permute-start | bytes 786440 | tf_op jit(solution)/shard_map/ppermute | solution.py:430
  43.8 1.1 %collective-permute-start.17 = (bf16[64,1024]{1,0:T(8,128)(2,1)S(1)}, bf16[64,1024]{1,0:T(8,128)(2,1)S(1)}, u32[]{:S(2)}, u32[]{:S(2)}) collective-permute-start(bf16[64,1024]{1,0:T(8,128)(2,1)S(1)} %get-tuple-element.68.refs_0_), channel_id=1, source_target_pairs={{0,1},{1,0},{2,3},{3,2},{4,5},{5,4},{6,7},{7,6},{8,9},{9,8},{10,11... | collective-permute-start | bytes 393224 | tf_op jit(solution)/shard_map/ppermute | solution.py:440
  44.9 5.2 %collective-permute-done.18.refs_2_ = bf16[64,1024]{1,0:T(8,128)(2,1)S(1)} collective-permute-done((bf16[64,1024]{1,0:T(8,128)(2,1)S(1)}, bf16[64,1024]{1,0:T(8,128)(2,1)S(1)}, u32[]{:S(2)}, u32[]{:S(2)}) %collective-permute-start.18) | collective-permute-done | bytes 131104 | tf_op jit(solution)/shard_map/ppermute | solution.py:440
  50.1 1.3 %mask.1 = (bf16[64,1024]{1,0:T(8,128)(2,1)}, f32[4,64]{1,0:T(4,128)S(1)}, f32[64,1]{1,0:T(8,128)S(1)}) custom-call(s32[8]{0:T(128)S(1)} %copy-done.5, s32[8]{0:T(128)S(1)} %copy-done.6, s32[8]{0:T(128)S(1)} %copy-done.7, bf16[64,1024]{1,0:T(8,128)(2,1)S(1)} %get-tuple-element.63.rows_ref), custom_call_target="tpu_custom_call" | custom-call | flops 100000000 | bytes 1000000 | tf_op jit(solution)/shard_map/mask/pallas_call | solution.py:503
  51.4 0.7 %collective-permute-done.17.refs_1_ = bf16[64,1024]{1,0:T(8,128)(2,1)S(1)} collective-permute-done((bf16[64,1024]{1,0:T(8,128)(2,1)S(1)}, bf16[64,1024]{1,0:T(8,128)(2,1)S(1)}, u32[]{:S(2)}, u32[]{:S(2)}) %collective-permute-start.17) | collective-permute-done | bytes 131104 | tf_op jit(solution)/shard_map/ppermute | solution.py:440
  52.1 3.4 %collective-permute-done.19.refs_3_ = bf16[64,1024]{1,0:T(8,128)(2,1)S(1)} collective-permute-done((bf16[64,1024]{1,0:T(8,128)(2,1)S(1)}, bf16[64,1024]{1,0:T(8,128)(2,1)S(1)}, u32[]{:S(2)}, u32[]{:S(2)}) %collective-permute-start.19) | collective-permute-done | bytes 131104 | tf_op jit(solution)/shard_map/ppermute | solution.py:440
  55.5 1.4 %attention.1 = (bf16[64,256]{1,0:T(8,128)(2,1)S(1)}, bf16[64,256]{1,0:T(8,128)(2,1)S(1)}, bf16[64,256]{1,0:T(8,128)(2,1)S(1)}, bf16[64,256]{1,0:T(8,128)(2,1)S(1)}, bf16[4,1024,128]{2,1,0:T(8,128)(2,1)S(1)}) custom-call(f32[4,64]{1,0:T(4,128)S(1)} %get-tuple-element.66.keys_ref, bf16[64,1024]{1,0:T(8,128)(2,1)S(1)} %get-tuple-element.68.refs_0_, ...), custom_call_target="tpu_custom_call" | custom-call | flops 1000000000 | bytes 2000000 | tf_op jit(solution)/shard_map/attention/pallas_call | solution.py:523
  56.9 0.1 collective-permute-start.25
  57.0 0.3 collective-permute-start.22
  57.3 2.4 %collective-permute-start.23 = (bf16[64,256]{1,0:T(8,128)(2,1)S(1)}, bf16[64,256]{1,0:T(8,128)(2,1)S(1)}, u32[]{:S(2)}, u32[]{:S(2)}) collective-permute-start(bf16[64,256]{1,0:T(8,128)(2,1)S(1)} %get-tuple-element.75), channel_id=1, source_target_pairs={{0,2},{1,3},{2,0},{3,1},{4,6},{5,7},{6,4},{7,5},{8,10},{9,11},{10,... | collective-permute-start | bytes 98312 | tf_op jit(solution)/shard_map/ppermute | solution.py:440
  59.7 1.7 %collective-permute-start.24 = (bf16[64,256]{1,0:T(8,128)(2,1)S(1)}, bf16[64,256]{1,0:T(8,128)(2,1)S(1)}, u32[]{:S(2)}, u32[]{:S(2)}) collective-permute-start(bf16[64,256]{1,0:T(8,128)(2,1)S(1)} %get-tuple-element.76), channel_id=1, source_target_pairs={{0,3},{1,2},{2,1},{3,0},{4,7},{5,6},{6,5},{7,4},{8,11},{9,10},{10,... | collective-permute-start | bytes 98312 | tf_op jit(solution)/shard_map/ppermute | solution.py:440
  61.4 1.3 %collective-permute-done.23.refs_2_ = bf16[64,256]{1,0:T(8,128)(2,1)S(1)} collective-permute-done((bf16[64,256]{1,0:T(8,128)(2,1)S(1)}, bf16[64,256]{1,0:T(8,128)(2,1)S(1)}, u32[]{:S(2)}, u32[]{:S(2)}) %collective-permute-start.23) | collective-permute-done | bytes 32800 | tf_op jit(solution)/shard_map/ppermute | solution.py:440
  62.7 2.8 %collective-permute-done.24.refs_3_ = bf16[64,256]{1,0:T(8,128)(2,1)S(1)} collective-permute-done((bf16[64,256]{1,0:T(8,128)(2,1)S(1)}, bf16[64,256]{1,0:T(8,128)(2,1)S(1)}, u32[]{:S(2)}, u32[]{:S(2)}) %collective-permute-start.24) | collective-permute-done | bytes 32800 | tf_op jit(solution)/shard_map/ppermute | solution.py:440
  65.4 1.1 %output.1 = bf16[64,1024]{1,0:T(8,128)(2,1)} custom-call(f32[64,1]{1,0:T(8,128)S(1)} %get-tuple-element.65.valid_ref, bf16[64,256]{1,0:T(8,128)(2,1)S(1)} %get-tuple-element.73.refs_0_, bf16[64,256]{1,0:T(8,128)(2,1)S(1)} %collective-permute-done.22.refs_1_, bf16[64,256]{1,0:T(8,128)(2,1)S(1)} %collective-permute-done.23.refs_2_, ...), custom_call_target="tpu_custom_call" | custom-call | flops 100000000 | bytes 3000000 | tf_op jit(solution)/shard_map/output/pallas_call | solution.py:542
  (31 shorter events, 0.1 us)
Async XLA Ops:
  0.6 14.1 %collective-permute-start.1 = (bf16[640,1024]{1,0:T(8,128)(2,1)}, bf16[640,1024]{1,0:T(8,128)(2,1)S(1)}, u32[]{:S(2)}, u32[]{:S(2)}) collective-permute-start(bf16[640,1024]{1,0:T(8,128)(2,1)} %refs_4_), channel_id=1, source_target_pairs={{0,4},{4,0},{8,12},{12,8},{16,20},{20,16},{24,28},{28,24},{1,5},{5... | collective-permute-start | bytes 3932168 | tf_op jit(solution)/shard_map/ppermute | solution.py:434
  1.9 22.7 %copy-start.1 = (bf16[640,1024]{1,0:T(8,128)(2,1)S(1)}, bf16[640,1024]{1,0:T(8,128)(2,1)}, u32[]{:S(2)}) copy-start(bf16[640,1024]{1,0:T(8,128)(2,1)} %refs_4_) | copy-start | bytes 3932164
  1.9 22.7 %copy-start.2 = (bf16[2304,256]{1,0:T(8,128)(2,1)S(1)}, bf16[2304,256]{1,0:T(8,128)(2,1)}, u32[]{:S(2)}) copy-start(bf16[2304,256]{1,0:T(8,128)(2,1)} %conv2_ref.1) | copy-start | bytes 3538948
  1.9 22.7 %copy-start.4 = (bf16[9,256]{1,0:T(8,128)(2,1)S(1)}, bf16[9,256]{1,0:T(8,128)(2,1)}, u32[]{:S(2)}) copy-start(bf16[9,256]{1,0:T(8,128)(2,1)} %conv1_ref.1) | copy-start | bytes 13828
  1.9 7.7 %collective-permute-start = (f32[8,1024]{1,0:T(8,128)S(1)}, f32[8,1024]{1,0:T(8,128)S(1)}, u32[]{:S(2)}, u32[]{:S(2)}) collective-permute-start(f32[8,1024]{1,0:T(8,128)S(1)} %slice.3), channel_id=1, source_target_pairs={{0,1},{1,2},{2,3},{3,4},{4,5},{5,6},{6,7},{7,8},{8,9},{9,10},{10,1... | collective-permute-start | bytes 98312 | tf_op jit(solution)/shard_map/ppermute | solution.py:426
  6.6 13.7 %collective-permute-start.5 = (bf16[1024,128]{1,0:T(8,128)(2,1)}, bf16[1024,128]{1,0:T(8,128)(2,1)S(1)}, u32[]{:S(2)}, u32[]{:S(2)}) collective-permute-start(bf16[1024,128]{1,0:T(8,128)(2,1)} %refs_6_), channel_id=1, source_target_pairs={{0,8},{4,12},{8,0},{12,4},{16,24},{20,28},{24,16},{28,20},{1,9},{5... | collective-permute-start | bytes 786440 | tf_op jit(solution)/shard_map/ppermute | solution.py:430
  8.1 14.2 %collective-permute-start.6 = (bf16[1024,128]{1,0:T(8,128)(2,1)}, bf16[1024,128]{1,0:T(8,128)(2,1)}, u32[]{:S(2)}, u32[]{:S(2)}) collective-permute-start(bf16[1024,128]{1,0:T(8,128)(2,1)} %refs_6_), channel_id=1, source_target_pairs={{0,16},{4,20},{8,24},{12,28},{16,0},{20,4},{24,8},{28,12},{1,17},{... | collective-permute-start | bytes 786440 | tf_op jit(solution)/shard_map/ppermute | solution.py:430
  9.6 0.6 copy-start.9
  14.7 8.0 %collective-permute-start.2 = (bf16[72,128]{1,0:T(8,128)(2,1)}, bf16[72,128]{1,0:T(8,128)(2,1)S(1)}, u32[]{:S(2)}, u32[]{:S(2)}) collective-permute-start(bf16[72,128]{1,0:T(8,128)(2,1)} %get-tuple-element.45), channel_id=1, source_target_pairs={{0,8},{4,12},{8,0},{12,4},{16,24},{20,28},{24,16},{28,20},{1,9},{5... | collective-permute-start | bytes 55304 | tf_op jit(solution)/shard_map/ppermute | solution.py:430
  17.8 6.1 %collective-permute-start.3 = (bf16[72,128]{1,0:T(8,128)(2,1)}, bf16[72,128]{1,0:T(8,128)(2,1)S(1)}, u32[]{:S(2)}, u32[]{:S(2)}) collective-permute-start(bf16[72,128]{1,0:T(8,128)(2,1)} %get-tuple-element.46), channel_id=1, source_target_pairs={{0,16},{4,20},{8,24},{12,28},{16,0},{20,4},{24,8},{28,12},{1,17},{... | collective-permute-start | bytes 55304 | tf_op jit(solution)/shard_map/ppermute | solution.py:430
  19.4 5.2 %collective-permute-start.4 = (bf16[72,128]{1,0:T(8,128)(2,1)}, bf16[72,128]{1,0:T(8,128)(2,1)S(1)}, u32[]{:S(2)}, u32[]{:S(2)}) collective-permute-start(bf16[72,128]{1,0:T(8,128)(2,1)} %get-tuple-element.47), channel_id=1, source_target_pairs={{0,24},{4,28},{8,16},{12,20},{16,8},{20,12},{24,0},{28,4},{1,25},{... | collective-permute-start | bytes 55304 | tf_op jit(solution)/shard_map/ppermute | solution.py:430
  20.3 20.6 %copy-start = (bf16[128,768]{1,0:T(8,128)(2,1)S(1)}, bf16[128,768]{1,0:T(8,128)(2,1)}, u32[]{:S(2)}) copy-start(bf16[128,768]{1,0:T(8,128)(2,1)} %get-tuple-element.62.refs_8_) | copy-start | bytes 589828
  20.3 11.7 %collective-permute-start.16 = (bf16[128,768]{1,0:T(8,128)(2,1)}, bf16[128,768]{1,0:T(8,128)(2,1)S(1)}, u32[]{:S(2)}, u32[]{:S(2)}) collective-permute-start(bf16[128,768]{1,0:T(8,128)(2,1)} %get-tuple-element.62.refs_8_), channel_id=1, source_target_pairs={{0,24},{4,28},{8,16},{12,20},{16,8},{20,12},{24,0},{28,4},{1,25},{... | collective-permute-start | bytes 589832 | tf_op jit(solution)/shard_map/ppermute | solution.py:430
  22.3 12.0 %collective-permute-start.15 = (bf16[128,768]{1,0:T(8,128)(2,1)}, bf16[128,768]{1,0:T(8,128)(2,1)S(1)}, u32[]{:S(2)}, u32[]{:S(2)}) collective-permute-start(bf16[128,768]{1,0:T(8,128)(2,1)} %get-tuple-element.62.refs_8_), channel_id=1, source_target_pairs={{0,16},{4,20},{8,24},{12,28},{16,0},{20,4},{24,8},{28,12},{1,17},{... | collective-permute-start | bytes 589832 | tf_op jit(solution)/shard_map/ppermute | solution.py:430
  22.7 12.4 %collective-permute-start.14 = (bf16[128,768]{1,0:T(8,128)(2,1)}, bf16[128,768]{1,0:T(8,128)(2,1)S(1)}, u32[]{:S(2)}, u32[]{:S(2)}) collective-permute-start(bf16[128,768]{1,0:T(8,128)(2,1)} %get-tuple-element.62.refs_8_), channel_id=1, source_target_pairs={{0,8},{4,12},{8,0},{12,4},{16,24},{20,28},{24,16},{28,20},{1,9},{5... | collective-permute-start | bytes 589832 | tf_op jit(solution)/shard_map/ppermute | solution.py:430
  24.6 0.7 %copy-start.8 = (bf16[72,128]{1,0:T(8,128)(2,1)S(1)}, bf16[72,128]{1,0:T(8,128)(2,1)}, u32[]{:S(2)}) copy-start(bf16[72,128]{1,0:T(8,128)(2,1)} %get-tuple-element.48.refs_0_) | copy-start | bytes 55300
  30.6 12.0 %copy-start.3 = (bf16[1024,128]{1,0:T(8,128)(2,1)S(1)}, bf16[1024,128]{1,0:T(8,128)(2,1)}, u32[]{:S(2)}) copy-start(bf16[1024,128]{1,0:T(8,128)(2,1)} %refs_6_) | copy-start | bytes 786436
  30.6 19.5 %copy-start.5 = (s32[8]{0:T(128)S(1)}, s32[8]{0:T(128)}, u32[]{:S(2)}) copy-start(s32[8]{0:T(128)} %slots_ref.1) | copy-start | bytes 100
  30.6 19.5 %copy-start.6 = (s32[8]{0:T(128)S(1)}, s32[8]{0:T(128)}, u32[]{:S(2)}) copy-start(s32[8]{0:T(128)} %starts_ref.1) | copy-start | bytes 100
  30.6 19.5 %copy-start.7 = (s32[8]{0:T(128)S(1)}, s32[8]{0:T(128)}, u32[]{:S(2)}) copy-start(s32[8]{0:T(128)} %lengths_ref.1) | copy-start | bytes 100
  30.6 4.7 %collective-permute-start.7 = (bf16[32,1024]{1,0:T(8,128)(2,1)S(1)}, bf16[32,1024]{1,0:T(8,128)(2,1)S(1)}, u32[]{:S(2)}, u32[]{:S(2)}) collective-permute-start(bf16[32,1024]{1,0:T(8,128)(2,1)S(1)} %get-tuple-element.54), channel_id=1, source_target_pairs={{0,28},{4,24},{8,20},{12,16},{16,12},{20,8},{24,4},{28,0},{1,29},{... | collective-permute-start | bytes 196616 | tf_op jit(solution)/shard_map/ppermute | solution.py:437
  30.7 6.2 %collective-permute-start.8 = (bf16[32,1024]{1,0:T(8,128)(2,1)S(1)}, bf16[32,1024]{1,0:T(8,128)(2,1)S(1)}, u32[]{:S(2)}, u32[]{:S(2)}) collective-permute-start(bf16[32,1024]{1,0:T(8,128)(2,1)S(1)} %get-tuple-element.55), channel_id=1, source_target_pairs={{0,24},{4,28},{8,16},{12,20},{16,8},{20,12},{24,0},{28,4},{1,25},{... | collective-permute-start | bytes 196616 | tf_op jit(solution)/shard_map/ppermute | solution.py:437
  32.0 6.0 %collective-permute-start.9 = (bf16[32,1024]{1,0:T(8,128)(2,1)S(1)}, bf16[32,1024]{1,0:T(8,128)(2,1)S(1)}, u32[]{:S(2)}, u32[]{:S(2)}) collective-permute-start(bf16[32,1024]{1,0:T(8,128)(2,1)S(1)} %get-tuple-element.56), channel_id=1, source_target_pairs={{0,20},{4,16},{8,28},{12,24},{16,4},{20,0},{24,12},{28,8},{1,21},{... | collective-permute-start | bytes 196616 | tf_op jit(solution)/shard_map/ppermute | solution.py:437
  34.3 5.2 %collective-permute-start.10 = (bf16[32,1024]{1,0:T(8,128)(2,1)S(1)}, bf16[32,1024]{1,0:T(8,128)(2,1)S(1)}, u32[]{:S(2)}, u32[]{:S(2)}) collective-permute-start(bf16[32,1024]{1,0:T(8,128)(2,1)S(1)} %get-tuple-element.57), channel_id=1, source_target_pairs={{0,16},{4,20},{8,24},{12,28},{16,0},{20,4},{24,8},{28,12},{1,17},{... | collective-permute-start | bytes 196616 | tf_op jit(solution)/shard_map/ppermute | solution.py:437
  35.1 4.4 %collective-permute-start.11 = (bf16[32,1024]{1,0:T(8,128)(2,1)S(1)}, bf16[32,1024]{1,0:T(8,128)(2,1)S(1)}, u32[]{:S(2)}, u32[]{:S(2)}) collective-permute-start(bf16[32,1024]{1,0:T(8,128)(2,1)S(1)} %get-tuple-element.58), channel_id=1, source_target_pairs={{0,12},{4,8},{8,4},{12,0},{16,28},{20,24},{24,20},{28,16},{1,13},{... | collective-permute-start | bytes 196616 | tf_op jit(solution)/shard_map/ppermute | solution.py:437
  35.4 5.5 %collective-permute-start.12 = (bf16[32,1024]{1,0:T(8,128)(2,1)S(1)}, bf16[32,1024]{1,0:T(8,128)(2,1)S(1)}, u32[]{:S(2)}, u32[]{:S(2)}) collective-permute-start(bf16[32,1024]{1,0:T(8,128)(2,1)S(1)} %get-tuple-element.59), channel_id=1, source_target_pairs={{0,8},{4,12},{8,0},{12,4},{16,24},{20,28},{24,16},{28,20},{1,9},{5... | collective-permute-start | bytes 196616 | tf_op jit(solution)/shard_map/ppermute | solution.py:437
  36.9 4.0 %collective-permute-start.13 = (bf16[32,1024]{1,0:T(8,128)(2,1)S(1)}, bf16[32,1024]{1,0:T(8,128)(2,1)S(1)}, u32[]{:S(2)}, u32[]{:S(2)}) collective-permute-start(bf16[32,1024]{1,0:T(8,128)(2,1)S(1)} %get-tuple-element.60), channel_id=1, source_target_pairs={{0,4},{4,0},{8,12},{12,8},{16,20},{20,16},{24,28},{28,24},{1,5},{5... | collective-permute-start | bytes 196616 | tf_op jit(solution)/shard_map/ppermute | solution.py:437
  42.4 13.1 %collective-permute-start.20 = (bf16[4,128,768]{2,1,0:T(8,128)(2,1)S(1)}, bf16[4,128,768]{2,1,0:T(8,128)(2,1)S(1)}, u32[]{:S(2)}, u32[]{:S(2)}) collective-permute-start(bf16[4,128,768]{2,1,0:T(8,128)(2,1)S(1)} %get-tuple-element.69.refs_4_), channel_id=1, source_target_pairs={{0,4},{4,0},{8,12},{12,8},{16,20},{20,16},{24,28},{28,24},{1,5},{5... | collective-permute-start | bytes 2359304 | tf_op jit(solution)/shard_map/ppermute | solution.py:434
  42.5 7.6 %collective-permute-start.18 = (bf16[64,1024]{1,0:T(8,128)(2,1)S(1)}, bf16[64,1024]{1,0:T(8,128)(2,1)S(1)}, u32[]{:S(2)}, u32[]{:S(2)}) collective-permute-start(bf16[64,1024]{1,0:T(8,128)(2,1)S(1)} %get-tuple-element.68.refs_0_), channel_id=1, source_target_pairs={{0,2},{1,3},{2,0},{3,1},{4,6},{5,7},{6,4},{7,5},{8,10},{9,11},{10,... | collective-permute-start | bytes 393224 | tf_op jit(solution)/shard_map/ppermute | solution.py:440
  42.5 13.0 %collective-permute-start.21 = (bf16[1024,128]{1,0:T(8,128)(2,1)S(1)}, bf16[1024,128]{1,0:T(8,128)(2,1)S(1)}, u32[]{:S(2)}, u32[]{:S(2)}) collective-permute-start(bf16[1024,128]{1,0:T(8,128)(2,1)S(1)} %copy-done.3), channel_id=1, source_target_pairs={{0,24},{4,28},{8,16},{12,20},{16,8},{20,12},{24,0},{28,4},{1,25},{... | collective-permute-start | bytes 786440 | tf_op jit(solution)/shard_map/ppermute | solution.py:430
  43.8 8.3 %collective-permute-start.17 = (bf16[64,1024]{1,0:T(8,128)(2,1)S(1)}, bf16[64,1024]{1,0:T(8,128)(2,1)S(1)}, u32[]{:S(2)}, u32[]{:S(2)}) collective-permute-start(bf16[64,1024]{1,0:T(8,128)(2,1)S(1)} %get-tuple-element.68.refs_0_), channel_id=1, source_target_pairs={{0,1},{1,0},{2,3},{3,2},{4,5},{5,4},{6,7},{7,6},{8,9},{9,8},{10,11... | collective-permute-start | bytes 393224 | tf_op jit(solution)/shard_map/ppermute | solution.py:440
  50.1 5.4 %collective-permute-start.19 = (bf16[64,1024]{1,0:T(8,128)(2,1)S(1)}, bf16[64,1024]{1,0:T(8,128)(2,1)S(1)}, u32[]{:S(2)}, u32[]{:S(2)}) collective-permute-start(bf16[64,1024]{1,0:T(8,128)(2,1)S(1)} %collective-permute-done.18.refs_2_), channel_id=1, source_target_pairs={{0,1},{1,0},{2,3},{3,2},{4,5},{5,4},{6,7},{7,6},{8,9},{9,8},{10,11... | collective-permute-start | bytes 393224 | tf_op jit(solution)/shard_map/ppermute | solution.py:440
  56.9 8.6 %collective-permute-start.25 = (bf16[4,1024,128]{2,1,0:T(8,128)(2,1)S(1)}, bf16[4,1024,128]{2,1,0:T(8,128)(2,1)S(1)}, u32[]{:S(2)}, u32[]{:S(2)}) collective-permute-start(bf16[4,1024,128]{2,1,0:T(8,128)(2,1)S(1)} %get-tuple-element.77.refs_4_), channel_id=1, source_target_pairs={{0,4},{4,0},{8,12},{12,8},{16,20},{20,16},{24,28},{28,24},{1,5},{5... | collective-permute-start | bytes 3145736 | tf_op jit(solution)/shard_map/ppermute | solution.py:434
  57.0 4.5 %collective-permute-start.22 = (bf16[64,256]{1,0:T(8,128)(2,1)S(1)}, bf16[64,256]{1,0:T(8,128)(2,1)S(1)}, u32[]{:S(2)}, u32[]{:S(2)}) collective-permute-start(bf16[64,256]{1,0:T(8,128)(2,1)S(1)} %get-tuple-element.74), channel_id=1, source_target_pairs={{0,1},{1,0},{2,3},{3,2},{4,5},{5,4},{6,7},{7,6},{8,9},{9,8},{10,11... | collective-permute-start | bytes 98312 | tf_op jit(solution)/shard_map/ppermute | solution.py:440
  57.3 5.4 %collective-permute-start.23 = (bf16[64,256]{1,0:T(8,128)(2,1)S(1)}, bf16[64,256]{1,0:T(8,128)(2,1)S(1)}, u32[]{:S(2)}, u32[]{:S(2)}) collective-permute-start(bf16[64,256]{1,0:T(8,128)(2,1)S(1)} %get-tuple-element.75), channel_id=1, source_target_pairs={{0,2},{1,3},{2,0},{3,1},{4,6},{5,7},{6,4},{7,5},{8,10},{9,11},{10,... | collective-permute-start | bytes 98312 | tf_op jit(solution)/shard_map/ppermute | solution.py:440
  59.7 5.7 %collective-permute-start.24 = (bf16[64,256]{1,0:T(8,128)(2,1)S(1)}, bf16[64,256]{1,0:T(8,128)(2,1)S(1)}, u32[]{:S(2)}, u32[]{:S(2)}) collective-permute-start(bf16[64,256]{1,0:T(8,128)(2,1)S(1)} %get-tuple-element.76), channel_id=1, source_target_pairs={{0,3},{1,2},{2,1},{3,0},{4,7},{5,6},{6,5},{7,4},{8,11},{9,10},{10,... | collective-permute-start | bytes 98312 | tf_op jit(solution)/shard_map/ppermute | solution.py:440

commit v9 on v8

--- a/solution.py
+++ b/solution.py
@@ -20,6 +20,7 @@
 SPAN = 4 * HOP
 JS = W + 1
 LANES = 128
+CUTS = 2
 SAMPLE_RATE = 16000.0
 EPS_LOG = 1e-06
 EPS_NORM = 1e-05
@@ -155,9 +156,13 @@
     load_slots = pltpu.make_async_copy(slots_here, slots_ref, sems.at[5])
     load_slots.start()
     load_audio = pltpu.make_async_copy(audio_ref, ext.at[:, pl.ds(RIM, audio_ref.shape[1])], sems.at[3])
-    load_table = pltpu.make_async_copy(table_ref, table, sems.at[4])
+    third = table_ref.shape[0] // 3
+    load_table = [
+        pltpu.make_async_copy(table_ref.at[pl.ds(i * third, third)], table.at[pl.ds(i * third, third)], sems.at[6 + i])
+        for i in range(3)
+    ]
     load_audio.start()
-    load_table.start()
+    start_all(load_table)
     pieces = mix_columns(group, qkv_ref, mix_out, sems)
     start_all(pieces)
     streams = audio_ref.shape[0]
@@ -176,7 +181,7 @@
             block = pltpu.roll(block, length - shift, 1)[:, :N_FFT]
         phases.append(block)
     frames = jnp.concatenate(phases, axis=0)
-    load_table.wait()
+    wait_all(load_table)
     half = N_FFT // 2
     frames = frames * table[half : half + 1, :N_FFT]
     low, high = frames[:, :half], frames[:, half:]
@@ -230,10 +235,17 @@
 
 def stacked(parts, pieces, stack_out, sems, base):
     part, _ = place(parts)
-    return [
-        pltpu.make_async_copy(pieces[step], stack_out.at[part ^ step], sems.at[base + step])
-        for step in range(parts)
-    ]
+    rows = stack_out.shape[1] // CUTS
+    copies = []
+    for step in range(parts):
+        for cut in range(CUTS):
+            at = pl.ds(cut * rows, rows)
+            copies.append(
+                pltpu.make_async_copy(
+                    pieces[step].at[at], stack_out.at[part ^ step, at], sems.at[base + len(copies)]
+                )
+            )
+    return copies
 
 
 def conv_kernel(parts, width, conv1_ref, conv2_ref, *refs):
@@ -244,29 +256,18 @@
     mel_refs, refs = refs[:parts], refs[parts:]
     proj_refs, refs = refs[:copies], refs[copies:]
     outs_refs, refs = refs[:windows], refs[windows:]
-    mel, own, banded_ref, even, odd, second, conv2, proj, partial, sems = refs
-    load_own = pltpu.make_async_copy(mel_refs[0], own, sems.at[1 + copies])
-    load_own.start()
-    load_conv2 = pltpu.make_async_copy(conv2_ref, conv2, sems.at[0])
-    load_conv2.start()
-    loads = []
-    for step in range(copies):
-        slot = copy_index ^ step
-        loads.append(pltpu.make_async_copy(proj_refs[step], proj.at[slot], sems.at[1 + step]))
-    start_all(loads)
+    mel, banded_ref, even, odd, second, by_slot, partial = refs
     banded_weights(width, conv1_ref, banded_ref)
     streams = mel_refs[0].shape[0] // JS
     n = parts * streams
-    load_own.wait()
-    mel[part] = own[...].astype(F32)
-    for step in range(1, parts):
+    for step in range(parts):
         mel[part ^ step] = mel_refs[step][...].astype(F32)
     evens = jnp.concatenate(
         [mel[p, j * streams : (j + 1) * streams, :] for j in range(JS) for p in range(parts)], axis=0
     )
     odds = pltpu.roll(evens[: W * n], LANES - 2 * width, 1).astype(BF16)
     evens = evens.astype(BF16)
-    channels = conv2.shape[1]
+    channels = conv2_ref.shape[1]
     outs = banded_ref.shape[1] // channels
     for g in range(outs):
         lanes = slice(g * channels, (g + 1) * channels)
@@ -274,15 +275,17 @@
         even[:, lanes] = jax.nn.relu(jnp.dot(evens, weight, preferred_element_type=F32)).astype(BF16)
         odd[:, lanes] = jax.nn.relu(jnp.dot(odds, weight, preferred_element_type=F32)).astype(BF16)
 
-    load_conv2.wait()
     for h in range((outs - 1) // 2):
         lanes = slice(2 * h * channels, (2 * h + 3) * channels)
         taps = jnp.concatenate([even[: W * n, lanes], odd[:, lanes], even[n:, lanes]], axis=1)
-        total = jnp.dot(taps, conv2[...], preferred_element_type=F32)
+        total = jnp.dot(taps, conv2_ref[...], preferred_element_type=F32)
         second[:, h * channels : (h + 1) * channels] = jax.nn.relu(total).astype(BF16)
-    wait_all(loads)
-    weights = proj[...].reshape(second.shape[1], proj.shape[2])
-    sums = jnp.dot(second[...], weights, preferred_element_type=F32)
+    depth = by_slot.shape[2]
+    for slot in range(copies):
+        by_slot[slot] = second[:, slot * depth : (slot + 1) * depth]
+    sums = jnp.dot(by_slot[copy_index], proj_refs[0][...], preferred_element_type=F32)
+    for step in range(1, copies):
+        sums += jnp.dot(by_slot[copy_index ^ step], proj_refs[step][...], preferred_element_type=F32)
     for block in range(partial.shape[0]):
         partial[block] = sums[:, block * LANES : (block + 1) * LANES]
     for step in range(windows):
@@ -453,7 +456,7 @@
             pltpu.VMEM(table.shape, F32),
             pltpu.VMEM((parts, rows, LANES), BF16),
             pltpu.SMEM((streams,), jnp.int32),
-            pltpu.SemaphoreType.DMA((6,)),
+            pltpu.SemaphoreType.DMA((9,)),
         ],
         compiler_params=params(60),
         cost_estimate=cost(1e10, 2e6),
@@ -469,19 +472,16 @@
     partials = pl.pallas_call(
         functools.partial(conv_kernel, parts, width),
         out_shape=tuple([jax.ShapeDtypeStruct((W * parts, features), BF16)] * windows),
-        in_specs=[vmem()] + [anywhere()] * 2 + [vmem()] * (parts - 1) + [anywhere()] * copies,
+        in_specs=[vmem()] * (2 + parts + copies),
         out_specs=tuple([vmem()] * windows),
         scratch_shapes=[
             pltpu.VMEM((parts, rows, LANES), F32),
-            pltpu.VMEM((rows, LANES), BF16),
             pltpu.VMEM((LANES, outs * channels), BF16),
             pltpu.VMEM((JS * n, outs * channels), BF16),
             pltpu.VMEM((W * n, outs * channels), BF16),
             pltpu.VMEM((W * n, share * channels), BF16),
-            pltpu.VMEM(conv2_weight.shape, BF16),
-            pltpu.VMEM((copies,) + proj_weight.shape, BF16),
+            pltpu.VMEM((copies, W * n, proj_weight.shape[0]), BF16),
             pltpu.VMEM((features // LANES, W * n, LANES), F32),
-            pltpu.SemaphoreType.DMA((2 + copies,)),
         ],
         compiler_params=params(min(40 + 4 * scale, 56)),
         cost_estimate=cost(2e9, 4e6),
@@ -494,7 +494,7 @@
         out_shape=(block, block, jax.ShapeDtypeStruct((parts,) + mix_piece.shape, BF16)),
         in_specs=[vmem()] * windows + [anywhere()] * parts,
         out_specs=(vmem(), vmem(), vmem()),
-        scratch_shapes=[pltpu.VMEM((local, features), BF16), pltpu.SemaphoreType.DMA((parts,))],
+        scratch_shapes=[pltpu.VMEM((local, features), BF16), pltpu.SemaphoreType.DMA((CUTS * parts,))],
         compiler_params=params(min(12 * scale, 32)),
         cost_estimate=cost(1e8, 1e6),
         name="layer_norm",
@@ -530,7 +530,7 @@
         out_specs=tuple([vmem()] * (group + 1)),
         scratch_shapes=[
             pltpu.VMEM((windows, group * local, qkv_weight.shape[0]), BF16),
-            pltpu.SemaphoreType.DMA((parts,)),
+            pltpu.SemaphoreType.DMA((CUTS * parts,)),
         ],
         compiler_params=params(min(16 * scale, 48)),
         cost_estimate=cost(1e9, 2e6),

time: 66.9 us -> 67.6 us (1.010)
  Pallas kernels: 14.9 us -> 15.6 us
    pallas_call x1, Pallas kernels: 1.35 us -> 2.35 us  [on_device(): pl.pallas_call(functools.partial(attention_kernel, parts, windows, group)...]
where the time goes in v9:
time: 67.6 us; the launch traced here: 67.2 us
  starting transfers between devices  30.4 us (45%)
  waiting for transfers between devices  18.3 us (27%)
  Pallas kernels  15.6 us (23%)
  local copies, waits for them, and re-layouts  2.13 us (3%)
  between operations  0.78 us (1%)
    ppermute x9, starting transfers between devices, to_part(): return lax.ppermute(block, 'dp', pairs)  13.5 us
    ppermute x6, waiting for transfers between devices, to_plane(): return lax.ppermute(block, 'seq', [(i, i ^ step) for i in range(group)])  13.3 us
    ppermute x7, starting transfers between devices, to_window(): return lax.ppermute(block, 'dp', [(i, i ^ step) for i in range(windows)])  6.04 us
    ppermute x6, starting transfers between devices, to_plane(): return lax.ppermute(block, 'seq', [(i, i ^ step) for i in range(group)])  5.52 us
    pallas_call x1, Pallas kernels, on_device(): pl.pallas_call(functools.partial(conv_kernel, parts, width), out_shape=tu...  4.77 us
    ppermute x1, starting transfers between devices, on_device(): rim = lax.ppermute(audio[:, audio.shape[1] - RIM:], ('dp', 'seq'), route)  4.63 us
    pallas_call x1, Pallas kernels, on_device(): pl.pallas_call(functools.partial(mel_kernel, parts, group), out_shape=tup...  4.55 us
    ppermute x7, waiting for transfers between devices, to_window(): return lax.ppermute(block, 'dp', [(i, i ^ step) for i in range(windows)])  4.21 us
  transfers between devices with their start and end apart: 26, of which 10 were waited for; matrix products, arithmetic and copies ran while one was open for 1% of the time, Pallas kernels for 16%

profile of v9, /device:TPU:0, one launch (start us, length us, event | category | flops | bytes accessed | tf_op | source)
XLA Modules:
  0.0 67.2 jit_solution(1958675551331497376)
XLA Ops:
  0.6 0.5 collective-permute-start.1
  1.1 0.8 %slice.3 = f32[8,1024]{1,0:T(8,128)S(1)} slice(f32[8,5120]{1,0:T(8,128)} %audio_ref.1), slice={[0:8], [4096:5120]} | slice | bytes 65536 | tf_op jit(solution)/shard_map/slice | solution.py:429
  1.9 4.6 %collective-permute-start = (f32[8,1024]{1,0:T(8,128)S(1)}, f32[8,1024]{1,0:T(8,128)S(1)}, u32[]{:S(2)}, u32[]{:S(2)}) collective-permute-start(f32[8,1024]{1,0:T(8,128)S(1)} %slice.3), channel_id=1, source_target_pairs={{0,1},{1,2},{2,3},{3,4},{4,5},{5,6},{6,7},{7,8},{8,9},{9,10},{10,1... | collective-permute-start | bytes 98312 | tf_op jit(solution)/shard_map/ppermute | solution.py:429
  6.6 1.6 %collective-permute-start.5 = (bf16[1024,128]{1,0:T(8,128)(2,1)}, bf16[1024,128]{1,0:T(8,128)(2,1)S(1)}, u32[]{:S(2)}, u32[]{:S(2)}) collective-permute-start(bf16[1024,128]{1,0:T(8,128)(2,1)} %refs_6_), channel_id=1, source_target_pairs={{0,8},{4,12},{8,0},{12,4},{16,24},{20,28},{24,16},{28,20},{1,9},{5... | collective-permute-start | bytes 786440 | tf_op jit(solution)/shard_map/ppermute | solution.py:433
  8.1 1.5 %collective-permute-start.6 = (bf16[1024,128]{1,0:T(8,128)(2,1)}, bf16[1024,128]{1,0:T(8,128)(2,1)}, u32[]{:S(2)}, u32[]{:S(2)}) collective-permute-start(bf16[1024,128]{1,0:T(8,128)(2,1)} %refs_6_), channel_id=1, source_target_pairs={{0,16},{4,20},{8,24},{12,28},{16,0},{20,4},{24,8},{28,12},{1,17},{... | collective-permute-start | bytes 786440 | tf_op jit(solution)/shard_map/ppermute | solution.py:433
  9.6 0.0 collective-permute-done.rim_ref
  9.6 0.6 copy-done.9
  10.2 4.5 %log_mel.1 = (bf16[72,128]{1,0:T(8,128)(2,1)}, bf16[72,128]{1,0:T(8,128)(2,1)}, bf16[72,128]{1,0:T(8,128)(2,1)}, bf16[72,128]{1,0:T(8,128)(2,1)}, bf16[128,768]{1,0:T(8,128)(2,1)}) custom-call(s32[8]{0:T(128)} %slots_ref.1, f32[8,1024]{1,0:T(8,128)} %copy-done.9, f32[8,5120]{1,0:T(8,128)} %audio_ref.1, f32[264,640]{1,0:T(8,128)} %constant.2.clone.table_ref, ...), custom_call_target="tpu_custom_call" | custom-call | flops 10000000000 | bytes 2000000 | tf_op jit(solution)/shard_map/log_mel/pallas_call | solution.py:449
  14.8 3.0 %collective-permute-start.2 = (bf16[72,128]{1,0:T(8,128)(2,1)}, bf16[72,128]{1,0:T(8,128)(2,1)S(1)}, u32[]{:S(2)}, u32[]{:S(2)}) collective-permute-start(bf16[72,128]{1,0:T(8,128)(2,1)} %get-tuple-element.45), channel_id=1, source_target_pairs={{0,8},{4,12},{8,0},{12,4},{16,24},{20,28},{24,16},{28,20},{1,9},{5... | collective-permute-start | bytes 55304 | tf_op jit(solution)/shard_map/ppermute | solution.py:433
  17.8 1.6 %collective-permute-start.3 = (bf16[72,128]{1,0:T(8,128)(2,1)}, bf16[72,128]{1,0:T(8,128)(2,1)S(1)}, u32[]{:S(2)}, u32[]{:S(2)}) collective-permute-start(bf16[72,128]{1,0:T(8,128)(2,1)} %get-tuple-element.46), channel_id=1, source_target_pairs={{0,16},{4,20},{8,24},{12,28},{16,0},{20,4},{24,8},{28,12},{1,17},{... | collective-permute-start | bytes 55304 | tf_op jit(solution)/shard_map/ppermute | solution.py:433
  19.5 0.9 %collective-permute-start.4 = (bf16[72,128]{1,0:T(8,128)(2,1)}, bf16[72,128]{1,0:T(8,128)(2,1)S(1)}, u32[]{:S(2)}, u32[]{:S(2)}) collective-permute-start(bf16[72,128]{1,0:T(8,128)(2,1)} %get-tuple-element.47), channel_id=1, source_target_pairs={{0,24},{4,28},{8,16},{12,20},{16,8},{20,12},{24,0},{28,4},{1,25},{... | collective-permute-start | bytes 55304 | tf_op jit(solution)/shard_map/ppermute | solution.py:433
  20.4 2.0 %collective-permute-start.16 = (bf16[128,768]{1,0:T(8,128)(2,1)}, bf16[128,768]{1,0:T(8,128)(2,1)S(1)}, u32[]{:S(2)}, u32[]{:S(2)}) collective-permute-start(bf16[128,768]{1,0:T(8,128)(2,1)} %get-tuple-element.62.refs_8_), channel_id=1, source_target_pairs={{0,24},{4,28},{8,16},{12,20},{16,8},{20,12},{24,0},{28,4},{1,25},{... | collective-permute-start | bytes 589832 | tf_op jit(solution)/shard_map/ppermute | solution.py:433
  22.4 0.4 collective-permute-start.15
  22.8 1.1 %collective-permute-start.14 = (bf16[128,768]{1,0:T(8,128)(2,1)}, bf16[128,768]{1,0:T(8,128)(2,1)S(1)}, u32[]{:S(2)}, u32[]{:S(2)}) collective-permute-start(bf16[128,768]{1,0:T(8,128)(2,1)} %get-tuple-element.62.refs_8_), channel_id=1, source_target_pairs={{0,8},{4,12},{8,0},{12,4},{16,24},{20,28},{24,16},{28,20},{1,9},{5... | collective-permute-start | bytes 589832 | tf_op jit(solution)/shard_map/ppermute | solution.py:433
  23.9 0.7 %collective-permute-done.4.refs_3_ = bf16[72,128]{1,0:T(8,128)(2,1)S(1)} collective-permute-done((bf16[72,128]{1,0:T(8,128)(2,1)}, bf16[72,128]{1,0:T(8,128)(2,1)S(1)}, u32[]{:S(2)}, u32[]{:S(2)}) %collective-permute-start.4) | collective-permute-done | bytes 18464 | tf_op jit(solution)/shard_map/ppermute | solution.py:433
  24.7 0.0 copy-start.8
  24.7 0.7 %copy-done.8 = bf16[72,128]{1,0:T(8,128)(2,1)S(1)} copy-done((bf16[72,128]{1,0:T(8,128)(2,1)S(1)}, bf16[72,128]{1,0:T(8,128)(2,1)}, u32[]{:S(2)}) %copy-start.8) | copy-done | bytes 18456
  25.4 4.8 %conv.1 = (bf16[32,1024]{1,0:T(8,128)(2,1)S(1)}, bf16[32,1024]{1,0:T(8,128)(2,1)S(1)}, bf16[32,1024]{1,0:T(8,128)(2,1)S(1)}, bf16[32,1024]{1,0:T(8,128)(2,1)S(1)...) custom-call(bf16[9,256]{1,0:T(8,128)(2,1)S(1)} %copy-done.4, ...), custom_call_target="tpu_custom_call" | custom-call | flops 2000000000 | bytes 4000000 | tf_op jit(solution)/shard_map/conv/pallas_call | solution.py:472
  30.2 0.0 copy-start.3
  30.2 0.0 copy-start.5
  30.2 0.0 copy-start.6
  30.2 0.0 copy-start.7
  30.2 0.1 collective-permute-start.7
  30.3 1.3 %collective-permute-start.8 = (bf16[32,1024]{1,0:T(8,128)(2,1)S(1)}, bf16[32,1024]{1,0:T(8,128)(2,1)S(1)}, u32[]{:S(2)}, u32[]{:S(2)}) collective-permute-start(bf16[32,1024]{1,0:T(8,128)(2,1)S(1)} %get-tuple-element.55), channel_id=1, source_target_pairs={{0,24},{4,28},{8,16},{12,20},{16,8},{20,12},{24,0},{28,4},{1,25},{... | collective-permute-start | bytes 196616 | tf_op jit(solution)/shard_map/ppermute | solution.py:440
  31.6 2.3 %collective-permute-start.9 = (bf16[32,1024]{1,0:T(8,128)(2,1)S(1)}, bf16[32,1024]{1,0:T(8,128)(2,1)S(1)}, u32[]{:S(2)}, u32[]{:S(2)}) collective-permute-start(bf16[32,1024]{1,0:T(8,128)(2,1)S(1)} %get-tuple-element.56), channel_id=1, source_target_pairs={{0,20},{4,16},{8,28},{12,24},{16,4},{20,0},{24,12},{28,8},{1,21},{... | collective-permute-start | bytes 196616 | tf_op jit(solution)/shard_map/ppermute | solution.py:440
  33.9 0.8 %collective-permute-start.10 = (bf16[32,1024]{1,0:T(8,128)(2,1)S(1)}, bf16[32,1024]{1,0:T(8,128)(2,1)S(1)}, u32[]{:S(2)}, u32[]{:S(2)}) collective-permute-start(bf16[32,1024]{1,0:T(8,128)(2,1)S(1)} %get-tuple-element.57), channel_id=1, source_target_pairs={{0,16},{4,20},{8,24},{12,28},{16,0},{20,4},{24,8},{28,12},{1,17},{... | collective-permute-start | bytes 196616 | tf_op jit(solution)/shard_map/ppermute | solution.py:440
  34.7 0.3 collective-permute-done.7.refs_0_
  35.0 1.5 %collective-permute-start.12 = (bf16[32,1024]{1,0:T(8,128)(2,1)S(1)}, bf16[32,1024]{1,0:T(8,128)(2,1)S(1)}, u32[]{:S(2)}, u32[]{:S(2)}) collective-permute-start(bf16[32,1024]{1,0:T(8,128)(2,1)S(1)} %get-tuple-element.59), channel_id=1, source_target_pairs={{0,8},{4,12},{8,0},{12,4},{16,24},{20,28},{24,16},{28,20},{1,9},{5... | collective-permute-start | bytes 196616 | tf_op jit(solution)/shard_map/ppermute | solution.py:440
  36.5 0.1 collective-permute-start.13
  36.6 1.0 %collective-permute-done.9.refs_2_ = bf16[32,1024]{1,0:T(8,128)(2,1)S(1)} collective-permute-done((bf16[32,1024]{1,0:T(8,128)(2,1)S(1)}, bf16[32,1024]{1,0:T(8,128)(2,1)S(1)}, u32[]{:S(2)}, u32[]{:S(2)}) %collective-permute-start.9) | collective-permute-done | bytes 65568 | tf_op jit(solution)/shard_map/ppermute | solution.py:440
  37.6 1.5 %collective-permute-done.10.refs_3_ = bf16[32,1024]{1,0:T(8,128)(2,1)S(1)} collective-permute-done((bf16[32,1024]{1,0:T(8,128)(2,1)S(1)}, bf16[32,1024]{1,0:T(8,128)(2,1)S(1)}, u32[]{:S(2)}, u32[]{:S(2)}) %collective-permute-start.10) | collective-permute-done | bytes 65568 | tf_op jit(solution)/shard_map/ppermute | solution.py:440
  39.1 1.4 %collective-permute-done.12.refs_5_ = bf16[32,1024]{1,0:T(8,128)(2,1)S(1)} collective-permute-done((bf16[32,1024]{1,0:T(8,128)(2,1)S(1)}, bf16[32,1024]{1,0:T(8,128)(2,1)S(1)}, u32[]{:S(2)}, u32[]{:S(2)}) %collective-permute-start.12) | collective-permute-done | bytes 65568 | tf_op jit(solution)/shard_map/ppermute | solution.py:440
  40.5 1.5 %layer_norm.1 = (bf16[64,1024]{1,0:T(8,128)(2,1)S(1)}, bf16[64,1024]{1,0:T(8,128)(2,1)S(1)}, bf16[4,128,768]{2,1,0:T(8,128)(2,1)S(1)}) custom-call(bf16[32,1024]{1,0:T(8,128)(2,1)S(1)} %collective-permute-done.7.refs_0_, bf16[32,1024]{1,0:T(8,128)(2,1)S(1)} %collective-permute-done.8.refs_1_, bf16[32,1024]{1,0:T(8,128)(2,1)S(1)} %collective-permute-done.9.refs_2_, ...), custom_call_target="tpu_custom_call" | custom-call | flops 100000000 | bytes 1000000 | tf_op jit(solution)/shard_map/layer_norm/pallas_call | solution.py:492
  42.0 0.2 collective-permute-start.20
  42.2 1.3 %collective-permute-start.21 = (bf16[1024,128]{1,0:T(8,128)(2,1)S(1)}, bf16[1024,128]{1,0:T(8,128)(2,1)S(1)}, u32[]{:S(2)}, u32[]{:S(2)}) collective-permute-start(bf16[1024,128]{1,0:T(8,128)(2,1)S(1)} %copy-done.3), channel_id=1, source_target_pairs={{0,24},{4,28},{8,16},{12,20},{16,8},{20,12},{24,0},{28,4},{1,25},{... | collective-permute-start | bytes 786440 | tf_op jit(solution)/shard_map/ppermute | solution.py:433
  43.5 1.1 %collective-permute-start.17 = (bf16[64,1024]{1,0:T(8,128)(2,1)S(1)}, bf16[64,1024]{1,0:T(8,128)(2,1)S(1)}, u32[]{:S(2)}, u32[]{:S(2)}) collective-permute-start(bf16[64,1024]{1,0:T(8,128)(2,1)S(1)} %get-tuple-element.68.refs_0_), channel_id=1, source_target_pairs={{0,1},{1,0},{2,3},{3,2},{4,5},{5,4},{6,7},{7,6},{8,9},{9,8},{10,11... | collective-permute-start | bytes 393224 | tf_op jit(solution)/shard_map/ppermute | solution.py:443
  44.5 5.2 %collective-permute-done.18.refs_2_ = bf16[64,1024]{1,0:T(8,128)(2,1)S(1)} collective-permute-done((bf16[64,1024]{1,0:T(8,128)(2,1)S(1)}, bf16[64,1024]{1,0:T(8,128)(2,1)S(1)}, u32[]{:S(2)}, u32[]{:S(2)}) %collective-permute-start.18) | collective-permute-done | bytes 131104 | tf_op jit(solution)/shard_map/ppermute | solution.py:443
  49.8 1.3 %mask.1 = (bf16[64,1024]{1,0:T(8,128)(2,1)}, f32[4,64]{1,0:T(4,128)S(1)}, f32[64,1]{1,0:T(8,128)S(1)}) custom-call(s32[8]{0:T(128)S(1)} %copy-done.5, s32[8]{0:T(128)S(1)} %copy-done.6, s32[8]{0:T(128)S(1)} %copy-done.7, bf16[64,1024]{1,0:T(8,128)(2,1)S(1)} %get-tuple-element.63.rows_ref), custom_call_target="tpu_custom_call" | custom-call | flops 100000000 | bytes 1000000 | tf_op jit(solution)/shard_map/mask/pallas_call | solution.py:503
  51.0 0.7 %collective-permute-done.17.refs_1_ = bf16[64,1024]{1,0:T(8,128)(2,1)S(1)} collective-permute-done((bf16[64,1024]{1,0:T(8,128)(2,1)S(1)}, bf16[64,1024]{1,0:T(8,128)(2,1)S(1)}, u32[]{:S(2)}, u32[]{:S(2)}) %collective-permute-start.17) | collective-permute-done | bytes 131104 | tf_op jit(solution)/shard_map/ppermute | solution.py:443
  51.8 3.4 %collective-permute-done.19.refs_3_ = bf16[64,1024]{1,0:T(8,128)(2,1)S(1)} collective-permute-done((bf16[64,1024]{1,0:T(8,128)(2,1)S(1)}, bf16[64,1024]{1,0:T(8,128)(2,1)S(1)}, u32[]{:S(2)}, u32[]{:S(2)}) %collective-permute-start.19) | collective-permute-done | bytes 131104 | tf_op jit(solution)/shard_map/ppermute | solution.py:443
  55.2 2.3 %attention.1 = (bf16[64,256]{1,0:T(8,128)(2,1)S(1)}, bf16[64,256]{1,0:T(8,128)(2,1)S(1)}, bf16[64,256]{1,0:T(8,128)(2,1)S(1)}, bf16[64,256]{1,0:T(8,128)(2,1)S(1)}, bf16[4,1024,128]{2,1,0:T(8,128)(2,1)S(1)}) custom-call(f32[4,64]{1,0:T(4,128)S(1)} %get-tuple-element.66.keys_ref, bf16[64,1024]{1,0:T(8,128)(2,1)S(1)} %get-tuple-element.68.refs_0_, ...), custom_call_target="tpu_custom_call" | custom-call | flops 1000000000 | bytes 2000000 | tf_op jit(solution)/shard_map/attention/pallas_call | solution.py:523
  57.5 0.1 collective-permute-start.25
  57.6 0.3 collective-permute-start.22
  57.9 2.4 %collective-permute-start.23 = (bf16[64,256]{1,0:T(8,128)(2,1)S(1)}, bf16[64,256]{1,0:T(8,128)(2,1)S(1)}, u32[]{:S(2)}, u32[]{:S(2)}) collective-permute-start(bf16[64,256]{1,0:T(8,128)(2,1)S(1)} %get-tuple-element.75), channel_id=1, source_target_pairs={{0,2},{1,3},{2,0},{3,1},{4,6},{5,7},{6,4},{7,5},{8,10},{9,11},{10,... | collective-permute-start | bytes 98312 | tf_op jit(solution)/shard_map/ppermute | solution.py:443
  60.4 1.7 %collective-permute-start.24 = (bf16[64,256]{1,0:T(8,128)(2,1)S(1)}, bf16[64,256]{1,0:T(8,128)(2,1)S(1)}, u32[]{:S(2)}, u32[]{:S(2)}) collective-permute-start(bf16[64,256]{1,0:T(8,128)(2,1)S(1)} %get-tuple-element.76), channel_id=1, source_target_pairs={{0,3},{1,2},{2,1},{3,0},{4,7},{5,6},{6,5},{7,4},{8,11},{9,10},{10,... | collective-permute-start | bytes 98312 | tf_op jit(solution)/shard_map/ppermute | solution.py:443
  62.1 1.2 %collective-permute-done.23.refs_2_ = bf16[64,256]{1,0:T(8,128)(2,1)S(1)} collective-permute-done((bf16[64,256]{1,0:T(8,128)(2,1)S(1)}, bf16[64,256]{1,0:T(8,128)(2,1)S(1)}, u32[]{:S(2)}, u32[]{:S(2)}) %collective-permute-start.23) | collective-permute-done | bytes 32800 | tf_op jit(solution)/shard_map/ppermute | solution.py:443
  63.3 2.8 %collective-permute-done.24.refs_3_ = bf16[64,256]{1,0:T(8,128)(2,1)S(1)} collective-permute-done((bf16[64,256]{1,0:T(8,128)(2,1)S(1)}, bf16[64,256]{1,0:T(8,128)(2,1)S(1)}, u32[]{:S(2)}, u32[]{:S(2)}) %collective-permute-start.24) | collective-permute-done | bytes 32800 | tf_op jit(solution)/shard_map/ppermute | solution.py:443
  66.1 1.1 %output.1 = bf16[64,1024]{1,0:T(8,128)(2,1)} custom-call(f32[64,1]{1,0:T(8,128)S(1)} %get-tuple-element.65.valid_ref, bf16[64,256]{1,0:T(8,128)(2,1)S(1)} %get-tuple-element.73.refs_0_, bf16[64,256]{1,0:T(8,128)(2,1)S(1)} %collective-permute-done.22.refs_1_, bf16[64,256]{1,0:T(8,128)(2,1)S(1)} %collective-permute-done.23.refs_2_, ...), custom_call_target="tpu_custom_call" | custom-call | flops 100000000 | bytes 3000000 | tf_op jit(solution)/shard_map/output/pallas_call | solution.py:542
  (31 shorter events, 0.1 us)
Async XLA Ops:
  0.6 14.2 %collective-permute-start.1 = (bf16[640,1024]{1,0:T(8,128)(2,1)}, bf16[640,1024]{1,0:T(8,128)(2,1)S(1)}, u32[]{:S(2)}, u32[]{:S(2)}) collective-permute-start(bf16[640,1024]{1,0:T(8,128)(2,1)} %refs_4_), channel_id=1, source_target_pairs={{0,4},{4,0},{8,12},{12,8},{16,20},{20,16},{24,28},{28,24},{1,5},{5... | collective-permute-start | bytes 3932168 | tf_op jit(solution)/shard_map/ppermute | solution.py:437
  1.9 22.8 %copy-start.1 = (bf16[640,1024]{1,0:T(8,128)(2,1)S(1)}, bf16[640,1024]{1,0:T(8,128)(2,1)}, u32[]{:S(2)}) copy-start(bf16[640,1024]{1,0:T(8,128)(2,1)} %refs_4_) | copy-start | bytes 3932164
  1.9 22.8 %copy-start.2 = (bf16[2304,256]{1,0:T(8,128)(2,1)S(1)}, bf16[2304,256]{1,0:T(8,128)(2,1)}, u32[]{:S(2)}) copy-start(bf16[2304,256]{1,0:T(8,128)(2,1)} %conv2_ref.1) | copy-start | bytes 3538948
  1.9 22.8 %copy-start.4 = (bf16[9,256]{1,0:T(8,128)(2,1)S(1)}, bf16[9,256]{1,0:T(8,128)(2,1)}, u32[]{:S(2)}) copy-start(bf16[9,256]{1,0:T(8,128)(2,1)} %conv1_ref.1) | copy-start | bytes 13828
  1.9 7.7 %collective-permute-start = (f32[8,1024]{1,0:T(8,128)S(1)}, f32[8,1024]{1,0:T(8,128)S(1)}, u32[]{:S(2)}, u32[]{:S(2)}) collective-permute-start(f32[8,1024]{1,0:T(8,128)S(1)} %slice.3), channel_id=1, source_target_pairs={{0,1},{1,2},{2,3},{3,4},{4,5},{5,6},{6,7},{7,8},{8,9},{9,10},{10,1... | collective-permute-start | bytes 98312 | tf_op jit(solution)/shard_map/ppermute | solution.py:429
  6.6 13.8 %collective-permute-start.5 = (bf16[1024,128]{1,0:T(8,128)(2,1)}, bf16[1024,128]{1,0:T(8,128)(2,1)S(1)}, u32[]{:S(2)}, u32[]{:S(2)}) collective-permute-start(bf16[1024,128]{1,0:T(8,128)(2,1)} %refs_6_), channel_id=1, source_target_pairs={{0,8},{4,12},{8,0},{12,4},{16,24},{20,28},{24,16},{28,20},{1,9},{5... | collective-permute-start | bytes 786440 | tf_op jit(solution)/shard_map/ppermute | solution.py:433
  8.1 14.3 %collective-permute-start.6 = (bf16[1024,128]{1,0:T(8,128)(2,1)}, bf16[1024,128]{1,0:T(8,128)(2,1)}, u32[]{:S(2)}, u32[]{:S(2)}) collective-permute-start(bf16[1024,128]{1,0:T(8,128)(2,1)} %refs_6_), channel_id=1, source_target_pairs={{0,16},{4,20},{8,24},{12,28},{16,0},{20,4},{24,8},{28,12},{1,17},{... | collective-permute-start | bytes 786440 | tf_op jit(solution)/shard_map/ppermute | solution.py:433
  9.6 0.6 copy-start.9
  14.8 8.0 %collective-permute-start.2 = (bf16[72,128]{1,0:T(8,128)(2,1)}, bf16[72,128]{1,0:T(8,128)(2,1)S(1)}, u32[]{:S(2)}, u32[]{:S(2)}) collective-permute-start(bf16[72,128]{1,0:T(8,128)(2,1)} %get-tuple-element.45), channel_id=1, source_target_pairs={{0,8},{4,12},{8,0},{12,4},{16,24},{20,28},{24,16},{28,20},{1,9},{5... | collective-permute-start | bytes 55304 | tf_op jit(solution)/shard_map/ppermute | solution.py:433
  17.8 6.1 %collective-permute-start.3 = (bf16[72,128]{1,0:T(8,128)(2,1)}, bf16[72,128]{1,0:T(8,128)(2,1)S(1)}, u32[]{:S(2)}, u32[]{:S(2)}) collective-permute-start(bf16[72,128]{1,0:T(8,128)(2,1)} %get-tuple-element.46), channel_id=1, source_target_pairs={{0,16},{4,20},{8,24},{12,28},{16,0},{20,4},{24,8},{28,12},{1,17},{... | collective-permute-start | bytes 55304 | tf_op jit(solution)/shard_map/ppermute | solution.py:433
  19.5 5.2 %collective-permute-start.4 = (bf16[72,128]{1,0:T(8,128)(2,1)}, bf16[72,128]{1,0:T(8,128)(2,1)S(1)}, u32[]{:S(2)}, u32[]{:S(2)}) collective-permute-start(bf16[72,128]{1,0:T(8,128)(2,1)} %get-tuple-element.47), channel_id=1, source_target_pairs={{0,24},{4,28},{8,16},{12,20},{16,8},{20,12},{24,0},{28,4},{1,25},{... | collective-permute-start | bytes 55304 | tf_op jit(solution)/shard_map/ppermute | solution.py:433
  20.4 20.2 %copy-start = (bf16[128,768]{1,0:T(8,128)(2,1)S(1)}, bf16[128,768]{1,0:T(8,128)(2,1)}, u32[]{:S(2)}) copy-start(bf16[128,768]{1,0:T(8,128)(2,1)} %get-tuple-element.62.refs_8_) | copy-start | bytes 589828
  20.4 11.3 %collective-permute-start.16 = (bf16[128,768]{1,0:T(8,128)(2,1)}, bf16[128,768]{1,0:T(8,128)(2,1)S(1)}, u32[]{:S(2)}, u32[]{:S(2)}) collective-permute-start(bf16[128,768]{1,0:T(8,128)(2,1)} %get-tuple-element.62.refs_8_), channel_id=1, source_target_pairs={{0,24},{4,28},{8,16},{12,20},{16,8},{20,12},{24,0},{28,4},{1,25},{... | collective-permute-start | bytes 589832 | tf_op jit(solution)/shard_map/ppermute | solution.py:433
  22.4 11.5 %collective-permute-start.15 = (bf16[128,768]{1,0:T(8,128)(2,1)}, bf16[128,768]{1,0:T(8,128)(2,1)S(1)}, u32[]{:S(2)}, u32[]{:S(2)}) collective-permute-start(bf16[128,768]{1,0:T(8,128)(2,1)} %get-tuple-element.62.refs_8_), channel_id=1, source_target_pairs={{0,16},{4,20},{8,24},{12,28},{16,0},{20,4},{24,8},{28,12},{1,17},{... | collective-permute-start | bytes 589832 | tf_op jit(solution)/shard_map/ppermute | solution.py:433
  22.8 11.9 %collective-permute-start.14 = (bf16[128,768]{1,0:T(8,128)(2,1)}, bf16[128,768]{1,0:T(8,128)(2,1)S(1)}, u32[]{:S(2)}, u32[]{:S(2)}) collective-permute-start(bf16[128,768]{1,0:T(8,128)(2,1)} %get-tuple-element.62.refs_8_), channel_id=1, source_target_pairs={{0,8},{4,12},{8,0},{12,4},{16,24},{20,28},{24,16},{28,20},{1,9},{5... | collective-permute-start | bytes 589832 | tf_op jit(solution)/shard_map/ppermute | solution.py:433
  24.7 0.7 %copy-start.8 = (bf16[72,128]{1,0:T(8,128)(2,1)S(1)}, bf16[72,128]{1,0:T(8,128)(2,1)}, u32[]{:S(2)}) copy-start(bf16[72,128]{1,0:T(8,128)(2,1)} %get-tuple-element.48.refs_0_) | copy-start | bytes 55300
  30.2 12.0 %copy-start.3 = (bf16[1024,128]{1,0:T(8,128)(2,1)S(1)}, bf16[1024,128]{1,0:T(8,128)(2,1)}, u32[]{:S(2)}) copy-start(bf16[1024,128]{1,0:T(8,128)(2,1)} %refs_6_) | copy-start | bytes 786436
  30.2 19.6 %copy-start.5 = (s32[8]{0:T(128)S(1)}, s32[8]{0:T(128)}, u32[]{:S(2)}) copy-start(s32[8]{0:T(128)} %slots_ref.1) | copy-start | bytes 100
  30.2 19.5 %copy-start.6 = (s32[8]{0:T(128)S(1)}, s32[8]{0:T(128)}, u32[]{:S(2)}) copy-start(s32[8]{0:T(128)} %starts_ref.1) | copy-start | bytes 100
  30.2 19.5 %copy-start.7 = (s32[8]{0:T(128)S(1)}, s32[8]{0:T(128)}, u32[]{:S(2)}) copy-start(s32[8]{0:T(128)} %lengths_ref.1) | copy-start | bytes 100
  30.2 4.7 %collective-permute-start.7 = (bf16[32,1024]{1,0:T(8,128)(2,1)S(1)}, bf16[32,1024]{1,0:T(8,128)(2,1)S(1)}, u32[]{:S(2)}, u32[]{:S(2)}) collective-permute-start(bf16[32,1024]{1,0:T(8,128)(2,1)S(1)} %get-tuple-element.54), channel_id=1, source_target_pairs={{0,28},{4,24},{8,20},{12,16},{16,12},{20,8},{24,4},{28,0},{1,29},{... | collective-permute-start | bytes 196616 | tf_op jit(solution)/shard_map/ppermute | solution.py:440
  30.3 6.2 %collective-permute-start.8 = (bf16[32,1024]{1,0:T(8,128)(2,1)S(1)}, bf16[32,1024]{1,0:T(8,128)(2,1)S(1)}, u32[]{:S(2)}, u32[]{:S(2)}) collective-permute-start(bf16[32,1024]{1,0:T(8,128)(2,1)S(1)} %get-tuple-element.55), channel_id=1, source_target_pairs={{0,24},{4,28},{8,16},{12,20},{16,8},{20,12},{24,0},{28,4},{1,25},{... | collective-permute-start | bytes 196616 | tf_op jit(solution)/shard_map/ppermute | solution.py:440
  31.6 6.0 %collective-permute-start.9 = (bf16[32,1024]{1,0:T(8,128)(2,1)S(1)}, bf16[32,1024]{1,0:T(8,128)(2,1)S(1)}, u32[]{:S(2)}, u32[]{:S(2)}) collective-permute-start(bf16[32,1024]{1,0:T(8,128)(2,1)S(1)} %get-tuple-element.56), channel_id=1, source_target_pairs={{0,20},{4,16},{8,28},{12,24},{16,4},{20,0},{24,12},{28,8},{1,21},{... | collective-permute-start | bytes 196616 | tf_op jit(solution)/shard_map/ppermute | solution.py:440
  33.9 5.2 %collective-permute-start.10 = (bf16[32,1024]{1,0:T(8,128)(2,1)S(1)}, bf16[32,1024]{1,0:T(8,128)(2,1)S(1)}, u32[]{:S(2)}, u32[]{:S(2)}) collective-permute-start(bf16[32,1024]{1,0:T(8,128)(2,1)S(1)} %get-tuple-element.57), channel_id=1, source_target_pairs={{0,16},{4,20},{8,24},{12,28},{16,0},{20,4},{24,8},{28,12},{1,17},{... | collective-permute-start | bytes 196616 | tf_op jit(solution)/shard_map/ppermute | solution.py:440
  34.7 4.4 %collective-permute-start.11 = (bf16[32,1024]{1,0:T(8,128)(2,1)S(1)}, bf16[32,1024]{1,0:T(8,128)(2,1)S(1)}, u32[]{:S(2)}, u32[]{:S(2)}) collective-permute-start(bf16[32,1024]{1,0:T(8,128)(2,1)S(1)} %get-tuple-element.58), channel_id=1, source_target_pairs={{0,12},{4,8},{8,4},{12,0},{16,28},{20,24},{24,20},{28,16},{1,13},{... | collective-permute-start | bytes 196616 | tf_op jit(solution)/shard_map/ppermute | solution.py:440
  35.0 5.5 %collective-permute-start.12 = (bf16[32,1024]{1,0:T(8,128)(2,1)S(1)}, bf16[32,1024]{1,0:T(8,128)(2,1)S(1)}, u32[]{:S(2)}, u32[]{:S(2)}) collective-permute-start(bf16[32,1024]{1,0:T(8,128)(2,1)S(1)} %get-tuple-element.59), channel_id=1, source_target_pairs={{0,8},{4,12},{8,0},{12,4},{16,24},{20,28},{24,16},{28,20},{1,9},{5... | collective-permute-start | bytes 196616 | tf_op jit(solution)/shard_map/ppermute | solution.py:440
  36.5 4.0 %collective-permute-start.13 = (bf16[32,1024]{1,0:T(8,128)(2,1)S(1)}, bf16[32,1024]{1,0:T(8,128)(2,1)S(1)}, u32[]{:S(2)}, u32[]{:S(2)}) collective-permute-start(bf16[32,1024]{1,0:T(8,128)(2,1)S(1)} %get-tuple-element.60), channel_id=1, source_target_pairs={{0,4},{4,0},{8,12},{12,8},{16,20},{20,16},{24,28},{28,24},{1,5},{5... | collective-permute-start | bytes 196616 | tf_op jit(solution)/shard_map/ppermute | solution.py:440
  42.0 13.1 %collective-permute-start.20 = (bf16[4,128,768]{2,1,0:T(8,128)(2,1)S(1)}, bf16[4,128,768]{2,1,0:T(8,128)(2,1)S(1)}, u32[]{:S(2)}, u32[]{:S(2)}) collective-permute-start(bf16[4,128,768]{2,1,0:T(8,128)(2,1)S(1)} %get-tuple-element.69.refs_4_), channel_id=1, source_target_pairs={{0,4},{4,0},{8,12},{12,8},{16,20},{20,16},{24,28},{28,24},{1,5},{5... | collective-permute-start | bytes 2359304 | tf_op jit(solution)/shard_map/ppermute | solution.py:437
  42.2 7.6 %collective-permute-start.18 = (bf16[64,1024]{1,0:T(8,128)(2,1)S(1)}, bf16[64,1024]{1,0:T(8,128)(2,1)S(1)}, u32[]{:S(2)}, u32[]{:S(2)}) collective-permute-start(bf16[64,1024]{1,0:T(8,128)(2,1)S(1)} %get-tuple-element.68.refs_0_), channel_id=1, source_target_pairs={{0,2},{1,3},{2,0},{3,1},{4,6},{5,7},{6,4},{7,5},{8,10},{9,11},{10,... | collective-permute-start | bytes 393224 | tf_op jit(solution)/shard_map/ppermute | solution.py:443
  42.2 13.0 %collective-permute-start.21 = (bf16[1024,128]{1,0:T(8,128)(2,1)S(1)}, bf16[1024,128]{1,0:T(8,128)(2,1)S(1)}, u32[]{:S(2)}, u32[]{:S(2)}) collective-permute-start(bf16[1024,128]{1,0:T(8,128)(2,1)S(1)} %copy-done.3), channel_id=1, source_target_pairs={{0,24},{4,28},{8,16},{12,20},{16,8},{20,12},{24,0},{28,4},{1,25},{... | collective-permute-start | bytes 786440 | tf_op jit(solution)/shard_map/ppermute | solution.py:433
  43.5 8.3 %collective-permute-start.17 = (bf16[64,1024]{1,0:T(8,128)(2,1)S(1)}, bf16[64,1024]{1,0:T(8,128)(2,1)S(1)}, u32[]{:S(2)}, u32[]{:S(2)}) collective-permute-start(bf16[64,1024]{1,0:T(8,128)(2,1)S(1)} %get-tuple-element.68.refs_0_), channel_id=1, source_target_pairs={{0,1},{1,0},{2,3},{3,2},{4,5},{5,4},{6,7},{7,6},{8,9},{9,8},{10,11... | collective-permute-start | bytes 393224 | tf_op jit(solution)/shard_map/ppermute | solution.py:443
  49.7 5.4 %collective-permute-start.19 = (bf16[64,1024]{1,0:T(8,128)(2,1)S(1)}, bf16[64,1024]{1,0:T(8,128)(2,1)S(1)}, u32[]{:S(2)}, u32[]{:S(2)}) collective-permute-start(bf16[64,1024]{1,0:T(8,128)(2,1)S(1)} %collective-permute-done.18.refs_2_), channel_id=1, source_target_pairs={{0,1},{1,0},{2,3},{3,2},{4,5},{5,4},{6,7},{7,6},{8,9},{9,8},{10,11... | collective-permute-start | bytes 393224 | tf_op jit(solution)/shard_map/ppermute | solution.py:443
  57.5 8.6 %collective-permute-start.25 = (bf16[4,1024,128]{2,1,0:T(8,128)(2,1)S(1)}, bf16[4,1024,128]{2,1,0:T(8,128)(2,1)S(1)}, u32[]{:S(2)}, u32[]{:S(2)}) collective-permute-start(bf16[4,1024,128]{2,1,0:T(8,128)(2,1)S(1)} %get-tuple-element.77.refs_4_), channel_id=1, source_target_pairs={{0,4},{4,0},{8,12},{12,8},{16,20},{20,16},{24,28},{28,24},{1,5},{5... | collective-permute-start | bytes 3145736 | tf_op jit(solution)/shard_map/ppermute | solution.py:437
  57.6 4.5 %collective-permute-start.22 = (bf16[64,256]{1,0:T(8,128)(2,1)S(1)}, bf16[64,256]{1,0:T(8,128)(2,1)S(1)}, u32[]{:S(2)}, u32[]{:S(2)}) collective-permute-start(bf16[64,256]{1,0:T(8,128)(2,1)S(1)} %get-tuple-element.74), channel_id=1, source_target_pairs={{0,1},{1,0},{2,3},{3,2},{4,5},{5,4},{6,7},{7,6},{8,9},{9,8},{10,11... | collective-permute-start | bytes 98312 | tf_op jit(solution)/shard_map/ppermute | solution.py:443
  57.9 5.4 %collective-permute-start.23 = (bf16[64,256]{1,0:T(8,128)(2,1)S(1)}, bf16[64,256]{1,0:T(8,128)(2,1)S(1)}, u32[]{:S(2)}, u32[]{:S(2)}) collective-permute-start(bf16[64,256]{1,0:T(8,128)(2,1)S(1)} %get-tuple-element.75), channel_id=1, source_target_pairs={{0,2},{1,3},{2,0},{3,1},{4,6},{5,7},{6,4},{7,5},{8,10},{9,11},{10,... | collective-permute-start | bytes 98312 | tf_op jit(solution)/shard_map/ppermute | solution.py:443
  60.4 5.7 %collective-permute-start.24 = (bf16[64,256]{1,0:T(8,128)(2,1)S(1)}, bf16[64,256]{1,0:T(8,128)(2,1)S(1)}, u32[]{:S(2)}, u32[]{:S(2)}) collective-permute-start(bf16[64,256]{1,0:T(8,128)(2,1)S(1)} %get-tuple-element.76), channel_id=1, source_target_pairs={{0,3},{1,2},{2,1},{3,0},{4,7},{5,6},{6,5},{7,4},{8,11},{9,10},{10,... | collective-permute-start | bytes 98312 | tf_op jit(solution)/shard_map/ppermute | solution.py:443

commit v10 on v9

--- a/solution.py
+++ b/solution.py
@@ -20,7 +20,6 @@
 SPAN = 4 * HOP
 JS = W + 1
 LANES = 128
-CUTS = 2
 SAMPLE_RATE = 16000.0
 EPS_LOG = 1e-06
 EPS_NORM = 1e-05
@@ -156,13 +155,9 @@
     load_slots = pltpu.make_async_copy(slots_here, slots_ref, sems.at[5])
     load_slots.start()
     load_audio = pltpu.make_async_copy(audio_ref, ext.at[:, pl.ds(RIM, audio_ref.shape[1])], sems.at[3])
-    third = table_ref.shape[0] // 3
-    load_table = [
-        pltpu.make_async_copy(table_ref.at[pl.ds(i * third, third)], table.at[pl.ds(i * third, third)], sems.at[6 + i])
-        for i in range(3)
-    ]
+    load_table = pltpu.make_async_copy(table_ref, table, sems.at[4])
     load_audio.start()
-    start_all(load_table)
+    load_table.start()
     pieces = mix_columns(group, qkv_ref, mix_out, sems)
     start_all(pieces)
     streams = audio_ref.shape[0]
@@ -181,7 +176,7 @@
             block = pltpu.roll(block, length - shift, 1)[:, :N_FFT]
         phases.append(block)
     frames = jnp.concatenate(phases, axis=0)
-    wait_all(load_table)
+    load_table.wait()
     half = N_FFT // 2
     frames = frames * table[half : half + 1, :N_FFT]
     low, high = frames[:, :half], frames[:, half:]
@@ -235,17 +230,10 @@
 
 def stacked(parts, pieces, stack_out, sems, base):
     part, _ = place(parts)
-    rows = stack_out.shape[1] // CUTS
-    copies = []
-    for step in range(parts):
-        for cut in range(CUTS):
-            at = pl.ds(cut * rows, rows)
-            copies.append(
-                pltpu.make_async_copy(
-                    pieces[step].at[at], stack_out.at[part ^ step, at], sems.at[base + len(copies)]
-                )
-            )
-    return copies
+    return [
+        pltpu.make_async_copy(pieces[step], stack_out.at[part ^ step], sems.at[base + step])
+        for step in range(parts)
+    ]
 
 
 def conv_kernel(parts, width, conv1_ref, conv2_ref, *refs):
@@ -304,14 +292,14 @@
 
 
 def norm_kernel(parts, *refs):
-    _, copy_index = place(parts)
+    part, copy_index = place(parts)
     windows = lax.axis_size("dp")
     copies = windows // parts
     part_refs, refs = refs[:windows][::-1], refs[windows:]
     piece_refs, refs = refs[:parts], refs[parts:]
-    rows_out, normed_out, stack_out, encoded, sems = refs
-    moves = stacked(parts, piece_refs, stack_out, sems, 0)
-    start_all(moves)
+    rows_out, normed_out, stack_out, encoded = refs
+    for step in range(parts):
+        stack_out[part ^ step] = piece_refs[step][...]
     rows = W * parts
     for copy in range(copies):
         total = part_refs[copy][...].astype(F32)
@@ -325,7 +313,6 @@
     centered = values - mean
     variance = jnp.mean(centered * centered, axis=-1, keepdims=True)
     normed_out[...] = (centered * lax.rsqrt(variance + EPS_NORM)).astype(BF16)
-    wait_all(moves)
 
 
 def mask_kernel(windows, group, slots_ref, starts_ref, lengths_ref, rows_ref, rows_out, keys_out, valid_out):
@@ -456,7 +443,7 @@
             pltpu.VMEM(table.shape, F32),
             pltpu.VMEM((parts, rows, LANES), BF16),
             pltpu.SMEM((streams,), jnp.int32),
-            pltpu.SemaphoreType.DMA((9,)),
+            pltpu.SemaphoreType.DMA((6,)),
         ],
         compiler_params=params(60),
         cost_estimate=cost(1e10, 2e6),
@@ -492,9 +479,9 @@
     ordered, normed, stack = pl.pallas_call(
         functools.partial(norm_kernel, parts),
         out_shape=(block, block, jax.ShapeDtypeStruct((parts,) + mix_piece.shape, BF16)),
-        in_specs=[vmem()] * windows + [anywhere()] * parts,
+        in_specs=[vmem()] * (windows + parts),
         out_specs=(vmem(), vmem(), vmem()),
-        scratch_shapes=[pltpu.VMEM((local, features), BF16), pltpu.SemaphoreType.DMA((CUTS * parts,))],
+        scratch_shapes=[pltpu.VMEM((local, features), BF16)],
         compiler_params=params(min(12 * scale, 32)),
         cost_estimate=cost(1e8, 1e6),
         name="layer_norm",
@@ -530,7 +517,7 @@
         out_specs=tuple([vmem()] * (group + 1)),
         scratch_shapes=[
             pltpu.VMEM((windows, group * local, qkv_weight.shape[0]), BF16),
-            pltpu.SemaphoreType.DMA((CUTS * parts,)),
+            pltpu.SemaphoreType.DMA((parts,)),
         ],
         compiler_params=params(min(16 * scale, 48)),
         cost_estimate=cost(1e9, 2e6),

time: 67.6 us -> 65.4 us (0.967)
  Pallas kernels: 15.6 us -> 13.5 us
    pallas_call x1, Pallas kernels: 1.52 us -> 0.49 us  [on_device(): pl.pallas_call(functools.partial(norm_kernel, parts), out_shape=(block, b...]
    pallas_call x1, Pallas kernels: 2.35 us -> 1.35 us  [on_device(): pl.pallas_call(functools.partial(attention_kernel, parts, windows, group)...]
where the time goes in v10:
time: 65.4 us; the launch traced here: 65.1 us
  starting transfers between devices  30.4 us (46%)
  waiting for transfers between devices  18.3 us (28%)
  Pallas kernels  13.5 us (21%)
  local copies, waits for them, and re-layouts  2.13 us (3%)
  between operations  0.78 us (1%)
    ppermute x9, starting transfers between devices, to_part(): return lax.ppermute(block, 'dp', pairs)  13.5 us
    ppermute x6, waiting for transfers between devices, to_plane(): return lax.ppermute(block, 'seq', [(i, i ^ step) for i in range(group)])  13.3 us
    ppermute x7, starting transfers between devices, to_window(): return lax.ppermute(block, 'dp', [(i, i ^ step) for i in range(windows)])  6.04 us
    ppermute x6, starting transfers between devices, to_plane(): return lax.ppermute(block, 'seq', [(i, i ^ step) for i in range(group)])  5.52 us
    pallas_call x1, Pallas kernels, on_device(): pl.pallas_call(functools.partial(conv_kernel, parts, width), out_shape=tu...  4.77 us
    ppermute x1, starting transfers between devices, on_device(): rim = lax.ppermute(audio[:, audio.shape[1] - RIM:], ('dp', 'seq'), route)  4.63 us
    pallas_call x1, Pallas kernels, on_device(): pl.pallas_call(functools.partial(mel_kernel, parts, group), out_shape=tup...  4.47 us
    ppermute x7, waiting for transfers between devices, to_window(): return lax.ppermute(block, 'dp', [(i, i ^ step) for i in range(windows)])  4.21 us
  transfers between devices with their start and end apart: 26, of which 10 were waited for; matrix products, arithmetic and copies ran while one was open for 1% of the time, Pallas kernels for 16%

profile of v10, /device:TPU:0, one launch (start us, length us, event | category | flops | bytes accessed | tf_op | source)
XLA Modules:
  0.0 65.1 jit_solution(12390389367754298031)
XLA Ops:
  0.6 0.5 collective-permute-start.1
  1.1 0.8 %slice.3 = f32[8,1024]{1,0:T(8,128)S(1)} slice(f32[8,5120]{1,0:T(8,128)} %audio_ref.1), slice={[0:8], [4096:5120]} | slice | bytes 65536 | tf_op jit(solution)/shard_map/slice | solution.py:416
  1.9 4.6 %collective-permute-start = (f32[8,1024]{1,0:T(8,128)S(1)}, f32[8,1024]{1,0:T(8,128)S(1)}, u32[]{:S(2)}, u32[]{:S(2)}) collective-permute-start(f32[8,1024]{1,0:T(8,128)S(1)} %slice.3), channel_id=1, source_target_pairs={{0,1},{1,2},{2,3},{3,4},{4,5},{5,6},{6,7},{7,8},{8,9},{9,10},{10,1... | collective-permute-start | bytes 98312 | tf_op jit(solution)/shard_map/ppermute | solution.py:416
  6.6 1.6 %collective-permute-start.5 = (bf16[1024,128]{1,0:T(8,128)(2,1)}, bf16[1024,128]{1,0:T(8,128)(2,1)S(1)}, u32[]{:S(2)}, u32[]{:S(2)}) collective-permute-start(bf16[1024,128]{1,0:T(8,128)(2,1)} %refs_6_), channel_id=1, source_target_pairs={{0,8},{4,12},{8,0},{12,4},{16,24},{20,28},{24,16},{28,20},{1,9},{5... | collective-permute-start | bytes 786440 | tf_op jit(solution)/shard_map/ppermute | solution.py:420
  8.1 1.5 %collective-permute-start.6 = (bf16[1024,128]{1,0:T(8,128)(2,1)}, bf16[1024,128]{1,0:T(8,128)(2,1)}, u32[]{:S(2)}, u32[]{:S(2)}) collective-permute-start(bf16[1024,128]{1,0:T(8,128)(2,1)} %refs_6_), channel_id=1, source_target_pairs={{0,16},{4,20},{8,24},{12,28},{16,0},{20,4},{24,8},{28,12},{1,17},{... | collective-permute-start | bytes 786440 | tf_op jit(solution)/shard_map/ppermute | solution.py:420
  9.6 0.0 collective-permute-done.rim_ref
  9.6 0.6 copy-done.9
  10.2 4.5 %log_mel.1 = (bf16[72,128]{1,0:T(8,128)(2,1)}, bf16[72,128]{1,0:T(8,128)(2,1)}, bf16[72,128]{1,0:T(8,128)(2,1)}, bf16[72,128]{1,0:T(8,128)(2,1)}, bf16[128,768]{1,0:T(8,128)(2,1)}) custom-call(s32[8]{0:T(128)} %slots_ref.1, f32[8,1024]{1,0:T(8,128)} %copy-done.9, f32[8,5120]{1,0:T(8,128)} %audio_ref.1, f32[264,640]{1,0:T(8,128)} %constant.2.clone.table_ref, ...), custom_call_target="tpu_custom_call" | custom-call | flops 10000000000 | bytes 2000000 | tf_op jit(solution)/shard_map/log_mel/pallas_call | solution.py:436
  14.7 3.0 %collective-permute-start.2 = (bf16[72,128]{1,0:T(8,128)(2,1)}, bf16[72,128]{1,0:T(8,128)(2,1)S(1)}, u32[]{:S(2)}, u32[]{:S(2)}) collective-permute-start(bf16[72,128]{1,0:T(8,128)(2,1)} %get-tuple-element.45), channel_id=1, source_target_pairs={{0,8},{4,12},{8,0},{12,4},{16,24},{20,28},{24,16},{28,20},{1,9},{5... | collective-permute-start | bytes 55304 | tf_op jit(solution)/shard_map/ppermute | solution.py:420
  17.8 1.6 %collective-permute-start.3 = (bf16[72,128]{1,0:T(8,128)(2,1)}, bf16[72,128]{1,0:T(8,128)(2,1)S(1)}, u32[]{:S(2)}, u32[]{:S(2)}) collective-permute-start(bf16[72,128]{1,0:T(8,128)(2,1)} %get-tuple-element.46), channel_id=1, source_target_pairs={{0,16},{4,20},{8,24},{12,28},{16,0},{20,4},{24,8},{28,12},{1,17},{... | collective-permute-start | bytes 55304 | tf_op jit(solution)/shard_map/ppermute | solution.py:420
  19.4 0.9 %collective-permute-start.4 = (bf16[72,128]{1,0:T(8,128)(2,1)}, bf16[72,128]{1,0:T(8,128)(2,1)S(1)}, u32[]{:S(2)}, u32[]{:S(2)}) collective-permute-start(bf16[72,128]{1,0:T(8,128)(2,1)} %get-tuple-element.47), channel_id=1, source_target_pairs={{0,24},{4,28},{8,16},{12,20},{16,8},{20,12},{24,0},{28,4},{1,25},{... | collective-permute-start | bytes 55304 | tf_op jit(solution)/shard_map/ppermute | solution.py:420
  20.3 2.0 %collective-permute-start.16 = (bf16[128,768]{1,0:T(8,128)(2,1)}, bf16[128,768]{1,0:T(8,128)(2,1)S(1)}, u32[]{:S(2)}, u32[]{:S(2)}) collective-permute-start(bf16[128,768]{1,0:T(8,128)(2,1)} %get-tuple-element.62.refs_8_), channel_id=1, source_target_pairs={{0,24},{4,28},{8,16},{12,20},{16,8},{20,12},{24,0},{28,4},{1,25},{... | collective-permute-start | bytes 589832 | tf_op jit(solution)/shard_map/ppermute | solution.py:420
  22.3 0.4 collective-permute-start.15
  22.7 1.1 %collective-permute-start.14 = (bf16[128,768]{1,0:T(8,128)(2,1)}, bf16[128,768]{1,0:T(8,128)(2,1)S(1)}, u32[]{:S(2)}, u32[]{:S(2)}) collective-permute-start(bf16[128,768]{1,0:T(8,128)(2,1)} %get-tuple-element.62.refs_8_), channel_id=1, source_target_pairs={{0,8},{4,12},{8,0},{12,4},{16,24},{20,28},{24,16},{28,20},{1,9},{5... | collective-permute-start | bytes 589832 | tf_op jit(solution)/shard_map/ppermute | solution.py:420
  23.8 0.7 %collective-permute-done.4.refs_3_ = bf16[72,128]{1,0:T(8,128)(2,1)S(1)} collective-permute-done((bf16[72,128]{1,0:T(8,128)(2,1)}, bf16[72,128]{1,0:T(8,128)(2,1)S(1)}, u32[]{:S(2)}, u32[]{:S(2)}) %collective-permute-start.4) | collective-permute-done | bytes 18464 | tf_op jit(solution)/shard_map/ppermute | solution.py:420
  24.6 0.0 copy-start.8
  24.6 0.7 %copy-done.8 = bf16[72,128]{1,0:T(8,128)(2,1)S(1)} copy-done((bf16[72,128]{1,0:T(8,128)(2,1)S(1)}, bf16[72,128]{1,0:T(8,128)(2,1)}, u32[]{:S(2)}) %copy-start.8) | copy-done | bytes 18456
  25.3 4.8 %conv.1 = (bf16[32,1024]{1,0:T(8,128)(2,1)S(1)}, bf16[32,1024]{1,0:T(8,128)(2,1)S(1)}, bf16[32,1024]{1,0:T(8,128)(2,1)S(1)}, bf16[32,1024]{1,0:T(8,128)(2,1)S(1)...) custom-call(bf16[9,256]{1,0:T(8,128)(2,1)S(1)} %copy-done.4, ...), custom_call_target="tpu_custom_call" | custom-call | flops 2000000000 | bytes 4000000 | tf_op jit(solution)/shard_map/conv/pallas_call | solution.py:459
  30.1 0.0 copy-start.3
  30.1 0.0 copy-start.5
  30.1 0.0 copy-start.6
  30.1 0.0 copy-start.7
  30.2 0.1 collective-permute-start.7
  30.2 1.3 %collective-permute-start.8 = (bf16[32,1024]{1,0:T(8,128)(2,1)S(1)}, bf16[32,1024]{1,0:T(8,128)(2,1)S(1)}, u32[]{:S(2)}, u32[]{:S(2)}) collective-permute-start(bf16[32,1024]{1,0:T(8,128)(2,1)S(1)} %get-tuple-element.55), channel_id=1, source_target_pairs={{0,24},{4,28},{8,16},{12,20},{16,8},{20,12},{24,0},{28,4},{1,25},{... | collective-permute-start | bytes 196616 | tf_op jit(solution)/shard_map/ppermute | solution.py:427
  31.5 2.3 %collective-permute-start.9 = (bf16[32,1024]{1,0:T(8,128)(2,1)S(1)}, bf16[32,1024]{1,0:T(8,128)(2,1)S(1)}, u32[]{:S(2)}, u32[]{:S(2)}) collective-permute-start(bf16[32,1024]{1,0:T(8,128)(2,1)S(1)} %get-tuple-element.56), channel_id=1, source_target_pairs={{0,20},{4,16},{8,28},{12,24},{16,4},{20,0},{24,12},{28,8},{1,21},{... | collective-permute-start | bytes 196616 | tf_op jit(solution)/shard_map/ppermute | solution.py:427
  33.8 0.8 %collective-permute-start.10 = (bf16[32,1024]{1,0:T(8,128)(2,1)S(1)}, bf16[32,1024]{1,0:T(8,128)(2,1)S(1)}, u32[]{:S(2)}, u32[]{:S(2)}) collective-permute-start(bf16[32,1024]{1,0:T(8,128)(2,1)S(1)} %get-tuple-element.57), channel_id=1, source_target_pairs={{0,16},{4,20},{8,24},{12,28},{16,0},{20,4},{24,8},{28,12},{1,17},{... | collective-permute-start | bytes 196616 | tf_op jit(solution)/shard_map/ppermute | solution.py:427
  34.6 0.3 collective-permute-done.7.refs_0_
  34.9 1.5 %collective-permute-start.12 = (bf16[32,1024]{1,0:T(8,128)(2,1)S(1)}, bf16[32,1024]{1,0:T(8,128)(2,1)S(1)}, u32[]{:S(2)}, u32[]{:S(2)}) collective-permute-start(bf16[32,1024]{1,0:T(8,128)(2,1)S(1)} %get-tuple-element.59), channel_id=1, source_target_pairs={{0,8},{4,12},{8,0},{12,4},{16,24},{20,28},{24,16},{28,20},{1,9},{5... | collective-permute-start | bytes 196616 | tf_op jit(solution)/shard_map/ppermute | solution.py:427
  36.4 0.1 collective-permute-start.13
  36.5 1.0 %collective-permute-done.9.refs_2_ = bf16[32,1024]{1,0:T(8,128)(2,1)S(1)} collective-permute-done((bf16[32,1024]{1,0:T(8,128)(2,1)S(1)}, bf16[32,1024]{1,0:T(8,128)(2,1)S(1)}, u32[]{:S(2)}, u32[]{:S(2)}) %collective-permute-start.9) | collective-permute-done | bytes 65568 | tf_op jit(solution)/shard_map/ppermute | solution.py:427
  37.5 1.5 %collective-permute-done.10.refs_3_ = bf16[32,1024]{1,0:T(8,128)(2,1)S(1)} collective-permute-done((bf16[32,1024]{1,0:T(8,128)(2,1)S(1)}, bf16[32,1024]{1,0:T(8,128)(2,1)S(1)}, u32[]{:S(2)}, u32[]{:S(2)}) %collective-permute-start.10) | collective-permute-done | bytes 65568 | tf_op jit(solution)/shard_map/ppermute | solution.py:427
  39.0 1.4 %collective-permute-done.12.refs_5_ = bf16[32,1024]{1,0:T(8,128)(2,1)S(1)} collective-permute-done((bf16[32,1024]{1,0:T(8,128)(2,1)S(1)}, bf16[32,1024]{1,0:T(8,128)(2,1)S(1)}, u32[]{:S(2)}, u32[]{:S(2)}) %collective-permute-start.12) | collective-permute-done | bytes 65568 | tf_op jit(solution)/shard_map/ppermute | solution.py:427
  40.4 0.5 layer_norm.1
  40.9 0.2 collective-permute-start.20
  41.1 1.3 %collective-permute-start.21 = (bf16[1024,128]{1,0:T(8,128)(2,1)S(1)}, bf16[1024,128]{1,0:T(8,128)(2,1)S(1)}, u32[]{:S(2)}, u32[]{:S(2)}) collective-permute-start(bf16[1024,128]{1,0:T(8,128)(2,1)S(1)} %copy-done.3), channel_id=1, source_target_pairs={{0,24},{4,28},{8,16},{12,20},{16,8},{20,12},{24,0},{28,4},{1,25},{... | collective-permute-start | bytes 786440 | tf_op jit(solution)/shard_map/ppermute | solution.py:420
  42.4 1.1 %collective-permute-start.17 = (bf16[64,1024]{1,0:T(8,128)(2,1)S(1)}, bf16[64,1024]{1,0:T(8,128)(2,1)S(1)}, u32[]{:S(2)}, u32[]{:S(2)}) collective-permute-start(bf16[64,1024]{1,0:T(8,128)(2,1)S(1)} %get-tuple-element.68.refs_0_), channel_id=1, source_target_pairs={{0,1},{1,0},{2,3},{3,2},{4,5},{5,4},{6,7},{7,6},{8,9},{9,8},{10,11... | collective-permute-start | bytes 393224 | tf_op jit(solution)/shard_map/ppermute | solution.py:430
  43.4 5.2 %collective-permute-done.18.refs_2_ = bf16[64,1024]{1,0:T(8,128)(2,1)S(1)} collective-permute-done((bf16[64,1024]{1,0:T(8,128)(2,1)S(1)}, bf16[64,1024]{1,0:T(8,128)(2,1)S(1)}, u32[]{:S(2)}, u32[]{:S(2)}) %collective-permute-start.18) | collective-permute-done | bytes 131104 | tf_op jit(solution)/shard_map/ppermute | solution.py:430
  48.7 1.3 %mask.1 = (bf16[64,1024]{1,0:T(8,128)(2,1)}, f32[4,64]{1,0:T(4,128)S(1)}, f32[64,1]{1,0:T(8,128)S(1)}) custom-call(s32[8]{0:T(128)S(1)} %copy-done.5, s32[8]{0:T(128)S(1)} %copy-done.6, s32[8]{0:T(128)S(1)} %copy-done.7, bf16[64,1024]{1,0:T(8,128)(2,1)S(1)} %get-tuple-element.63.rows_ref), custom_call_target="tpu_custom_call" | custom-call | flops 100000000 | bytes 1000000 | tf_op jit(solution)/shard_map/mask/pallas_call | solution.py:490
  49.9 0.7 %collective-permute-done.17.refs_1_ = bf16[64,1024]{1,0:T(8,128)(2,1)S(1)} collective-permute-done((bf16[64,1024]{1,0:T(8,128)(2,1)S(1)}, bf16[64,1024]{1,0:T(8,128)(2,1)S(1)}, u32[]{:S(2)}, u32[]{:S(2)}) %collective-permute-start.17) | collective-permute-done | bytes 131104 | tf_op jit(solution)/shard_map/ppermute | solution.py:430
  50.7 3.4 %collective-permute-done.19.refs_3_ = bf16[64,1024]{1,0:T(8,128)(2,1)S(1)} collective-permute-done((bf16[64,1024]{1,0:T(8,128)(2,1)S(1)}, bf16[64,1024]{1,0:T(8,128)(2,1)S(1)}, u32[]{:S(2)}, u32[]{:S(2)}) %collective-permute-start.19) | collective-permute-done | bytes 131104 | tf_op jit(solution)/shard_map/ppermute | solution.py:430
  54.1 1.4 %attention.1 = (bf16[64,256]{1,0:T(8,128)(2,1)S(1)}, bf16[64,256]{1,0:T(8,128)(2,1)S(1)}, bf16[64,256]{1,0:T(8,128)(2,1)S(1)}, bf16[64,256]{1,0:T(8,128)(2,1)S(1)}, bf16[4,1024,128]{2,1,0:T(8,128)(2,1)S(1)}) custom-call(f32[4,64]{1,0:T(4,128)S(1)} %get-tuple-element.66.keys_ref, bf16[64,1024]{1,0:T(8,128)(2,1)S(1)} %get-tuple-element.68.refs_0_, ...), custom_call_target="tpu_custom_call" | custom-call | flops 1000000000 | bytes 2000000 | tf_op jit(solution)/shard_map/attention/pallas_call | solution.py:510
  55.4 0.1 collective-permute-start.25
  55.5 0.3 collective-permute-start.22
  55.8 2.4 %collective-permute-start.23 = (bf16[64,256]{1,0:T(8,128)(2,1)S(1)}, bf16[64,256]{1,0:T(8,128)(2,1)S(1)}, u32[]{:S(2)}, u32[]{:S(2)}) collective-permute-start(bf16[64,256]{1,0:T(8,128)(2,1)S(1)} %get-tuple-element.75), channel_id=1, source_target_pairs={{0,2},{1,3},{2,0},{3,1},{4,6},{5,7},{6,4},{7,5},{8,10},{9,11},{10,... | collective-permute-start | bytes 98312 | tf_op jit(solution)/shard_map/ppermute | solution.py:430
  58.3 1.7 %collective-permute-start.24 = (bf16[64,256]{1,0:T(8,128)(2,1)S(1)}, bf16[64,256]{1,0:T(8,128)(2,1)S(1)}, u32[]{:S(2)}, u32[]{:S(2)}) collective-permute-start(bf16[64,256]{1,0:T(8,128)(2,1)S(1)} %get-tuple-element.76), channel_id=1, source_target_pairs={{0,3},{1,2},{2,1},{3,0},{4,7},{5,6},{6,5},{7,4},{8,11},{9,10},{10,... | collective-permute-start | bytes 98312 | tf_op jit(solution)/shard_map/ppermute | solution.py:430
  60.0 1.3 %collective-permute-done.23.refs_2_ = bf16[64,256]{1,0:T(8,128)(2,1)S(1)} collective-permute-done((bf16[64,256]{1,0:T(8,128)(2,1)S(1)}, bf16[64,256]{1,0:T(8,128)(2,1)S(1)}, u32[]{:S(2)}, u32[]{:S(2)}) %collective-permute-start.23) | collective-permute-done | bytes 32800 | tf_op jit(solution)/shard_map/ppermute | solution.py:430
  61.2 2.8 %collective-permute-done.24.refs_3_ = bf16[64,256]{1,0:T(8,128)(2,1)S(1)} collective-permute-done((bf16[64,256]{1,0:T(8,128)(2,1)S(1)}, bf16[64,256]{1,0:T(8,128)(2,1)S(1)}, u32[]{:S(2)}, u32[]{:S(2)}) %collective-permute-start.24) | collective-permute-done | bytes 32800 | tf_op jit(solution)/shard_map/ppermute | solution.py:430
  64.0 1.1 %output.1 = bf16[64,1024]{1,0:T(8,128)(2,1)} custom-call(f32[64,1]{1,0:T(8,128)S(1)} %get-tuple-element.65.valid_ref, bf16[64,256]{1,0:T(8,128)(2,1)S(1)} %get-tuple-element.73.refs_0_, bf16[64,256]{1,0:T(8,128)(2,1)S(1)} %collective-permute-done.22.refs_1_, bf16[64,256]{1,0:T(8,128)(2,1)S(1)} %collective-permute-done.23.refs_2_, ...), custom_call_target="tpu_custom_call" | custom-call | flops 100000000 | bytes 3000000 | tf_op jit(solution)/shard_map/output/pallas_call | solution.py:529
  (31 shorter events, 0.1 us)
Async XLA Ops:
  0.6 14.1 %collective-permute-start.1 = (bf16[640,1024]{1,0:T(8,128)(2,1)}, bf16[640,1024]{1,0:T(8,128)(2,1)S(1)}, u32[]{:S(2)}, u32[]{:S(2)}) collective-permute-start(bf16[640,1024]{1,0:T(8,128)(2,1)} %refs_4_), channel_id=1, source_target_pairs={{0,4},{4,0},{8,12},{12,8},{16,20},{20,16},{24,28},{28,24},{1,5},{5... | collective-permute-start | bytes 3932168 | tf_op jit(solution)/shard_map/ppermute | solution.py:424
  1.9 22.7 %copy-start.1 = (bf16[640,1024]{1,0:T(8,128)(2,1)S(1)}, bf16[640,1024]{1,0:T(8,128)(2,1)}, u32[]{:S(2)}) copy-start(bf16[640,1024]{1,0:T(8,128)(2,1)} %refs_4_) | copy-start | bytes 3932164
  1.9 22.7 %copy-start.2 = (bf16[2304,256]{1,0:T(8,128)(2,1)S(1)}, bf16[2304,256]{1,0:T(8,128)(2,1)}, u32[]{:S(2)}) copy-start(bf16[2304,256]{1,0:T(8,128)(2,1)} %conv2_ref.1) | copy-start | bytes 3538948
  1.9 22.7 %copy-start.4 = (bf16[9,256]{1,0:T(8,128)(2,1)S(1)}, bf16[9,256]{1,0:T(8,128)(2,1)}, u32[]{:S(2)}) copy-start(bf16[9,256]{1,0:T(8,128)(2,1)} %conv1_ref.1) | copy-start | bytes 13828
  1.9 7.7 %collective-permute-start = (f32[8,1024]{1,0:T(8,128)S(1)}, f32[8,1024]{1,0:T(8,128)S(1)}, u32[]{:S(2)}, u32[]{:S(2)}) collective-permute-start(f32[8,1024]{1,0:T(8,128)S(1)} %slice.3), channel_id=1, source_target_pairs={{0,1},{1,2},{2,3},{3,4},{4,5},{5,6},{6,7},{7,8},{8,9},{9,10},{10,1... | collective-permute-start | bytes 98312 | tf_op jit(solution)/shard_map/ppermute | solution.py:416
  6.6 13.7 %collective-permute-start.5 = (bf16[1024,128]{1,0:T(8,128)(2,1)}, bf16[1024,128]{1,0:T(8,128)(2,1)S(1)}, u32[]{:S(2)}, u32[]{:S(2)}) collective-permute-start(bf16[1024,128]{1,0:T(8,128)(2,1)} %refs_6_), channel_id=1, source_target_pairs={{0,8},{4,12},{8,0},{12,4},{16,24},{20,28},{24,16},{28,20},{1,9},{5... | collective-permute-start | bytes 786440 | tf_op jit(solution)/shard_map/ppermute | solution.py:420
  8.1 14.2 %collective-permute-start.6 = (bf16[1024,128]{1,0:T(8,128)(2,1)}, bf16[1024,128]{1,0:T(8,128)(2,1)}, u32[]{:S(2)}, u32[]{:S(2)}) collective-permute-start(bf16[1024,128]{1,0:T(8,128)(2,1)} %refs_6_), channel_id=1, source_target_pairs={{0,16},{4,20},{8,24},{12,28},{16,0},{20,4},{24,8},{28,12},{1,17},{... | collective-permute-start | bytes 786440 | tf_op jit(solution)/shard_map/ppermute | solution.py:420
  9.6 0.6 copy-start.9
  14.7 8.0 %collective-permute-start.2 = (bf16[72,128]{1,0:T(8,128)(2,1)}, bf16[72,128]{1,0:T(8,128)(2,1)S(1)}, u32[]{:S(2)}, u32[]{:S(2)}) collective-permute-start(bf16[72,128]{1,0:T(8,128)(2,1)} %get-tuple-element.45), channel_id=1, source_target_pairs={{0,8},{4,12},{8,0},{12,4},{16,24},{20,28},{24,16},{28,20},{1,9},{5... | collective-permute-start | bytes 55304 | tf_op jit(solution)/shard_map/ppermute | solution.py:420
  17.8 6.1 %collective-permute-start.3 = (bf16[72,128]{1,0:T(8,128)(2,1)}, bf16[72,128]{1,0:T(8,128)(2,1)S(1)}, u32[]{:S(2)}, u32[]{:S(2)}) collective-permute-start(bf16[72,128]{1,0:T(8,128)(2,1)} %get-tuple-element.46), channel_id=1, source_target_pairs={{0,16},{4,20},{8,24},{12,28},{16,0},{20,4},{24,8},{28,12},{1,17},{... | collective-permute-start | bytes 55304 | tf_op jit(solution)/shard_map/ppermute | solution.py:420
  19.4 5.2 %collective-permute-start.4 = (bf16[72,128]{1,0:T(8,128)(2,1)}, bf16[72,128]{1,0:T(8,128)(2,1)S(1)}, u32[]{:S(2)}, u32[]{:S(2)}) collective-permute-start(bf16[72,128]{1,0:T(8,128)(2,1)} %get-tuple-element.47), channel_id=1, source_target_pairs={{0,24},{4,28},{8,16},{12,20},{16,8},{20,12},{24,0},{28,4},{1,25},{... | collective-permute-start | bytes 55304 | tf_op jit(solution)/shard_map/ppermute | solution.py:420
  20.3 20.2 %copy-start = (bf16[128,768]{1,0:T(8,128)(2,1)S(1)}, bf16[128,768]{1,0:T(8,128)(2,1)}, u32[]{:S(2)}) copy-start(bf16[128,768]{1,0:T(8,128)(2,1)} %get-tuple-element.62.refs_8_) | copy-start | bytes 589828
  20.3 11.3 %collective-permute-start.16 = (bf16[128,768]{1,0:T(8,128)(2,1)}, bf16[128,768]{1,0:T(8,128)(2,1)S(1)}, u32[]{:S(2)}, u32[]{:S(2)}) collective-permute-start(bf16[128,768]{1,0:T(8,128)(2,1)} %get-tuple-element.62.refs_8_), channel_id=1, source_target_pairs={{0,24},{4,28},{8,16},{12,20},{16,8},{20,12},{24,0},{28,4},{1,25},{... | collective-permute-start | bytes 589832 | tf_op jit(solution)/shard_map/ppermute | solution.py:420
  22.3 11.5 %collective-permute-start.15 = (bf16[128,768]{1,0:T(8,128)(2,1)}, bf16[128,768]{1,0:T(8,128)(2,1)S(1)}, u32[]{:S(2)}, u32[]{:S(2)}) collective-permute-start(bf16[128,768]{1,0:T(8,128)(2,1)} %get-tuple-element.62.refs_8_), channel_id=1, source_target_pairs={{0,16},{4,20},{8,24},{12,28},{16,0},{20,4},{24,8},{28,12},{1,17},{... | collective-permute-start | bytes 589832 | tf_op jit(solution)/shard_map/ppermute | solution.py:420
  22.7 11.9 %collective-permute-start.14 = (bf16[128,768]{1,0:T(8,128)(2,1)}, bf16[128,768]{1,0:T(8,128)(2,1)S(1)}, u32[]{:S(2)}, u32[]{:S(2)}) collective-permute-start(bf16[128,768]{1,0:T(8,128)(2,1)} %get-tuple-element.62.refs_8_), channel_id=1, source_target_pairs={{0,8},{4,12},{8,0},{12,4},{16,24},{20,28},{24,16},{28,20},{1,9},{5... | collective-permute-start | bytes 589832 | tf_op jit(solution)/shard_map/ppermute | solution.py:420
  24.6 0.7 %copy-start.8 = (bf16[72,128]{1,0:T(8,128)(2,1)S(1)}, bf16[72,128]{1,0:T(8,128)(2,1)}, u32[]{:S(2)}) copy-start(bf16[72,128]{1,0:T(8,128)(2,1)} %get-tuple-element.48.refs_0_) | copy-start | bytes 55300
  30.1 11.0 %copy-start.3 = (bf16[1024,128]{1,0:T(8,128)(2,1)S(1)}, bf16[1024,128]{1,0:T(8,128)(2,1)}, u32[]{:S(2)}) copy-start(bf16[1024,128]{1,0:T(8,128)(2,1)} %refs_6_) | copy-start | bytes 786436
  30.1 18.5 %copy-start.5 = (s32[8]{0:T(128)S(1)}, s32[8]{0:T(128)}, u32[]{:S(2)}) copy-start(s32[8]{0:T(128)} %slots_ref.1) | copy-start | bytes 100
  30.1 18.5 %copy-start.6 = (s32[8]{0:T(128)S(1)}, s32[8]{0:T(128)}, u32[]{:S(2)}) copy-start(s32[8]{0:T(128)} %starts_ref.1) | copy-start | bytes 100
  30.1 18.5 %copy-start.7 = (s32[8]{0:T(128)S(1)}, s32[8]{0:T(128)}, u32[]{:S(2)}) copy-start(s32[8]{0:T(128)} %lengths_ref.1) | copy-start | bytes 100
  30.2 4.7 %collective-permute-start.7 = (bf16[32,1024]{1,0:T(8,128)(2,1)S(1)}, bf16[32,1024]{1,0:T(8,128)(2,1)S(1)}, u32[]{:S(2)}, u32[]{:S(2)}) collective-permute-start(bf16[32,1024]{1,0:T(8,128)(2,1)S(1)} %get-tuple-element.54), channel_id=1, source_target_pairs={{0,28},{4,24},{8,20},{12,16},{16,12},{20,8},{24,4},{28,0},{1,29},{... | collective-permute-start | bytes 196616 | tf_op jit(solution)/shard_map/ppermute | solution.py:427
  30.2 6.2 %collective-permute-start.8 = (bf16[32,1024]{1,0:T(8,128)(2,1)S(1)}, bf16[32,1024]{1,0:T(8,128)(2,1)S(1)}, u32[]{:S(2)}, u32[]{:S(2)}) collective-permute-start(bf16[32,1024]{1,0:T(8,128)(2,1)S(1)} %get-tuple-element.55), channel_id=1, source_target_pairs={{0,24},{4,28},{8,16},{12,20},{16,8},{20,12},{24,0},{28,4},{1,25},{... | collective-permute-start | bytes 196616 | tf_op jit(solution)/shard_map/ppermute | solution.py:427
  31.5 6.0 %collective-permute-start.9 = (bf16[32,1024]{1,0:T(8,128)(2,1)S(1)}, bf16[32,1024]{1,0:T(8,128)(2,1)S(1)}, u32[]{:S(2)}, u32[]{:S(2)}) collective-permute-start(bf16[32,1024]{1,0:T(8,128)(2,1)S(1)} %get-tuple-element.56), channel_id=1, source_target_pairs={{0,20},{4,16},{8,28},{12,24},{16,4},{20,0},{24,12},{28,8},{1,21},{... | collective-permute-start | bytes 196616 | tf_op jit(solution)/shard_map/ppermute | solution.py:427
  33.8 5.2 %collective-permute-start.10 = (bf16[32,1024]{1,0:T(8,128)(2,1)S(1)}, bf16[32,1024]{1,0:T(8,128)(2,1)S(1)}, u32[]{:S(2)}, u32[]{:S(2)}) collective-permute-start(bf16[32,1024]{1,0:T(8,128)(2,1)S(1)} %get-tuple-element.57), channel_id=1, source_target_pairs={{0,16},{4,20},{8,24},{12,28},{16,0},{20,4},{24,8},{28,12},{1,17},{... | collective-permute-start | bytes 196616 | tf_op jit(solution)/shard_map/ppermute | solution.py:427
  34.6 4.4 %collective-permute-start.11 = (bf16[32,1024]{1,0:T(8,128)(2,1)S(1)}, bf16[32,1024]{1,0:T(8,128)(2,1)S(1)}, u32[]{:S(2)}, u32[]{:S(2)}) collective-permute-start(bf16[32,1024]{1,0:T(8,128)(2,1)S(1)} %get-tuple-element.58), channel_id=1, source_target_pairs={{0,12},{4,8},{8,4},{12,0},{16,28},{20,24},{24,20},{28,16},{1,13},{... | collective-permute-start | bytes 196616 | tf_op jit(solution)/shard_map/ppermute | solution.py:427
  34.9 5.5 %collective-permute-start.12 = (bf16[32,1024]{1,0:T(8,128)(2,1)S(1)}, bf16[32,1024]{1,0:T(8,128)(2,1)S(1)}, u32[]{:S(2)}, u32[]{:S(2)}) collective-permute-start(bf16[32,1024]{1,0:T(8,128)(2,1)S(1)} %get-tuple-element.59), channel_id=1, source_target_pairs={{0,8},{4,12},{8,0},{12,4},{16,24},{20,28},{24,16},{28,20},{1,9},{5... | collective-permute-start | bytes 196616 | tf_op jit(solution)/shard_map/ppermute | solution.py:427
  36.4 4.0 %collective-permute-start.13 = (bf16[32,1024]{1,0:T(8,128)(2,1)S(1)}, bf16[32,1024]{1,0:T(8,128)(2,1)S(1)}, u32[]{:S(2)}, u32[]{:S(2)}) collective-permute-start(bf16[32,1024]{1,0:T(8,128)(2,1)S(1)} %get-tuple-element.60), channel_id=1, source_target_pairs={{0,4},{4,0},{8,12},{12,8},{16,20},{20,16},{24,28},{28,24},{1,5},{5... | collective-permute-start | bytes 196616 | tf_op jit(solution)/shard_map/ppermute | solution.py:427
  40.9 13.1 %collective-permute-start.20 = (bf16[4,128,768]{2,1,0:T(8,128)(2,1)S(1)}, bf16[4,128,768]{2,1,0:T(8,128)(2,1)S(1)}, u32[]{:S(2)}, u32[]{:S(2)}) collective-permute-start(bf16[4,128,768]{2,1,0:T(8,128)(2,1)S(1)} %get-tuple-element.69.refs_4_), channel_id=1, source_target_pairs={{0,4},{4,0},{8,12},{12,8},{16,20},{20,16},{24,28},{28,24},{1,5},{5... | collective-permute-start | bytes 2359304 | tf_op jit(solution)/shard_map/ppermute | solution.py:424
  41.1 7.6 %collective-permute-start.18 = (bf16[64,1024]{1,0:T(8,128)(2,1)S(1)}, bf16[64,1024]{1,0:T(8,128)(2,1)S(1)}, u32[]{:S(2)}, u32[]{:S(2)}) collective-permute-start(bf16[64,1024]{1,0:T(8,128)(2,1)S(1)} %get-tuple-element.68.refs_0_), channel_id=1, source_target_pairs={{0,2},{1,3},{2,0},{3,1},{4,6},{5,7},{6,4},{7,5},{8,10},{9,11},{10,... | collective-permute-start | bytes 393224 | tf_op jit(solution)/shard_map/ppermute | solution.py:430
  41.1 13.0 %collective-permute-start.21 = (bf16[1024,128]{1,0:T(8,128)(2,1)S(1)}, bf16[1024,128]{1,0:T(8,128)(2,1)S(1)}, u32[]{:S(2)}, u32[]{:S(2)}) collective-permute-start(bf16[1024,128]{1,0:T(8,128)(2,1)S(1)} %copy-done.3), channel_id=1, source_target_pairs={{0,24},{4,28},{8,16},{12,20},{16,8},{20,12},{24,0},{28,4},{1,25},{... | collective-permute-start | bytes 786440 | tf_op jit(solution)/shard_map/ppermute | solution.py:420
  42.4 8.3 %collective-permute-start.17 = (bf16[64,1024]{1,0:T(8,128)(2,1)S(1)}, bf16[64,1024]{1,0:T(8,128)(2,1)S(1)}, u32[]{:S(2)}, u32[]{:S(2)}) collective-permute-start(bf16[64,1024]{1,0:T(8,128)(2,1)S(1)} %get-tuple-element.68.refs_0_), channel_id=1, source_target_pairs={{0,1},{1,0},{2,3},{3,2},{4,5},{5,4},{6,7},{7,6},{8,9},{9,8},{10,11... | collective-permute-start | bytes 393224 | tf_op jit(solution)/shard_map/ppermute | solution.py:430
  48.6 5.4 %collective-permute-start.19 = (bf16[64,1024]{1,0:T(8,128)(2,1)S(1)}, bf16[64,1024]{1,0:T(8,128)(2,1)S(1)}, u32[]{:S(2)}, u32[]{:S(2)}) collective-permute-start(bf16[64,1024]{1,0:T(8,128)(2,1)S(1)} %collective-permute-done.18.refs_2_), channel_id=1, source_target_pairs={{0,1},{1,0},{2,3},{3,2},{4,5},{5,4},{6,7},{7,6},{8,9},{9,8},{10,11... | collective-permute-start | bytes 393224 | tf_op jit(solution)/shard_map/ppermute | solution.py:430
  55.4 8.6 %collective-permute-start.25 = (bf16[4,1024,128]{2,1,0:T(8,128)(2,1)S(1)}, bf16[4,1024,128]{2,1,0:T(8,128)(2,1)S(1)}, u32[]{:S(2)}, u32[]{:S(2)}) collective-permute-start(bf16[4,1024,128]{2,1,0:T(8,128)(2,1)S(1)} %get-tuple-element.77.refs_4_), channel_id=1, source_target_pairs={{0,4},{4,0},{8,12},{12,8},{16,20},{20,16},{24,28},{28,24},{1,5},{5... | collective-permute-start | bytes 3145736 | tf_op jit(solution)/shard_map/ppermute | solution.py:424
  55.5 4.5 %collective-permute-start.22 = (bf16[64,256]{1,0:T(8,128)(2,1)S(1)}, bf16[64,256]{1,0:T(8,128)(2,1)S(1)}, u32[]{:S(2)}, u32[]{:S(2)}) collective-permute-start(bf16[64,256]{1,0:T(8,128)(2,1)S(1)} %get-tuple-element.74), channel_id=1, source_target_pairs={{0,1},{1,0},{2,3},{3,2},{4,5},{5,4},{6,7},{7,6},{8,9},{9,8},{10,11... | collective-permute-start | bytes 98312 | tf_op jit(solution)/shard_map/ppermute | solution.py:430
  55.8 5.4 %collective-permute-start.23 = (bf16[64,256]{1,0:T(8,128)(2,1)S(1)}, bf16[64,256]{1,0:T(8,128)(2,1)S(1)}, u32[]{:S(2)}, u32[]{:S(2)}) collective-permute-start(bf16[64,256]{1,0:T(8,128)(2,1)S(1)} %get-tuple-element.75), channel_id=1, source_target_pairs={{0,2},{1,3},{2,0},{3,1},{4,6},{5,7},{6,4},{7,5},{8,10},{9,11},{10,... | collective-permute-start | bytes 98312 | tf_op jit(solution)/shard_map/ppermute | solution.py:430
  58.3 5.7 %collective-permute-start.24 = (bf16[64,256]{1,0:T(8,128)(2,1)S(1)}, bf16[64,256]{1,0:T(8,128)(2,1)S(1)}, u32[]{:S(2)}, u32[]{:S(2)}) collective-permute-start(bf16[64,256]{1,0:T(8,128)(2,1)S(1)} %get-tuple-element.76), channel_id=1, source_target_pairs={{0,3},{1,2},{2,1},{3,0},{4,7},{5,6},{6,5},{7,4},{8,11},{9,10},{10,... | collective-permute-start | bytes 98312 | tf_op jit(solution)/shard_map/ppermute | solution.py:430

commit v11 on v10

--- a/solution.py
+++ b/solution.py
@@ -228,14 +228,6 @@
     wait_all(pieces)
 
 
-def stacked(parts, pieces, stack_out, sems, base):
-    part, _ = place(parts)
-    return [
-        pltpu.make_async_copy(pieces[step], stack_out.at[part ^ step], sems.at[base + step])
-        for step in range(parts)
-    ]
-
-
 def conv_kernel(parts, width, conv1_ref, conv2_ref, *refs):
     part, copy_index = place(parts)
     mine = lax.axis_index("dp")
@@ -326,15 +318,15 @@
 
 
 def attention_kernel(parts, windows, group, keys_ref, *refs):
-    _, copy_index = place(parts)
+    part, copy_index = place(parts)
     plane = lax.axis_index("seq")
     copies = windows // parts
     normed_refs, refs = refs[:group], refs[group:]
     stack_refs, refs = refs[:copies], refs[copies:]
     weight_refs, refs = refs[:parts], refs[parts:]
-    outs_refs, (stack_out, pieces, sems) = refs[:group], refs[group:]
-    moves = stacked(parts, weight_refs, stack_out, sems, 0)
-    start_all(moves)
+    outs_refs, (stack_out, pieces) = refs[:group], refs[group:]
+    for step in range(parts):
+        stack_out[part ^ step] = weight_refs[step][...]
     keys = [keys_ref[pl.ds(plane ^ step, 1), :] for step in range(group)]
     valid = jnp.concatenate(keys, axis=1) > 0.5
     local = normed_refs[0].shape[0]
@@ -367,7 +359,6 @@
         context = (summed / total).astype(BF16)
         for step in range(group):
             outs_refs[step][:, at : at + HEAD_DIM] = context[step * local : (step + 1) * local]
-    wait_all(moves)
 
 
 def output_kernel(parts, windows, group, valid_ref, *refs):
@@ -513,12 +504,9 @@
             [jax.ShapeDtypeStruct((local, head_width), BF16)] * group
             + [jax.ShapeDtypeStruct((parts,) + out_weight.shape, BF16)]
         ),
-        in_specs=[vmem()] * (1 + group + copies) + [anywhere()] * parts,
+        in_specs=[vmem()] * (1 + group + copies + parts),
         out_specs=tuple([vmem()] * (group + 1)),
-        scratch_shapes=[
-            pltpu.VMEM((windows, group * local, qkv_weight.shape[0]), BF16),
-            pltpu.SemaphoreType.DMA((parts,)),
-        ],
+        scratch_shapes=[pltpu.VMEM((windows, group * local, qkv_weight.shape[0]), BF16)],
         compiler_params=params(min(16 * scale, 48)),
         cost_estimate=cost(1e9, 2e6),
         name="attention",

time: 65.4 us -> 66.4 us (1.015)
  Pallas kernels: 13.5 us -> 14.4 us
    pallas_call x1, Pallas kernels: 1.35 us -> 2.31 us  [on_device(): pl.pallas_call(functools.partial(attention_kernel, parts, windows, group)...]
where the time goes in v11:
time: 66.4 us; the launch traced here: 66 us
  starting transfers between devices  30.4 us (46%)
  waiting for transfers between devices  18.3 us (28%)
  Pallas kernels  14.4 us (22%)
  local copies, waits for them, and re-layouts  2.13 us (3%)
  between operations  0.78 us (1%)
    ppermute x9, starting transfers between devices, to_part(): return lax.ppermute(block, 'dp', pairs)  13.5 us
    ppermute x6, waiting for transfers between devices, to_plane(): return lax.ppermute(block, 'seq', [(i, i ^ step) for i in range(group)])  13.3 us
    ppermute x7, starting transfers between devices, to_window(): return lax.ppermute(block, 'dp', [(i, i ^ step) for i in range(windows)])  6.04 us
    ppermute x6, starting transfers between devices, to_plane(): return lax.ppermute(block, 'seq', [(i, i ^ step) for i in range(group)])  5.52 us
    pallas_call x1, Pallas kernels, on_device(): pl.pallas_call(functools.partial(conv_kernel, parts, width), out_shape=tu...  4.77 us
    ppermute x1, starting transfers between devices, on_device(): rim = lax.ppermute(audio[:, audio.shape[1] - RIM:], ('dp', 'seq'), route)  4.63 us
    pallas_call x1, Pallas kernels, on_device(): pl.pallas_call(functools.partial(mel_kernel, parts, group), out_shape=tup...  4.47 us
    ppermute x7, waiting for transfers between devices, to_window(): return lax.ppermute(block, 'dp', [(i, i ^ step) for i in range(windows)])  4.21 us
  transfers between devices with their start and end apart: 26, of which 10 were waited for; matrix products, arithmetic and copies ran while one was open for 1% of the time, Pallas kernels for 16%

profile of v11, /device:TPU:0, one launch (start us, length us, event | category | flops | bytes accessed | tf_op | source)
XLA Modules:
  0.0 66.0 jit_solution(10712451964662577170)
XLA Ops:
  0.6 0.5 collective-permute-start.1
  1.1 0.8 %slice.3 = f32[8,1024]{1,0:T(8,128)S(1)} slice(f32[8,5120]{1,0:T(8,128)} %audio_ref.1), slice={[0:8], [4096:5120]} | slice | bytes 65536 | tf_op jit(solution)/shard_map/slice | solution.py:407
  1.9 4.6 %collective-permute-start = (f32[8,1024]{1,0:T(8,128)S(1)}, f32[8,1024]{1,0:T(8,128)S(1)}, u32[]{:S(2)}, u32[]{:S(2)}) collective-permute-start(f32[8,1024]{1,0:T(8,128)S(1)} %slice.3), channel_id=1, source_target_pairs={{0,1},{1,2},{2,3},{3,4},{4,5},{5,6},{6,7},{7,8},{8,9},{9,10},{10,1... | collective-permute-start | bytes 98312 | tf_op jit(solution)/shard_map/ppermute | solution.py:407
  6.6 1.6 %collective-permute-start.5 = (bf16[1024,128]{1,0:T(8,128)(2,1)}, bf16[1024,128]{1,0:T(8,128)(2,1)S(1)}, u32[]{:S(2)}, u32[]{:S(2)}) collective-permute-start(bf16[1024,128]{1,0:T(8,128)(2,1)} %refs_6_), channel_id=1, source_target_pairs={{0,8},{4,12},{8,0},{12,4},{16,24},{20,28},{24,16},{28,20},{1,9},{5... | collective-permute-start | bytes 786440 | tf_op jit(solution)/shard_map/ppermute | solution.py:411
  8.1 1.5 %collective-permute-start.6 = (bf16[1024,128]{1,0:T(8,128)(2,1)}, bf16[1024,128]{1,0:T(8,128)(2,1)}, u32[]{:S(2)}, u32[]{:S(2)}) collective-permute-start(bf16[1024,128]{1,0:T(8,128)(2,1)} %refs_6_), channel_id=1, source_target_pairs={{0,16},{4,20},{8,24},{12,28},{16,0},{20,4},{24,8},{28,12},{1,17},{... | collective-permute-start | bytes 786440 | tf_op jit(solution)/shard_map/ppermute | solution.py:411
  9.6 0.0 collective-permute-done.rim_ref
  9.6 0.6 copy-done.9
  10.2 4.5 %log_mel.1 = (bf16[72,128]{1,0:T(8,128)(2,1)}, bf16[72,128]{1,0:T(8,128)(2,1)}, bf16[72,128]{1,0:T(8,128)(2,1)}, bf16[72,128]{1,0:T(8,128)(2,1)}, bf16[128,768]{1,0:T(8,128)(2,1)}) custom-call(s32[8]{0:T(128)} %slots_ref.1, f32[8,1024]{1,0:T(8,128)} %copy-done.9, f32[8,5120]{1,0:T(8,128)} %audio_ref.1, f32[264,640]{1,0:T(8,128)} %constant.2.clone.table_ref, ...), custom_call_target="tpu_custom_call" | custom-call | flops 10000000000 | bytes 2000000 | tf_op jit(solution)/shard_map/log_mel/pallas_call | solution.py:427
  14.7 3.0 %collective-permute-start.2 = (bf16[72,128]{1,0:T(8,128)(2,1)}, bf16[72,128]{1,0:T(8,128)(2,1)S(1)}, u32[]{:S(2)}, u32[]{:S(2)}) collective-permute-start(bf16[72,128]{1,0:T(8,128)(2,1)} %get-tuple-element.45), channel_id=1, source_target_pairs={{0,8},{4,12},{8,0},{12,4},{16,24},{20,28},{24,16},{28,20},{1,9},{5... | collective-permute-start | bytes 55304 | tf_op jit(solution)/shard_map/ppermute | solution.py:411
  17.8 1.6 %collective-permute-start.3 = (bf16[72,128]{1,0:T(8,128)(2,1)}, bf16[72,128]{1,0:T(8,128)(2,1)S(1)}, u32[]{:S(2)}, u32[]{:S(2)}) collective-permute-start(bf16[72,128]{1,0:T(8,128)(2,1)} %get-tuple-element.46), channel_id=1, source_target_pairs={{0,16},{4,20},{8,24},{12,28},{16,0},{20,4},{24,8},{28,12},{1,17},{... | collective-permute-start | bytes 55304 | tf_op jit(solution)/shard_map/ppermute | solution.py:411
  19.4 0.9 %collective-permute-start.4 = (bf16[72,128]{1,0:T(8,128)(2,1)}, bf16[72,128]{1,0:T(8,128)(2,1)S(1)}, u32[]{:S(2)}, u32[]{:S(2)}) collective-permute-start(bf16[72,128]{1,0:T(8,128)(2,1)} %get-tuple-element.47), channel_id=1, source_target_pairs={{0,24},{4,28},{8,16},{12,20},{16,8},{20,12},{24,0},{28,4},{1,25},{... | collective-permute-start | bytes 55304 | tf_op jit(solution)/shard_map/ppermute | solution.py:411
  20.3 2.0 %collective-permute-start.16 = (bf16[128,768]{1,0:T(8,128)(2,1)}, bf16[128,768]{1,0:T(8,128)(2,1)S(1)}, u32[]{:S(2)}, u32[]{:S(2)}) collective-permute-start(bf16[128,768]{1,0:T(8,128)(2,1)} %get-tuple-element.62.refs_8_), channel_id=1, source_target_pairs={{0,24},{4,28},{8,16},{12,20},{16,8},{20,12},{24,0},{28,4},{1,25},{... | collective-permute-start | bytes 589832 | tf_op jit(solution)/shard_map/ppermute | solution.py:411
  22.3 0.4 collective-permute-start.15
  22.7 1.1 %collective-permute-start.14 = (bf16[128,768]{1,0:T(8,128)(2,1)}, bf16[128,768]{1,0:T(8,128)(2,1)S(1)}, u32[]{:S(2)}, u32[]{:S(2)}) collective-permute-start(bf16[128,768]{1,0:T(8,128)(2,1)} %get-tuple-element.62.refs_8_), channel_id=1, source_target_pairs={{0,8},{4,12},{8,0},{12,4},{16,24},{20,28},{24,16},{28,20},{1,9},{5... | collective-permute-start | bytes 589832 | tf_op jit(solution)/shard_map/ppermute | solution.py:411
  23.8 0.7 %collective-permute-done.4.refs_3_ = bf16[72,128]{1,0:T(8,128)(2,1)S(1)} collective-permute-done((bf16[72,128]{1,0:T(8,128)(2,1)}, bf16[72,128]{1,0:T(8,128)(2,1)S(1)}, u32[]{:S(2)}, u32[]{:S(2)}) %collective-permute-start.4) | collective-permute-done | bytes 18464 | tf_op jit(solution)/shard_map/ppermute | solution.py:411
  24.6 0.0 copy-start.8
  24.6 0.7 %copy-done.8 = bf16[72,128]{1,0:T(8,128)(2,1)S(1)} copy-done((bf16[72,128]{1,0:T(8,128)(2,1)S(1)}, bf16[72,128]{1,0:T(8,128)(2,1)}, u32[]{:S(2)}) %copy-start.8) | copy-done | bytes 18456
  25.3 4.8 %conv.1 = (bf16[32,1024]{1,0:T(8,128)(2,1)S(1)}, bf16[32,1024]{1,0:T(8,128)(2,1)S(1)}, bf16[32,1024]{1,0:T(8,128)(2,1)S(1)}, bf16[32,1024]{1,0:T(8,128)(2,1)S(1)...) custom-call(bf16[9,256]{1,0:T(8,128)(2,1)S(1)} %copy-done.4, ...), custom_call_target="tpu_custom_call" | custom-call | flops 2000000000 | bytes 4000000 | tf_op jit(solution)/shard_map/conv/pallas_call | solution.py:450
  30.1 0.0 copy-start.3
  30.1 0.0 copy-start.5
  30.1 0.0 copy-start.6
  30.1 0.0 copy-start.7
  30.2 0.1 collective-permute-start.7
  30.2 1.3 %collective-permute-start.8 = (bf16[32,1024]{1,0:T(8,128)(2,1)S(1)}, bf16[32,1024]{1,0:T(8,128)(2,1)S(1)}, u32[]{:S(2)}, u32[]{:S(2)}) collective-permute-start(bf16[32,1024]{1,0:T(8,128)(2,1)S(1)} %get-tuple-element.55), channel_id=1, source_target_pairs={{0,24},{4,28},{8,16},{12,20},{16,8},{20,12},{24,0},{28,4},{1,25},{... | collective-permute-start | bytes 196616 | tf_op jit(solution)/shard_map/ppermute | solution.py:418
  31.5 2.3 %collective-permute-start.9 = (bf16[32,1024]{1,0:T(8,128)(2,1)S(1)}, bf16[32,1024]{1,0:T(8,128)(2,1)S(1)}, u32[]{:S(2)}, u32[]{:S(2)}) collective-permute-start(bf16[32,1024]{1,0:T(8,128)(2,1)S(1)} %get-tuple-element.56), channel_id=1, source_target_pairs={{0,20},{4,16},{8,28},{12,24},{16,4},{20,0},{24,12},{28,8},{1,21},{... | collective-permute-start | bytes 196616 | tf_op jit(solution)/shard_map/ppermute | solution.py:418
  33.8 0.8 %collective-permute-start.10 = (bf16[32,1024]{1,0:T(8,128)(2,1)S(1)}, bf16[32,1024]{1,0:T(8,128)(2,1)S(1)}, u32[]{:S(2)}, u32[]{:S(2)}) collective-permute-start(bf16[32,1024]{1,0:T(8,128)(2,1)S(1)} %get-tuple-element.57), channel_id=1, source_target_pairs={{0,16},{4,20},{8,24},{12,28},{16,0},{20,4},{24,8},{28,12},{1,17},{... | collective-permute-start | bytes 196616 | tf_op jit(solution)/shard_map/ppermute | solution.py:418
  34.6 0.3 collective-permute-done.7.refs_0_
  34.9 1.5 %collective-permute-start.12 = (bf16[32,1024]{1,0:T(8,128)(2,1)S(1)}, bf16[32,1024]{1,0:T(8,128)(2,1)S(1)}, u32[]{:S(2)}, u32[]{:S(2)}) collective-permute-start(bf16[32,1024]{1,0:T(8,128)(2,1)S(1)} %get-tuple-element.59), channel_id=1, source_target_pairs={{0,8},{4,12},{8,0},{12,4},{16,24},{20,28},{24,16},{28,20},{1,9},{5... | collective-permute-start | bytes 196616 | tf_op jit(solution)/shard_map/ppermute | solution.py:418
  36.4 0.1 collective-permute-start.13
  36.5 1.0 %collective-permute-done.9.refs_2_ = bf16[32,1024]{1,0:T(8,128)(2,1)S(1)} collective-permute-done((bf16[32,1024]{1,0:T(8,128)(2,1)S(1)}, bf16[32,1024]{1,0:T(8,128)(2,1)S(1)}, u32[]{:S(2)}, u32[]{:S(2)}) %collective-permute-start.9) | collective-permute-done | bytes 65568 | tf_op jit(solution)/shard_map/ppermute | solution.py:418
  37.5 1.5 %collective-permute-done.10.refs_3_ = bf16[32,1024]{1,0:T(8,128)(2,1)S(1)} collective-permute-done((bf16[32,1024]{1,0:T(8,128)(2,1)S(1)}, bf16[32,1024]{1,0:T(8,128)(2,1)S(1)}, u32[]{:S(2)}, u32[]{:S(2)}) %collective-permute-start.10) | collective-permute-done | bytes 65568 | tf_op jit(solution)/shard_map/ppermute | solution.py:418
  39.0 1.4 %collective-permute-done.12.refs_5_ = bf16[32,1024]{1,0:T(8,128)(2,1)S(1)} collective-permute-done((bf16[32,1024]{1,0:T(8,128)(2,1)S(1)}, bf16[32,1024]{1,0:T(8,128)(2,1)S(1)}, u32[]{:S(2)}, u32[]{:S(2)}) %collective-permute-start.12) | collective-permute-done | bytes 65568 | tf_op jit(solution)/shard_map/ppermute | solution.py:418
  40.4 0.5 layer_norm.1
  40.9 0.2 collective-permute-start.20
  41.1 1.3 %collective-permute-start.21 = (bf16[1024,128]{1,0:T(8,128)(2,1)S(1)}, bf16[1024,128]{1,0:T(8,128)(2,1)S(1)}, u32[]{:S(2)}, u32[]{:S(2)}) collective-permute-start(bf16[1024,128]{1,0:T(8,128)(2,1)S(1)} %copy-done.3), channel_id=1, source_target_pairs={{0,24},{4,28},{8,16},{12,20},{16,8},{20,12},{24,0},{28,4},{1,25},{... | collective-permute-start | bytes 786440 | tf_op jit(solution)/shard_map/ppermute | solution.py:411
  42.4 1.1 %collective-permute-start.17 = (bf16[64,1024]{1,0:T(8,128)(2,1)S(1)}, bf16[64,1024]{1,0:T(8,128)(2,1)S(1)}, u32[]{:S(2)}, u32[]{:S(2)}) collective-permute-start(bf16[64,1024]{1,0:T(8,128)(2,1)S(1)} %get-tuple-element.68.refs_0_), channel_id=1, source_target_pairs={{0,1},{1,0},{2,3},{3,2},{4,5},{5,4},{6,7},{7,6},{8,9},{9,8},{10,11... | collective-permute-start | bytes 393224 | tf_op jit(solution)/shard_map/ppermute | solution.py:421
  43.4 5.2 %collective-permute-done.18.refs_2_ = bf16[64,1024]{1,0:T(8,128)(2,1)S(1)} collective-permute-done((bf16[64,1024]{1,0:T(8,128)(2,1)S(1)}, bf16[64,1024]{1,0:T(8,128)(2,1)S(1)}, u32[]{:S(2)}, u32[]{:S(2)}) %collective-permute-start.18) | collective-permute-done | bytes 131104 | tf_op jit(solution)/shard_map/ppermute | solution.py:421
  48.7 1.3 %mask.1 = (bf16[64,1024]{1,0:T(8,128)(2,1)}, f32[4,64]{1,0:T(4,128)S(1)}, f32[64,1]{1,0:T(8,128)S(1)}) custom-call(s32[8]{0:T(128)S(1)} %copy-done.5, s32[8]{0:T(128)S(1)} %copy-done.6, s32[8]{0:T(128)S(1)} %copy-done.7, bf16[64,1024]{1,0:T(8,128)(2,1)S(1)} %get-tuple-element.63.rows_ref), custom_call_target="tpu_custom_call" | custom-call | flops 100000000 | bytes 1000000 | tf_op jit(solution)/shard_map/mask/pallas_call | solution.py:481
  49.9 0.7 %collective-permute-done.17.refs_1_ = bf16[64,1024]{1,0:T(8,128)(2,1)S(1)} collective-permute-done((bf16[64,1024]{1,0:T(8,128)(2,1)S(1)}, bf16[64,1024]{1,0:T(8,128)(2,1)S(1)}, u32[]{:S(2)}, u32[]{:S(2)}) %collective-permute-start.17) | collective-permute-done | bytes 131104 | tf_op jit(solution)/shard_map/ppermute | solution.py:421
  50.7 3.4 %collective-permute-done.19.refs_3_ = bf16[64,1024]{1,0:T(8,128)(2,1)S(1)} collective-permute-done((bf16[64,1024]{1,0:T(8,128)(2,1)S(1)}, bf16[64,1024]{1,0:T(8,128)(2,1)S(1)}, u32[]{:S(2)}, u32[]{:S(2)}) %collective-permute-start.19) | collective-permute-done | bytes 131104 | tf_op jit(solution)/shard_map/ppermute | solution.py:421
  54.1 2.3 %attention.1 = (bf16[64,256]{1,0:T(8,128)(2,1)S(1)}, bf16[64,256]{1,0:T(8,128)(2,1)S(1)}, bf16[64,256]{1,0:T(8,128)(2,1)S(1)}, bf16[64,256]{1,0:T(8,128)(2,1)S(1)}, bf16[4,1024,128]{2,1,0:T(8,128)(2,1)S(1)}) custom-call(f32[4,64]{1,0:T(4,128)S(1)} %get-tuple-element.66.keys_ref, bf16[64,1024]{1,0:T(8,128)(2,1)S(1)} %get-tuple-element.68.refs_0_, ...), custom_call_target="tpu_custom_call" | custom-call | flops 1000000000 | bytes 2000000 | tf_op jit(solution)/shard_map/attention/pallas_call | solution.py:501
  56.4 0.1 collective-permute-start.25
  56.5 0.3 collective-permute-start.22
  56.8 2.4 %collective-permute-start.23 = (bf16[64,256]{1,0:T(8,128)(2,1)S(1)}, bf16[64,256]{1,0:T(8,128)(2,1)S(1)}, u32[]{:S(2)}, u32[]{:S(2)}) collective-permute-start(bf16[64,256]{1,0:T(8,128)(2,1)S(1)} %get-tuple-element.75), channel_id=1, source_target_pairs={{0,2},{1,3},{2,0},{3,1},{4,6},{5,7},{6,4},{7,5},{8,10},{9,11},{10,... | collective-permute-start | bytes 98312 | tf_op jit(solution)/shard_map/ppermute | solution.py:421
  59.2 1.7 %collective-permute-start.24 = (bf16[64,256]{1,0:T(8,128)(2,1)S(1)}, bf16[64,256]{1,0:T(8,128)(2,1)S(1)}, u32[]{:S(2)}, u32[]{:S(2)}) collective-permute-start(bf16[64,256]{1,0:T(8,128)(2,1)S(1)} %get-tuple-element.76), channel_id=1, source_target_pairs={{0,3},{1,2},{2,1},{3,0},{4,7},{5,6},{6,5},{7,4},{8,11},{9,10},{10,... | collective-permute-start | bytes 98312 | tf_op jit(solution)/shard_map/ppermute | solution.py:421
  60.9 1.3 %collective-permute-done.23.refs_2_ = bf16[64,256]{1,0:T(8,128)(2,1)S(1)} collective-permute-done((bf16[64,256]{1,0:T(8,128)(2,1)S(1)}, bf16[64,256]{1,0:T(8,128)(2,1)S(1)}, u32[]{:S(2)}, u32[]{:S(2)}) %collective-permute-start.23) | collective-permute-done | bytes 32800 | tf_op jit(solution)/shard_map/ppermute | solution.py:421
  62.2 2.8 %collective-permute-done.24.refs_3_ = bf16[64,256]{1,0:T(8,128)(2,1)S(1)} collective-permute-done((bf16[64,256]{1,0:T(8,128)(2,1)S(1)}, bf16[64,256]{1,0:T(8,128)(2,1)S(1)}, u32[]{:S(2)}, u32[]{:S(2)}) %collective-permute-start.24) | collective-permute-done | bytes 32800 | tf_op jit(solution)/shard_map/ppermute | solution.py:421
  64.9 1.1 %output.1 = bf16[64,1024]{1,0:T(8,128)(2,1)} custom-call(f32[64,1]{1,0:T(8,128)S(1)} %get-tuple-element.65.valid_ref, bf16[64,256]{1,0:T(8,128)(2,1)S(1)} %get-tuple-element.73.refs_0_, bf16[64,256]{1,0:T(8,128)(2,1)S(1)} %collective-permute-done.22.refs_1_, bf16[64,256]{1,0:T(8,128)(2,1)S(1)} %collective-permute-done.23.refs_2_, ...), custom_call_target="tpu_custom_call" | custom-call | flops 100000000 | bytes 3000000 | tf_op jit(solution)/shard_map/output/pallas_call | solution.py:517
  (31 shorter events, 0.1 us)
Async XLA Ops:
  0.6 14.1 %collective-permute-start.1 = (bf16[640,1024]{1,0:T(8,128)(2,1)}, bf16[640,1024]{1,0:T(8,128)(2,1)S(1)}, u32[]{:S(2)}, u32[]{:S(2)}) collective-permute-start(bf16[640,1024]{1,0:T(8,128)(2,1)} %refs_4_), channel_id=1, source_target_pairs={{0,4},{4,0},{8,12},{12,8},{16,20},{20,16},{24,28},{28,24},{1,5},{5... | collective-permute-start | bytes 3932168 | tf_op jit(solution)/shard_map/ppermute | solution.py:415
  1.9 22.7 %copy-start.1 = (bf16[640,1024]{1,0:T(8,128)(2,1)S(1)}, bf16[640,1024]{1,0:T(8,128)(2,1)}, u32[]{:S(2)}) copy-start(bf16[640,1024]{1,0:T(8,128)(2,1)} %refs_4_) | copy-start | bytes 3932164
  1.9 22.7 %copy-start.2 = (bf16[2304,256]{1,0:T(8,128)(2,1)S(1)}, bf16[2304,256]{1,0:T(8,128)(2,1)}, u32[]{:S(2)}) copy-start(bf16[2304,256]{1,0:T(8,128)(2,1)} %conv2_ref.1) | copy-start | bytes 3538948
  1.9 22.7 %copy-start.4 = (bf16[9,256]{1,0:T(8,128)(2,1)S(1)}, bf16[9,256]{1,0:T(8,128)(2,1)}, u32[]{:S(2)}) copy-start(bf16[9,256]{1,0:T(8,128)(2,1)} %conv1_ref.1) | copy-start | bytes 13828
  1.9 7.7 %collective-permute-start = (f32[8,1024]{1,0:T(8,128)S(1)}, f32[8,1024]{1,0:T(8,128)S(1)}, u32[]{:S(2)}, u32[]{:S(2)}) collective-permute-start(f32[8,1024]{1,0:T(8,128)S(1)} %slice.3), channel_id=1, source_target_pairs={{0,1},{1,2},{2,3},{3,4},{4,5},{5,6},{6,7},{7,8},{8,9},{9,10},{10,1... | collective-permute-start | bytes 98312 | tf_op jit(solution)/shard_map/ppermute | solution.py:407
  6.6 13.7 %collective-permute-start.5 = (bf16[1024,128]{1,0:T(8,128)(2,1)}, bf16[1024,128]{1,0:T(8,128)(2,1)S(1)}, u32[]{:S(2)}, u32[]{:S(2)}) collective-permute-start(bf16[1024,128]{1,0:T(8,128)(2,1)} %refs_6_), channel_id=1, source_target_pairs={{0,8},{4,12},{8,0},{12,4},{16,24},{20,28},{24,16},{28,20},{1,9},{5... | collective-permute-start | bytes 786440 | tf_op jit(solution)/shard_map/ppermute | solution.py:411
  8.1 14.2 %collective-permute-start.6 = (bf16[1024,128]{1,0:T(8,128)(2,1)}, bf16[1024,128]{1,0:T(8,128)(2,1)}, u32[]{:S(2)}, u32[]{:S(2)}) collective-permute-start(bf16[1024,128]{1,0:T(8,128)(2,1)} %refs_6_), channel_id=1, source_target_pairs={{0,16},{4,20},{8,24},{12,28},{16,0},{20,4},{24,8},{28,12},{1,17},{... | collective-permute-start | bytes 786440 | tf_op jit(solution)/shard_map/ppermute | solution.py:411
  9.6 0.6 copy-start.9
  14.7 8.0 %collective-permute-start.2 = (bf16[72,128]{1,0:T(8,128)(2,1)}, bf16[72,128]{1,0:T(8,128)(2,1)S(1)}, u32[]{:S(2)}, u32[]{:S(2)}) collective-permute-start(bf16[72,128]{1,0:T(8,128)(2,1)} %get-tuple-element.45), channel_id=1, source_target_pairs={{0,8},{4,12},{8,0},{12,4},{16,24},{20,28},{24,16},{28,20},{1,9},{5... | collective-permute-start | bytes 55304 | tf_op jit(solution)/shard_map/ppermute | solution.py:411
  17.8 6.1 %collective-permute-start.3 = (bf16[72,128]{1,0:T(8,128)(2,1)}, bf16[72,128]{1,0:T(8,128)(2,1)S(1)}, u32[]{:S(2)}, u32[]{:S(2)}) collective-permute-start(bf16[72,128]{1,0:T(8,128)(2,1)} %get-tuple-element.46), channel_id=1, source_target_pairs={{0,16},{4,20},{8,24},{12,28},{16,0},{20,4},{24,8},{28,12},{1,17},{... | collective-permute-start | bytes 55304 | tf_op jit(solution)/shard_map/ppermute | solution.py:411
  19.4 5.2 %collective-permute-start.4 = (bf16[72,128]{1,0:T(8,128)(2,1)}, bf16[72,128]{1,0:T(8,128)(2,1)S(1)}, u32[]{:S(2)}, u32[]{:S(2)}) collective-permute-start(bf16[72,128]{1,0:T(8,128)(2,1)} %get-tuple-element.47), channel_id=1, source_target_pairs={{0,24},{4,28},{8,16},{12,20},{16,8},{20,12},{24,0},{28,4},{1,25},{... | collective-permute-start | bytes 55304 | tf_op jit(solution)/shard_map/ppermute | solution.py:411
  20.3 20.2 %copy-start = (bf16[128,768]{1,0:T(8,128)(2,1)S(1)}, bf16[128,768]{1,0:T(8,128)(2,1)}, u32[]{:S(2)}) copy-start(bf16[128,768]{1,0:T(8,128)(2,1)} %get-tuple-element.62.refs_8_) | copy-start | bytes 589828
  20.3 11.3 %collective-permute-start.16 = (bf16[128,768]{1,0:T(8,128)(2,1)}, bf16[128,768]{1,0:T(8,128)(2,1)S(1)}, u32[]{:S(2)}, u32[]{:S(2)}) collective-permute-start(bf16[128,768]{1,0:T(8,128)(2,1)} %get-tuple-element.62.refs_8_), channel_id=1, source_target_pairs={{0,24},{4,28},{8,16},{12,20},{16,8},{20,12},{24,0},{28,4},{1,25},{... | collective-permute-start | bytes 589832 | tf_op jit(solution)/shard_map/ppermute | solution.py:411
  22.3 11.5 %collective-permute-start.15 = (bf16[128,768]{1,0:T(8,128)(2,1)}, bf16[128,768]{1,0:T(8,128)(2,1)S(1)}, u32[]{:S(2)}, u32[]{:S(2)}) collective-permute-start(bf16[128,768]{1,0:T(8,128)(2,1)} %get-tuple-element.62.refs_8_), channel_id=1, source_target_pairs={{0,16},{4,20},{8,24},{12,28},{16,0},{20,4},{24,8},{28,12},{1,17},{... | collective-permute-start | bytes 589832 | tf_op jit(solution)/shard_map/ppermute | solution.py:411
  22.7 11.9 %collective-permute-start.14 = (bf16[128,768]{1,0:T(8,128)(2,1)}, bf16[128,768]{1,0:T(8,128)(2,1)S(1)}, u32[]{:S(2)}, u32[]{:S(2)}) collective-permute-start(bf16[128,768]{1,0:T(8,128)(2,1)} %get-tuple-element.62.refs_8_), channel_id=1, source_target_pairs={{0,8},{4,12},{8,0},{12,4},{16,24},{20,28},{24,16},{28,20},{1,9},{5... | collective-permute-start | bytes 589832 | tf_op jit(solution)/shard_map/ppermute | solution.py:411
  24.6 0.7 %copy-start.8 = (bf16[72,128]{1,0:T(8,128)(2,1)S(1)}, bf16[72,128]{1,0:T(8,128)(2,1)}, u32[]{:S(2)}) copy-start(bf16[72,128]{1,0:T(8,128)(2,1)} %get-tuple-element.48.refs_0_) | copy-start | bytes 55300
  30.1 11.0 %copy-start.3 = (bf16[1024,128]{1,0:T(8,128)(2,1)S(1)}, bf16[1024,128]{1,0:T(8,128)(2,1)}, u32[]{:S(2)}) copy-start(bf16[1024,128]{1,0:T(8,128)(2,1)} %refs_6_) | copy-start | bytes 786436
  30.1 18.5 %copy-start.5 = (s32[8]{0:T(128)S(1)}, s32[8]{0:T(128)}, u32[]{:S(2)}) copy-start(s32[8]{0:T(128)} %slots_ref.1) | copy-start | bytes 100
  30.1 18.5 %copy-start.6 = (s32[8]{0:T(128)S(1)}, s32[8]{0:T(128)}, u32[]{:S(2)}) copy-start(s32[8]{0:T(128)} %starts_ref.1) | copy-start | bytes 100
  30.1 18.5 %copy-start.7 = (s32[8]{0:T(128)S(1)}, s32[8]{0:T(128)}, u32[]{:S(2)}) copy-start(s32[8]{0:T(128)} %lengths_ref.1) | copy-start | bytes 100
  30.2 4.7 %collective-permute-start.7 = (bf16[32,1024]{1,0:T(8,128)(2,1)S(1)}, bf16[32,1024]{1,0:T(8,128)(2,1)S(1)}, u32[]{:S(2)}, u32[]{:S(2)}) collective-permute-start(bf16[32,1024]{1,0:T(8,128)(2,1)S(1)} %get-tuple-element.54), channel_id=1, source_target_pairs={{0,28},{4,24},{8,20},{12,16},{16,12},{20,8},{24,4},{28,0},{1,29},{... | collective-permute-start | bytes 196616 | tf_op jit(solution)/shard_map/ppermute | solution.py:418
  30.2 6.2 %collective-permute-start.8 = (bf16[32,1024]{1,0:T(8,128)(2,1)S(1)}, bf16[32,1024]{1,0:T(8,128)(2,1)S(1)}, u32[]{:S(2)}, u32[]{:S(2)}) collective-permute-start(bf16[32,1024]{1,0:T(8,128)(2,1)S(1)} %get-tuple-element.55), channel_id=1, source_target_pairs={{0,24},{4,28},{8,16},{12,20},{16,8},{20,12},{24,0},{28,4},{1,25},{... | collective-permute-start | bytes 196616 | tf_op jit(solution)/shard_map/ppermute | solution.py:418
  31.5 6.0 %collective-permute-start.9 = (bf16[32,1024]{1,0:T(8,128)(2,1)S(1)}, bf16[32,1024]{1,0:T(8,128)(2,1)S(1)}, u32[]{:S(2)}, u32[]{:S(2)}) collective-permute-start(bf16[32,1024]{1,0:T(8,128)(2,1)S(1)} %get-tuple-element.56), channel_id=1, source_target_pairs={{0,20},{4,16},{8,28},{12,24},{16,4},{20,0},{24,12},{28,8},{1,21},{... | collective-permute-start | bytes 196616 | tf_op jit(solution)/shard_map/ppermute | solution.py:418
  33.8 5.2 %collective-permute-start.10 = (bf16[32,1024]{1,0:T(8,128)(2,1)S(1)}, bf16[32,1024]{1,0:T(8,128)(2,1)S(1)}, u32[]{:S(2)}, u32[]{:S(2)}) collective-permute-start(bf16[32,1024]{1,0:T(8,128)(2,1)S(1)} %get-tuple-element.57), channel_id=1, source_target_pairs={{0,16},{4,20},{8,24},{12,28},{16,0},{20,4},{24,8},{28,12},{1,17},{... | collective-permute-start | bytes 196616 | tf_op jit(solution)/shard_map/ppermute | solution.py:418
  34.6 4.4 %collective-permute-start.11 = (bf16[32,1024]{1,0:T(8,128)(2,1)S(1)}, bf16[32,1024]{1,0:T(8,128)(2,1)S(1)}, u32[]{:S(2)}, u32[]{:S(2)}) collective-permute-start(bf16[32,1024]{1,0:T(8,128)(2,1)S(1)} %get-tuple-element.58), channel_id=1, source_target_pairs={{0,12},{4,8},{8,4},{12,0},{16,28},{20,24},{24,20},{28,16},{1,13},{... | collective-permute-start | bytes 196616 | tf_op jit(solution)/shard_map/ppermute | solution.py:418
  34.9 5.5 %collective-permute-start.12 = (bf16[32,1024]{1,0:T(8,128)(2,1)S(1)}, bf16[32,1024]{1,0:T(8,128)(2,1)S(1)}, u32[]{:S(2)}, u32[]{:S(2)}) collective-permute-start(bf16[32,1024]{1,0:T(8,128)(2,1)S(1)} %get-tuple-element.59), channel_id=1, source_target_pairs={{0,8},{4,12},{8,0},{12,4},{16,24},{20,28},{24,16},{28,20},{1,9},{5... | collective-permute-start | bytes 196616 | tf_op jit(solution)/shard_map/ppermute | solution.py:418
  36.4 4.0 %collective-permute-start.13 = (bf16[32,1024]{1,0:T(8,128)(2,1)S(1)}, bf16[32,1024]{1,0:T(8,128)(2,1)S(1)}, u32[]{:S(2)}, u32[]{:S(2)}) collective-permute-start(bf16[32,1024]{1,0:T(8,128)(2,1)S(1)} %get-tuple-element.60), channel_id=1, source_target_pairs={{0,4},{4,0},{8,12},{12,8},{16,20},{20,16},{24,28},{28,24},{1,5},{5... | collective-permute-start | bytes 196616 | tf_op jit(solution)/shard_map/ppermute | solution.py:418
  40.9 13.1 %collective-permute-start.20 = (bf16[4,128,768]{2,1,0:T(8,128)(2,1)S(1)}, bf16[4,128,768]{2,1,0:T(8,128)(2,1)S(1)}, u32[]{:S(2)}, u32[]{:S(2)}) collective-permute-start(bf16[4,128,768]{2,1,0:T(8,128)(2,1)S(1)} %get-tuple-element.69.refs_4_), channel_id=1, source_target_pairs={{0,4},{4,0},{8,12},{12,8},{16,20},{20,16},{24,28},{28,24},{1,5},{5... | collective-permute-start | bytes 2359304 | tf_op jit(solution)/shard_map/ppermute | solution.py:415
  41.1 7.6 %collective-permute-start.18 = (bf16[64,1024]{1,0:T(8,128)(2,1)S(1)}, bf16[64,1024]{1,0:T(8,128)(2,1)S(1)}, u32[]{:S(2)}, u32[]{:S(2)}) collective-permute-start(bf16[64,1024]{1,0:T(8,128)(2,1)S(1)} %get-tuple-element.68.refs_0_), channel_id=1, source_target_pairs={{0,2},{1,3},{2,0},{3,1},{4,6},{5,7},{6,4},{7,5},{8,10},{9,11},{10,... | collective-permute-start | bytes 393224 | tf_op jit(solution)/shard_map/ppermute | solution.py:421
  41.1 13.0 %collective-permute-start.21 = (bf16[1024,128]{1,0:T(8,128)(2,1)S(1)}, bf16[1024,128]{1,0:T(8,128)(2,1)S(1)}, u32[]{:S(2)}, u32[]{:S(2)}) collective-permute-start(bf16[1024,128]{1,0:T(8,128)(2,1)S(1)} %copy-done.3), channel_id=1, source_target_pairs={{0,24},{4,28},{8,16},{12,20},{16,8},{20,12},{24,0},{28,4},{1,25},{... | collective-permute-start | bytes 786440 | tf_op jit(solution)/shard_map/ppermute | solution.py:411
  42.4 8.3 %collective-permute-start.17 = (bf16[64,1024]{1,0:T(8,128)(2,1)S(1)}, bf16[64,1024]{1,0:T(8,128)(2,1)S(1)}, u32[]{:S(2)}, u32[]{:S(2)}) collective-permute-start(bf16[64,1024]{1,0:T(8,128)(2,1)S(1)} %get-tuple-element.68.refs_0_), channel_id=1, source_target_pairs={{0,1},{1,0},{2,3},{3,2},{4,5},{5,4},{6,7},{7,6},{8,9},{9,8},{10,11... | collective-permute-start | bytes 393224 | tf_op jit(solution)/shard_map/ppermute | solution.py:421
  48.6 5.4 %collective-permute-start.19 = (bf16[64,1024]{1,0:T(8,128)(2,1)S(1)}, bf16[64,1024]{1,0:T(8,128)(2,1)S(1)}, u32[]{:S(2)}, u32[]{:S(2)}) collective-permute-start(bf16[64,1024]{1,0:T(8,128)(2,1)S(1)} %collective-permute-done.18.refs_2_), channel_id=1, source_target_pairs={{0,1},{1,0},{2,3},{3,2},{4,5},{5,4},{6,7},{7,6},{8,9},{9,8},{10,11... | collective-permute-start | bytes 393224 | tf_op jit(solution)/shard_map/ppermute | solution.py:421
  56.4 8.6 %collective-permute-start.25 = (bf16[4,1024,128]{2,1,0:T(8,128)(2,1)S(1)}, bf16[4,1024,128]{2,1,0:T(8,128)(2,1)S(1)}, u32[]{:S(2)}, u32[]{:S(2)}) collective-permute-start(bf16[4,1024,128]{2,1,0:T(8,128)(2,1)S(1)} %get-tuple-element.77.refs_4_), channel_id=1, source_target_pairs={{0,4},{4,0},{8,12},{12,8},{16,20},{20,16},{24,28},{28,24},{1,5},{5... | collective-permute-start | bytes 3145736 | tf_op jit(solution)/shard_map/ppermute | solution.py:415
  56.5 4.5 %collective-permute-start.22 = (bf16[64,256]{1,0:T(8,128)(2,1)S(1)}, bf16[64,256]{1,0:T(8,128)(2,1)S(1)}, u32[]{:S(2)}, u32[]{:S(2)}) collective-permute-start(bf16[64,256]{1,0:T(8,128)(2,1)S(1)} %get-tuple-element.74), channel_id=1, source_target_pairs={{0,1},{1,0},{2,3},{3,2},{4,5},{5,4},{6,7},{7,6},{8,9},{9,8},{10,11... | collective-permute-start | bytes 98312 | tf_op jit(solution)/shard_map/ppermute | solution.py:421
  56.8 5.4 %collective-permute-start.23 = (bf16[64,256]{1,0:T(8,128)(2,1)S(1)}, bf16[64,256]{1,0:T(8,128)(2,1)S(1)}, u32[]{:S(2)}, u32[]{:S(2)}) collective-permute-start(bf16[64,256]{1,0:T(8,128)(2,1)S(1)} %get-tuple-element.75), channel_id=1, source_target_pairs={{0,2},{1,3},{2,0},{3,1},{4,6},{5,7},{6,4},{7,5},{8,10},{9,11},{10,... | collective-permute-start | bytes 98312 | tf_op jit(solution)/shard_map/ppermute | solution.py:421
  59.2 5.7 %collective-permute-start.24 = (bf16[64,256]{1,0:T(8,128)(2,1)S(1)}, bf16[64,256]{1,0:T(8,128)(2,1)S(1)}, u32[]{:S(2)}, u32[]{:S(2)}) collective-permute-start(bf16[64,256]{1,0:T(8,128)(2,1)S(1)} %get-tuple-element.76), channel_id=1, source_target_pairs={{0,3},{1,2},{2,1},{3,0},{4,7},{5,6},{6,5},{7,4},{8,11},{9,10},{10,... | collective-permute-start | bytes 98312 | tf_op jit(solution)/shard_map/ppermute | solution.py:421

commit v12 on v10

--- a/solution.py
+++ b/solution.py
@@ -156,13 +156,15 @@
     load_slots.start()
     load_audio = pltpu.make_async_copy(audio_ref, ext.at[:, pl.ds(RIM, audio_ref.shape[1])], sems.at[3])
     load_table = pltpu.make_async_copy(table_ref, table, sems.at[4])
+    load_rim = pltpu.make_async_copy(rim_ref, ext.at[:, pl.ds(0, RIM)], sems.at[6])
+    load_rim.start()
     load_audio.start()
     load_table.start()
     pieces = mix_columns(group, qkv_ref, mix_out, sems)
     start_all(pieces)
     streams = audio_ref.shape[0]
     rows = JS * streams
-    ext[:, :RIM] = rim_ref[...]
+    load_rim.wait()
     load_audio.wait()
     phases = []
     for phase in range(4):
@@ -436,14 +438,14 @@
     *mel_all, mix = pl.pallas_call(
         functools.partial(mel_kernel, parts, group),
         out_shape=tuple([jax.ShapeDtypeStruct((rows, LANES), BF16)] * parts + [mix_piece]),
-        in_specs=[anywhere(), vmem()] + [anywhere()] * 3,
+        in_specs=[anywhere()] * 5,
         out_specs=tuple([vmem()] * (parts + 1)),
         scratch_shapes=[
             pltpu.VMEM((streams, RIM + audio.shape[1]), F32),
             pltpu.VMEM(table.shape, F32),
             pltpu.VMEM((parts, rows, LANES), BF16),
             pltpu.SMEM((streams,), jnp.int32),
-            pltpu.SemaphoreType.DMA((6,)),
+            pltpu.SemaphoreType.DMA((7,)),
         ],
         compiler_params=params(60),
         cost_estimate=cost(1e10, 2e6),

time: 65.4 us -> 64.7 us (0.989)
  Pallas kernels: 13.5 us -> 12.7 us
    pallas_call x1, Pallas kernels: 4.47 us -> 3.73 us  [on_device(): pl.pallas_call(functools.partial(mel_kernel, parts, group), out_shape=tup...]
  transfers between devices with their start and end apart: 26 -> 26, of which waited for: 10 -> 10; matrix products, arithmetic and copies ran while one was open for 1% -> 1% of each run, Pallas kernels for 16% -> 15%
where the time goes in v12:
time: 64.7 us; the launch traced here: 64.4 us
  starting transfers between devices  30.4 us (47%)
  waiting for transfers between devices  18.3 us (28%)
  Pallas kernels  12.7 us (20%)
  local copies, waits for them, and re-layouts  2.13 us (3%)
  between operations  0.78 us (1%)
    ppermute x9, starting transfers between devices, to_part(): return lax.ppermute(block, 'dp', pairs)  13.5 us
    ppermute x6, waiting for transfers between devices, to_plane(): return lax.ppermute(block, 'seq', [(i, i ^ step) for i in range(group)])  13.3 us
    ppermute x7, starting transfers between devices, to_window(): return lax.ppermute(block, 'dp', [(i, i ^ step) for i in range(windows)])  6.04 us
    ppermute x6, starting transfers between devices, to_plane(): return lax.ppermute(block, 'seq', [(i, i ^ step) for i in range(group)])  5.52 us
    pallas_call x1, Pallas kernels, on_device(): pl.pallas_call(functools.partial(conv_kernel, parts, width), out_shape=tu...  4.77 us
    ppermute x1, starting transfers between devices, on_device(): rim = lax.ppermute(audio[:, audio.shape[1] - RIM:], ('dp', 'seq'), route)  4.63 us
    ppermute x7, waiting for transfers between devices, to_window(): return lax.ppermute(block, 'dp', [(i, i ^ step) for i in range(windows)])  4.21 us
    pallas_call x1, Pallas kernels, on_device(): pl.pallas_call(functools.partial(mel_kernel, parts, group), out_shape=tup...  3.73 us
  transfers between devices with their start and end apart: 26, of which 10 were waited for; matrix products, arithmetic and copies ran while one was open for 1% of the time, Pallas kernels for 15%

profile of v12, /device:TPU:0, one launch (start us, length us, event | category | flops | bytes accessed | tf_op | source)
XLA Modules:
  0.0 64.4 jit_solution(2898072071482685582)
XLA Ops:
  0.6 0.5 collective-permute-start.1
  1.1 0.8 %slice.3 = f32[8,1024]{1,0:T(8,128)S(1)} slice(f32[8,5120]{1,0:T(8,128)} %audio_ref.1), slice={[0:8], [4096:5120]} | slice | bytes 65536 | tf_op jit(solution)/shard_map/slice | solution.py:418
  1.9 4.6 %collective-permute-start = (f32[8,1024]{1,0:T(8,128)S(1)}, f32[8,1024]{1,0:T(8,128)S(1)}, u32[]{:S(2)}, u32[]{:S(2)}) collective-permute-start(f32[8,1024]{1,0:T(8,128)S(1)} %slice.3), channel_id=1, source_target_pairs={{0,1},{1,2},{2,3},{3,4},{4,5},{5,6},{6,7},{7,8},{8,9},{9,10},{10,1... | collective-permute-start | bytes 98312 | tf_op jit(solution)/shard_map/ppermute | solution.py:418
  6.6 1.6 %collective-permute-start.5 = (bf16[1024,128]{1,0:T(8,128)(2,1)}, bf16[1024,128]{1,0:T(8,128)(2,1)S(1)}, u32[]{:S(2)}, u32[]{:S(2)}) collective-permute-start(bf16[1024,128]{1,0:T(8,128)(2,1)} %refs_6_), channel_id=1, source_target_pairs={{0,8},{4,12},{8,0},{12,4},{16,24},{20,28},{24,16},{28,20},{1,9},{5... | collective-permute-start | bytes 786440 | tf_op jit(solution)/shard_map/ppermute | solution.py:422
  8.1 1.5 %collective-permute-start.6 = (bf16[1024,128]{1,0:T(8,128)(2,1)}, bf16[1024,128]{1,0:T(8,128)(2,1)}, u32[]{:S(2)}, u32[]{:S(2)}) collective-permute-start(bf16[1024,128]{1,0:T(8,128)(2,1)} %refs_6_), channel_id=1, source_target_pairs={{0,16},{4,20},{8,24},{12,28},{16,0},{20,4},{24,8},{28,12},{1,17},{... | collective-permute-start | bytes 786440 | tf_op jit(solution)/shard_map/ppermute | solution.py:422
  9.6 0.0 collective-permute-done.rim_ref
  9.6 0.6 copy-done.9
  10.2 3.7 %log_mel.1 = (bf16[72,128]{1,0:T(8,128)(2,1)}, bf16[72,128]{1,0:T(8,128)(2,1)}, bf16[72,128]{1,0:T(8,128)(2,1)}, bf16[72,128]{1,0:T(8,128)(2,1)}, bf16[128,768]{1,0:T(8,128)(2,1)}) custom-call(s32[8]{0:T(128)} %slots_ref.1, f32[8,1024]{1,0:T(8,128)} %copy-done.9, f32[8,5120]{1,0:T(8,128)} %audio_ref.1, f32[264,640]{1,0:T(8,128)} %constant.2.clone.table_ref, ...), custom_call_target="tpu_custom_call" | custom-call | flops 10000000000 | bytes 2000000 | tf_op jit(solution)/shard_map/log_mel/pallas_call | solution.py:438
  14.0 3.0 %collective-permute-start.2 = (bf16[72,128]{1,0:T(8,128)(2,1)}, bf16[72,128]{1,0:T(8,128)(2,1)S(1)}, u32[]{:S(2)}, u32[]{:S(2)}) collective-permute-start(bf16[72,128]{1,0:T(8,128)(2,1)} %get-tuple-element.45), channel_id=1, source_target_pairs={{0,8},{4,12},{8,0},{12,4},{16,24},{20,28},{24,16},{28,20},{1,9},{5... | collective-permute-start | bytes 55304 | tf_op jit(solution)/shard_map/ppermute | solution.py:422
  17.0 1.6 %collective-permute-start.3 = (bf16[72,128]{1,0:T(8,128)(2,1)}, bf16[72,128]{1,0:T(8,128)(2,1)S(1)}, u32[]{:S(2)}, u32[]{:S(2)}) collective-permute-start(bf16[72,128]{1,0:T(8,128)(2,1)} %get-tuple-element.46), channel_id=1, source_target_pairs={{0,16},{4,20},{8,24},{12,28},{16,0},{20,4},{24,8},{28,12},{1,17},{... | collective-permute-start | bytes 55304 | tf_op jit(solution)/shard_map/ppermute | solution.py:422
  18.6 0.9 %collective-permute-start.4 = (bf16[72,128]{1,0:T(8,128)(2,1)}, bf16[72,128]{1,0:T(8,128)(2,1)S(1)}, u32[]{:S(2)}, u32[]{:S(2)}) collective-permute-start(bf16[72,128]{1,0:T(8,128)(2,1)} %get-tuple-element.47), channel_id=1, source_target_pairs={{0,24},{4,28},{8,16},{12,20},{16,8},{20,12},{24,0},{28,4},{1,25},{... | collective-permute-start | bytes 55304 | tf_op jit(solution)/shard_map/ppermute | solution.py:422
  19.5 2.0 %collective-permute-start.16 = (bf16[128,768]{1,0:T(8,128)(2,1)}, bf16[128,768]{1,0:T(8,128)(2,1)S(1)}, u32[]{:S(2)}, u32[]{:S(2)}) collective-permute-start(bf16[128,768]{1,0:T(8,128)(2,1)} %get-tuple-element.62.refs_8_), channel_id=1, source_target_pairs={{0,24},{4,28},{8,16},{12,20},{16,8},{20,12},{24,0},{28,4},{1,25},{... | collective-permute-start | bytes 589832 | tf_op jit(solution)/shard_map/ppermute | solution.py:422
  21.6 0.4 collective-permute-start.15
  22.0 1.1 %collective-permute-start.14 = (bf16[128,768]{1,0:T(8,128)(2,1)}, bf16[128,768]{1,0:T(8,128)(2,1)S(1)}, u32[]{:S(2)}, u32[]{:S(2)}) collective-permute-start(bf16[128,768]{1,0:T(8,128)(2,1)} %get-tuple-element.62.refs_8_), channel_id=1, source_target_pairs={{0,8},{4,12},{8,0},{12,4},{16,24},{20,28},{24,16},{28,20},{1,9},{5... | collective-permute-start | bytes 589832 | tf_op jit(solution)/shard_map/ppermute | solution.py:422
  23.1 0.7 %collective-permute-done.4.refs_3_ = bf16[72,128]{1,0:T(8,128)(2,1)S(1)} collective-permute-done((bf16[72,128]{1,0:T(8,128)(2,1)}, bf16[72,128]{1,0:T(8,128)(2,1)S(1)}, u32[]{:S(2)}, u32[]{:S(2)}) %collective-permute-start.4) | collective-permute-done | bytes 18464 | tf_op jit(solution)/shard_map/ppermute | solution.py:422
  23.9 0.0 copy-start.8
  23.9 0.7 %copy-done.8 = bf16[72,128]{1,0:T(8,128)(2,1)S(1)} copy-done((bf16[72,128]{1,0:T(8,128)(2,1)S(1)}, bf16[72,128]{1,0:T(8,128)(2,1)}, u32[]{:S(2)}) %copy-start.8) | copy-done | bytes 18456
  24.6 4.8 %conv.1 = (bf16[32,1024]{1,0:T(8,128)(2,1)S(1)}, bf16[32,1024]{1,0:T(8,128)(2,1)S(1)}, bf16[32,1024]{1,0:T(8,128)(2,1)S(1)}, bf16[32,1024]{1,0:T(8,128)(2,1)S(1)...) custom-call(bf16[9,256]{1,0:T(8,128)(2,1)S(1)} %copy-done.4, ...), custom_call_target="tpu_custom_call" | custom-call | flops 2000000000 | bytes 4000000 | tf_op jit(solution)/shard_map/conv/pallas_call | solution.py:461
  29.4 0.0 copy-start.3
  29.4 0.0 copy-start.5
  29.4 0.0 copy-start.6
  29.4 0.0 copy-start.7
  29.4 0.1 collective-permute-start.7
  29.5 1.3 %collective-permute-start.8 = (bf16[32,1024]{1,0:T(8,128)(2,1)S(1)}, bf16[32,1024]{1,0:T(8,128)(2,1)S(1)}, u32[]{:S(2)}, u32[]{:S(2)}) collective-permute-start(bf16[32,1024]{1,0:T(8,128)(2,1)S(1)} %get-tuple-element.55), channel_id=1, source_target_pairs={{0,24},{4,28},{8,16},{12,20},{16,8},{20,12},{24,0},{28,4},{1,25},{... | collective-permute-start | bytes 196616 | tf_op jit(solution)/shard_map/ppermute | solution.py:429
  30.8 2.3 %collective-permute-start.9 = (bf16[32,1024]{1,0:T(8,128)(2,1)S(1)}, bf16[32,1024]{1,0:T(8,128)(2,1)S(1)}, u32[]{:S(2)}, u32[]{:S(2)}) collective-permute-start(bf16[32,1024]{1,0:T(8,128)(2,1)S(1)} %get-tuple-element.56), channel_id=1, source_target_pairs={{0,20},{4,16},{8,28},{12,24},{16,4},{20,0},{24,12},{28,8},{1,21},{... | collective-permute-start | bytes 196616 | tf_op jit(solution)/shard_map/ppermute | solution.py:429
  33.1 0.8 %collective-permute-start.10 = (bf16[32,1024]{1,0:T(8,128)(2,1)S(1)}, bf16[32,1024]{1,0:T(8,128)(2,1)S(1)}, u32[]{:S(2)}, u32[]{:S(2)}) collective-permute-start(bf16[32,1024]{1,0:T(8,128)(2,1)S(1)} %get-tuple-element.57), channel_id=1, source_target_pairs={{0,16},{4,20},{8,24},{12,28},{16,0},{20,4},{24,8},{28,12},{1,17},{... | collective-permute-start | bytes 196616 | tf_op jit(solution)/shard_map/ppermute | solution.py:429
  33.9 0.3 collective-permute-done.7.refs_0_
  34.2 1.5 %collective-permute-start.12 = (bf16[32,1024]{1,0:T(8,128)(2,1)S(1)}, bf16[32,1024]{1,0:T(8,128)(2,1)S(1)}, u32[]{:S(2)}, u32[]{:S(2)}) collective-permute-start(bf16[32,1024]{1,0:T(8,128)(2,1)S(1)} %get-tuple-element.59), channel_id=1, source_target_pairs={{0,8},{4,12},{8,0},{12,4},{16,24},{20,28},{24,16},{28,20},{1,9},{5... | collective-permute-start | bytes 196616 | tf_op jit(solution)/shard_map/ppermute | solution.py:429
  35.7 0.1 collective-permute-start.13
  35.8 1.0 %collective-permute-done.9.refs_2_ = bf16[32,1024]{1,0:T(8,128)(2,1)S(1)} collective-permute-done((bf16[32,1024]{1,0:T(8,128)(2,1)S(1)}, bf16[32,1024]{1,0:T(8,128)(2,1)S(1)}, u32[]{:S(2)}, u32[]{:S(2)}) %collective-permute-start.9) | collective-permute-done | bytes 65568 | tf_op jit(solution)/shard_map/ppermute | solution.py:429
  36.8 1.5 %collective-permute-done.10.refs_3_ = bf16[32,1024]{1,0:T(8,128)(2,1)S(1)} collective-permute-done((bf16[32,1024]{1,0:T(8,128)(2,1)S(1)}, bf16[32,1024]{1,0:T(8,128)(2,1)S(1)}, u32[]{:S(2)}, u32[]{:S(2)}) %collective-permute-start.10) | collective-permute-done | bytes 65568 | tf_op jit(solution)/shard_map/ppermute | solution.py:429
  38.3 1.4 %collective-permute-done.12.refs_5_ = bf16[32,1024]{1,0:T(8,128)(2,1)S(1)} collective-permute-done((bf16[32,1024]{1,0:T(8,128)(2,1)S(1)}, bf16[32,1024]{1,0:T(8,128)(2,1)S(1)}, u32[]{:S(2)}, u32[]{:S(2)}) %collective-permute-start.12) | collective-permute-done | bytes 65568 | tf_op jit(solution)/shard_map/ppermute | solution.py:429
  39.7 0.5 layer_norm.1
  40.2 0.2 collective-permute-start.20
  40.4 1.3 %collective-permute-start.21 = (bf16[1024,128]{1,0:T(8,128)(2,1)S(1)}, bf16[1024,128]{1,0:T(8,128)(2,1)S(1)}, u32[]{:S(2)}, u32[]{:S(2)}) collective-permute-start(bf16[1024,128]{1,0:T(8,128)(2,1)S(1)} %copy-done.3), channel_id=1, source_target_pairs={{0,24},{4,28},{8,16},{12,20},{16,8},{20,12},{24,0},{28,4},{1,25},{... | collective-permute-start | bytes 786440 | tf_op jit(solution)/shard_map/ppermute | solution.py:422
  41.7 1.1 %collective-permute-start.17 = (bf16[64,1024]{1,0:T(8,128)(2,1)S(1)}, bf16[64,1024]{1,0:T(8,128)(2,1)S(1)}, u32[]{:S(2)}, u32[]{:S(2)}) collective-permute-start(bf16[64,1024]{1,0:T(8,128)(2,1)S(1)} %get-tuple-element.68.refs_0_), channel_id=1, source_target_pairs={{0,1},{1,0},{2,3},{3,2},{4,5},{5,4},{6,7},{7,6},{8,9},{9,8},{10,11... | collective-permute-start | bytes 393224 | tf_op jit(solution)/shard_map/ppermute | solution.py:432
  42.7 5.2 %collective-permute-done.18.refs_2_ = bf16[64,1024]{1,0:T(8,128)(2,1)S(1)} collective-permute-done((bf16[64,1024]{1,0:T(8,128)(2,1)S(1)}, bf16[64,1024]{1,0:T(8,128)(2,1)S(1)}, u32[]{:S(2)}, u32[]{:S(2)}) %collective-permute-start.18) | collective-permute-done | bytes 131104 | tf_op jit(solution)/shard_map/ppermute | solution.py:432
  47.9 1.3 %mask.1 = (bf16[64,1024]{1,0:T(8,128)(2,1)}, f32[4,64]{1,0:T(4,128)S(1)}, f32[64,1]{1,0:T(8,128)S(1)}) custom-call(s32[8]{0:T(128)S(1)} %copy-done.5, s32[8]{0:T(128)S(1)} %copy-done.6, s32[8]{0:T(128)S(1)} %copy-done.7, bf16[64,1024]{1,0:T(8,128)(2,1)S(1)} %get-tuple-element.63.rows_ref), custom_call_target="tpu_custom_call" | custom-call | flops 100000000 | bytes 1000000 | tf_op jit(solution)/shard_map/mask/pallas_call | solution.py:492
  49.2 0.7 %collective-permute-done.17.refs_1_ = bf16[64,1024]{1,0:T(8,128)(2,1)S(1)} collective-permute-done((bf16[64,1024]{1,0:T(8,128)(2,1)S(1)}, bf16[64,1024]{1,0:T(8,128)(2,1)S(1)}, u32[]{:S(2)}, u32[]{:S(2)}) %collective-permute-start.17) | collective-permute-done | bytes 131104 | tf_op jit(solution)/shard_map/ppermute | solution.py:432
  49.9 3.4 %collective-permute-done.19.refs_3_ = bf16[64,1024]{1,0:T(8,128)(2,1)S(1)} collective-permute-done((bf16[64,1024]{1,0:T(8,128)(2,1)S(1)}, bf16[64,1024]{1,0:T(8,128)(2,1)S(1)}, u32[]{:S(2)}, u32[]{:S(2)}) %collective-permute-start.19) | collective-permute-done | bytes 131104 | tf_op jit(solution)/shard_map/ppermute | solution.py:432
  53.3 1.4 %attention.1 = (bf16[64,256]{1,0:T(8,128)(2,1)S(1)}, bf16[64,256]{1,0:T(8,128)(2,1)S(1)}, bf16[64,256]{1,0:T(8,128)(2,1)S(1)}, bf16[64,256]{1,0:T(8,128)(2,1)S(1)}, bf16[4,1024,128]{2,1,0:T(8,128)(2,1)S(1)}) custom-call(f32[4,64]{1,0:T(4,128)S(1)} %get-tuple-element.66.keys_ref, bf16[64,1024]{1,0:T(8,128)(2,1)S(1)} %get-tuple-element.68.refs_0_, ...), custom_call_target="tpu_custom_call" | custom-call | flops 1000000000 | bytes 2000000 | tf_op jit(solution)/shard_map/attention/pallas_call | solution.py:512
  54.7 0.1 collective-permute-start.25
  54.8 0.3 collective-permute-start.22
  55.1 2.4 %collective-permute-start.23 = (bf16[64,256]{1,0:T(8,128)(2,1)S(1)}, bf16[64,256]{1,0:T(8,128)(2,1)S(1)}, u32[]{:S(2)}, u32[]{:S(2)}) collective-permute-start(bf16[64,256]{1,0:T(8,128)(2,1)S(1)} %get-tuple-element.75), channel_id=1, source_target_pairs={{0,2},{1,3},{2,0},{3,1},{4,6},{5,7},{6,4},{7,5},{8,10},{9,11},{10,... | collective-permute-start | bytes 98312 | tf_op jit(solution)/shard_map/ppermute | solution.py:432
  57.5 1.7 %collective-permute-start.24 = (bf16[64,256]{1,0:T(8,128)(2,1)S(1)}, bf16[64,256]{1,0:T(8,128)(2,1)S(1)}, u32[]{:S(2)}, u32[]{:S(2)}) collective-permute-start(bf16[64,256]{1,0:T(8,128)(2,1)S(1)} %get-tuple-element.76), channel_id=1, source_target_pairs={{0,3},{1,2},{2,1},{3,0},{4,7},{5,6},{6,5},{7,4},{8,11},{9,10},{10,... | collective-permute-start | bytes 98312 | tf_op jit(solution)/shard_map/ppermute | solution.py:432
  59.2 1.2 %collective-permute-done.23.refs_2_ = bf16[64,256]{1,0:T(8,128)(2,1)S(1)} collective-permute-done((bf16[64,256]{1,0:T(8,128)(2,1)S(1)}, bf16[64,256]{1,0:T(8,128)(2,1)S(1)}, u32[]{:S(2)}, u32[]{:S(2)}) %collective-permute-start.23) | collective-permute-done | bytes 32800 | tf_op jit(solution)/shard_map/ppermute | solution.py:432
  60.5 2.8 %collective-permute-done.24.refs_3_ = bf16[64,256]{1,0:T(8,128)(2,1)S(1)} collective-permute-done((bf16[64,256]{1,0:T(8,128)(2,1)S(1)}, bf16[64,256]{1,0:T(8,128)(2,1)S(1)}, u32[]{:S(2)}, u32[]{:S(2)}) %collective-permute-start.24) | collective-permute-done | bytes 32800 | tf_op jit(solution)/shard_map/ppermute | solution.py:432
  63.2 1.1 %output.1 = bf16[64,1024]{1,0:T(8,128)(2,1)} custom-call(f32[64,1]{1,0:T(8,128)S(1)} %get-tuple-element.65.valid_ref, bf16[64,256]{1,0:T(8,128)(2,1)S(1)} %get-tuple-element.73.refs_0_, bf16[64,256]{1,0:T(8,128)(2,1)S(1)} %collective-permute-done.22.refs_1_, bf16[64,256]{1,0:T(8,128)(2,1)S(1)} %collective-permute-done.23.refs_2_, ...), custom_call_target="tpu_custom_call" | custom-call | flops 100000000 | bytes 3000000 | tf_op jit(solution)/shard_map/output/pallas_call | solution.py:531
  (31 shorter events, 0.1 us)
Async XLA Ops:
  0.6 13.4 %collective-permute-start.1 = (bf16[640,1024]{1,0:T(8,128)(2,1)}, bf16[640,1024]{1,0:T(8,128)(2,1)S(1)}, u32[]{:S(2)}, u32[]{:S(2)}) collective-permute-start(bf16[640,1024]{1,0:T(8,128)(2,1)} %refs_4_), channel_id=1, source_target_pairs={{0,4},{4,0},{8,12},{12,8},{16,20},{20,16},{24,28},{28,24},{1,5},{5... | collective-permute-start | bytes 3932168 | tf_op jit(solution)/shard_map/ppermute | solution.py:426
  1.9 22.0 %copy-start.1 = (bf16[640,1024]{1,0:T(8,128)(2,1)S(1)}, bf16[640,1024]{1,0:T(8,128)(2,1)}, u32[]{:S(2)}) copy-start(bf16[640,1024]{1,0:T(8,128)(2,1)} %refs_4_) | copy-start | bytes 3932164
  1.9 22.0 %copy-start.2 = (bf16[2304,256]{1,0:T(8,128)(2,1)S(1)}, bf16[2304,256]{1,0:T(8,128)(2,1)}, u32[]{:S(2)}) copy-start(bf16[2304,256]{1,0:T(8,128)(2,1)} %conv2_ref.1) | copy-start | bytes 3538948
  1.9 22.0 %copy-start.4 = (bf16[9,256]{1,0:T(8,128)(2,1)S(1)}, bf16[9,256]{1,0:T(8,128)(2,1)}, u32[]{:S(2)}) copy-start(bf16[9,256]{1,0:T(8,128)(2,1)} %conv1_ref.1) | copy-start | bytes 13828
  1.9 7.7 %collective-permute-start = (f32[8,1024]{1,0:T(8,128)S(1)}, f32[8,1024]{1,0:T(8,128)S(1)}, u32[]{:S(2)}, u32[]{:S(2)}) collective-permute-start(f32[8,1024]{1,0:T(8,128)S(1)} %slice.3), channel_id=1, source_target_pairs={{0,1},{1,2},{2,3},{3,4},{4,5},{5,6},{6,7},{7,8},{8,9},{9,10},{10,1... | collective-permute-start | bytes 98312 | tf_op jit(solution)/shard_map/ppermute | solution.py:418
  6.6 13.0 %collective-permute-start.5 = (bf16[1024,128]{1,0:T(8,128)(2,1)}, bf16[1024,128]{1,0:T(8,128)(2,1)S(1)}, u32[]{:S(2)}, u32[]{:S(2)}) collective-permute-start(bf16[1024,128]{1,0:T(8,128)(2,1)} %refs_6_), channel_id=1, source_target_pairs={{0,8},{4,12},{8,0},{12,4},{16,24},{20,28},{24,16},{28,20},{1,9},{5... | collective-permute-start | bytes 786440 | tf_op jit(solution)/shard_map/ppermute | solution.py:422
  8.1 13.5 %collective-permute-start.6 = (bf16[1024,128]{1,0:T(8,128)(2,1)}, bf16[1024,128]{1,0:T(8,128)(2,1)}, u32[]{:S(2)}, u32[]{:S(2)}) collective-permute-start(bf16[1024,128]{1,0:T(8,128)(2,1)} %refs_6_), channel_id=1, source_target_pairs={{0,16},{4,20},{8,24},{12,28},{16,0},{20,4},{24,8},{28,12},{1,17},{... | collective-permute-start | bytes 786440 | tf_op jit(solution)/shard_map/ppermute | solution.py:422
  9.6 0.6 copy-start.9
  14.0 8.0 %collective-permute-start.2 = (bf16[72,128]{1,0:T(8,128)(2,1)}, bf16[72,128]{1,0:T(8,128)(2,1)S(1)}, u32[]{:S(2)}, u32[]{:S(2)}) collective-permute-start(bf16[72,128]{1,0:T(8,128)(2,1)} %get-tuple-element.45), channel_id=1, source_target_pairs={{0,8},{4,12},{8,0},{12,4},{16,24},{20,28},{24,16},{28,20},{1,9},{5... | collective-permute-start | bytes 55304 | tf_op jit(solution)/shard_map/ppermute | solution.py:422
  17.0 6.1 %collective-permute-start.3 = (bf16[72,128]{1,0:T(8,128)(2,1)}, bf16[72,128]{1,0:T(8,128)(2,1)S(1)}, u32[]{:S(2)}, u32[]{:S(2)}) collective-permute-start(bf16[72,128]{1,0:T(8,128)(2,1)} %get-tuple-element.46), channel_id=1, source_target_pairs={{0,16},{4,20},{8,24},{12,28},{16,0},{20,4},{24,8},{28,12},{1,17},{... | collective-permute-start | bytes 55304 | tf_op jit(solution)/shard_map/ppermute | solution.py:422
  18.6 5.2 %collective-permute-start.4 = (bf16[72,128]{1,0:T(8,128)(2,1)}, bf16[72,128]{1,0:T(8,128)(2,1)S(1)}, u32[]{:S(2)}, u32[]{:S(2)}) collective-permute-start(bf16[72,128]{1,0:T(8,128)(2,1)} %get-tuple-element.47), channel_id=1, source_target_pairs={{0,24},{4,28},{8,16},{12,20},{16,8},{20,12},{24,0},{28,4},{1,25},{... | collective-permute-start | bytes 55304 | tf_op jit(solution)/shard_map/ppermute | solution.py:422
  19.5 20.2 %copy-start = (bf16[128,768]{1,0:T(8,128)(2,1)S(1)}, bf16[128,768]{1,0:T(8,128)(2,1)}, u32[]{:S(2)}) copy-start(bf16[128,768]{1,0:T(8,128)(2,1)} %get-tuple-element.62.refs_8_) | copy-start | bytes 589828
  19.5 11.3 %collective-permute-start.16 = (bf16[128,768]{1,0:T(8,128)(2,1)}, bf16[128,768]{1,0:T(8,128)(2,1)S(1)}, u32[]{:S(2)}, u32[]{:S(2)}) collective-permute-start(bf16[128,768]{1,0:T(8,128)(2,1)} %get-tuple-element.62.refs_8_), channel_id=1, source_target_pairs={{0,24},{4,28},{8,16},{12,20},{16,8},{20,12},{24,0},{28,4},{1,25},{... | collective-permute-start | bytes 589832 | tf_op jit(solution)/shard_map/ppermute | solution.py:422
  21.6 11.5 %collective-permute-start.15 = (bf16[128,768]{1,0:T(8,128)(2,1)}, bf16[128,768]{1,0:T(8,128)(2,1)S(1)}, u32[]{:S(2)}, u32[]{:S(2)}) collective-permute-start(bf16[128,768]{1,0:T(8,128)(2,1)} %get-tuple-element.62.refs_8_), channel_id=1, source_target_pairs={{0,16},{4,20},{8,24},{12,28},{16,0},{20,4},{24,8},{28,12},{1,17},{... | collective-permute-start | bytes 589832 | tf_op jit(solution)/shard_map/ppermute | solution.py:422
  22.0 11.9 %collective-permute-start.14 = (bf16[128,768]{1,0:T(8,128)(2,1)}, bf16[128,768]{1,0:T(8,128)(2,1)S(1)}, u32[]{:S(2)}, u32[]{:S(2)}) collective-permute-start(bf16[128,768]{1,0:T(8,128)(2,1)} %get-tuple-element.62.refs_8_), channel_id=1, source_target_pairs={{0,8},{4,12},{8,0},{12,4},{16,24},{20,28},{24,16},{28,20},{1,9},{5... | collective-permute-start | bytes 589832 | tf_op jit(solution)/shard_map/ppermute | solution.py:422
  23.9 0.7 %copy-start.8 = (bf16[72,128]{1,0:T(8,128)(2,1)S(1)}, bf16[72,128]{1,0:T(8,128)(2,1)}, u32[]{:S(2)}) copy-start(bf16[72,128]{1,0:T(8,128)(2,1)} %get-tuple-element.48.refs_0_) | copy-start | bytes 55300
  29.4 11.0 %copy-start.3 = (bf16[1024,128]{1,0:T(8,128)(2,1)S(1)}, bf16[1024,128]{1,0:T(8,128)(2,1)}, u32[]{:S(2)}) copy-start(bf16[1024,128]{1,0:T(8,128)(2,1)} %refs_6_) | copy-start | bytes 786436
  29.4 18.5 %copy-start.5 = (s32[8]{0:T(128)S(1)}, s32[8]{0:T(128)}, u32[]{:S(2)}) copy-start(s32[8]{0:T(128)} %slots_ref.1) | copy-start | bytes 100
  29.4 18.5 %copy-start.6 = (s32[8]{0:T(128)S(1)}, s32[8]{0:T(128)}, u32[]{:S(2)}) copy-start(s32[8]{0:T(128)} %starts_ref.1) | copy-start | bytes 100
  29.4 18.5 %copy-start.7 = (s32[8]{0:T(128)S(1)}, s32[8]{0:T(128)}, u32[]{:S(2)}) copy-start(s32[8]{0:T(128)} %lengths_ref.1) | copy-start | bytes 100
  29.4 4.7 %collective-permute-start.7 = (bf16[32,1024]{1,0:T(8,128)(2,1)S(1)}, bf16[32,1024]{1,0:T(8,128)(2,1)S(1)}, u32[]{:S(2)}, u32[]{:S(2)}) collective-permute-start(bf16[32,1024]{1,0:T(8,128)(2,1)S(1)} %get-tuple-element.54), channel_id=1, source_target_pairs={{0,28},{4,24},{8,20},{12,16},{16,12},{20,8},{24,4},{28,0},{1,29},{... | collective-permute-start | bytes 196616 | tf_op jit(solution)/shard_map/ppermute | solution.py:429
  29.5 6.2 %collective-permute-start.8 = (bf16[32,1024]{1,0:T(8,128)(2,1)S(1)}, bf16[32,1024]{1,0:T(8,128)(2,1)S(1)}, u32[]{:S(2)}, u32[]{:S(2)}) collective-permute-start(bf16[32,1024]{1,0:T(8,128)(2,1)S(1)} %get-tuple-element.55), channel_id=1, source_target_pairs={{0,24},{4,28},{8,16},{12,20},{16,8},{20,12},{24,0},{28,4},{1,25},{... | collective-permute-start | bytes 196616 | tf_op jit(solution)/shard_map/ppermute | solution.py:429
  30.8 6.0 %collective-permute-start.9 = (bf16[32,1024]{1,0:T(8,128)(2,1)S(1)}, bf16[32,1024]{1,0:T(8,128)(2,1)S(1)}, u32[]{:S(2)}, u32[]{:S(2)}) collective-permute-start(bf16[32,1024]{1,0:T(8,128)(2,1)S(1)} %get-tuple-element.56), channel_id=1, source_target_pairs={{0,20},{4,16},{8,28},{12,24},{16,4},{20,0},{24,12},{28,8},{1,21},{... | collective-permute-start | bytes 196616 | tf_op jit(solution)/shard_map/ppermute | solution.py:429
  33.1 5.2 %collective-permute-start.10 = (bf16[32,1024]{1,0:T(8,128)(2,1)S(1)}, bf16[32,1024]{1,0:T(8,128)(2,1)S(1)}, u32[]{:S(2)}, u32[]{:S(2)}) collective-permute-start(bf16[32,1024]{1,0:T(8,128)(2,1)S(1)} %get-tuple-element.57), channel_id=1, source_target_pairs={{0,16},{4,20},{8,24},{12,28},{16,0},{20,4},{24,8},{28,12},{1,17},{... | collective-permute-start | bytes 196616 | tf_op jit(solution)/shard_map/ppermute | solution.py:429
  33.9 4.4 %collective-permute-start.11 = (bf16[32,1024]{1,0:T(8,128)(2,1)S(1)}, bf16[32,1024]{1,0:T(8,128)(2,1)S(1)}, u32[]{:S(2)}, u32[]{:S(2)}) collective-permute-start(bf16[32,1024]{1,0:T(8,128)(2,1)S(1)} %get-tuple-element.58), channel_id=1, source_target_pairs={{0,12},{4,8},{8,4},{12,0},{16,28},{20,24},{24,20},{28,16},{1,13},{... | collective-permute-start | bytes 196616 | tf_op jit(solution)/shard_map/ppermute | solution.py:429
  34.2 5.5 %collective-permute-start.12 = (bf16[32,1024]{1,0:T(8,128)(2,1)S(1)}, bf16[32,1024]{1,0:T(8,128)(2,1)S(1)}, u32[]{:S(2)}, u32[]{:S(2)}) collective-permute-start(bf16[32,1024]{1,0:T(8,128)(2,1)S(1)} %get-tuple-element.59), channel_id=1, source_target_pairs={{0,8},{4,12},{8,0},{12,4},{16,24},{20,28},{24,16},{28,20},{1,9},{5... | collective-permute-start | bytes 196616 | tf_op jit(solution)/shard_map/ppermute | solution.py:429
  35.7 4.0 %collective-permute-start.13 = (bf16[32,1024]{1,0:T(8,128)(2,1)S(1)}, bf16[32,1024]{1,0:T(8,128)(2,1)S(1)}, u32[]{:S(2)}, u32[]{:S(2)}) collective-permute-start(bf16[32,1024]{1,0:T(8,128)(2,1)S(1)} %get-tuple-element.60), channel_id=1, source_target_pairs={{0,4},{4,0},{8,12},{12,8},{16,20},{20,16},{24,28},{28,24},{1,5},{5... | collective-permute-start | bytes 196616 | tf_op jit(solution)/shard_map/ppermute | solution.py:429
  40.2 13.1 %collective-permute-start.20 = (bf16[4,128,768]{2,1,0:T(8,128)(2,1)S(1)}, bf16[4,128,768]{2,1,0:T(8,128)(2,1)S(1)}, u32[]{:S(2)}, u32[]{:S(2)}) collective-permute-start(bf16[4,128,768]{2,1,0:T(8,128)(2,1)S(1)} %get-tuple-element.69.refs_4_), channel_id=1, source_target_pairs={{0,4},{4,0},{8,12},{12,8},{16,20},{20,16},{24,28},{28,24},{1,5},{5... | collective-permute-start | bytes 2359304 | tf_op jit(solution)/shard_map/ppermute | solution.py:426
  40.4 7.6 %collective-permute-start.18 = (bf16[64,1024]{1,0:T(8,128)(2,1)S(1)}, bf16[64,1024]{1,0:T(8,128)(2,1)S(1)}, u32[]{:S(2)}, u32[]{:S(2)}) collective-permute-start(bf16[64,1024]{1,0:T(8,128)(2,1)S(1)} %get-tuple-element.68.refs_0_), channel_id=1, source_target_pairs={{0,2},{1,3},{2,0},{3,1},{4,6},{5,7},{6,4},{7,5},{8,10},{9,11},{10,... | collective-permute-start | bytes 393224 | tf_op jit(solution)/shard_map/ppermute | solution.py:432
  40.4 13.0 %collective-permute-start.21 = (bf16[1024,128]{1,0:T(8,128)(2,1)S(1)}, bf16[1024,128]{1,0:T(8,128)(2,1)S(1)}, u32[]{:S(2)}, u32[]{:S(2)}) collective-permute-start(bf16[1024,128]{1,0:T(8,128)(2,1)S(1)} %copy-done.3), channel_id=1, source_target_pairs={{0,24},{4,28},{8,16},{12,20},{16,8},{20,12},{24,0},{28,4},{1,25},{... | collective-permute-start | bytes 786440 | tf_op jit(solution)/shard_map/ppermute | solution.py:422
  41.7 8.3 %collective-permute-start.17 = (bf16[64,1024]{1,0:T(8,128)(2,1)S(1)}, bf16[64,1024]{1,0:T(8,128)(2,1)S(1)}, u32[]{:S(2)}, u32[]{:S(2)}) collective-permute-start(bf16[64,1024]{1,0:T(8,128)(2,1)S(1)} %get-tuple-element.68.refs_0_), channel_id=1, source_target_pairs={{0,1},{1,0},{2,3},{3,2},{4,5},{5,4},{6,7},{7,6},{8,9},{9,8},{10,11... | collective-permute-start | bytes 393224 | tf_op jit(solution)/shard_map/ppermute | solution.py:432
  47.9 5.4 %collective-permute-start.19 = (bf16[64,1024]{1,0:T(8,128)(2,1)S(1)}, bf16[64,1024]{1,0:T(8,128)(2,1)S(1)}, u32[]{:S(2)}, u32[]{:S(2)}) collective-permute-start(bf16[64,1024]{1,0:T(8,128)(2,1)S(1)} %collective-permute-done.18.refs_2_), channel_id=1, source_target_pairs={{0,1},{1,0},{2,3},{3,2},{4,5},{5,4},{6,7},{7,6},{8,9},{9,8},{10,11... | collective-permute-start | bytes 393224 | tf_op jit(solution)/shard_map/ppermute | solution.py:432
  54.7 8.6 %collective-permute-start.25 = (bf16[4,1024,128]{2,1,0:T(8,128)(2,1)S(1)}, bf16[4,1024,128]{2,1,0:T(8,128)(2,1)S(1)}, u32[]{:S(2)}, u32[]{:S(2)}) collective-permute-start(bf16[4,1024,128]{2,1,0:T(8,128)(2,1)S(1)} %get-tuple-element.77.refs_4_), channel_id=1, source_target_pairs={{0,4},{4,0},{8,12},{12,8},{16,20},{20,16},{24,28},{28,24},{1,5},{5... | collective-permute-start | bytes 3145736 | tf_op jit(solution)/shard_map/ppermute | solution.py:426
  54.8 4.5 %collective-permute-start.22 = (bf16[64,256]{1,0:T(8,128)(2,1)S(1)}, bf16[64,256]{1,0:T(8,128)(2,1)S(1)}, u32[]{:S(2)}, u32[]{:S(2)}) collective-permute-start(bf16[64,256]{1,0:T(8,128)(2,1)S(1)} %get-tuple-element.74), channel_id=1, source_target_pairs={{0,1},{1,0},{2,3},{3,2},{4,5},{5,4},{6,7},{7,6},{8,9},{9,8},{10,11... | collective-permute-start | bytes 98312 | tf_op jit(solution)/shard_map/ppermute | solution.py:432
  55.1 5.4 %collective-permute-start.23 = (bf16[64,256]{1,0:T(8,128)(2,1)S(1)}, bf16[64,256]{1,0:T(8,128)(2,1)S(1)}, u32[]{:S(2)}, u32[]{:S(2)}) collective-permute-start(bf16[64,256]{1,0:T(8,128)(2,1)S(1)} %get-tuple-element.75), channel_id=1, source_target_pairs={{0,2},{1,3},{2,0},{3,1},{4,6},{5,7},{6,4},{7,5},{8,10},{9,11},{10,... | collective-permute-start | bytes 98312 | tf_op jit(solution)/shard_map/ppermute | solution.py:432
  57.5 5.7 %collective-permute-start.24 = (bf16[64,256]{1,0:T(8,128)(2,1)S(1)}, bf16[64,256]{1,0:T(8,128)(2,1)S(1)}, u32[]{:S(2)}, u32[]{:S(2)}) collective-permute-start(bf16[64,256]{1,0:T(8,128)(2,1)S(1)} %get-tuple-element.76), channel_id=1, source_target_pairs={{0,3},{1,2},{2,1},{3,0},{4,7},{5,6},{6,5},{7,4},{8,11},{9,10},{10,... | collective-permute-start | bytes 98312 | tf_op jit(solution)/shard_map/ppermute | solution.py:432

commit v13 on v12

--- a/solution.py
+++ b/solution.py
@@ -153,13 +153,13 @@
 def mel_kernel(parts, group, slots_here, rim_ref, audio_ref, table_ref, qkv_ref, *refs):
     outs_refs, (mix_out, ext, table, blocks, slots_ref, sems) = refs[:parts], refs[parts:]
     load_slots = pltpu.make_async_copy(slots_here, slots_ref, sems.at[5])
-    load_slots.start()
     load_audio = pltpu.make_async_copy(audio_ref, ext.at[:, pl.ds(RIM, audio_ref.shape[1])], sems.at[3])
     load_table = pltpu.make_async_copy(table_ref, table, sems.at[4])
+    load_table.start()
     load_rim = pltpu.make_async_copy(rim_ref, ext.at[:, pl.ds(0, RIM)], sems.at[6])
     load_rim.start()
     load_audio.start()
-    load_table.start()
+    load_slots.start()
     pieces = mix_columns(group, qkv_ref, mix_out, sems)
     start_all(pieces)
     streams = audio_ref.shape[0]
@@ -415,7 +415,8 @@
     scale = max(1, windows * group // 32)
 
     route = [(i, i + 1) for i in range(windows * group - 1)]
-    rim = lax.ppermute(audio[:, audio.shape[1] - RIM :], ("dp", "seq"), route)
+    edge, proj_weight = lax.optimization_barrier((audio[:, audio.shape[1] - RIM :], proj_weight))
+    rim = lax.ppermute(edge, ("dp", "seq"), route)
 
     def to_part(block, step):
         pairs = [(p * copies + c, (p ^ step) * copies + c) for p in range(parts) for c in range(copies)]

time: 64.7 us -> 64.8 us (level)
  transfers between devices with their start and end apart: 26 -> 26, of which waited for: 10 -> 10; matrix products, arithmetic and copies ran while one was open for 1% -> 0% of each run, Pallas kernels for 15% -> 15%
where the time goes in v13:
time: 64.8 us; the launch traced here: 64.5 us
  starting transfers between devices  30.4 us (47%)
  waiting for transfers between devices  18.3 us (28%)
  Pallas kernels  12.9 us (20%)
  local copies, waits for them, and re-layouts  2.14 us (3%)
  between operations  0.78 us (1%)
    ppermute x9, starting transfers between devices, to_part(): return lax.ppermute(block, 'dp', pairs)  13.5 us
    ppermute x6, waiting for transfers between devices, to_plane(): return lax.ppermute(block, 'seq', [(i, i ^ step) for i in range(group)])  13.3 us
    ppermute x7, starting transfers between devices, to_window(): return lax.ppermute(block, 'dp', [(i, i ^ step) for i in range(windows)])  6.04 us
    ppermute x6, starting transfers between devices, to_plane(): return lax.ppermute(block, 'seq', [(i, i ^ step) for i in range(group)])  5.52 us
    pallas_call x1, Pallas kernels, on_device(): pl.pallas_call(functools.partial(conv_kernel, parts, width), out_shape=tu...  4.77 us
    ppermute x1, starting transfers between devices, on_device(): rim = lax.ppermute(edge, ('dp', 'seq'), route)  4.62 us
    ppermute x7, waiting for transfers between devices, to_window(): return lax.ppermute(block, 'dp', [(i, i ^ step) for i in range(windows)])  4.21 us
    pallas_call x1, Pallas kernels, on_device(): pl.pallas_call(functools.partial(mel_kernel, parts, group), out_shape=tup...  3.88 us
  transfers between devices with their start and end apart: 26, of which 10 were waited for; matrix products, arithmetic and copies ran while one was open for 0% of the time, Pallas kernels for 15%

profile of v13, /device:TPU:0, one launch (start us, length us, event | category | flops | bytes accessed | tf_op | source)
XLA Modules:
  0.0 64.5 jit_solution(7481934253105960025)
XLA Ops:
  0.6 0.8 %slice.3 = f32[8,1024]{1,0:T(8,128)S(1)} slice(f32[8,5120]{1,0:T(8,128)} %audio_ref.1), slice={[0:8], [4096:5120]} | slice | bytes 65536 | tf_op jit(solution)/shard_map/slice | solution.py:418
  1.4 0.5 collective-permute-start.1
  1.9 4.6 %collective-permute-start = (f32[8,1024]{1,0:T(8,128)S(1)}, f32[8,1024]{1,0:T(8,128)S(1)}, u32[]{:S(2)}, u32[]{:S(2)}) collective-permute-start(f32[8,1024]{1,0:T(8,128)S(1)} %slice.3), channel_id=1, source_target_pairs={{0,1},{1,2},{2,3},{3,4},{4,5},{5,6},{6,7},{7,8},{8,9},{9,10},{10,1... | collective-permute-start | bytes 98312 | tf_op jit(solution)/shard_map/ppermute | solution.py:419
  6.5 1.6 %collective-permute-start.5 = (bf16[1024,128]{1,0:T(8,128)(2,1)}, bf16[1024,128]{1,0:T(8,128)(2,1)S(1)}, u32[]{:S(2)}, u32[]{:S(2)}) collective-permute-start(bf16[1024,128]{1,0:T(8,128)(2,1)} %refs_6_), channel_id=1, source_target_pairs={{0,8},{4,12},{8,0},{12,4},{16,24},{20,28},{24,16},{28,20},{1,9},{5... | collective-permute-start | bytes 786440 | tf_op jit(solution)/shard_map/ppermute | solution.py:423
  8.1 1.5 %collective-permute-start.6 = (bf16[1024,128]{1,0:T(8,128)(2,1)}, bf16[1024,128]{1,0:T(8,128)(2,1)}, u32[]{:S(2)}, u32[]{:S(2)}) collective-permute-start(bf16[1024,128]{1,0:T(8,128)(2,1)} %refs_6_), channel_id=1, source_target_pairs={{0,16},{4,20},{8,24},{12,28},{16,0},{20,4},{24,8},{28,12},{1,17},{... | collective-permute-start | bytes 786440 | tf_op jit(solution)/shard_map/ppermute | solution.py:423
  9.6 0.0 collective-permute-done.rim_ref
  9.6 0.6 copy-done.9
  10.2 3.9 %log_mel.1 = (bf16[72,128]{1,0:T(8,128)(2,1)}, bf16[72,128]{1,0:T(8,128)(2,1)}, bf16[72,128]{1,0:T(8,128)(2,1)}, bf16[72,128]{1,0:T(8,128)(2,1)}, bf16[128,768]{1,0:T(8,128)(2,1)}) custom-call(s32[8]{0:T(128)} %slots_ref.1, f32[8,1024]{1,0:T(8,128)} %copy-done.9, f32[8,5120]{1,0:T(8,128)} %audio_ref.1, f32[264,640]{1,0:T(8,128)} %constant.2.clone.table_ref, ...), custom_call_target="tpu_custom_call" | custom-call | flops 10000000000 | bytes 2000000 | tf_op jit(solution)/shard_map/log_mel/pallas_call | solution.py:439
  14.1 3.0 %collective-permute-start.2 = (bf16[72,128]{1,0:T(8,128)(2,1)}, bf16[72,128]{1,0:T(8,128)(2,1)S(1)}, u32[]{:S(2)}, u32[]{:S(2)}) collective-permute-start(bf16[72,128]{1,0:T(8,128)(2,1)} %get-tuple-element.49), channel_id=1, source_target_pairs={{0,8},{4,12},{8,0},{12,4},{16,24},{20,28},{24,16},{28,20},{1,9},{5... | collective-permute-start | bytes 55304 | tf_op jit(solution)/shard_map/ppermute | solution.py:423
  17.2 1.6 %collective-permute-start.3 = (bf16[72,128]{1,0:T(8,128)(2,1)}, bf16[72,128]{1,0:T(8,128)(2,1)S(1)}, u32[]{:S(2)}, u32[]{:S(2)}) collective-permute-start(bf16[72,128]{1,0:T(8,128)(2,1)} %get-tuple-element.50), channel_id=1, source_target_pairs={{0,16},{4,20},{8,24},{12,28},{16,0},{20,4},{24,8},{28,12},{1,17},{... | collective-permute-start | bytes 55304 | tf_op jit(solution)/shard_map/ppermute | solution.py:423
  18.8 0.9 %collective-permute-start.4 = (bf16[72,128]{1,0:T(8,128)(2,1)}, bf16[72,128]{1,0:T(8,128)(2,1)S(1)}, u32[]{:S(2)}, u32[]{:S(2)}) collective-permute-start(bf16[72,128]{1,0:T(8,128)(2,1)} %get-tuple-element.51), channel_id=1, source_target_pairs={{0,24},{4,28},{8,16},{12,20},{16,8},{20,12},{24,0},{28,4},{1,25},{... | collective-permute-start | bytes 55304 | tf_op jit(solution)/shard_map/ppermute | solution.py:423
  19.7 2.0 %collective-permute-start.16 = (bf16[128,768]{1,0:T(8,128)(2,1)}, bf16[128,768]{1,0:T(8,128)(2,1)S(1)}, u32[]{:S(2)}, u32[]{:S(2)}) collective-permute-start(bf16[128,768]{1,0:T(8,128)(2,1)} %get-tuple-element.66.refs_8_), channel_id=1, source_target_pairs={{0,24},{4,28},{8,16},{12,20},{16,8},{20,12},{24,0},{28,4},{1,25},{... | collective-permute-start | bytes 589832 | tf_op jit(solution)/shard_map/ppermute | solution.py:423
  21.7 0.4 collective-permute-start.15
  22.1 1.1 %collective-permute-start.14 = (bf16[128,768]{1,0:T(8,128)(2,1)}, bf16[128,768]{1,0:T(8,128)(2,1)S(1)}, u32[]{:S(2)}, u32[]{:S(2)}) collective-permute-start(bf16[128,768]{1,0:T(8,128)(2,1)} %get-tuple-element.66.refs_8_), channel_id=1, source_target_pairs={{0,8},{4,12},{8,0},{12,4},{16,24},{20,28},{24,16},{28,20},{1,9},{5... | collective-permute-start | bytes 589832 | tf_op jit(solution)/shard_map/ppermute | solution.py:423
  23.2 0.7 %collective-permute-done.4.refs_3_ = bf16[72,128]{1,0:T(8,128)(2,1)S(1)} collective-permute-done((bf16[72,128]{1,0:T(8,128)(2,1)}, bf16[72,128]{1,0:T(8,128)(2,1)S(1)}, u32[]{:S(2)}, u32[]{:S(2)}) %collective-permute-start.4) | collective-permute-done | bytes 18464 | tf_op jit(solution)/shard_map/ppermute | solution.py:423
  24.0 0.0 copy-start.8
  24.0 0.7 %copy-done.8 = bf16[72,128]{1,0:T(8,128)(2,1)S(1)} copy-done((bf16[72,128]{1,0:T(8,128)(2,1)S(1)}, bf16[72,128]{1,0:T(8,128)(2,1)}, u32[]{:S(2)}) %copy-start.8) | copy-done | bytes 18456
  24.7 4.8 %conv.1 = (bf16[32,1024]{1,0:T(8,128)(2,1)S(1)}, bf16[32,1024]{1,0:T(8,128)(2,1)S(1)}, bf16[32,1024]{1,0:T(8,128)(2,1)S(1)}, bf16[32,1024]{1,0:T(8,128)(2,1)S(1)...) custom-call(bf16[9,256]{1,0:T(8,128)(2,1)S(1)} %copy-done.4, ...), custom_call_target="tpu_custom_call" | custom-call | flops 2000000000 | bytes 4000000 | tf_op jit(solution)/shard_map/conv/pallas_call | solution.py:462
  29.5 0.0 copy-start.3
  29.5 0.0 copy-start.5
  29.5 0.0 copy-start.6
  29.5 0.0 copy-start.7
  29.6 0.1 collective-permute-start.7
  29.6 1.3 %collective-permute-start.8 = (bf16[32,1024]{1,0:T(8,128)(2,1)S(1)}, bf16[32,1024]{1,0:T(8,128)(2,1)S(1)}, u32[]{:S(2)}, u32[]{:S(2)}) collective-permute-start(bf16[32,1024]{1,0:T(8,128)(2,1)S(1)} %get-tuple-element.59), channel_id=1, source_target_pairs={{0,24},{4,28},{8,16},{12,20},{16,8},{20,12},{24,0},{28,4},{1,25},{... | collective-permute-start | bytes 196616 | tf_op jit(solution)/shard_map/ppermute | solution.py:430
  30.9 2.3 %collective-permute-start.9 = (bf16[32,1024]{1,0:T(8,128)(2,1)S(1)}, bf16[32,1024]{1,0:T(8,128)(2,1)S(1)}, u32[]{:S(2)}, u32[]{:S(2)}) collective-permute-start(bf16[32,1024]{1,0:T(8,128)(2,1)S(1)} %get-tuple-element.60), channel_id=1, source_target_pairs={{0,20},{4,16},{8,28},{12,24},{16,4},{20,0},{24,12},{28,8},{1,21},{... | collective-permute-start | bytes 196616 | tf_op jit(solution)/shard_map/ppermute | solution.py:430
  33.2 0.8 %collective-permute-start.10 = (bf16[32,1024]{1,0:T(8,128)(2,1)S(1)}, bf16[32,1024]{1,0:T(8,128)(2,1)S(1)}, u32[]{:S(2)}, u32[]{:S(2)}) collective-permute-start(bf16[32,1024]{1,0:T(8,128)(2,1)S(1)} %get-tuple-element.61), channel_id=1, source_target_pairs={{0,16},{4,20},{8,24},{12,28},{16,0},{20,4},{24,8},{28,12},{1,17},{... | collective-permute-start | bytes 196616 | tf_op jit(solution)/shard_map/ppermute | solution.py:430
  34.0 0.3 collective-permute-done.7.refs_0_
  34.3 1.5 %collective-permute-start.12 = (bf16[32,1024]{1,0:T(8,128)(2,1)S(1)}, bf16[32,1024]{1,0:T(8,128)(2,1)S(1)}, u32[]{:S(2)}, u32[]{:S(2)}) collective-permute-start(bf16[32,1024]{1,0:T(8,128)(2,1)S(1)} %get-tuple-element.63), channel_id=1, source_target_pairs={{0,8},{4,12},{8,0},{12,4},{16,24},{20,28},{24,16},{28,20},{1,9},{5... | collective-permute-start | bytes 196616 | tf_op jit(solution)/shard_map/ppermute | solution.py:430
  35.8 0.1 collective-permute-start.13
  35.9 1.0 %collective-permute-done.9.refs_2_ = bf16[32,1024]{1,0:T(8,128)(2,1)S(1)} collective-permute-done((bf16[32,1024]{1,0:T(8,128)(2,1)S(1)}, bf16[32,1024]{1,0:T(8,128)(2,1)S(1)}, u32[]{:S(2)}, u32[]{:S(2)}) %collective-permute-start.9) | collective-permute-done | bytes 65568 | tf_op jit(solution)/shard_map/ppermute | solution.py:430
  36.9 1.5 %collective-permute-done.10.refs_3_ = bf16[32,1024]{1,0:T(8,128)(2,1)S(1)} collective-permute-done((bf16[32,1024]{1,0:T(8,128)(2,1)S(1)}, bf16[32,1024]{1,0:T(8,128)(2,1)S(1)}, u32[]{:S(2)}, u32[]{:S(2)}) %collective-permute-start.10) | collective-permute-done | bytes 65568 | tf_op jit(solution)/shard_map/ppermute | solution.py:430
  38.4 1.4 %collective-permute-done.12.refs_5_ = bf16[32,1024]{1,0:T(8,128)(2,1)S(1)} collective-permute-done((bf16[32,1024]{1,0:T(8,128)(2,1)S(1)}, bf16[32,1024]{1,0:T(8,128)(2,1)S(1)}, u32[]{:S(2)}, u32[]{:S(2)}) %collective-permute-start.12) | collective-permute-done | bytes 65568 | tf_op jit(solution)/shard_map/ppermute | solution.py:430
  39.8 0.5 layer_norm.1
  40.3 0.2 collective-permute-start.20
  40.5 1.3 %collective-permute-start.21 = (bf16[1024,128]{1,0:T(8,128)(2,1)S(1)}, bf16[1024,128]{1,0:T(8,128)(2,1)S(1)}, u32[]{:S(2)}, u32[]{:S(2)}) collective-permute-start(bf16[1024,128]{1,0:T(8,128)(2,1)S(1)} %copy-done.3), channel_id=1, source_target_pairs={{0,24},{4,28},{8,16},{12,20},{16,8},{20,12},{24,0},{28,4},{1,25},{... | collective-permute-start | bytes 786440 | tf_op jit(solution)/shard_map/ppermute | solution.py:423
  41.8 1.1 %collective-permute-start.17 = (bf16[64,1024]{1,0:T(8,128)(2,1)S(1)}, bf16[64,1024]{1,0:T(8,128)(2,1)S(1)}, u32[]{:S(2)}, u32[]{:S(2)}) collective-permute-start(bf16[64,1024]{1,0:T(8,128)(2,1)S(1)} %get-tuple-element.72.refs_0_), channel_id=1, source_target_pairs={{0,1},{1,0},{2,3},{3,2},{4,5},{5,4},{6,7},{7,6},{8,9},{9,8},{10,11... | collective-permute-start | bytes 393224 | tf_op jit(solution)/shard_map/ppermute | solution.py:433
  42.9 5.2 %collective-permute-done.18.refs_2_ = bf16[64,1024]{1,0:T(8,128)(2,1)S(1)} collective-permute-done((bf16[64,1024]{1,0:T(8,128)(2,1)S(1)}, bf16[64,1024]{1,0:T(8,128)(2,1)S(1)}, u32[]{:S(2)}, u32[]{:S(2)}) %collective-permute-start.18) | collective-permute-done | bytes 131104 | tf_op jit(solution)/shard_map/ppermute | solution.py:433
  48.1 1.3 %mask.1 = (bf16[64,1024]{1,0:T(8,128)(2,1)}, f32[4,64]{1,0:T(4,128)S(1)}, f32[64,1]{1,0:T(8,128)S(1)}) custom-call(s32[8]{0:T(128)S(1)} %copy-done.5, s32[8]{0:T(128)S(1)} %copy-done.6, s32[8]{0:T(128)S(1)} %copy-done.7, bf16[64,1024]{1,0:T(8,128)(2,1)S(1)} %get-tuple-element.67.rows_ref), custom_call_target="tpu_custom_call" | custom-call | flops 100000000 | bytes 1000000 | tf_op jit(solution)/shard_map/mask/pallas_call | solution.py:493
  49.3 0.7 %collective-permute-done.17.refs_1_ = bf16[64,1024]{1,0:T(8,128)(2,1)S(1)} collective-permute-done((bf16[64,1024]{1,0:T(8,128)(2,1)S(1)}, bf16[64,1024]{1,0:T(8,128)(2,1)S(1)}, u32[]{:S(2)}, u32[]{:S(2)}) %collective-permute-start.17) | collective-permute-done | bytes 131104 | tf_op jit(solution)/shard_map/ppermute | solution.py:433
  50.1 3.4 %collective-permute-done.19.refs_3_ = bf16[64,1024]{1,0:T(8,128)(2,1)S(1)} collective-permute-done((bf16[64,1024]{1,0:T(8,128)(2,1)S(1)}, bf16[64,1024]{1,0:T(8,128)(2,1)S(1)}, u32[]{:S(2)}, u32[]{:S(2)}) %collective-permute-start.19) | collective-permute-done | bytes 131104 | tf_op jit(solution)/shard_map/ppermute | solution.py:433
  53.5 1.4 %attention.1 = (bf16[64,256]{1,0:T(8,128)(2,1)S(1)}, bf16[64,256]{1,0:T(8,128)(2,1)S(1)}, bf16[64,256]{1,0:T(8,128)(2,1)S(1)}, bf16[64,256]{1,0:T(8,128)(2,1)S(1)}, bf16[4,1024,128]{2,1,0:T(8,128)(2,1)S(1)}) custom-call(f32[4,64]{1,0:T(4,128)S(1)} %get-tuple-element.70.keys_ref, bf16[64,1024]{1,0:T(8,128)(2,1)S(1)} %get-tuple-element.72.refs_0_, ...), custom_call_target="tpu_custom_call" | custom-call | flops 1000000000 | bytes 2000000 | tf_op jit(solution)/shard_map/attention/pallas_call | solution.py:513
  54.8 0.1 collective-permute-start.25
  54.9 0.3 collective-permute-start.22
  55.3 2.4 %collective-permute-start.23 = (bf16[64,256]{1,0:T(8,128)(2,1)S(1)}, bf16[64,256]{1,0:T(8,128)(2,1)S(1)}, u32[]{:S(2)}, u32[]{:S(2)}) collective-permute-start(bf16[64,256]{1,0:T(8,128)(2,1)S(1)} %get-tuple-element.79), channel_id=1, source_target_pairs={{0,2},{1,3},{2,0},{3,1},{4,6},{5,7},{6,4},{7,5},{8,10},{9,11},{10,... | collective-permute-start | bytes 98312 | tf_op jit(solution)/shard_map/ppermute | solution.py:433
  57.7 1.7 %collective-permute-start.24 = (bf16[64,256]{1,0:T(8,128)(2,1)S(1)}, bf16[64,256]{1,0:T(8,128)(2,1)S(1)}, u32[]{:S(2)}, u32[]{:S(2)}) collective-permute-start(bf16[64,256]{1,0:T(8,128)(2,1)S(1)} %get-tuple-element.80), channel_id=1, source_target_pairs={{0,3},{1,2},{2,1},{3,0},{4,7},{5,6},{6,5},{7,4},{8,11},{9,10},{10,... | collective-permute-start | bytes 98312 | tf_op jit(solution)/shard_map/ppermute | solution.py:433
  59.4 1.3 %collective-permute-done.23.refs_2_ = bf16[64,256]{1,0:T(8,128)(2,1)S(1)} collective-permute-done((bf16[64,256]{1,0:T(8,128)(2,1)S(1)}, bf16[64,256]{1,0:T(8,128)(2,1)S(1)}, u32[]{:S(2)}, u32[]{:S(2)}) %collective-permute-start.23) | collective-permute-done | bytes 32800 | tf_op jit(solution)/shard_map/ppermute | solution.py:433
  60.6 2.7 %collective-permute-done.24.refs_3_ = bf16[64,256]{1,0:T(8,128)(2,1)S(1)} collective-permute-done((bf16[64,256]{1,0:T(8,128)(2,1)S(1)}, bf16[64,256]{1,0:T(8,128)(2,1)S(1)}, u32[]{:S(2)}, u32[]{:S(2)}) %collective-permute-start.24) | collective-permute-done | bytes 32800 | tf_op jit(solution)/shard_map/ppermute | solution.py:433
  63.4 1.1 %output.1 = bf16[64,1024]{1,0:T(8,128)(2,1)} custom-call(f32[64,1]{1,0:T(8,128)S(1)} %get-tuple-element.69.valid_ref, bf16[64,256]{1,0:T(8,128)(2,1)S(1)} %get-tuple-element.77.refs_0_, bf16[64,256]{1,0:T(8,128)(2,1)S(1)} %collective-permute-done.22.refs_1_, bf16[64,256]{1,0:T(8,128)(2,1)S(1)} %collective-permute-done.23.refs_2_, ...), custom_call_target="tpu_custom_call" | custom-call | flops 100000000 | bytes 3000000 | tf_op jit(solution)/shard_map/output/pallas_call | solution.py:532
  (31 shorter events, 0.1 us)
Async XLA Ops:
  1.4 22.6 %copy-start.1 = (bf16[640,1024]{1,0:T(8,128)(2,1)S(1)}, bf16[640,1024]{1,0:T(8,128)(2,1)}, u32[]{:S(2)}) copy-start(bf16[640,1024]{1,0:T(8,128)(2,1)} %refs_4_) | copy-start | bytes 3932164
  1.4 22.6 %copy-start.2 = (bf16[2304,256]{1,0:T(8,128)(2,1)S(1)}, bf16[2304,256]{1,0:T(8,128)(2,1)}, u32[]{:S(2)}) copy-start(bf16[2304,256]{1,0:T(8,128)(2,1)} %conv2_ref.1) | copy-start | bytes 3538948
  1.4 22.6 %copy-start.4 = (bf16[9,256]{1,0:T(8,128)(2,1)S(1)}, bf16[9,256]{1,0:T(8,128)(2,1)}, u32[]{:S(2)}) copy-start(bf16[9,256]{1,0:T(8,128)(2,1)} %conv1_ref.1) | copy-start | bytes 13828
  1.4 12.7 %collective-permute-start.1 = (bf16[640,1024]{1,0:T(8,128)(2,1)}, bf16[640,1024]{1,0:T(8,128)(2,1)S(1)}, u32[]{:S(2)}, u32[]{:S(2)}) collective-permute-start(bf16[640,1024]{1,0:T(8,128)(2,1)} %refs_4_), channel_id=1, source_target_pairs={{0,4},{4,0},{8,12},{12,8},{16,20},{20,16},{24,28},{28,24},{1,5},{5... | collective-permute-start | bytes 3932168 | tf_op jit(solution)/shard_map/ppermute | solution.py:427
  1.9 7.7 %collective-permute-start = (f32[8,1024]{1,0:T(8,128)S(1)}, f32[8,1024]{1,0:T(8,128)S(1)}, u32[]{:S(2)}, u32[]{:S(2)}) collective-permute-start(f32[8,1024]{1,0:T(8,128)S(1)} %slice.3), channel_id=1, source_target_pairs={{0,1},{1,2},{2,3},{3,4},{4,5},{5,6},{6,7},{7,8},{8,9},{9,10},{10,1... | collective-permute-start | bytes 98312 | tf_op jit(solution)/shard_map/ppermute | solution.py:419
  6.5 13.1 %collective-permute-start.5 = (bf16[1024,128]{1,0:T(8,128)(2,1)}, bf16[1024,128]{1,0:T(8,128)(2,1)S(1)}, u32[]{:S(2)}, u32[]{:S(2)}) collective-permute-start(bf16[1024,128]{1,0:T(8,128)(2,1)} %refs_6_), channel_id=1, source_target_pairs={{0,8},{4,12},{8,0},{12,4},{16,24},{20,28},{24,16},{28,20},{1,9},{5... | collective-permute-start | bytes 786440 | tf_op jit(solution)/shard_map/ppermute | solution.py:423
  8.1 13.6 %collective-permute-start.6 = (bf16[1024,128]{1,0:T(8,128)(2,1)}, bf16[1024,128]{1,0:T(8,128)(2,1)}, u32[]{:S(2)}, u32[]{:S(2)}) collective-permute-start(bf16[1024,128]{1,0:T(8,128)(2,1)} %refs_6_), channel_id=1, source_target_pairs={{0,16},{4,20},{8,24},{12,28},{16,0},{20,4},{24,8},{28,12},{1,17},{... | collective-permute-start | bytes 786440 | tf_op jit(solution)/shard_map/ppermute | solution.py:423
  9.6 0.6 copy-start.9
  14.1 8.0 %collective-permute-start.2 = (bf16[72,128]{1,0:T(8,128)(2,1)}, bf16[72,128]{1,0:T(8,128)(2,1)S(1)}, u32[]{:S(2)}, u32[]{:S(2)}) collective-permute-start(bf16[72,128]{1,0:T(8,128)(2,1)} %get-tuple-element.49), channel_id=1, source_target_pairs={{0,8},{4,12},{8,0},{12,4},{16,24},{20,28},{24,16},{28,20},{1,9},{5... | collective-permute-start | bytes 55304 | tf_op jit(solution)/shard_map/ppermute | solution.py:423
  17.2 6.1 %collective-permute-start.3 = (bf16[72,128]{1,0:T(8,128)(2,1)}, bf16[72,128]{1,0:T(8,128)(2,1)S(1)}, u32[]{:S(2)}, u32[]{:S(2)}) collective-permute-start(bf16[72,128]{1,0:T(8,128)(2,1)} %get-tuple-element.50), channel_id=1, source_target_pairs={{0,16},{4,20},{8,24},{12,28},{16,0},{20,4},{24,8},{28,12},{1,17},{... | collective-permute-start | bytes 55304 | tf_op jit(solution)/shard_map/ppermute | solution.py:423
  18.8 5.2 %collective-permute-start.4 = (bf16[72,128]{1,0:T(8,128)(2,1)}, bf16[72,128]{1,0:T(8,128)(2,1)S(1)}, u32[]{:S(2)}, u32[]{:S(2)}) collective-permute-start(bf16[72,128]{1,0:T(8,128)(2,1)} %get-tuple-element.51), channel_id=1, source_target_pairs={{0,24},{4,28},{8,16},{12,20},{16,8},{20,12},{24,0},{28,4},{1,25},{... | collective-permute-start | bytes 55304 | tf_op jit(solution)/shard_map/ppermute | solution.py:423
  19.7 20.2 %copy-start = (bf16[128,768]{1,0:T(8,128)(2,1)S(1)}, bf16[128,768]{1,0:T(8,128)(2,1)}, u32[]{:S(2)}) copy-start(bf16[128,768]{1,0:T(8,128)(2,1)} %get-tuple-element.66.refs_8_) | copy-start | bytes 589828
  19.7 11.3 %collective-permute-start.16 = (bf16[128,768]{1,0:T(8,128)(2,1)}, bf16[128,768]{1,0:T(8,128)(2,1)S(1)}, u32[]{:S(2)}, u32[]{:S(2)}) collective-permute-start(bf16[128,768]{1,0:T(8,128)(2,1)} %get-tuple-element.66.refs_8_), channel_id=1, source_target_pairs={{0,24},{4,28},{8,16},{12,20},{16,8},{20,12},{24,0},{28,4},{1,25},{... | collective-permute-start | bytes 589832 | tf_op jit(solution)/shard_map/ppermute | solution.py:423
  21.7 11.5 %collective-permute-start.15 = (bf16[128,768]{1,0:T(8,128)(2,1)}, bf16[128,768]{1,0:T(8,128)(2,1)S(1)}, u32[]{:S(2)}, u32[]{:S(2)}) collective-permute-start(bf16[128,768]{1,0:T(8,128)(2,1)} %get-tuple-element.66.refs_8_), channel_id=1, source_target_pairs={{0,16},{4,20},{8,24},{12,28},{16,0},{20,4},{24,8},{28,12},{1,17},{... | collective-permute-start | bytes 589832 | tf_op jit(solution)/shard_map/ppermute | solution.py:423
  22.1 11.9 %collective-permute-start.14 = (bf16[128,768]{1,0:T(8,128)(2,1)}, bf16[128,768]{1,0:T(8,128)(2,1)S(1)}, u32[]{:S(2)}, u32[]{:S(2)}) collective-permute-start(bf16[128,768]{1,0:T(8,128)(2,1)} %get-tuple-element.66.refs_8_), channel_id=1, source_target_pairs={{0,8},{4,12},{8,0},{12,4},{16,24},{20,28},{24,16},{28,20},{1,9},{5... | collective-permute-start | bytes 589832 | tf_op jit(solution)/shard_map/ppermute | solution.py:423
  24.0 0.7 %copy-start.8 = (bf16[72,128]{1,0:T(8,128)(2,1)S(1)}, bf16[72,128]{1,0:T(8,128)(2,1)}, u32[]{:S(2)}) copy-start(bf16[72,128]{1,0:T(8,128)(2,1)} %get-tuple-element.52.refs_0_) | copy-start | bytes 55300
  29.5 11.0 %copy-start.3 = (bf16[1024,128]{1,0:T(8,128)(2,1)S(1)}, bf16[1024,128]{1,0:T(8,128)(2,1)}, u32[]{:S(2)}) copy-start(bf16[1024,128]{1,0:T(8,128)(2,1)} %refs_6_) | copy-start | bytes 786436
  29.5 18.6 %copy-start.5 = (s32[8]{0:T(128)S(1)}, s32[8]{0:T(128)}, u32[]{:S(2)}) copy-start(s32[8]{0:T(128)} %slots_ref.1) | copy-start | bytes 100
  29.5 18.5 %copy-start.6 = (s32[8]{0:T(128)S(1)}, s32[8]{0:T(128)}, u32[]{:S(2)}) copy-start(s32[8]{0:T(128)} %starts_ref.1) | copy-start | bytes 100
  29.5 18.5 %copy-start.7 = (s32[8]{0:T(128)S(1)}, s32[8]{0:T(128)}, u32[]{:S(2)}) copy-start(s32[8]{0:T(128)} %lengths_ref.1) | copy-start | bytes 100
  29.6 4.7 %collective-permute-start.7 = (bf16[32,1024]{1,0:T(8,128)(2,1)S(1)}, bf16[32,1024]{1,0:T(8,128)(2,1)S(1)}, u32[]{:S(2)}, u32[]{:S(2)}) collective-permute-start(bf16[32,1024]{1,0:T(8,128)(2,1)S(1)} %get-tuple-element.58), channel_id=1, source_target_pairs={{0,28},{4,24},{8,20},{12,16},{16,12},{20,8},{24,4},{28,0},{1,29},{... | collective-permute-start | bytes 196616 | tf_op jit(solution)/shard_map/ppermute | solution.py:430
  29.6 6.2 %collective-permute-start.8 = (bf16[32,1024]{1,0:T(8,128)(2,1)S(1)}, bf16[32,1024]{1,0:T(8,128)(2,1)S(1)}, u32[]{:S(2)}, u32[]{:S(2)}) collective-permute-start(bf16[32,1024]{1,0:T(8,128)(2,1)S(1)} %get-tuple-element.59), channel_id=1, source_target_pairs={{0,24},{4,28},{8,16},{12,20},{16,8},{20,12},{24,0},{28,4},{1,25},{... | collective-permute-start | bytes 196616 | tf_op jit(solution)/shard_map/ppermute | solution.py:430
  30.9 6.0 %collective-permute-start.9 = (bf16[32,1024]{1,0:T(8,128)(2,1)S(1)}, bf16[32,1024]{1,0:T(8,128)(2,1)S(1)}, u32[]{:S(2)}, u32[]{:S(2)}) collective-permute-start(bf16[32,1024]{1,0:T(8,128)(2,1)S(1)} %get-tuple-element.60), channel_id=1, source_target_pairs={{0,20},{4,16},{8,28},{12,24},{16,4},{20,0},{24,12},{28,8},{1,21},{... | collective-permute-start | bytes 196616 | tf_op jit(solution)/shard_map/ppermute | solution.py:430
  33.2 5.2 %collective-permute-start.10 = (bf16[32,1024]{1,0:T(8,128)(2,1)S(1)}, bf16[32,1024]{1,0:T(8,128)(2,1)S(1)}, u32[]{:S(2)}, u32[]{:S(2)}) collective-permute-start(bf16[32,1024]{1,0:T(8,128)(2,1)S(1)} %get-tuple-element.61), channel_id=1, source_target_pairs={{0,16},{4,20},{8,24},{12,28},{16,0},{20,4},{24,8},{28,12},{1,17},{... | collective-permute-start | bytes 196616 | tf_op jit(solution)/shard_map/ppermute | solution.py:430
  34.0 4.4 %collective-permute-start.11 = (bf16[32,1024]{1,0:T(8,128)(2,1)S(1)}, bf16[32,1024]{1,0:T(8,128)(2,1)S(1)}, u32[]{:S(2)}, u32[]{:S(2)}) collective-permute-start(bf16[32,1024]{1,0:T(8,128)(2,1)S(1)} %get-tuple-element.62), channel_id=1, source_target_pairs={{0,12},{4,8},{8,4},{12,0},{16,28},{20,24},{24,20},{28,16},{1,13},{... | collective-permute-start | bytes 196616 | tf_op jit(solution)/shard_map/ppermute | solution.py:430
  34.3 5.5 %collective-permute-start.12 = (bf16[32,1024]{1,0:T(8,128)(2,1)S(1)}, bf16[32,1024]{1,0:T(8,128)(2,1)S(1)}, u32[]{:S(2)}, u32[]{:S(2)}) collective-permute-start(bf16[32,1024]{1,0:T(8,128)(2,1)S(1)} %get-tuple-element.63), channel_id=1, source_target_pairs={{0,8},{4,12},{8,0},{12,4},{16,24},{20,28},{24,16},{28,20},{1,9},{5... | collective-permute-start | bytes 196616 | tf_op jit(solution)/shard_map/ppermute | solution.py:430
  35.8 4.0 %collective-permute-start.13 = (bf16[32,1024]{1,0:T(8,128)(2,1)S(1)}, bf16[32,1024]{1,0:T(8,128)(2,1)S(1)}, u32[]{:S(2)}, u32[]{:S(2)}) collective-permute-start(bf16[32,1024]{1,0:T(8,128)(2,1)S(1)} %get-tuple-element.64), channel_id=1, source_target_pairs={{0,4},{4,0},{8,12},{12,8},{16,20},{20,16},{24,28},{28,24},{1,5},{5... | collective-permute-start | bytes 196616 | tf_op jit(solution)/shard_map/ppermute | solution.py:430
  40.3 13.2 %collective-permute-start.20 = (bf16[4,128,768]{2,1,0:T(8,128)(2,1)S(1)}, bf16[4,128,768]{2,1,0:T(8,128)(2,1)S(1)}, u32[]{:S(2)}, u32[]{:S(2)}) collective-permute-start(bf16[4,128,768]{2,1,0:T(8,128)(2,1)S(1)} %get-tuple-element.73.refs_4_), channel_id=1, source_target_pairs={{0,4},{4,0},{8,12},{12,8},{16,20},{20,16},{24,28},{28,24},{1,5},{5... | collective-permute-start | bytes 2359304 | tf_op jit(solution)/shard_map/ppermute | solution.py:427
  40.5 7.6 %collective-permute-start.18 = (bf16[64,1024]{1,0:T(8,128)(2,1)S(1)}, bf16[64,1024]{1,0:T(8,128)(2,1)S(1)}, u32[]{:S(2)}, u32[]{:S(2)}) collective-permute-start(bf16[64,1024]{1,0:T(8,128)(2,1)S(1)} %get-tuple-element.72.refs_0_), channel_id=1, source_target_pairs={{0,2},{1,3},{2,0},{3,1},{4,6},{5,7},{6,4},{7,5},{8,10},{9,11},{10,... | collective-permute-start | bytes 393224 | tf_op jit(solution)/shard_map/ppermute | solution.py:433
  40.5 13.0 %collective-permute-start.21 = (bf16[1024,128]{1,0:T(8,128)(2,1)S(1)}, bf16[1024,128]{1,0:T(8,128)(2,1)S(1)}, u32[]{:S(2)}, u32[]{:S(2)}) collective-permute-start(bf16[1024,128]{1,0:T(8,128)(2,1)S(1)} %copy-done.3), channel_id=1, source_target_pairs={{0,24},{4,28},{8,16},{12,20},{16,8},{20,12},{24,0},{28,4},{1,25},{... | collective-permute-start | bytes 786440 | tf_op jit(solution)/shard_map/ppermute | solution.py:423
  41.8 8.3 %collective-permute-start.17 = (bf16[64,1024]{1,0:T(8,128)(2,1)S(1)}, bf16[64,1024]{1,0:T(8,128)(2,1)S(1)}, u32[]{:S(2)}, u32[]{:S(2)}) collective-permute-start(bf16[64,1024]{1,0:T(8,128)(2,1)S(1)} %get-tuple-element.72.refs_0_), channel_id=1, source_target_pairs={{0,1},{1,0},{2,3},{3,2},{4,5},{5,4},{6,7},{7,6},{8,9},{9,8},{10,11... | collective-permute-start | bytes 393224 | tf_op jit(solution)/shard_map/ppermute | solution.py:433
  48.1 5.4 %collective-permute-start.19 = (bf16[64,1024]{1,0:T(8,128)(2,1)S(1)}, bf16[64,1024]{1,0:T(8,128)(2,1)S(1)}, u32[]{:S(2)}, u32[]{:S(2)}) collective-permute-start(bf16[64,1024]{1,0:T(8,128)(2,1)S(1)} %collective-permute-done.18.refs_2_), channel_id=1, source_target_pairs={{0,1},{1,0},{2,3},{3,2},{4,5},{5,4},{6,7},{7,6},{8,9},{9,8},{10,11... | collective-permute-start | bytes 393224 | tf_op jit(solution)/shard_map/ppermute | solution.py:433
  54.8 8.5 %collective-permute-start.25 = (bf16[4,1024,128]{2,1,0:T(8,128)(2,1)S(1)}, bf16[4,1024,128]{2,1,0:T(8,128)(2,1)S(1)}, u32[]{:S(2)}, u32[]{:S(2)}) collective-permute-start(bf16[4,1024,128]{2,1,0:T(8,128)(2,1)S(1)} %get-tuple-element.81.refs_4_), channel_id=1, source_target_pairs={{0,4},{4,0},{8,12},{12,8},{16,20},{20,16},{24,28},{28,24},{1,5},{5... | collective-permute-start | bytes 3145736 | tf_op jit(solution)/shard_map/ppermute | solution.py:427
  54.9 4.5 %collective-permute-start.22 = (bf16[64,256]{1,0:T(8,128)(2,1)S(1)}, bf16[64,256]{1,0:T(8,128)(2,1)S(1)}, u32[]{:S(2)}, u32[]{:S(2)}) collective-permute-start(bf16[64,256]{1,0:T(8,128)(2,1)S(1)} %get-tuple-element.78), channel_id=1, source_target_pairs={{0,1},{1,0},{2,3},{3,2},{4,5},{5,4},{6,7},{7,6},{8,9},{9,8},{10,11... | collective-permute-start | bytes 98312 | tf_op jit(solution)/shard_map/ppermute | solution.py:433
  55.3 5.4 %collective-permute-start.23 = (bf16[64,256]{1,0:T(8,128)(2,1)S(1)}, bf16[64,256]{1,0:T(8,128)(2,1)S(1)}, u32[]{:S(2)}, u32[]{:S(2)}) collective-permute-start(bf16[64,256]{1,0:T(8,128)(2,1)S(1)} %get-tuple-element.79), channel_id=1, source_target_pairs={{0,2},{1,3},{2,0},{3,1},{4,6},{5,7},{6,4},{7,5},{8,10},{9,11},{10,... | collective-permute-start | bytes 98312 | tf_op jit(solution)/shard_map/ppermute | solution.py:433
  57.7 5.7 %collective-permute-start.24 = (bf16[64,256]{1,0:T(8,128)(2,1)S(1)}, bf16[64,256]{1,0:T(8,128)(2,1)S(1)}, u32[]{:S(2)}, u32[]{:S(2)}) collective-permute-start(bf16[64,256]{1,0:T(8,128)(2,1)S(1)} %get-tuple-element.80), channel_id=1, source_target_pairs={{0,3},{1,2},{2,1},{3,0},{4,7},{5,6},{6,5},{7,4},{8,11},{9,10},{10,... | collective-permute-start | bytes 98312 | tf_op jit(solution)/shard_map/ppermute | solution.py:433

commit v14 on v12

--- a/solution.py
+++ b/solution.py
@@ -215,6 +215,7 @@
         return jnp.concatenate([frames[streams:], jnp.zeros((streams, LANES), F32)], axis=0)
 
     taps = [by_phase[1], by_phase[2], by_phase[3], next_four(by_phase[0]), next_four(by_phase[1])]
+    by_part = []
     for part in range(parts):
         first = 4 * share * part - 4
         block = jnp.zeros((rows, LANES), F32)
@@ -223,7 +224,10 @@
             here = (lane >= width * delta) & (lane < width * (delta + 1)) & (band >= 0) & (band < MELS)
             shift = (width * delta - first) % LANES
             block = jnp.where(here, pltpu.roll(frames, shift, 1) if shift else frames, block)
-        blocks[part] = jnp.dot(routing, block.astype(BF16), preferred_element_type=F32).astype(BF16)
+        by_part.append(block.astype(BF16))
+    routed = jnp.dot(routing, jnp.concatenate(by_part, axis=1), preferred_element_type=F32).astype(BF16)
+    for part in range(parts):
+        blocks[part] = routed[:, part * LANES : (part + 1) * LANES]
     mine, _ = place(parts)
     for step in range(parts):
         outs_refs[step][...] = blocks[mine ^ step]
@@ -256,14 +260,15 @@
         [mel[p, j * streams : (j + 1) * streams, :] for j in range(JS) for p in range(parts)], axis=0
     )
     odds = pltpu.roll(evens[: W * n], LANES - 2 * width, 1).astype(BF16)
-    evens = evens.astype(BF16)
+    both = jnp.concatenate([evens.astype(BF16), odds], axis=0)
     channels = conv2_ref.shape[1]
     outs = banded_ref.shape[1] // channels
     for g in range(outs):
         lanes = slice(g * channels, (g + 1) * channels)
         weight = banded_ref[:, lanes]
-        even[:, lanes] = jax.nn.relu(jnp.dot(evens, weight, preferred_element_type=F32)).astype(BF16)
-        odd[:, lanes] = jax.nn.relu(jnp.dot(odds, weight, preferred_element_type=F32)).astype(BF16)
+        first = jax.nn.relu(jnp.dot(both, weight, preferred_element_type=F32)).astype(BF16)
+        even[:, lanes] = first[: JS * n]
+        odd[:, lanes] = first[JS * n :]
 
     for h in range((outs - 1) // 2):
         lanes = slice(2 * h * channels, (2 * h + 3) * channels)

time: 64.7 us -> 64.6 us (level)
  no operation moved by 1% of the time
where the time goes in v14:
time: 64.6 us; the launch traced here: 64.3 us
  starting transfers between devices  30.4 us (47%)
  waiting for transfers between devices  18.3 us (28%)
  Pallas kernels  12.6 us (20%)
  local copies, waits for them, and re-layouts  2.13 us (3%)
  between operations  0.78 us (1%)
    ppermute x9, starting transfers between devices, to_part(): return lax.ppermute(block, 'dp', pairs)  13.5 us
    ppermute x6, waiting for transfers between devices, to_plane(): return lax.ppermute(block, 'seq', [(i, i ^ step) for i in range(group)])  13.3 us
    ppermute x7, starting transfers between devices, to_window(): return lax.ppermute(block, 'dp', [(i, i ^ step) for i in range(windows)])  6.04 us
    ppermute x6, starting transfers between devices, to_plane(): return lax.ppermute(block, 'seq', [(i, i ^ step) for i in range(group)])  5.52 us
    pallas_call x1, Pallas kernels, on_device(): pl.pallas_call(functools.partial(conv_kernel, parts, width), out_shape=tu...  4.77 us
    ppermute x1, starting transfers between devices, on_device(): rim = lax.ppermute(audio[:, audio.shape[1] - RIM:], ('dp', 'seq'), route)  4.63 us
    ppermute x7, waiting for transfers between devices, to_window(): return lax.ppermute(block, 'dp', [(i, i ^ step) for i in range(windows)])  4.21 us
    pallas_call x1, Pallas kernels, on_device(): pl.pallas_call(functools.partial(mel_kernel, parts, group), out_shape=tup...  3.64 us
  transfers between devices with their start and end apart: 26, of which 10 were waited for; matrix products, arithmetic and copies ran while one was open for 1% of the time, Pallas kernels for 15%

profile of v14, /device:TPU:0, one launch (start us, length us, event | category | flops | bytes accessed | tf_op | source)
XLA Modules:
  0.0 64.3 jit_solution(8521513385667533067)
XLA Ops:
  0.6 0.5 collective-permute-start.1
  1.1 0.8 %slice.3 = f32[8,1024]{1,0:T(8,128)S(1)} slice(f32[8,5120]{1,0:T(8,128)} %audio_ref.1), slice={[0:8], [4096:5120]} | slice | bytes 65536 | tf_op jit(solution)/shard_map/slice | solution.py:423
  1.9 4.6 %collective-permute-start = (f32[8,1024]{1,0:T(8,128)S(1)}, f32[8,1024]{1,0:T(8,128)S(1)}, u32[]{:S(2)}, u32[]{:S(2)}) collective-permute-start(f32[8,1024]{1,0:T(8,128)S(1)} %slice.3), channel_id=1, source_target_pairs={{0,1},{1,2},{2,3},{3,4},{4,5},{5,6},{6,7},{7,8},{8,9},{9,10},{10,1... | collective-permute-start | bytes 98312 | tf_op jit(solution)/shard_map/ppermute | solution.py:423
  6.6 1.6 %collective-permute-start.5 = (bf16[1024,128]{1,0:T(8,128)(2,1)}, bf16[1024,128]{1,0:T(8,128)(2,1)S(1)}, u32[]{:S(2)}, u32[]{:S(2)}) collective-permute-start(bf16[1024,128]{1,0:T(8,128)(2,1)} %refs_6_), channel_id=1, source_target_pairs={{0,8},{4,12},{8,0},{12,4},{16,24},{20,28},{24,16},{28,20},{1,9},{5... | collective-permute-start | bytes 786440 | tf_op jit(solution)/shard_map/ppermute | solution.py:427
  8.1 1.5 %collective-permute-start.6 = (bf16[1024,128]{1,0:T(8,128)(2,1)}, bf16[1024,128]{1,0:T(8,128)(2,1)}, u32[]{:S(2)}, u32[]{:S(2)}) collective-permute-start(bf16[1024,128]{1,0:T(8,128)(2,1)} %refs_6_), channel_id=1, source_target_pairs={{0,16},{4,20},{8,24},{12,28},{16,0},{20,4},{24,8},{28,12},{1,17},{... | collective-permute-start | bytes 786440 | tf_op jit(solution)/shard_map/ppermute | solution.py:427
  9.6 0.0 collective-permute-done.rim_ref
  9.6 0.6 copy-done.9
  10.2 3.6 %log_mel.1 = (bf16[72,128]{1,0:T(8,128)(2,1)}, bf16[72,128]{1,0:T(8,128)(2,1)}, bf16[72,128]{1,0:T(8,128)(2,1)}, bf16[72,128]{1,0:T(8,128)(2,1)}, bf16[128,768]{1,0:T(8,128)(2,1)}) custom-call(s32[8]{0:T(128)} %slots_ref.1, f32[8,1024]{1,0:T(8,128)} %copy-done.9, f32[8,5120]{1,0:T(8,128)} %audio_ref.1, f32[264,640]{1,0:T(8,128)} %constant.2.clone.table_ref, ...), custom_call_target="tpu_custom_call" | custom-call | flops 10000000000 | bytes 2000000 | tf_op jit(solution)/shard_map/log_mel/pallas_call | solution.py:443
  13.9 3.0 %collective-permute-start.2 = (bf16[72,128]{1,0:T(8,128)(2,1)}, bf16[72,128]{1,0:T(8,128)(2,1)S(1)}, u32[]{:S(2)}, u32[]{:S(2)}) collective-permute-start(bf16[72,128]{1,0:T(8,128)(2,1)} %get-tuple-element.45), channel_id=1, source_target_pairs={{0,8},{4,12},{8,0},{12,4},{16,24},{20,28},{24,16},{28,20},{1,9},{5... | collective-permute-start | bytes 55304 | tf_op jit(solution)/shard_map/ppermute | solution.py:427
  16.9 1.6 %collective-permute-start.3 = (bf16[72,128]{1,0:T(8,128)(2,1)}, bf16[72,128]{1,0:T(8,128)(2,1)S(1)}, u32[]{:S(2)}, u32[]{:S(2)}) collective-permute-start(bf16[72,128]{1,0:T(8,128)(2,1)} %get-tuple-element.46), channel_id=1, source_target_pairs={{0,16},{4,20},{8,24},{12,28},{16,0},{20,4},{24,8},{28,12},{1,17},{... | collective-permute-start | bytes 55304 | tf_op jit(solution)/shard_map/ppermute | solution.py:427
  18.5 0.9 %collective-permute-start.4 = (bf16[72,128]{1,0:T(8,128)(2,1)}, bf16[72,128]{1,0:T(8,128)(2,1)S(1)}, u32[]{:S(2)}, u32[]{:S(2)}) collective-permute-start(bf16[72,128]{1,0:T(8,128)(2,1)} %get-tuple-element.47), channel_id=1, source_target_pairs={{0,24},{4,28},{8,16},{12,20},{16,8},{20,12},{24,0},{28,4},{1,25},{... | collective-permute-start | bytes 55304 | tf_op jit(solution)/shard_map/ppermute | solution.py:427
  19.4 2.0 %collective-permute-start.16 = (bf16[128,768]{1,0:T(8,128)(2,1)}, bf16[128,768]{1,0:T(8,128)(2,1)S(1)}, u32[]{:S(2)}, u32[]{:S(2)}) collective-permute-start(bf16[128,768]{1,0:T(8,128)(2,1)} %get-tuple-element.62.refs_8_), channel_id=1, source_target_pairs={{0,24},{4,28},{8,16},{12,20},{16,8},{20,12},{24,0},{28,4},{1,25},{... | collective-permute-start | bytes 589832 | tf_op jit(solution)/shard_map/ppermute | solution.py:427
  21.5 0.4 collective-permute-start.15
  21.9 1.1 %collective-permute-start.14 = (bf16[128,768]{1,0:T(8,128)(2,1)}, bf16[128,768]{1,0:T(8,128)(2,1)S(1)}, u32[]{:S(2)}, u32[]{:S(2)}) collective-permute-start(bf16[128,768]{1,0:T(8,128)(2,1)} %get-tuple-element.62.refs_8_), channel_id=1, source_target_pairs={{0,8},{4,12},{8,0},{12,4},{16,24},{20,28},{24,16},{28,20},{1,9},{5... | collective-permute-start | bytes 589832 | tf_op jit(solution)/shard_map/ppermute | solution.py:427
  23.0 0.7 %collective-permute-done.4.refs_3_ = bf16[72,128]{1,0:T(8,128)(2,1)S(1)} collective-permute-done((bf16[72,128]{1,0:T(8,128)(2,1)}, bf16[72,128]{1,0:T(8,128)(2,1)S(1)}, u32[]{:S(2)}, u32[]{:S(2)}) %collective-permute-start.4) | collective-permute-done | bytes 18464 | tf_op jit(solution)/shard_map/ppermute | solution.py:427
  23.8 0.0 copy-start.8
  23.8 0.7 %copy-done.8 = bf16[72,128]{1,0:T(8,128)(2,1)S(1)} copy-done((bf16[72,128]{1,0:T(8,128)(2,1)S(1)}, bf16[72,128]{1,0:T(8,128)(2,1)}, u32[]{:S(2)}) %copy-start.8) | copy-done | bytes 18456
  24.5 4.8 %conv.1 = (bf16[32,1024]{1,0:T(8,128)(2,1)S(1)}, bf16[32,1024]{1,0:T(8,128)(2,1)S(1)}, bf16[32,1024]{1,0:T(8,128)(2,1)S(1)}, bf16[32,1024]{1,0:T(8,128)(2,1)S(1)...) custom-call(bf16[9,256]{1,0:T(8,128)(2,1)S(1)} %copy-done.4, ...), custom_call_target="tpu_custom_call" | custom-call | flops 2000000000 | bytes 4000000 | tf_op jit(solution)/shard_map/conv/pallas_call | solution.py:466
  29.3 0.0 copy-start.3
  29.3 0.0 copy-start.5
  29.3 0.0 copy-start.6
  29.3 0.0 copy-start.7
  29.3 0.1 collective-permute-start.7
  29.4 1.3 %collective-permute-start.8 = (bf16[32,1024]{1,0:T(8,128)(2,1)S(1)}, bf16[32,1024]{1,0:T(8,128)(2,1)S(1)}, u32[]{:S(2)}, u32[]{:S(2)}) collective-permute-start(bf16[32,1024]{1,0:T(8,128)(2,1)S(1)} %get-tuple-element.55), channel_id=1, source_target_pairs={{0,24},{4,28},{8,16},{12,20},{16,8},{20,12},{24,0},{28,4},{1,25},{... | collective-permute-start | bytes 196616 | tf_op jit(solution)/shard_map/ppermute | solution.py:434
  30.7 2.3 %collective-permute-start.9 = (bf16[32,1024]{1,0:T(8,128)(2,1)S(1)}, bf16[32,1024]{1,0:T(8,128)(2,1)S(1)}, u32[]{:S(2)}, u32[]{:S(2)}) collective-permute-start(bf16[32,1024]{1,0:T(8,128)(2,1)S(1)} %get-tuple-element.56), channel_id=1, source_target_pairs={{0,20},{4,16},{8,28},{12,24},{16,4},{20,0},{24,12},{28,8},{1,21},{... | collective-permute-start | bytes 196616 | tf_op jit(solution)/shard_map/ppermute | solution.py:434
  33.0 0.8 %collective-permute-start.10 = (bf16[32,1024]{1,0:T(8,128)(2,1)S(1)}, bf16[32,1024]{1,0:T(8,128)(2,1)S(1)}, u32[]{:S(2)}, u32[]{:S(2)}) collective-permute-start(bf16[32,1024]{1,0:T(8,128)(2,1)S(1)} %get-tuple-element.57), channel_id=1, source_target_pairs={{0,16},{4,20},{8,24},{12,28},{16,0},{20,4},{24,8},{28,12},{1,17},{... | collective-permute-start | bytes 196616 | tf_op jit(solution)/shard_map/ppermute | solution.py:434
  33.8 0.3 collective-permute-done.7.refs_0_
  34.1 1.5 %collective-permute-start.12 = (bf16[32,1024]{1,0:T(8,128)(2,1)S(1)}, bf16[32,1024]{1,0:T(8,128)(2,1)S(1)}, u32[]{:S(2)}, u32[]{:S(2)}) collective-permute-start(bf16[32,1024]{1,0:T(8,128)(2,1)S(1)} %get-tuple-element.59), channel_id=1, source_target_pairs={{0,8},{4,12},{8,0},{12,4},{16,24},{20,28},{24,16},{28,20},{1,9},{5... | collective-permute-start | bytes 196616 | tf_op jit(solution)/shard_map/ppermute | solution.py:434
  35.6 0.1 collective-permute-start.13
  35.7 1.0 %collective-permute-done.9.refs_2_ = bf16[32,1024]{1,0:T(8,128)(2,1)S(1)} collective-permute-done((bf16[32,1024]{1,0:T(8,128)(2,1)S(1)}, bf16[32,1024]{1,0:T(8,128)(2,1)S(1)}, u32[]{:S(2)}, u32[]{:S(2)}) %collective-permute-start.9) | collective-permute-done | bytes 65568 | tf_op jit(solution)/shard_map/ppermute | solution.py:434
  36.7 1.5 %collective-permute-done.10.refs_3_ = bf16[32,1024]{1,0:T(8,128)(2,1)S(1)} collective-permute-done((bf16[32,1024]{1,0:T(8,128)(2,1)S(1)}, bf16[32,1024]{1,0:T(8,128)(2,1)S(1)}, u32[]{:S(2)}, u32[]{:S(2)}) %collective-permute-start.10) | collective-permute-done | bytes 65568 | tf_op jit(solution)/shard_map/ppermute | solution.py:434
  38.2 1.4 %collective-permute-done.12.refs_5_ = bf16[32,1024]{1,0:T(8,128)(2,1)S(1)} collective-permute-done((bf16[32,1024]{1,0:T(8,128)(2,1)S(1)}, bf16[32,1024]{1,0:T(8,128)(2,1)S(1)}, u32[]{:S(2)}, u32[]{:S(2)}) %collective-permute-start.12) | collective-permute-done | bytes 65568 | tf_op jit(solution)/shard_map/ppermute | solution.py:434
  39.6 0.5 layer_norm.1
  40.1 0.2 collective-permute-start.20
  40.3 1.3 %collective-permute-start.21 = (bf16[1024,128]{1,0:T(8,128)(2,1)S(1)}, bf16[1024,128]{1,0:T(8,128)(2,1)S(1)}, u32[]{:S(2)}, u32[]{:S(2)}) collective-permute-start(bf16[1024,128]{1,0:T(8,128)(2,1)S(1)} %copy-done.3), channel_id=1, source_target_pairs={{0,24},{4,28},{8,16},{12,20},{16,8},{20,12},{24,0},{28,4},{1,25},{... | collective-permute-start | bytes 786440 | tf_op jit(solution)/shard_map/ppermute | solution.py:427
  41.6 1.1 %collective-permute-start.17 = (bf16[64,1024]{1,0:T(8,128)(2,1)S(1)}, bf16[64,1024]{1,0:T(8,128)(2,1)S(1)}, u32[]{:S(2)}, u32[]{:S(2)}) collective-permute-start(bf16[64,1024]{1,0:T(8,128)(2,1)S(1)} %get-tuple-element.68.refs_0_), channel_id=1, source_target_pairs={{0,1},{1,0},{2,3},{3,2},{4,5},{5,4},{6,7},{7,6},{8,9},{9,8},{10,11... | collective-permute-start | bytes 393224 | tf_op jit(solution)/shard_map/ppermute | solution.py:437
  42.6 5.2 %collective-permute-done.18.refs_2_ = bf16[64,1024]{1,0:T(8,128)(2,1)S(1)} collective-permute-done((bf16[64,1024]{1,0:T(8,128)(2,1)S(1)}, bf16[64,1024]{1,0:T(8,128)(2,1)S(1)}, u32[]{:S(2)}, u32[]{:S(2)}) %collective-permute-start.18) | collective-permute-done | bytes 131104 | tf_op jit(solution)/shard_map/ppermute | solution.py:437
  47.8 1.3 %mask.1 = (bf16[64,1024]{1,0:T(8,128)(2,1)}, f32[4,64]{1,0:T(4,128)S(1)}, f32[64,1]{1,0:T(8,128)S(1)}) custom-call(s32[8]{0:T(128)S(1)} %copy-done.5, s32[8]{0:T(128)S(1)} %copy-done.6, s32[8]{0:T(128)S(1)} %copy-done.7, bf16[64,1024]{1,0:T(8,128)(2,1)S(1)} %get-tuple-element.63.rows_ref), custom_call_target="tpu_custom_call" | custom-call | flops 100000000 | bytes 1000000 | tf_op jit(solution)/shard_map/mask/pallas_call | solution.py:497
  49.1 0.7 %collective-permute-done.17.refs_1_ = bf16[64,1024]{1,0:T(8,128)(2,1)S(1)} collective-permute-done((bf16[64,1024]{1,0:T(8,128)(2,1)S(1)}, bf16[64,1024]{1,0:T(8,128)(2,1)S(1)}, u32[]{:S(2)}, u32[]{:S(2)}) %collective-permute-start.17) | collective-permute-done | bytes 131104 | tf_op jit(solution)/shard_map/ppermute | solution.py:437
  49.8 3.4 %collective-permute-done.19.refs_3_ = bf16[64,1024]{1,0:T(8,128)(2,1)S(1)} collective-permute-done((bf16[64,1024]{1,0:T(8,128)(2,1)S(1)}, bf16[64,1024]{1,0:T(8,128)(2,1)S(1)}, u32[]{:S(2)}, u32[]{:S(2)}) %collective-permute-start.19) | collective-permute-done | bytes 131104 | tf_op jit(solution)/shard_map/ppermute | solution.py:437
  53.2 1.4 %attention.1 = (bf16[64,256]{1,0:T(8,128)(2,1)S(1)}, bf16[64,256]{1,0:T(8,128)(2,1)S(1)}, bf16[64,256]{1,0:T(8,128)(2,1)S(1)}, bf16[64,256]{1,0:T(8,128)(2,1)S(1)}, bf16[4,1024,128]{2,1,0:T(8,128)(2,1)S(1)}) custom-call(f32[4,64]{1,0:T(4,128)S(1)} %get-tuple-element.66.keys_ref, bf16[64,1024]{1,0:T(8,128)(2,1)S(1)} %get-tuple-element.68.refs_0_, ...), custom_call_target="tpu_custom_call" | custom-call | flops 1000000000 | bytes 2000000 | tf_op jit(solution)/shard_map/attention/pallas_call | solution.py:517
  54.6 0.1 collective-permute-start.25
  54.7 0.3 collective-permute-start.22
  55.0 2.4 %collective-permute-start.23 = (bf16[64,256]{1,0:T(8,128)(2,1)S(1)}, bf16[64,256]{1,0:T(8,128)(2,1)S(1)}, u32[]{:S(2)}, u32[]{:S(2)}) collective-permute-start(bf16[64,256]{1,0:T(8,128)(2,1)S(1)} %get-tuple-element.75), channel_id=1, source_target_pairs={{0,2},{1,3},{2,0},{3,1},{4,6},{5,7},{6,4},{7,5},{8,10},{9,11},{10,... | collective-permute-start | bytes 98312 | tf_op jit(solution)/shard_map/ppermute | solution.py:437
  57.4 1.7 %collective-permute-start.24 = (bf16[64,256]{1,0:T(8,128)(2,1)S(1)}, bf16[64,256]{1,0:T(8,128)(2,1)S(1)}, u32[]{:S(2)}, u32[]{:S(2)}) collective-permute-start(bf16[64,256]{1,0:T(8,128)(2,1)S(1)} %get-tuple-element.76), channel_id=1, source_target_pairs={{0,3},{1,2},{2,1},{3,0},{4,7},{5,6},{6,5},{7,4},{8,11},{9,10},{10,... | collective-permute-start | bytes 98312 | tf_op jit(solution)/shard_map/ppermute | solution.py:437
  59.1 1.3 %collective-permute-done.23.refs_2_ = bf16[64,256]{1,0:T(8,128)(2,1)S(1)} collective-permute-done((bf16[64,256]{1,0:T(8,128)(2,1)S(1)}, bf16[64,256]{1,0:T(8,128)(2,1)S(1)}, u32[]{:S(2)}, u32[]{:S(2)}) %collective-permute-start.23) | collective-permute-done | bytes 32800 | tf_op jit(solution)/shard_map/ppermute | solution.py:437
  60.4 2.8 %collective-permute-done.24.refs_3_ = bf16[64,256]{1,0:T(8,128)(2,1)S(1)} collective-permute-done((bf16[64,256]{1,0:T(8,128)(2,1)S(1)}, bf16[64,256]{1,0:T(8,128)(2,1)S(1)}, u32[]{:S(2)}, u32[]{:S(2)}) %collective-permute-start.24) | collective-permute-done | bytes 32800 | tf_op jit(solution)/shard_map/ppermute | solution.py:437
  63.2 1.1 %output.1 = bf16[64,1024]{1,0:T(8,128)(2,1)} custom-call(f32[64,1]{1,0:T(8,128)S(1)} %get-tuple-element.65.valid_ref, bf16[64,256]{1,0:T(8,128)(2,1)S(1)} %get-tuple-element.73.refs_0_, bf16[64,256]{1,0:T(8,128)(2,1)S(1)} %collective-permute-done.22.refs_1_, bf16[64,256]{1,0:T(8,128)(2,1)S(1)} %collective-permute-done.23.refs_2_, ...), custom_call_target="tpu_custom_call" | custom-call | flops 100000000 | bytes 3000000 | tf_op jit(solution)/shard_map/output/pallas_call | solution.py:536
  (31 shorter events, 0.1 us)
Async XLA Ops:
  0.6 13.3 %collective-permute-start.1 = (bf16[640,1024]{1,0:T(8,128)(2,1)}, bf16[640,1024]{1,0:T(8,128)(2,1)S(1)}, u32[]{:S(2)}, u32[]{:S(2)}) collective-permute-start(bf16[640,1024]{1,0:T(8,128)(2,1)} %refs_4_), channel_id=1, source_target_pairs={{0,4},{4,0},{8,12},{12,8},{16,20},{20,16},{24,28},{28,24},{1,5},{5... | collective-permute-start | bytes 3932168 | tf_op jit(solution)/shard_map/ppermute | solution.py:431
  1.9 21.9 %copy-start.1 = (bf16[640,1024]{1,0:T(8,128)(2,1)S(1)}, bf16[640,1024]{1,0:T(8,128)(2,1)}, u32[]{:S(2)}) copy-start(bf16[640,1024]{1,0:T(8,128)(2,1)} %refs_4_) | copy-start | bytes 3932164
  1.9 21.9 %copy-start.2 = (bf16[2304,256]{1,0:T(8,128)(2,1)S(1)}, bf16[2304,256]{1,0:T(8,128)(2,1)}, u32[]{:S(2)}) copy-start(bf16[2304,256]{1,0:T(8,128)(2,1)} %conv2_ref.1) | copy-start | bytes 3538948
  1.9 21.9 %copy-start.4 = (bf16[9,256]{1,0:T(8,128)(2,1)S(1)}, bf16[9,256]{1,0:T(8,128)(2,1)}, u32[]{:S(2)}) copy-start(bf16[9,256]{1,0:T(8,128)(2,1)} %conv1_ref.1) | copy-start | bytes 13828
  1.9 7.7 %collective-permute-start = (f32[8,1024]{1,0:T(8,128)S(1)}, f32[8,1024]{1,0:T(8,128)S(1)}, u32[]{:S(2)}, u32[]{:S(2)}) collective-permute-start(f32[8,1024]{1,0:T(8,128)S(1)} %slice.3), channel_id=1, source_target_pairs={{0,1},{1,2},{2,3},{3,4},{4,5},{5,6},{6,7},{7,8},{8,9},{9,10},{10,1... | collective-permute-start | bytes 98312 | tf_op jit(solution)/shard_map/ppermute | solution.py:423
  6.6 12.9 %collective-permute-start.5 = (bf16[1024,128]{1,0:T(8,128)(2,1)}, bf16[1024,128]{1,0:T(8,128)(2,1)S(1)}, u32[]{:S(2)}, u32[]{:S(2)}) collective-permute-start(bf16[1024,128]{1,0:T(8,128)(2,1)} %refs_6_), channel_id=1, source_target_pairs={{0,8},{4,12},{8,0},{12,4},{16,24},{20,28},{24,16},{28,20},{1,9},{5... | collective-permute-start | bytes 786440 | tf_op jit(solution)/shard_map/ppermute | solution.py:427
  8.1 13.4 %collective-permute-start.6 = (bf16[1024,128]{1,0:T(8,128)(2,1)}, bf16[1024,128]{1,0:T(8,128)(2,1)}, u32[]{:S(2)}, u32[]{:S(2)}) collective-permute-start(bf16[1024,128]{1,0:T(8,128)(2,1)} %refs_6_), channel_id=1, source_target_pairs={{0,16},{4,20},{8,24},{12,28},{16,0},{20,4},{24,8},{28,12},{1,17},{... | collective-permute-start | bytes 786440 | tf_op jit(solution)/shard_map/ppermute | solution.py:427
  9.6 0.6 copy-start.9
  13.9 8.0 %collective-permute-start.2 = (bf16[72,128]{1,0:T(8,128)(2,1)}, bf16[72,128]{1,0:T(8,128)(2,1)S(1)}, u32[]{:S(2)}, u32[]{:S(2)}) collective-permute-start(bf16[72,128]{1,0:T(8,128)(2,1)} %get-tuple-element.45), channel_id=1, source_target_pairs={{0,8},{4,12},{8,0},{12,4},{16,24},{20,28},{24,16},{28,20},{1,9},{5... | collective-permute-start | bytes 55304 | tf_op jit(solution)/shard_map/ppermute | solution.py:427
  16.9 6.1 %collective-permute-start.3 = (bf16[72,128]{1,0:T(8,128)(2,1)}, bf16[72,128]{1,0:T(8,128)(2,1)S(1)}, u32[]{:S(2)}, u32[]{:S(2)}) collective-permute-start(bf16[72,128]{1,0:T(8,128)(2,1)} %get-tuple-element.46), channel_id=1, source_target_pairs={{0,16},{4,20},{8,24},{12,28},{16,0},{20,4},{24,8},{28,12},{1,17},{... | collective-permute-start | bytes 55304 | tf_op jit(solution)/shard_map/ppermute | solution.py:427
  18.5 5.2 %collective-permute-start.4 = (bf16[72,128]{1,0:T(8,128)(2,1)}, bf16[72,128]{1,0:T(8,128)(2,1)S(1)}, u32[]{:S(2)}, u32[]{:S(2)}) collective-permute-start(bf16[72,128]{1,0:T(8,128)(2,1)} %get-tuple-element.47), channel_id=1, source_target_pairs={{0,24},{4,28},{8,16},{12,20},{16,8},{20,12},{24,0},{28,4},{1,25},{... | collective-permute-start | bytes 55304 | tf_op jit(solution)/shard_map/ppermute | solution.py:427
  19.4 20.2 %copy-start = (bf16[128,768]{1,0:T(8,128)(2,1)S(1)}, bf16[128,768]{1,0:T(8,128)(2,1)}, u32[]{:S(2)}) copy-start(bf16[128,768]{1,0:T(8,128)(2,1)} %get-tuple-element.62.refs_8_) | copy-start | bytes 589828
  19.4 11.3 %collective-permute-start.16 = (bf16[128,768]{1,0:T(8,128)(2,1)}, bf16[128,768]{1,0:T(8,128)(2,1)S(1)}, u32[]{:S(2)}, u32[]{:S(2)}) collective-permute-start(bf16[128,768]{1,0:T(8,128)(2,1)} %get-tuple-element.62.refs_8_), channel_id=1, source_target_pairs={{0,24},{4,28},{8,16},{12,20},{16,8},{20,12},{24,0},{28,4},{1,25},{... | collective-permute-start | bytes 589832 | tf_op jit(solution)/shard_map/ppermute | solution.py:427
  21.5 11.5 %collective-permute-start.15 = (bf16[128,768]{1,0:T(8,128)(2,1)}, bf16[128,768]{1,0:T(8,128)(2,1)S(1)}, u32[]{:S(2)}, u32[]{:S(2)}) collective-permute-start(bf16[128,768]{1,0:T(8,128)(2,1)} %get-tuple-element.62.refs_8_), channel_id=1, source_target_pairs={{0,16},{4,20},{8,24},{12,28},{16,0},{20,4},{24,8},{28,12},{1,17},{... | collective-permute-start | bytes 589832 | tf_op jit(solution)/shard_map/ppermute | solution.py:427
  21.9 11.9 %collective-permute-start.14 = (bf16[128,768]{1,0:T(8,128)(2,1)}, bf16[128,768]{1,0:T(8,128)(2,1)S(1)}, u32[]{:S(2)}, u32[]{:S(2)}) collective-permute-start(bf16[128,768]{1,0:T(8,128)(2,1)} %get-tuple-element.62.refs_8_), channel_id=1, source_target_pairs={{0,8},{4,12},{8,0},{12,4},{16,24},{20,28},{24,16},{28,20},{1,9},{5... | collective-permute-start | bytes 589832 | tf_op jit(solution)/shard_map/ppermute | solution.py:427
  23.8 0.7 %copy-start.8 = (bf16[72,128]{1,0:T(8,128)(2,1)S(1)}, bf16[72,128]{1,0:T(8,128)(2,1)}, u32[]{:S(2)}) copy-start(bf16[72,128]{1,0:T(8,128)(2,1)} %get-tuple-element.48.refs_0_) | copy-start | bytes 55300
  29.3 11.0 %copy-start.3 = (bf16[1024,128]{1,0:T(8,128)(2,1)S(1)}, bf16[1024,128]{1,0:T(8,128)(2,1)}, u32[]{:S(2)}) copy-start(bf16[1024,128]{1,0:T(8,128)(2,1)} %refs_6_) | copy-start | bytes 786436
  29.3 18.5 %copy-start.5 = (s32[8]{0:T(128)S(1)}, s32[8]{0:T(128)}, u32[]{:S(2)}) copy-start(s32[8]{0:T(128)} %slots_ref.1) | copy-start | bytes 100
  29.3 18.5 %copy-start.6 = (s32[8]{0:T(128)S(1)}, s32[8]{0:T(128)}, u32[]{:S(2)}) copy-start(s32[8]{0:T(128)} %starts_ref.1) | copy-start | bytes 100
  29.3 18.5 %copy-start.7 = (s32[8]{0:T(128)S(1)}, s32[8]{0:T(128)}, u32[]{:S(2)}) copy-start(s32[8]{0:T(128)} %lengths_ref.1) | copy-start | bytes 100
  29.3 4.7 %collective-permute-start.7 = (bf16[32,1024]{1,0:T(8,128)(2,1)S(1)}, bf16[32,1024]{1,0:T(8,128)(2,1)S(1)}, u32[]{:S(2)}, u32[]{:S(2)}) collective-permute-start(bf16[32,1024]{1,0:T(8,128)(2,1)S(1)} %get-tuple-element.54), channel_id=1, source_target_pairs={{0,28},{4,24},{8,20},{12,16},{16,12},{20,8},{24,4},{28,0},{1,29},{... | collective-permute-start | bytes 196616 | tf_op jit(solution)/shard_map/ppermute | solution.py:434
  29.4 6.2 %collective-permute-start.8 = (bf16[32,1024]{1,0:T(8,128)(2,1)S(1)}, bf16[32,1024]{1,0:T(8,128)(2,1)S(1)}, u32[]{:S(2)}, u32[]{:S(2)}) collective-permute-start(bf16[32,1024]{1,0:T(8,128)(2,1)S(1)} %get-tuple-element.55), channel_id=1, source_target_pairs={{0,24},{4,28},{8,16},{12,20},{16,8},{20,12},{24,0},{28,4},{1,25},{... | collective-permute-start | bytes 196616 | tf_op jit(solution)/shard_map/ppermute | solution.py:434
  30.7 6.0 %collective-permute-start.9 = (bf16[32,1024]{1,0:T(8,128)(2,1)S(1)}, bf16[32,1024]{1,0:T(8,128)(2,1)S(1)}, u32[]{:S(2)}, u32[]{:S(2)}) collective-permute-start(bf16[32,1024]{1,0:T(8,128)(2,1)S(1)} %get-tuple-element.56), channel_id=1, source_target_pairs={{0,20},{4,16},{8,28},{12,24},{16,4},{20,0},{24,12},{28,8},{1,21},{... | collective-permute-start | bytes 196616 | tf_op jit(solution)/shard_map/ppermute | solution.py:434
  33.0 5.2 %collective-permute-start.10 = (bf16[32,1024]{1,0:T(8,128)(2,1)S(1)}, bf16[32,1024]{1,0:T(8,128)(2,1)S(1)}, u32[]{:S(2)}, u32[]{:S(2)}) collective-permute-start(bf16[32,1024]{1,0:T(8,128)(2,1)S(1)} %get-tuple-element.57), channel_id=1, source_target_pairs={{0,16},{4,20},{8,24},{12,28},{16,0},{20,4},{24,8},{28,12},{1,17},{... | collective-permute-start | bytes 196616 | tf_op jit(solution)/shard_map/ppermute | solution.py:434
  33.8 4.4 %collective-permute-start.11 = (bf16[32,1024]{1,0:T(8,128)(2,1)S(1)}, bf16[32,1024]{1,0:T(8,128)(2,1)S(1)}, u32[]{:S(2)}, u32[]{:S(2)}) collective-permute-start(bf16[32,1024]{1,0:T(8,128)(2,1)S(1)} %get-tuple-element.58), channel_id=1, source_target_pairs={{0,12},{4,8},{8,4},{12,0},{16,28},{20,24},{24,20},{28,16},{1,13},{... | collective-permute-start | bytes 196616 | tf_op jit(solution)/shard_map/ppermute | solution.py:434
  34.1 5.5 %collective-permute-start.12 = (bf16[32,1024]{1,0:T(8,128)(2,1)S(1)}, bf16[32,1024]{1,0:T(8,128)(2,1)S(1)}, u32[]{:S(2)}, u32[]{:S(2)}) collective-permute-start(bf16[32,1024]{1,0:T(8,128)(2,1)S(1)} %get-tuple-element.59), channel_id=1, source_target_pairs={{0,8},{4,12},{8,0},{12,4},{16,24},{20,28},{24,16},{28,20},{1,9},{5... | collective-permute-start | bytes 196616 | tf_op jit(solution)/shard_map/ppermute | solution.py:434
  35.6 4.0 %collective-permute-start.13 = (bf16[32,1024]{1,0:T(8,128)(2,1)S(1)}, bf16[32,1024]{1,0:T(8,128)(2,1)S(1)}, u32[]{:S(2)}, u32[]{:S(2)}) collective-permute-start(bf16[32,1024]{1,0:T(8,128)(2,1)S(1)} %get-tuple-element.60), channel_id=1, source_target_pairs={{0,4},{4,0},{8,12},{12,8},{16,20},{20,16},{24,28},{28,24},{1,5},{5... | collective-permute-start | bytes 196616 | tf_op jit(solution)/shard_map/ppermute | solution.py:434
  40.1 13.1 %collective-permute-start.20 = (bf16[4,128,768]{2,1,0:T(8,128)(2,1)S(1)}, bf16[4,128,768]{2,1,0:T(8,128)(2,1)S(1)}, u32[]{:S(2)}, u32[]{:S(2)}) collective-permute-start(bf16[4,128,768]{2,1,0:T(8,128)(2,1)S(1)} %get-tuple-element.69.refs_4_), channel_id=1, source_target_pairs={{0,4},{4,0},{8,12},{12,8},{16,20},{20,16},{24,28},{28,24},{1,5},{5... | collective-permute-start | bytes 2359304 | tf_op jit(solution)/shard_map/ppermute | solution.py:431
  40.3 7.6 %collective-permute-start.18 = (bf16[64,1024]{1,0:T(8,128)(2,1)S(1)}, bf16[64,1024]{1,0:T(8,128)(2,1)S(1)}, u32[]{:S(2)}, u32[]{:S(2)}) collective-permute-start(bf16[64,1024]{1,0:T(8,128)(2,1)S(1)} %get-tuple-element.68.refs_0_), channel_id=1, source_target_pairs={{0,2},{1,3},{2,0},{3,1},{4,6},{5,7},{6,4},{7,5},{8,10},{9,11},{10,... | collective-permute-start | bytes 393224 | tf_op jit(solution)/shard_map/ppermute | solution.py:437
  40.3 13.0 %collective-permute-start.21 = (bf16[1024,128]{1,0:T(8,128)(2,1)S(1)}, bf16[1024,128]{1,0:T(8,128)(2,1)S(1)}, u32[]{:S(2)}, u32[]{:S(2)}) collective-permute-start(bf16[1024,128]{1,0:T(8,128)(2,1)S(1)} %copy-done.3), channel_id=1, source_target_pairs={{0,24},{4,28},{8,16},{12,20},{16,8},{20,12},{24,0},{28,4},{1,25},{... | collective-permute-start | bytes 786440 | tf_op jit(solution)/shard_map/ppermute | solution.py:427
  41.6 8.3 %collective-permute-start.17 = (bf16[64,1024]{1,0:T(8,128)(2,1)S(1)}, bf16[64,1024]{1,0:T(8,128)(2,1)S(1)}, u32[]{:S(2)}, u32[]{:S(2)}) collective-permute-start(bf16[64,1024]{1,0:T(8,128)(2,1)S(1)} %get-tuple-element.68.refs_0_), channel_id=1, source_target_pairs={{0,1},{1,0},{2,3},{3,2},{4,5},{5,4},{6,7},{7,6},{8,9},{9,8},{10,11... | collective-permute-start | bytes 393224 | tf_op jit(solution)/shard_map/ppermute | solution.py:437
  47.8 5.4 %collective-permute-start.19 = (bf16[64,1024]{1,0:T(8,128)(2,1)S(1)}, bf16[64,1024]{1,0:T(8,128)(2,1)S(1)}, u32[]{:S(2)}, u32[]{:S(2)}) collective-permute-start(bf16[64,1024]{1,0:T(8,128)(2,1)S(1)} %collective-permute-done.18.refs_2_), channel_id=1, source_target_pairs={{0,1},{1,0},{2,3},{3,2},{4,5},{5,4},{6,7},{7,6},{8,9},{9,8},{10,11... | collective-permute-start | bytes 393224 | tf_op jit(solution)/shard_map/ppermute | solution.py:437
  54.6 8.6 %collective-permute-start.25 = (bf16[4,1024,128]{2,1,0:T(8,128)(2,1)S(1)}, bf16[4,1024,128]{2,1,0:T(8,128)(2,1)S(1)}, u32[]{:S(2)}, u32[]{:S(2)}) collective-permute-start(bf16[4,1024,128]{2,1,0:T(8,128)(2,1)S(1)} %get-tuple-element.77.refs_4_), channel_id=1, source_target_pairs={{0,4},{4,0},{8,12},{12,8},{16,20},{20,16},{24,28},{28,24},{1,5},{5... | collective-permute-start | bytes 3145736 | tf_op jit(solution)/shard_map/ppermute | solution.py:431
  54.7 4.5 %collective-permute-start.22 = (bf16[64,256]{1,0:T(8,128)(2,1)S(1)}, bf16[64,256]{1,0:T(8,128)(2,1)S(1)}, u32[]{:S(2)}, u32[]{:S(2)}) collective-permute-start(bf16[64,256]{1,0:T(8,128)(2,1)S(1)} %get-tuple-element.74), channel_id=1, source_target_pairs={{0,1},{1,0},{2,3},{3,2},{4,5},{5,4},{6,7},{7,6},{8,9},{9,8},{10,11... | collective-permute-start | bytes 98312 | tf_op jit(solution)/shard_map/ppermute | solution.py:437
  55.0 5.4 %collective-permute-start.23 = (bf16[64,256]{1,0:T(8,128)(2,1)S(1)}, bf16[64,256]{1,0:T(8,128)(2,1)S(1)}, u32[]{:S(2)}, u32[]{:S(2)}) collective-permute-start(bf16[64,256]{1,0:T(8,128)(2,1)S(1)} %get-tuple-element.75), channel_id=1, source_target_pairs={{0,2},{1,3},{2,0},{3,1},{4,6},{5,7},{6,4},{7,5},{8,10},{9,11},{10,... | collective-permute-start | bytes 98312 | tf_op jit(solution)/shard_map/ppermute | solution.py:437
  57.4 5.7 %collective-permute-start.24 = (bf16[64,256]{1,0:T(8,128)(2,1)S(1)}, bf16[64,256]{1,0:T(8,128)(2,1)S(1)}, u32[]{:S(2)}, u32[]{:S(2)}) collective-permute-start(bf16[64,256]{1,0:T(8,128)(2,1)S(1)} %get-tuple-element.76), channel_id=1, source_target_pairs={{0,3},{1,2},{2,1},{3,0},{4,7},{5,6},{6,5},{7,4},{8,11},{9,10},{10,... | collective-permute-start | bytes 98312 | tf_op jit(solution)/shard_map/ppermute | solution.py:437

commit v15 on v14

--- a/solution.py
+++ b/solution.py
@@ -347,14 +347,19 @@
     local = normed_refs[0].shape[0]
     depth = pieces.shape[2]
     for step in range(group):
-        for piece in range(windows):
+        for piece in range(windows if depth % LANES else 0):
             pieces[piece, step * local : (step + 1) * local, :] = normed_refs[step][
                 :, piece * depth : (piece + 1) * depth
             ]
     mixed = 0.0
     for step in range(copies):
         slot = copy_index ^ step
-        normed = jnp.concatenate([pieces[piece * copies + slot] for piece in range(parts)], axis=1)
+        if depth % LANES:
+            normed = jnp.concatenate([pieces[piece * copies + slot] for piece in range(parts)], axis=1)
+        else:
+            places = [pl.multiple_of((piece * copies + slot) * depth, LANES) for piece in range(parts)]
+            columns = [[ref[:, pl.ds(at, depth)] for at in places] for ref in normed_refs]
+            normed = jnp.concatenate([jnp.concatenate(row, axis=1) for row in columns], axis=0)
         weights = stack_refs[step][...].reshape(parts * depth, stack_refs[step].shape[2])
         mixed += jnp.dot(normed, weights, preferred_element_type=F32)
     mixed = mixed.astype(BF16)

time: 64.6 us -> 64.5 us (level)
  no operation moved by 1% of the time
where the time goes in v15:
time: 64.5 us; the launch traced here: 64.2 us
  starting transfers between devices  30.4 us (47%)
  waiting for transfers between devices  18.3 us (28%)
  Pallas kernels  12.6 us (20%)
  local copies, waits for them, and re-layouts  2.13 us (3%)
  between operations  0.78 us (1%)
    ppermute x9, starting transfers between devices, to_part(): return lax.ppermute(block, 'dp', pairs)  13.5 us
    ppermute x6, waiting for transfers between devices, to_plane(): return lax.ppermute(block, 'seq', [(i, i ^ step) for i in range(group)])  13.3 us
    ppermute x7, starting transfers between devices, to_window(): return lax.ppermute(block, 'dp', [(i, i ^ step) for i in range(windows)])  6.04 us
    ppermute x6, starting transfers between devices, to_plane(): return lax.ppermute(block, 'seq', [(i, i ^ step) for i in range(group)])  5.52 us
    pallas_call x1, Pallas kernels, on_device(): pl.pallas_call(functools.partial(conv_kernel, parts, width), out_shape=tu...  4.77 us
    ppermute x1, starting transfers between devices, on_device(): rim = lax.ppermute(audio[:, audio.shape[1] - RIM:], ('dp', 'seq'), route)  4.63 us
    ppermute x7, waiting for transfers between devices, to_window(): return lax.ppermute(block, 'dp', [(i, i ^ step) for i in range(windows)])  4.21 us
    pallas_call x1, Pallas kernels, on_device(): pl.pallas_call(functools.partial(mel_kernel, parts, group), out_shape=tup...  3.64 us
  transfers between devices with their start and end apart: 26, of which 10 were waited for; matrix products, arithmetic and copies ran while one was open for 1% of the time, Pallas kernels for 15%

profile of v15, /device:TPU:0, one launch (start us, length us, event | category | flops | bytes accessed | tf_op | source)
XLA Modules:
  0.0 64.2 jit_solution(10865470201291375608)
XLA Ops:
  0.6 0.5 collective-permute-start.1
  1.1 0.8 %slice.3 = f32[8,1024]{1,0:T(8,128)S(1)} slice(f32[8,5120]{1,0:T(8,128)} %audio_ref.1), slice={[0:8], [4096:5120]} | slice | bytes 65536 | tf_op jit(solution)/shard_map/slice | solution.py:428
  1.9 4.6 %collective-permute-start = (f32[8,1024]{1,0:T(8,128)S(1)}, f32[8,1024]{1,0:T(8,128)S(1)}, u32[]{:S(2)}, u32[]{:S(2)}) collective-permute-start(f32[8,1024]{1,0:T(8,128)S(1)} %slice.3), channel_id=1, source_target_pairs={{0,1},{1,2},{2,3},{3,4},{4,5},{5,6},{6,7},{7,8},{8,9},{9,10},{10,1... | collective-permute-start | bytes 98312 | tf_op jit(solution)/shard_map/ppermute | solution.py:428
  6.6 1.6 %collective-permute-start.5 = (bf16[1024,128]{1,0:T(8,128)(2,1)}, bf16[1024,128]{1,0:T(8,128)(2,1)S(1)}, u32[]{:S(2)}, u32[]{:S(2)}) collective-permute-start(bf16[1024,128]{1,0:T(8,128)(2,1)} %refs_6_), channel_id=1, source_target_pairs={{0,8},{4,12},{8,0},{12,4},{16,24},{20,28},{24,16},{28,20},{1,9},{5... | collective-permute-start | bytes 786440 | tf_op jit(solution)/shard_map/ppermute | solution.py:432
  8.1 1.5 %collective-permute-start.6 = (bf16[1024,128]{1,0:T(8,128)(2,1)}, bf16[1024,128]{1,0:T(8,128)(2,1)}, u32[]{:S(2)}, u32[]{:S(2)}) collective-permute-start(bf16[1024,128]{1,0:T(8,128)(2,1)} %refs_6_), channel_id=1, source_target_pairs={{0,16},{4,20},{8,24},{12,28},{16,0},{20,4},{24,8},{28,12},{1,17},{... | collective-permute-start | bytes 786440 | tf_op jit(solution)/shard_map/ppermute | solution.py:432
  9.6 0.0 collective-permute-done.rim_ref
  9.6 0.6 copy-done.9
  10.2 3.6 %log_mel.1 = (bf16[72,128]{1,0:T(8,128)(2,1)}, bf16[72,128]{1,0:T(8,128)(2,1)}, bf16[72,128]{1,0:T(8,128)(2,1)}, bf16[72,128]{1,0:T(8,128)(2,1)}, bf16[128,768]{1,0:T(8,128)(2,1)}) custom-call(s32[8]{0:T(128)} %slots_ref.1, f32[8,1024]{1,0:T(8,128)} %copy-done.9, f32[8,5120]{1,0:T(8,128)} %audio_ref.1, f32[264,640]{1,0:T(8,128)} %constant.2.clone.table_ref, ...), custom_call_target="tpu_custom_call" | custom-call | flops 10000000000 | bytes 2000000 | tf_op jit(solution)/shard_map/log_mel/pallas_call | solution.py:448
  13.9 3.0 %collective-permute-start.2 = (bf16[72,128]{1,0:T(8,128)(2,1)}, bf16[72,128]{1,0:T(8,128)(2,1)S(1)}, u32[]{:S(2)}, u32[]{:S(2)}) collective-permute-start(bf16[72,128]{1,0:T(8,128)(2,1)} %get-tuple-element.45), channel_id=1, source_target_pairs={{0,8},{4,12},{8,0},{12,4},{16,24},{20,28},{24,16},{28,20},{1,9},{5... | collective-permute-start | bytes 55304 | tf_op jit(solution)/shard_map/ppermute | solution.py:432
  16.9 1.6 %collective-permute-start.3 = (bf16[72,128]{1,0:T(8,128)(2,1)}, bf16[72,128]{1,0:T(8,128)(2,1)S(1)}, u32[]{:S(2)}, u32[]{:S(2)}) collective-permute-start(bf16[72,128]{1,0:T(8,128)(2,1)} %get-tuple-element.46), channel_id=1, source_target_pairs={{0,16},{4,20},{8,24},{12,28},{16,0},{20,4},{24,8},{28,12},{1,17},{... | collective-permute-start | bytes 55304 | tf_op jit(solution)/shard_map/ppermute | solution.py:432
  18.5 0.9 %collective-permute-start.4 = (bf16[72,128]{1,0:T(8,128)(2,1)}, bf16[72,128]{1,0:T(8,128)(2,1)S(1)}, u32[]{:S(2)}, u32[]{:S(2)}) collective-permute-start(bf16[72,128]{1,0:T(8,128)(2,1)} %get-tuple-element.47), channel_id=1, source_target_pairs={{0,24},{4,28},{8,16},{12,20},{16,8},{20,12},{24,0},{28,4},{1,25},{... | collective-permute-start | bytes 55304 | tf_op jit(solution)/shard_map/ppermute | solution.py:432
  19.4 2.0 %collective-permute-start.16 = (bf16[128,768]{1,0:T(8,128)(2,1)}, bf16[128,768]{1,0:T(8,128)(2,1)S(1)}, u32[]{:S(2)}, u32[]{:S(2)}) collective-permute-start(bf16[128,768]{1,0:T(8,128)(2,1)} %get-tuple-element.62.refs_8_), channel_id=1, source_target_pairs={{0,24},{4,28},{8,16},{12,20},{16,8},{20,12},{24,0},{28,4},{1,25},{... | collective-permute-start | bytes 589832 | tf_op jit(solution)/shard_map/ppermute | solution.py:432
  21.5 0.4 collective-permute-start.15
  21.9 1.1 %collective-permute-start.14 = (bf16[128,768]{1,0:T(8,128)(2,1)}, bf16[128,768]{1,0:T(8,128)(2,1)S(1)}, u32[]{:S(2)}, u32[]{:S(2)}) collective-permute-start(bf16[128,768]{1,0:T(8,128)(2,1)} %get-tuple-element.62.refs_8_), channel_id=1, source_target_pairs={{0,8},{4,12},{8,0},{12,4},{16,24},{20,28},{24,16},{28,20},{1,9},{5... | collective-permute-start | bytes 589832 | tf_op jit(solution)/shard_map/ppermute | solution.py:432
  23.0 0.7 %collective-permute-done.4.refs_3_ = bf16[72,128]{1,0:T(8,128)(2,1)S(1)} collective-permute-done((bf16[72,128]{1,0:T(8,128)(2,1)}, bf16[72,128]{1,0:T(8,128)(2,1)S(1)}, u32[]{:S(2)}, u32[]{:S(2)}) %collective-permute-start.4) | collective-permute-done | bytes 18464 | tf_op jit(solution)/shard_map/ppermute | solution.py:432
  23.8 0.0 copy-start.8
  23.8 0.7 %copy-done.8 = bf16[72,128]{1,0:T(8,128)(2,1)S(1)} copy-done((bf16[72,128]{1,0:T(8,128)(2,1)S(1)}, bf16[72,128]{1,0:T(8,128)(2,1)}, u32[]{:S(2)}) %copy-start.8) | copy-done | bytes 18456
  24.5 4.8 %conv.1 = (bf16[32,1024]{1,0:T(8,128)(2,1)S(1)}, bf16[32,1024]{1,0:T(8,128)(2,1)S(1)}, bf16[32,1024]{1,0:T(8,128)(2,1)S(1)}, bf16[32,1024]{1,0:T(8,128)(2,1)S(1)...) custom-call(bf16[9,256]{1,0:T(8,128)(2,1)S(1)} %copy-done.4, ...), custom_call_target="tpu_custom_call" | custom-call | flops 2000000000 | bytes 4000000 | tf_op jit(solution)/shard_map/conv/pallas_call | solution.py:471
  29.3 0.0 copy-start.3
  29.3 0.0 copy-start.5
  29.3 0.0 copy-start.6
  29.3 0.0 copy-start.7
  29.3 0.1 collective-permute-start.7
  29.4 1.3 %collective-permute-start.8 = (bf16[32,1024]{1,0:T(8,128)(2,1)S(1)}, bf16[32,1024]{1,0:T(8,128)(2,1)S(1)}, u32[]{:S(2)}, u32[]{:S(2)}) collective-permute-start(bf16[32,1024]{1,0:T(8,128)(2,1)S(1)} %get-tuple-element.55), channel_id=1, source_target_pairs={{0,24},{4,28},{8,16},{12,20},{16,8},{20,12},{24,0},{28,4},{1,25},{... | collective-permute-start | bytes 196616 | tf_op jit(solution)/shard_map/ppermute | solution.py:439
  30.7 2.3 %collective-permute-start.9 = (bf16[32,1024]{1,0:T(8,128)(2,1)S(1)}, bf16[32,1024]{1,0:T(8,128)(2,1)S(1)}, u32[]{:S(2)}, u32[]{:S(2)}) collective-permute-start(bf16[32,1024]{1,0:T(8,128)(2,1)S(1)} %get-tuple-element.56), channel_id=1, source_target_pairs={{0,20},{4,16},{8,28},{12,24},{16,4},{20,0},{24,12},{28,8},{1,21},{... | collective-permute-start | bytes 196616 | tf_op jit(solution)/shard_map/ppermute | solution.py:439
  33.0 0.8 %collective-permute-start.10 = (bf16[32,1024]{1,0:T(8,128)(2,1)S(1)}, bf16[32,1024]{1,0:T(8,128)(2,1)S(1)}, u32[]{:S(2)}, u32[]{:S(2)}) collective-permute-start(bf16[32,1024]{1,0:T(8,128)(2,1)S(1)} %get-tuple-element.57), channel_id=1, source_target_pairs={{0,16},{4,20},{8,24},{12,28},{16,0},{20,4},{24,8},{28,12},{1,17},{... | collective-permute-start | bytes 196616 | tf_op jit(solution)/shard_map/ppermute | solution.py:439
  33.8 0.3 collective-permute-done.7.refs_0_
  34.1 1.5 %collective-permute-start.12 = (bf16[32,1024]{1,0:T(8,128)(2,1)S(1)}, bf16[32,1024]{1,0:T(8,128)(2,1)S(1)}, u32[]{:S(2)}, u32[]{:S(2)}) collective-permute-start(bf16[32,1024]{1,0:T(8,128)(2,1)S(1)} %get-tuple-element.59), channel_id=1, source_target_pairs={{0,8},{4,12},{8,0},{12,4},{16,24},{20,28},{24,16},{28,20},{1,9},{5... | collective-permute-start | bytes 196616 | tf_op jit(solution)/shard_map/ppermute | solution.py:439
  35.6 0.1 collective-permute-start.13
  35.7 1.0 %collective-permute-done.9.refs_2_ = bf16[32,1024]{1,0:T(8,128)(2,1)S(1)} collective-permute-done((bf16[32,1024]{1,0:T(8,128)(2,1)S(1)}, bf16[32,1024]{1,0:T(8,128)(2,1)S(1)}, u32[]{:S(2)}, u32[]{:S(2)}) %collective-permute-start.9) | collective-permute-done | bytes 65568 | tf_op jit(solution)/shard_map/ppermute | solution.py:439
  36.7 1.5 %collective-permute-done.10.refs_3_ = bf16[32,1024]{1,0:T(8,128)(2,1)S(1)} collective-permute-done((bf16[32,1024]{1,0:T(8,128)(2,1)S(1)}, bf16[32,1024]{1,0:T(8,128)(2,1)S(1)}, u32[]{:S(2)}, u32[]{:S(2)}) %collective-permute-start.10) | collective-permute-done | bytes 65568 | tf_op jit(solution)/shard_map/ppermute | solution.py:439
  38.2 1.4 %collective-permute-done.12.refs_5_ = bf16[32,1024]{1,0:T(8,128)(2,1)S(1)} collective-permute-done((bf16[32,1024]{1,0:T(8,128)(2,1)S(1)}, bf16[32,1024]{1,0:T(8,128)(2,1)S(1)}, u32[]{:S(2)}, u32[]{:S(2)}) %collective-permute-start.12) | collective-permute-done | bytes 65568 | tf_op jit(solution)/shard_map/ppermute | solution.py:439
  39.6 0.5 layer_norm.1
  40.1 0.2 collective-permute-start.20
  40.3 1.3 %collective-permute-start.21 = (bf16[1024,128]{1,0:T(8,128)(2,1)S(1)}, bf16[1024,128]{1,0:T(8,128)(2,1)S(1)}, u32[]{:S(2)}, u32[]{:S(2)}) collective-permute-start(bf16[1024,128]{1,0:T(8,128)(2,1)S(1)} %copy-done.3), channel_id=1, source_target_pairs={{0,24},{4,28},{8,16},{12,20},{16,8},{20,12},{24,0},{28,4},{1,25},{... | collective-permute-start | bytes 786440 | tf_op jit(solution)/shard_map/ppermute | solution.py:432
  41.6 1.1 %collective-permute-start.17 = (bf16[64,1024]{1,0:T(8,128)(2,1)S(1)}, bf16[64,1024]{1,0:T(8,128)(2,1)S(1)}, u32[]{:S(2)}, u32[]{:S(2)}) collective-permute-start(bf16[64,1024]{1,0:T(8,128)(2,1)S(1)} %get-tuple-element.68.refs_0_), channel_id=1, source_target_pairs={{0,1},{1,0},{2,3},{3,2},{4,5},{5,4},{6,7},{7,6},{8,9},{9,8},{10,11... | collective-permute-start | bytes 393224 | tf_op jit(solution)/shard_map/ppermute | solution.py:442
  42.6 5.2 %collective-permute-done.18.refs_2_ = bf16[64,1024]{1,0:T(8,128)(2,1)S(1)} collective-permute-done((bf16[64,1024]{1,0:T(8,128)(2,1)S(1)}, bf16[64,1024]{1,0:T(8,128)(2,1)S(1)}, u32[]{:S(2)}, u32[]{:S(2)}) %collective-permute-start.18) | collective-permute-done | bytes 131104 | tf_op jit(solution)/shard_map/ppermute | solution.py:442
  47.8 1.3 %mask.1 = (bf16[64,1024]{1,0:T(8,128)(2,1)}, f32[4,64]{1,0:T(4,128)S(1)}, f32[64,1]{1,0:T(8,128)S(1)}) custom-call(s32[8]{0:T(128)S(1)} %copy-done.5, s32[8]{0:T(128)S(1)} %copy-done.6, s32[8]{0:T(128)S(1)} %copy-done.7, bf16[64,1024]{1,0:T(8,128)(2,1)S(1)} %get-tuple-element.63.rows_ref), custom_call_target="tpu_custom_call" | custom-call | flops 100000000 | bytes 1000000 | tf_op jit(solution)/shard_map/mask/pallas_call | solution.py:502
  49.1 0.7 %collective-permute-done.17.refs_1_ = bf16[64,1024]{1,0:T(8,128)(2,1)S(1)} collective-permute-done((bf16[64,1024]{1,0:T(8,128)(2,1)S(1)}, bf16[64,1024]{1,0:T(8,128)(2,1)S(1)}, u32[]{:S(2)}, u32[]{:S(2)}) %collective-permute-start.17) | collective-permute-done | bytes 131104 | tf_op jit(solution)/shard_map/ppermute | solution.py:442
  49.8 3.4 %collective-permute-done.19.refs_3_ = bf16[64,1024]{1,0:T(8,128)(2,1)S(1)} collective-permute-done((bf16[64,1024]{1,0:T(8,128)(2,1)S(1)}, bf16[64,1024]{1,0:T(8,128)(2,1)S(1)}, u32[]{:S(2)}, u32[]{:S(2)}) %collective-permute-start.19) | collective-permute-done | bytes 131104 | tf_op jit(solution)/shard_map/ppermute | solution.py:442
  53.2 1.3 %attention.1 = (bf16[64,256]{1,0:T(8,128)(2,1)S(1)}, bf16[64,256]{1,0:T(8,128)(2,1)S(1)}, bf16[64,256]{1,0:T(8,128)(2,1)S(1)}, bf16[64,256]{1,0:T(8,128)(2,1)S(1)}, bf16[4,1024,128]{2,1,0:T(8,128)(2,1)S(1)}) custom-call(f32[4,64]{1,0:T(4,128)S(1)} %get-tuple-element.66.keys_ref, bf16[64,1024]{1,0:T(8,128)(2,1)S(1)} %get-tuple-element.68.refs_0_, ...), custom_call_target="tpu_custom_call" | custom-call | flops 1000000000 | bytes 2000000 | tf_op jit(solution)/shard_map/attention/pallas_call | solution.py:522
  54.5 0.1 collective-permute-start.25
  54.6 0.3 collective-permute-start.22
  55.0 2.4 %collective-permute-start.23 = (bf16[64,256]{1,0:T(8,128)(2,1)S(1)}, bf16[64,256]{1,0:T(8,128)(2,1)S(1)}, u32[]{:S(2)}, u32[]{:S(2)}) collective-permute-start(bf16[64,256]{1,0:T(8,128)(2,1)S(1)} %get-tuple-element.75), channel_id=1, source_target_pairs={{0,2},{1,3},{2,0},{3,1},{4,6},{5,7},{6,4},{7,5},{8,10},{9,11},{10,... | collective-permute-start | bytes 98312 | tf_op jit(solution)/shard_map/ppermute | solution.py:442
  57.4 1.7 %collective-permute-start.24 = (bf16[64,256]{1,0:T(8,128)(2,1)S(1)}, bf16[64,256]{1,0:T(8,128)(2,1)S(1)}, u32[]{:S(2)}, u32[]{:S(2)}) collective-permute-start(bf16[64,256]{1,0:T(8,128)(2,1)S(1)} %get-tuple-element.76), channel_id=1, source_target_pairs={{0,3},{1,2},{2,1},{3,0},{4,7},{5,6},{6,5},{7,4},{8,11},{9,10},{10,... | collective-permute-start | bytes 98312 | tf_op jit(solution)/shard_map/ppermute | solution.py:442
  59.1 1.3 %collective-permute-done.23.refs_2_ = bf16[64,256]{1,0:T(8,128)(2,1)S(1)} collective-permute-done((bf16[64,256]{1,0:T(8,128)(2,1)S(1)}, bf16[64,256]{1,0:T(8,128)(2,1)S(1)}, u32[]{:S(2)}, u32[]{:S(2)}) %collective-permute-start.23) | collective-permute-done | bytes 32800 | tf_op jit(solution)/shard_map/ppermute | solution.py:442
  60.3 2.8 %collective-permute-done.24.refs_3_ = bf16[64,256]{1,0:T(8,128)(2,1)S(1)} collective-permute-done((bf16[64,256]{1,0:T(8,128)(2,1)S(1)}, bf16[64,256]{1,0:T(8,128)(2,1)S(1)}, u32[]{:S(2)}, u32[]{:S(2)}) %collective-permute-start.24) | collective-permute-done | bytes 32800 | tf_op jit(solution)/shard_map/ppermute | solution.py:442
  63.1 1.1 %output.1 = bf16[64,1024]{1,0:T(8,128)(2,1)} custom-call(f32[64,1]{1,0:T(8,128)S(1)} %get-tuple-element.65.valid_ref, bf16[64,256]{1,0:T(8,128)(2,1)S(1)} %get-tuple-element.73.refs_0_, bf16[64,256]{1,0:T(8,128)(2,1)S(1)} %collective-permute-done.22.refs_1_, bf16[64,256]{1,0:T(8,128)(2,1)S(1)} %collective-permute-done.23.refs_2_, ...), custom_call_target="tpu_custom_call" | custom-call | flops 100000000 | bytes 3000000 | tf_op jit(solution)/shard_map/output/pallas_call | solution.py:541
  (31 shorter events, 0.1 us)
Async XLA Ops:
  0.6 13.3 %collective-permute-start.1 = (bf16[640,1024]{1,0:T(8,128)(2,1)}, bf16[640,1024]{1,0:T(8,128)(2,1)S(1)}, u32[]{:S(2)}, u32[]{:S(2)}) collective-permute-start(bf16[640,1024]{1,0:T(8,128)(2,1)} %refs_4_), channel_id=1, source_target_pairs={{0,4},{4,0},{8,12},{12,8},{16,20},{20,16},{24,28},{28,24},{1,5},{5... | collective-permute-start | bytes 3932168 | tf_op jit(solution)/shard_map/ppermute | solution.py:436
  1.9 21.9 %copy-start.1 = (bf16[640,1024]{1,0:T(8,128)(2,1)S(1)}, bf16[640,1024]{1,0:T(8,128)(2,1)}, u32[]{:S(2)}) copy-start(bf16[640,1024]{1,0:T(8,128)(2,1)} %refs_4_) | copy-start | bytes 3932164
  1.9 21.9 %copy-start.2 = (bf16[2304,256]{1,0:T(8,128)(2,1)S(1)}, bf16[2304,256]{1,0:T(8,128)(2,1)}, u32[]{:S(2)}) copy-start(bf16[2304,256]{1,0:T(8,128)(2,1)} %conv2_ref.1) | copy-start | bytes 3538948
  1.9 21.9 %copy-start.4 = (bf16[9,256]{1,0:T(8,128)(2,1)S(1)}, bf16[9,256]{1,0:T(8,128)(2,1)}, u32[]{:S(2)}) copy-start(bf16[9,256]{1,0:T(8,128)(2,1)} %conv1_ref.1) | copy-start | bytes 13828
  1.9 7.7 %collective-permute-start = (f32[8,1024]{1,0:T(8,128)S(1)}, f32[8,1024]{1,0:T(8,128)S(1)}, u32[]{:S(2)}, u32[]{:S(2)}) collective-permute-start(f32[8,1024]{1,0:T(8,128)S(1)} %slice.3), channel_id=1, source_target_pairs={{0,1},{1,2},{2,3},{3,4},{4,5},{5,6},{6,7},{7,8},{8,9},{9,10},{10,1... | collective-permute-start | bytes 98312 | tf_op jit(solution)/shard_map/ppermute | solution.py:428
  6.6 12.9 %collective-permute-start.5 = (bf16[1024,128]{1,0:T(8,128)(2,1)}, bf16[1024,128]{1,0:T(8,128)(2,1)S(1)}, u32[]{:S(2)}, u32[]{:S(2)}) collective-permute-start(bf16[1024,128]{1,0:T(8,128)(2,1)} %refs_6_), channel_id=1, source_target_pairs={{0,8},{4,12},{8,0},{12,4},{16,24},{20,28},{24,16},{28,20},{1,9},{5... | collective-permute-start | bytes 786440 | tf_op jit(solution)/shard_map/ppermute | solution.py:432
  8.1 13.4 %collective-permute-start.6 = (bf16[1024,128]{1,0:T(8,128)(2,1)}, bf16[1024,128]{1,0:T(8,128)(2,1)}, u32[]{:S(2)}, u32[]{:S(2)}) collective-permute-start(bf16[1024,128]{1,0:T(8,128)(2,1)} %refs_6_), channel_id=1, source_target_pairs={{0,16},{4,20},{8,24},{12,28},{16,0},{20,4},{24,8},{28,12},{1,17},{... | collective-permute-start | bytes 786440 | tf_op jit(solution)/shard_map/ppermute | solution.py:432
  9.6 0.6 copy-start.9
  13.9 8.0 %collective-permute-start.2 = (bf16[72,128]{1,0:T(8,128)(2,1)}, bf16[72,128]{1,0:T(8,128)(2,1)S(1)}, u32[]{:S(2)}, u32[]{:S(2)}) collective-permute-start(bf16[72,128]{1,0:T(8,128)(2,1)} %get-tuple-element.45), channel_id=1, source_target_pairs={{0,8},{4,12},{8,0},{12,4},{16,24},{20,28},{24,16},{28,20},{1,9},{5... | collective-permute-start | bytes 55304 | tf_op jit(solution)/shard_map/ppermute | solution.py:432
  16.9 6.1 %collective-permute-start.3 = (bf16[72,128]{1,0:T(8,128)(2,1)}, bf16[72,128]{1,0:T(8,128)(2,1)S(1)}, u32[]{:S(2)}, u32[]{:S(2)}) collective-permute-start(bf16[72,128]{1,0:T(8,128)(2,1)} %get-tuple-element.46), channel_id=1, source_target_pairs={{0,16},{4,20},{8,24},{12,28},{16,0},{20,4},{24,8},{28,12},{1,17},{... | collective-permute-start | bytes 55304 | tf_op jit(solution)/shard_map/ppermute | solution.py:432
  18.5 5.2 %collective-permute-start.4 = (bf16[72,128]{1,0:T(8,128)(2,1)}, bf16[72,128]{1,0:T(8,128)(2,1)S(1)}, u32[]{:S(2)}, u32[]{:S(2)}) collective-permute-start(bf16[72,128]{1,0:T(8,128)(2,1)} %get-tuple-element.47), channel_id=1, source_target_pairs={{0,24},{4,28},{8,16},{12,20},{16,8},{20,12},{24,0},{28,4},{1,25},{... | collective-permute-start | bytes 55304 | tf_op jit(solution)/shard_map/ppermute | solution.py:432
  19.4 20.2 %copy-start = (bf16[128,768]{1,0:T(8,128)(2,1)S(1)}, bf16[128,768]{1,0:T(8,128)(2,1)}, u32[]{:S(2)}) copy-start(bf16[128,768]{1,0:T(8,128)(2,1)} %get-tuple-element.62.refs_8_) | copy-start | bytes 589828
  19.4 11.3 %collective-permute-start.16 = (bf16[128,768]{1,0:T(8,128)(2,1)}, bf16[128,768]{1,0:T(8,128)(2,1)S(1)}, u32[]{:S(2)}, u32[]{:S(2)}) collective-permute-start(bf16[128,768]{1,0:T(8,128)(2,1)} %get-tuple-element.62.refs_8_), channel_id=1, source_target_pairs={{0,24},{4,28},{8,16},{12,20},{16,8},{20,12},{24,0},{28,4},{1,25},{... | collective-permute-start | bytes 589832 | tf_op jit(solution)/shard_map/ppermute | solution.py:432
  21.5 11.5 %collective-permute-start.15 = (bf16[128,768]{1,0:T(8,128)(2,1)}, bf16[128,768]{1,0:T(8,128)(2,1)S(1)}, u32[]{:S(2)}, u32[]{:S(2)}) collective-permute-start(bf16[128,768]{1,0:T(8,128)(2,1)} %get-tuple-element.62.refs_8_), channel_id=1, source_target_pairs={{0,16},{4,20},{8,24},{12,28},{16,0},{20,4},{24,8},{28,12},{1,17},{... | collective-permute-start | bytes 589832 | tf_op jit(solution)/shard_map/ppermute | solution.py:432
  21.9 11.9 %collective-permute-start.14 = (bf16[128,768]{1,0:T(8,128)(2,1)}, bf16[128,768]{1,0:T(8,128)(2,1)S(1)}, u32[]{:S(2)}, u32[]{:S(2)}) collective-permute-start(bf16[128,768]{1,0:T(8,128)(2,1)} %get-tuple-element.62.refs_8_), channel_id=1, source_target_pairs={{0,8},{4,12},{8,0},{12,4},{16,24},{20,28},{24,16},{28,20},{1,9},{5... | collective-permute-start | bytes 589832 | tf_op jit(solution)/shard_map/ppermute | solution.py:432
  23.8 0.7 %copy-start.8 = (bf16[72,128]{1,0:T(8,128)(2,1)S(1)}, bf16[72,128]{1,0:T(8,128)(2,1)}, u32[]{:S(2)}) copy-start(bf16[72,128]{1,0:T(8,128)(2,1)} %get-tuple-element.48.refs_0_) | copy-start | bytes 55300
  29.3 11.0 %copy-start.3 = (bf16[1024,128]{1,0:T(8,128)(2,1)S(1)}, bf16[1024,128]{1,0:T(8,128)(2,1)}, u32[]{:S(2)}) copy-start(bf16[1024,128]{1,0:T(8,128)(2,1)} %refs_6_) | copy-start | bytes 786436
  29.3 18.5 %copy-start.5 = (s32[8]{0:T(128)S(1)}, s32[8]{0:T(128)}, u32[]{:S(2)}) copy-start(s32[8]{0:T(128)} %slots_ref.1) | copy-start | bytes 100
  29.3 18.5 %copy-start.6 = (s32[8]{0:T(128)S(1)}, s32[8]{0:T(128)}, u32[]{:S(2)}) copy-start(s32[8]{0:T(128)} %starts_ref.1) | copy-start | bytes 100
  29.3 18.5 %copy-start.7 = (s32[8]{0:T(128)S(1)}, s32[8]{0:T(128)}, u32[]{:S(2)}) copy-start(s32[8]{0:T(128)} %lengths_ref.1) | copy-start | bytes 100
  29.3 4.7 %collective-permute-start.7 = (bf16[32,1024]{1,0:T(8,128)(2,1)S(1)}, bf16[32,1024]{1,0:T(8,128)(2,1)S(1)}, u32[]{:S(2)}, u32[]{:S(2)}) collective-permute-start(bf16[32,1024]{1,0:T(8,128)(2,1)S(1)} %get-tuple-element.54), channel_id=1, source_target_pairs={{0,28},{4,24},{8,20},{12,16},{16,12},{20,8},{24,4},{28,0},{1,29},{... | collective-permute-start | bytes 196616 | tf_op jit(solution)/shard_map/ppermute | solution.py:439
  29.4 6.2 %collective-permute-start.8 = (bf16[32,1024]{1,0:T(8,128)(2,1)S(1)}, bf16[32,1024]{1,0:T(8,128)(2,1)S(1)}, u32[]{:S(2)}, u32[]{:S(2)}) collective-permute-start(bf16[32,1024]{1,0:T(8,128)(2,1)S(1)} %get-tuple-element.55), channel_id=1, source_target_pairs={{0,24},{4,28},{8,16},{12,20},{16,8},{20,12},{24,0},{28,4},{1,25},{... | collective-permute-start | bytes 196616 | tf_op jit(solution)/shard_map/ppermute | solution.py:439
  30.7 6.0 %collective-permute-start.9 = (bf16[32,1024]{1,0:T(8,128)(2,1)S(1)}, bf16[32,1024]{1,0:T(8,128)(2,1)S(1)}, u32[]{:S(2)}, u32[]{:S(2)}) collective-permute-start(bf16[32,1024]{1,0:T(8,128)(2,1)S(1)} %get-tuple-element.56), channel_id=1, source_target_pairs={{0,20},{4,16},{8,28},{12,24},{16,4},{20,0},{24,12},{28,8},{1,21},{... | collective-permute-start | bytes 196616 | tf_op jit(solution)/shard_map/ppermute | solution.py:439
  33.0 5.2 %collective-permute-start.10 = (bf16[32,1024]{1,0:T(8,128)(2,1)S(1)}, bf16[32,1024]{1,0:T(8,128)(2,1)S(1)}, u32[]{:S(2)}, u32[]{:S(2)}) collective-permute-start(bf16[32,1024]{1,0:T(8,128)(2,1)S(1)} %get-tuple-element.57), channel_id=1, source_target_pairs={{0,16},{4,20},{8,24},{12,28},{16,0},{20,4},{24,8},{28,12},{1,17},{... | collective-permute-start | bytes 196616 | tf_op jit(solution)/shard_map/ppermute | solution.py:439
  33.8 4.4 %collective-permute-start.11 = (bf16[32,1024]{1,0:T(8,128)(2,1)S(1)}, bf16[32,1024]{1,0:T(8,128)(2,1)S(1)}, u32[]{:S(2)}, u32[]{:S(2)}) collective-permute-start(bf16[32,1024]{1,0:T(8,128)(2,1)S(1)} %get-tuple-element.58), channel_id=1, source_target_pairs={{0,12},{4,8},{8,4},{12,0},{16,28},{20,24},{24,20},{28,16},{1,13},{... | collective-permute-start | bytes 196616 | tf_op jit(solution)/shard_map/ppermute | solution.py:439
  34.1 5.5 %collective-permute-start.12 = (bf16[32,1024]{1,0:T(8,128)(2,1)S(1)}, bf16[32,1024]{1,0:T(8,128)(2,1)S(1)}, u32[]{:S(2)}, u32[]{:S(2)}) collective-permute-start(bf16[32,1024]{1,0:T(8,128)(2,1)S(1)} %get-tuple-element.59), channel_id=1, source_target_pairs={{0,8},{4,12},{8,0},{12,4},{16,24},{20,28},{24,16},{28,20},{1,9},{5... | collective-permute-start | bytes 196616 | tf_op jit(solution)/shard_map/ppermute | solution.py:439
  35.6 4.0 %collective-permute-start.13 = (bf16[32,1024]{1,0:T(8,128)(2,1)S(1)}, bf16[32,1024]{1,0:T(8,128)(2,1)S(1)}, u32[]{:S(2)}, u32[]{:S(2)}) collective-permute-start(bf16[32,1024]{1,0:T(8,128)(2,1)S(1)} %get-tuple-element.60), channel_id=1, source_target_pairs={{0,4},{4,0},{8,12},{12,8},{16,20},{20,16},{24,28},{28,24},{1,5},{5... | collective-permute-start | bytes 196616 | tf_op jit(solution)/shard_map/ppermute | solution.py:439
  40.1 13.1 %collective-permute-start.20 = (bf16[4,128,768]{2,1,0:T(8,128)(2,1)S(1)}, bf16[4,128,768]{2,1,0:T(8,128)(2,1)S(1)}, u32[]{:S(2)}, u32[]{:S(2)}) collective-permute-start(bf16[4,128,768]{2,1,0:T(8,128)(2,1)S(1)} %get-tuple-element.69.refs_4_), channel_id=1, source_target_pairs={{0,4},{4,0},{8,12},{12,8},{16,20},{20,16},{24,28},{28,24},{1,5},{5... | collective-permute-start | bytes 2359304 | tf_op jit(solution)/shard_map/ppermute | solution.py:436
  40.3 7.6 %collective-permute-start.18 = (bf16[64,1024]{1,0:T(8,128)(2,1)S(1)}, bf16[64,1024]{1,0:T(8,128)(2,1)S(1)}, u32[]{:S(2)}, u32[]{:S(2)}) collective-permute-start(bf16[64,1024]{1,0:T(8,128)(2,1)S(1)} %get-tuple-element.68.refs_0_), channel_id=1, source_target_pairs={{0,2},{1,3},{2,0},{3,1},{4,6},{5,7},{6,4},{7,5},{8,10},{9,11},{10,... | collective-permute-start | bytes 393224 | tf_op jit(solution)/shard_map/ppermute | solution.py:442
  40.3 13.0 %collective-permute-start.21 = (bf16[1024,128]{1,0:T(8,128)(2,1)S(1)}, bf16[1024,128]{1,0:T(8,128)(2,1)S(1)}, u32[]{:S(2)}, u32[]{:S(2)}) collective-permute-start(bf16[1024,128]{1,0:T(8,128)(2,1)S(1)} %copy-done.3), channel_id=1, source_target_pairs={{0,24},{4,28},{8,16},{12,20},{16,8},{20,12},{24,0},{28,4},{1,25},{... | collective-permute-start | bytes 786440 | tf_op jit(solution)/shard_map/ppermute | solution.py:432
  41.6 8.3 %collective-permute-start.17 = (bf16[64,1024]{1,0:T(8,128)(2,1)S(1)}, bf16[64,1024]{1,0:T(8,128)(2,1)S(1)}, u32[]{:S(2)}, u32[]{:S(2)}) collective-permute-start(bf16[64,1024]{1,0:T(8,128)(2,1)S(1)} %get-tuple-element.68.refs_0_), channel_id=1, source_target_pairs={{0,1},{1,0},{2,3},{3,2},{4,5},{5,4},{6,7},{7,6},{8,9},{9,8},{10,11... | collective-permute-start | bytes 393224 | tf_op jit(solution)/shard_map/ppermute | solution.py:442
  47.8 5.4 %collective-permute-start.19 = (bf16[64,1024]{1,0:T(8,128)(2,1)S(1)}, bf16[64,1024]{1,0:T(8,128)(2,1)S(1)}, u32[]{:S(2)}, u32[]{:S(2)}) collective-permute-start(bf16[64,1024]{1,0:T(8,128)(2,1)S(1)} %collective-permute-done.18.refs_2_), channel_id=1, source_target_pairs={{0,1},{1,0},{2,3},{3,2},{4,5},{5,4},{6,7},{7,6},{8,9},{9,8},{10,11... | collective-permute-start | bytes 393224 | tf_op jit(solution)/shard_map/ppermute | solution.py:442
  54.5 8.6 %collective-permute-start.25 = (bf16[4,1024,128]{2,1,0:T(8,128)(2,1)S(1)}, bf16[4,1024,128]{2,1,0:T(8,128)(2,1)S(1)}, u32[]{:S(2)}, u32[]{:S(2)}) collective-permute-start(bf16[4,1024,128]{2,1,0:T(8,128)(2,1)S(1)} %get-tuple-element.77.refs_4_), channel_id=1, source_target_pairs={{0,4},{4,0},{8,12},{12,8},{16,20},{20,16},{24,28},{28,24},{1,5},{5... | collective-permute-start | bytes 3145736 | tf_op jit(solution)/shard_map/ppermute | solution.py:436
  54.6 4.5 %collective-permute-start.22 = (bf16[64,256]{1,0:T(8,128)(2,1)S(1)}, bf16[64,256]{1,0:T(8,128)(2,1)S(1)}, u32[]{:S(2)}, u32[]{:S(2)}) collective-permute-start(bf16[64,256]{1,0:T(8,128)(2,1)S(1)} %get-tuple-element.74), channel_id=1, source_target_pairs={{0,1},{1,0},{2,3},{3,2},{4,5},{5,4},{6,7},{7,6},{8,9},{9,8},{10,11... | collective-permute-start | bytes 98312 | tf_op jit(solution)/shard_map/ppermute | solution.py:442
  55.0 5.4 %collective-permute-start.23 = (bf16[64,256]{1,0:T(8,128)(2,1)S(1)}, bf16[64,256]{1,0:T(8,128)(2,1)S(1)}, u32[]{:S(2)}, u32[]{:S(2)}) collective-permute-start(bf16[64,256]{1,0:T(8,128)(2,1)S(1)} %get-tuple-element.75), channel_id=1, source_target_pairs={{0,2},{1,3},{2,0},{3,1},{4,6},{5,7},{6,4},{7,5},{8,10},{9,11},{10,... | collective-permute-start | bytes 98312 | tf_op jit(solution)/shard_map/ppermute | solution.py:442
  57.4 5.7 %collective-permute-start.24 = (bf16[64,256]{1,0:T(8,128)(2,1)S(1)}, bf16[64,256]{1,0:T(8,128)(2,1)S(1)}, u32[]{:S(2)}, u32[]{:S(2)}) collective-permute-start(bf16[64,256]{1,0:T(8,128)(2,1)S(1)} %get-tuple-element.76), channel_id=1, source_target_pairs={{0,3},{1,2},{2,1},{3,0},{4,7},{5,6},{6,5},{7,4},{8,11},{9,10},{10,... | collective-permute-start | bytes 98312 | tf_op jit(solution)/shard_map/ppermute | solution.py:442
